TPU v7x, 32 devices: a whole 2x2x4 slice. The times are simulated.
32 devices in a mesh: tm: 8 (over z, y), space: 4 (over x, core).
Axes of the slice: x: 2, y: 2, z: 4, core: 2. Of those that a mesh axis runs over, the one named last changes fastest.
Arguments:
- snapshots: bfloat16 [3, 2048, 4096], P(None, 'tm', 'space'), may hold values from -6 to 6
- tile_table: int32 [8, 10, 2], P('tm'), may hold values from -1 to 7, as said below
Outputs:
- gram_tiles: float32 [8, 10, 256, 256], P('tm', None, 'space')
Inputs may be any that keep to these rules, and one draw needn't show every extreme that they name: `tile_table`: every pair a <= b of block numbers below 8 stands in exactly one slot of the table, with a as row block and b as column block. In each owner's row the filled slots come first and the empty slots, -1 in both entries, last. Some owner has all 10 slots filled; owners may have no tiles.
All inputs are finite; a program needn't handle non-finite values.
Results may differ from a plain program's by a relative error of at most 0.0003.
Values may be sent and summed in bfloat16 or wider, within the bound.
No kernel may reach another device: no remote copies, remote signals or barrier semaphores. Data moves between devices by JAX's collectives and lax.ppermute only.
A program may use at most 128 MiB of HBM per device.

v0:
```python
import math

import jax
import jax.numpy as jnp
from jax import lax
from jax.sharding import PartitionSpec as P


def pair_tile(left_block, right_block):
    return jnp.einsum("kic,kjc->ij", left_block, right_block, preferred_element_type=jnp.float32)


def per_device(snapshots, tile_table):
    block_size = snapshots.shape[1]
    cells_dev = snapshots.shape[2]
    space_count = lax.axis_size("space")
    scale_factor = 1.0 / math.sqrt(3 * cells_dev * space_count)
    table = tile_table[0]
    row_block = table[:, 0]
    col_block = table[:, 1]
    slot_count = table.shape[0]
    valid = row_block >= 0
    whole = lax.all_gather(snapshots, "tm", axis=1, tiled=True)
    filled = jnp.sum(valid.astype(jnp.int32))

    def add_tile(slot, stacked):
        first = jnp.maximum(row_block[slot], 0)
        second = jnp.maximum(col_block[slot], 0)
        left_block = lax.dynamic_slice_in_dim(whole, first * block_size, block_size, 1)
        right_block = lax.dynamic_slice_in_dim(whole, second * block_size, block_size, 1)
        product = pair_tile(left_block, right_block)
        return lax.dynamic_update_index_in_dim(stacked, product, slot, 0)

    empty = jnp.zeros((slot_count, block_size, block_size), jnp.float32)
    partial_tiles = lax.fori_loop(0, filled, add_tile, empty)
    summed = lax.psum_scatter(partial_tiles, "space", scatter_dimension=1, tiled=True)
    result = summed * scale_factor
    zeros_tile = jnp.zeros_like(result)
    result = jnp.where(valid[:, None, None], result, zeros_tile)
    return result[None]


def solution(mesh):
    in_specs = (P(None, "tm", "space"), P("tm", None, None))
    out_specs = P("tm", None, "space", None)
    return jax.shard_map(
        per_device, mesh=mesh, in_specs=in_specs, out_specs=out_specs, check_vma=False
    )
```

profile of v0, /device:TPU:0, one launch (start us, length us, event | category | flops | bytes accessed | tf_op | source)
XLA Modules:
  0.0 286.0 jit_solution(10712930423423601443)
XLA Ops:
  6.5 0.0 all-gather.2.cloned.1.call-start
  6.5 0.7 all-gather.2.cloned.1.call-update
  7.3 0.0 reduce-scatter.2.cloned.1.call-start
  7.3 1.3 convert_reduce_fusion
  8.6 0.8 slice_bitcast_fusion
  9.4 179.3 %all-gather.2.cloned.1.call-done = bf16[3,2048,1024]{2,1,0:T(8,128)(2,1)} async-done(((bf16[3,256,1024]{2,1,0:T(8,128)(2,1)}), bf16[3,2048,1024]{2,1,0:T(8,128)(2,1)}) %all-gather.2.cloned.1.call-update) | async-done | bytes 12582928 | tf_op jit(solution)/shard_map/all_gather | solution.py:23
  188.7 0.2 broadcast_in_dim.23
  188.9 54.6 %while.10 = (s32[]{:T(128)}, f32[10,256,256]{2,1,0:T(8,128)S(1)}, s32[]{:T(128)}, s32[10]{0:T(128)S(1)}, bf16[3,2048,1024]{2,1,0:T(8,128)(2,1)}, /*index=5*/s32[...) while((s32[]{:T(128)}, f32[10,256,256]{2,1,0:T(8,128)S(1)}, ...), condition=%wide.region_2.3_spmd, body=%wide.region_1.2_spmd.sunk | while | flops 402653184 | bytes 3408175 | solution.py:35
  189.6 0.6 dynamic_slice.31
  190.7 0.6 dynamic_slice.30
  191.8 2.5 fusion.19
  195.0 0.6 dynamic_slice.31
  196.1 0.6 dynamic_slice.30
  197.2 2.5 fusion.19
  200.3 0.6 dynamic_slice.31
  201.5 0.6 dynamic_slice.30
  202.6 2.6 fusion.19
  205.8 0.6 dynamic_slice.31
  206.9 0.6 dynamic_slice.30
  208.0 2.5 fusion.19
  211.2 0.6 dynamic_slice.31
  212.3 0.6 dynamic_slice.30
  213.4 2.5 fusion.19
  216.6 0.6 dynamic_slice.31
  217.7 0.6 dynamic_slice.30
  218.8 2.5 fusion.19
  222.0 0.6 dynamic_slice.31
  223.1 0.6 dynamic_slice.30
  224.2 2.5 fusion.19
  227.3 0.6 dynamic_slice.31
  228.5 0.6 dynamic_slice.30
  229.6 2.5 fusion.19
  232.7 0.6 dynamic_slice.31
  233.9 0.6 dynamic_slice.30
  235.0 2.5 fusion.19
  238.1 0.6 dynamic_slice.31
  239.2 0.6 dynamic_slice.30
  240.4 2.5 fusion.19
  243.5 0.0 copy-start
  243.5 0.0 copy-start.1
  243.5 1.5 copy-done
  245.0 0.0 reduce-scatter.2.cloned.1.call-update
  245.0 0.0 copy-done.1
  245.0 32.0 %reduce-scatter.2.cloned.1.call-done = f32[10,64,256]{2,1,0:T(8,128)} async-done(((f32[10,256,256]{2,1,0:T(8,128)}), f32[10,64,256]{2,1,0:T(8,128)}) %reduce-scatter.2.cloned.1.call-update) | async-done | bytes 655376 | tf_op jit(solution)/shard_map/reduce_scatter | solution.py:36
  277.1 2.0 select_bitcast_fusion
  (1 shorter events, 0.0 us)
Async XLA Ops:
  6.5 182.2 %all-gather.2.cloned.1.call-start = ((), (), s32[]{:S(2)}) async-start(), calls=%async_computation.1 | async-start | bytes 14155776 | tf_op jit(solution)/shard_map/all_gather | solution.py:23
  7.3 269.8 %reduce-scatter.2.cloned.1.call-start = ((), (), s32[]{:S(2)}) async-start(), calls=%async_computation.2 | async-start | bytes 3276800 | tf_op jit(solution)/shard_map/reduce_scatter | solution.py:36
  243.5 1.5 copy-start
  243.5 1.5 copy-start.1
Sparse Core Ops, SparseCore 0:
  9.5 179.1 all-gather.1
  245.1 31.8 reduce-scatter.1
where the time goes:
time: 287 us; the launch traced here: 286 us
  waiting for transfers between devices  212 us (74%)
  matrix products  25.1 us (9%)
  loops' own time  18.3 us (6%)
  local copies, waits for them, and re-layouts  13.6 us (5%)
  between operations  13.4 us (5%)
  other arithmetic  3.38 us (1%)
    all_gather x1, waiting for transfers between devices, per_device(): whole = lax.all_gather(snapshots, 'tm', axis=1, tiled=True)  179 us
    reduce_scatter x1, waiting for transfers between devices, per_device(): lax.psum_scatter(partial_tiles, 'space', scatter_dimension=1, tiled=True)  32 us
    dot_general x10, matrix products, pair_tile(): jnp.einsum('kic,kjc->ij', left_block, right_block, preferred_element_type...  25.1 us
    another operation x1, loops' own time, per_device(): partial_tiles = lax.fori_loop(0, filled, add_tile, empty)  18.3 us
  transfers between devices with their start and end apart: 2, of which 2 were waited for; matrix products, arithmetic and copies ran while one was open for 1% of the time, Pallas kernels for 0%

commit v1 on v0

v1 whole, which is shorter than its diff:
```python
import math

import jax
import jax.numpy as jnp
import numpy as np
from jax import lax
from jax.sharding import PartitionSpec as P


def per_device(snapshots, tile_table):
    components, block_size, cells_dev = snapshots.shape
    space_count = lax.axis_size("space")
    block_count = lax.axis_size("tm")
    scale_factor = 1.0 / math.sqrt(components * cells_dev * space_count)
    rows_dev = block_size // space_count
    upper_rows, upper_cols = np.triu_indices(block_count)

    mixed = lax.all_to_all(snapshots, "tm", split_axis=2, concat_axis=1, tiled=True)
    deep = lax.all_gather(mixed, "space", axis=2, tiled=True)
    blocks = deep.reshape(components, block_count, block_size, deep.shape[2])
    mine = lax.dynamic_slice_in_dim(
        blocks, lax.axis_index("space") * rows_dev, rows_dev, 2
    )
    product = jnp.einsum(
        "kaic,kbjc->abij", mine, blocks, preferred_element_type=jnp.float32
    )
    pairs = product[upper_rows, upper_cols]
    summed = lax.psum(pairs, "tm") * scale_factor

    table = tile_table[0]
    row_block = table[:, 0]
    col_block = table[:, 1]
    valid = row_block >= 0
    first = jnp.maximum(row_block, 0)
    second = jnp.maximum(col_block, 0)
    pair = first * block_count - (first * (first - 1)) // 2 + second - first
    result = summed[pair]
    result = jnp.where(valid[:, None, None], result, jnp.zeros_like(result))
    return result[None]


def solution(mesh):
    in_specs = (P(None, "tm", "space"), P("tm", None, None))
    out_specs = P("tm", None, "space", None)
    return jax.shard_map(
        per_device, mesh=mesh, in_specs=in_specs, out_specs=out_specs, check_vma=False
    )
```

time: 287 us -> 245 us (0.85)
  waiting for transfers between devices: 212 us -> 155 us
  blocking collectives: 0 us -> 55.3 us
  matrix products: 25.1 us -> 5 us
  loops' own time: 18.3 us -> 0 us
    all_gather x1, waiting for transfers between devices: 179 us -> 46.3 us  [per_device(): deep = lax.all_gather(mixed, 'space', axis=2, tiled=True)]
    psum x0 -> x1, waiting for transfers between devices: none -> 108 us  [per_device(): summed = lax.psum(pairs, 'tm') * scale_factor]
    all_to_all x0 -> x1, blocking collectives: none -> 55.3 us  [per_device(): lax.all_to_all(snapshots, 'tm', split_axis=2, concat_axis=1, tiled=True)]
    reduce_scatter x1 -> x0, waiting for transfers between devices: 32 us -> none  [per_device(): lax.psum_scatter(partial_tiles, 'space', scatter_dimension=1, tiled=True)]
    dot_general x10 -> x1, matrix products: 25.1 us -> 5 us  [per_device(): jnp.einsum('kaic,kbjc->abij', mine, blocks, preferred_element_type=jnp.fl...]
    another operation x1 -> x0, loops' own time: 18.3 us -> none  [per_device(): partial_tiles = lax.fori_loop(0, filled, add_tile, empty)]
    dynamic_slice x20 -> x0, local copies, waits for them, and re-layouts: 11.2 us -> none  [the longest x10 5.59 us: add_tile(): second = jnp.maximum(col_block[slot], 0)]
    gather x0 -> x2, local copies, waits for them, and re-layouts: none -> 5.07 us  [the longest x1 4.48 us: per_device(): pairs = product[upper_rows, upper_cols]]
  transfers between devices with their start and end apart: 2 -> 2, of which waited for: 2 -> 2; matrix products, arithmetic and copies ran while one was open for 1% -> 0% of each run, Pallas kernels for 0% -> 0%
where the time goes in v1:
time: 245 us
  waiting for transfers between devices  155 us (63%)
  blocking collectives  55.3 us (23%)
  local copies, waits for them, and re-layouts  13.9 us (6%)
  between operations  13.5 us (6%)
  matrix products  5 us (2%)
  other arithmetic  2.86 us (1%)
    psum x1, waiting for transfers between devices, per_device(): summed = lax.psum(pairs, 'tm') * scale_factor  108 us
    all_to_all x1, blocking collectives, per_device(): lax.all_to_all(snapshots, 'tm', split_axis=2, concat_axis=1, tiled=True)  55.3 us
    all_gather x1, waiting for transfers between devices, per_device(): deep = lax.all_gather(mixed, 'space', axis=2, tiled=True)  46.3 us
    dot_general x1, matrix products, per_device(): jnp.einsum('kaic,kbjc->abij', mine, blocks, preferred_element_type=jnp.fl...  5 us
  transfers between devices with their start and end apart: 2, of which 2 were waited for; matrix products, arithmetic and copies ran while one was open for 0% of the time, Pallas kernels for 0%

profile of v1, /device:TPU:0, one launch (start us, length us, event | category | flops | bytes accessed | tf_op | source)
XLA Modules:
  0.0 245.1 jit_solution(9838678806976646247)
XLA Ops:
  6.5 0.0 all-gather.2.cloned.1.call-start
  6.5 2.9 %copy.13 = bf16[3,256,1024]{1,0,2:T(4,128)(2,1)S(1)} copy(bf16[3,256,1024]{2,1,0:T(8,128)(2,1)} %param.6) | data formatting | bytes 3145728 | tf_op args[0]
  9.5 55.3 %all_to_all.18 = bf16[3,256,1024]{1,0,2:T(4,128)(2,1)S(1)} all-to-all(bf16[3,256,1024]{1,0,2:T(4,128)(2,1)S(1)} %copy.13), channel_id=1, replica_groups=mesh['tm'=8,'space'=4] {'tm'}, dimensions={2} | all-to-all | bytes 3145728 | tf_op jit(solution)/shard_map/all_to_all | solution.py:18
  64.8 0.2 copy.14
  65.0 1.6 copy.15
  66.6 0.0 all-gather.2.cloned.1.call-update
  66.7 0.0 all-reduce.2.cloned.1.call-start
  66.7 46.3 %all-gather.2.cloned.1.call-done = bf16[3,2048,512]{2,1,0:T(8,128)(2,1)} async-done(((bf16[3,2048,128]{2,1,0:T(8,128)(2,1)}), bf16[3,2048,512]{2,1,0:T(8,128)(2,1)}) %all-gather.2.cloned.1.call-update) | async-done | bytes 6291472 | tf_op jit(solution)/shard_map/all_gather | solution.py:19
  113.0 3.4 %copy.16 = bf16[3,8,256,512]{3,2,0,1:T(8,128)(2,1)S(1)} copy(bf16[3,8,256,512]{3,2,1,0:T(8,128)(2,1)} %bitcast.27) | data formatting | bytes 12582912 | tf_op jit(solution)/shard_map/reshape | solution.py:20
  116.5 0.0 copy-start
  116.5 5.0 %fusion.2 = f32[8,8,64,256]{3,2,1,0:T(8,128)} fusion(bf16[3,8,256,512]{3,2,0,1:T(8,128)(2,1)S(1)} %copy.16, s32[]{:T(128)S(6)} %select_n.30), kind=kOutput, calls=%fused_computation.4 | convolution fusion | flops 3221225472 | bytes 12058628 | tf_op jit(solution)/shard_map/kaic,kbjc->abij/dot_general | solution.py:24
  121.5 0.0 copy-done
  121.5 4.5 %gather_fusion = f32[36,64,256]{2,1,0:T(8,128)} fusion(f32[8,8,64,256]{3,2,1,0:T(8,128)} %fusion.2, s32[36]{0:T(128)S(1)} %copy-done), kind=kCustom, calls=%fused_computation | custom fusion | bytes 4718880 | tf_op jit(solution)/shard_map/gather | solution.py:27
  125.9 0.0 copy-start.1
  126.0 0.0 all-reduce.2.cloned.1.call-update
  126.0 0.7 copy-done.1
  126.7 108.2 %all-reduce.2.cloned.1.call-done = f32[36,64,256]{2,1,0:T(8,128)} async-done(((f32[36,64,256]{2,1,0:T(8,128)}), f32[36,64,256]{2,1,0:T(8,128)}) %all-reduce.2.cloned.1.call-update) | async-done | bytes 2359312 | tf_op jit(solution)/shard_map/psum | solution.py:28
  234.8 1.9 broadcast_multiply_fusion
  236.7 0.6 gather_fusion.1
  237.3 0.9 bitcast_select_fusion
  (3 shorter events, 0.0 us)
Async XLA Ops:
  6.5 106.5 %all-gather.2.cloned.1.call-start = ((), (), s32[]{:S(2)}) async-start(), calls=%async_computation.1 | async-start | bytes 7864320 | tf_op jit(solution)/shard_map/all_gather | solution.py:19
  66.7 168.2 %all-reduce.2.cloned.1.call-start = ((), (), s32[]{:S(2)}) async-start(), calls=%async_computation.2 | async-start | bytes 4718592 | tf_op jit(solution)/shard_map/psum | solution.py:28
  116.5 5.0 %copy-start = (s32[36]{0:T(128)S(1)}, s32[36]{0:T(128)}, u32[]{:S(2)}) copy-start(s32[36]{0:T(128)} %constant.68) | copy-start | bytes 436
  125.9 0.7 copy-start.1
Sparse Core Ops, SparseCore 0:
  66.8 46.2 all-gather.1
  126.1 108.6 all-reduce.1

commit v2 on v1

v2 whole, which is shorter than its diff:
```python
import functools
import math

import jax
import jax.numpy as jnp
import numpy as np
from jax import lax
from jax.experimental import pallas as pl
from jax.experimental.pallas import tpu as pltpu
from jax.sharding import Mesh, PartitionSpec as P

GROUPS = 2


def tile_plan(block_count):
    rows, cols = np.triu_indices(block_count)
    pairs = np.stack([rows, cols], axis=1)
    part = len(pairs) // 4
    lists = pairs.reshape(2, 2, part, 2)
    sizes = [len(piece) for piece in np.array_split(np.arange(part), GROUPS)]
    return lists, sizes


def multiply_kernel(group_size, chunk_count, position, pairs, *refs):
    chunks = refs[: 2 * chunk_count]
    keep_ref, send_ref, blocks, arrived = refs[2 * chunk_count :]
    z, y, x, core = position[0], position[1], position[2], position[3]
    copies = []
    for index, chunk in enumerate(chunks):
        other, step = divmod(index, chunk_count)
        block = (z ^ step) * 2 + (y ^ other)
        copy = pltpu.make_async_copy(chunk, blocks.at[block], arrived.at[index])
        copy.start()
        copies.append(copy)
    for copy in copies:
        copy.wait()
    components = blocks.shape[1]
    rows_dev = keep_ref.shape[2]

    def one_tile(slot, carry):
        first, second = pairs[2 * slot], pairs[2 * slot + 1]
        tile = jnp.zeros((blocks.shape[2], blocks.shape[2]), jnp.float32)
        for component in range(components):
            tile += lax.dot_general(
                blocks[first, component],
                blocks[second, component],
                (((1,), (1,)), ((), ())),
                preferred_element_type=jnp.float32,
            )
        parts = [tile[row : row + rows_dev] for row in range(0, tile.shape[0], rows_dev)]
        half = len(parts) // 2
        for step in range(half):
            low, high = parts[2 * step], parts[2 * step + 1]
            target = x ^ step
            keep_ref[target, slot] = jnp.where(core == 0, low, high)
            send_ref[target, slot] = jnp.where(core == 0, high, low)
        return carry

    lax.fori_loop(0, group_size, one_tile, 0)


def per_device(z_count, y_count, x_count, core_count, snapshots, tile_table):
    components, block_size, cells_dev = snapshots.shape
    block_count = z_count * y_count
    space_count = x_count * core_count
    rows_dev = block_size // space_count
    scale_factor = 1.0 / math.sqrt(components * cells_dev * space_count)
    z, y, x, core = (lax.axis_index(name) for name in ("z", "y", "x", "core"))
    position = jnp.stack([z, y, x, core]).astype(jnp.int32)
    cells = cells_dev // z_count

    def swap(value, axis, bits):
        size = lax.axis_size(axis)
        return lax.ppermute(value, axis, [(i, i ^ bits) for i in range(size)])

    def part(step):
        return lax.dynamic_slice_in_dim(snapshots, (z ^ step) * cells, cells, 2)

    own = {step: swap(part(step), "z", step) for step in range(z_count - 1, 0, -1)}
    own[0] = part(0)
    other = {step: swap(own[step], "y", 1) for step in range(z_count)}
    chunks = [own[step] for step in range(z_count)] + [other[step] for step in range(z_count)]

    lists, sizes = tile_plan(block_count)
    lists = jnp.asarray(lists, jnp.int32)
    low_bit = z & 1
    mine = lists[y, low_bit]
    theirs = lists[y, 1 - low_bit]

    finals = []
    start = 0
    for size in sizes:
        pairs = jnp.concatenate([mine[start : start + size], theirs[start : start + size]])
        start += size
        shape = jax.ShapeDtypeStruct(
            (x_count, 2 * size, rows_dev, block_size), jnp.float32
        )
        keep, send = pl.pallas_call(
            functools.partial(multiply_kernel, 2 * size, z_count),
            out_shape=(shape, shape),
            in_specs=[pl.BlockSpec(memory_space=pltpu.SMEM)] * 2
            + [pl.BlockSpec(memory_space=pl.ANY)] * len(chunks),
            out_specs=(pl.BlockSpec(memory_space=pltpu.VMEM),) * 2,
            scratch_shapes=[
                pltpu.VMEM((block_count, components, block_size, cells), jnp.bfloat16),
                pltpu.SemaphoreType.DMA((len(chunks),)),
            ],
            compiler_params=pltpu.CompilerParams(vmem_limit_bytes=40 * 2**20),
            cost_estimate=pl.CostEstimate(
                flops=4 * size * block_size * block_size * components * cells,
                bytes_accessed=4 * 2**20,
                transcendentals=0,
            ),
            name="partial_tiles",
        )(position, pairs.reshape(-1), *chunks)
        total = keep + swap(send, "core", 1)
        mine_x = total[0]
        for step in range(1, x_count):
            mine_x = mine_x + swap(total[step], "x", step)
        held = mine_x[:size] + swap(mine_x[size:], "z", 1)
        bits = 2
        while bits < z_count:
            held = held + swap(held, "z", bits)
            bits *= 2
        held = held * scale_factor
        column = jnp.stack([held, swap(held, "z", 1)])
        finals.append(jnp.stack([column, swap(column, "y", 1)]))

    whole = jnp.concatenate(finals, axis=2)
    part_count = whole.shape[2]
    flat = whole.reshape(4 * part_count, rows_dev, block_size)
    table = tile_table[0]
    row_block = table[:, 0]
    col_block = table[:, 1]
    valid = row_block >= 0
    first = jnp.maximum(row_block, 0)
    second = jnp.maximum(col_block, 0)
    pair = first * block_count - (first * (first - 1)) // 2 + second - first
    quarter, slot = pair // part_count, pair % part_count
    quarter = ((quarter // 2) ^ y) * 2 + ((quarter % 2) ^ low_bit)
    result = flat[quarter * part_count + slot]
    result = jnp.where(valid[:, None, None], result, jnp.zeros_like(result))
    return result[None]


def solution(mesh):
    tm, space = mesh.shape["tm"], mesh.shape["space"]
    sizes = (tm // 2, 2, space // 2, 2)
    grid = Mesh(mesh.devices.reshape(sizes), ("z", "y", "x", "core"))
    in_specs = (P(None, ("z", "y"), ("x", "core")), P(("z", "y"), None, None))
    out_specs = P(("z", "y"), None, ("x", "core"), None)
    return jax.shard_map(
        functools.partial(per_device, *sizes),
        mesh=grid,
        in_specs=in_specs,
        out_specs=out_specs,
        check_vma=False,
    )
```

time: 245 us -> 165 us (0.67)
  blocking collectives: 55.3 us -> 0 us
  waiting for transfers between devices: 155 us -> 114 us
  starting transfers between devices: 0.04 us -> 24.9 us
  between operations: 13.5 us -> 0.2 us
  Pallas kernels: 0 us -> 11 us
  matrix products: 5 us -> 0 us
  local copies, waits for them, and re-layouts: 13.9 us -> 10.8 us
    ppermute x0 -> x19, waiting for transfers between devices: none -> 114 us  [swap(): return lax.ppermute(value, axis, [(i, i ^ bits) for i in range(size)])]
    psum x1 -> x0, waiting for transfers between devices: 108 us -> none  [per_device(): summed = lax.psum(pairs, 'tm') * scale_factor]
    all_to_all x1 -> x0, blocking collectives: 55.3 us -> none  [per_device(): lax.all_to_all(snapshots, 'tm', split_axis=2, concat_axis=1, tiled=True)]
    all_gather x1 -> x0, waiting for transfers between devices: 46.3 us -> none  [per_device(): deep = lax.all_gather(mixed, 'space', axis=2, tiled=True)]
    ppermute x0 -> x19, starting transfers between devices: none -> 24.9 us  [swap(): return lax.ppermute(value, axis, [(i, i ^ bits) for i in range(size)])]
    pallas_call x0 -> x2, Pallas kernels: none -> 11 us  [per_device(): pl.pallas_call(functools.partial(multiply_kernel, 2 * size, z_count), out...]
    dot_general x1 -> x0, matrix products: 5 us -> none  [per_device(): jnp.einsum('kaic,kbjc->abij', mine, blocks, preferred_element_type=jnp.fl...]
    unnamed x5 -> x22, local copies, waits for them, and re-layouts: 3.59 us -> 8.2 us
  transfers between devices with their start and end apart: 2 -> 19, of which waited for: 2 -> 12; matrix products, arithmetic and copies ran while one was open for 0% -> 2% of each run, Pallas kernels for 0% -> 3%
where the time goes in v2:
time: 165 us
  waiting for transfers between devices  114 us (69%)
  starting transfers between devices  24.9 us (15%)
  Pallas kernels  11 us (7%)
  local copies, waits for them, and re-layouts  10.8 us (7%)
  other arithmetic  3.68 us (2%)
    ppermute x19, waiting for transfers between devices, swap(): return lax.ppermute(value, axis, [(i, i ^ bits) for i in range(size)])  114 us
    ppermute x19, starting transfers between devices, swap(): return lax.ppermute(value, axis, [(i, i ^ bits) for i in range(size)])  24.9 us
    pallas_call x2, Pallas kernels, per_device(): pl.pallas_call(functools.partial(multiply_kernel, 2 * size, z_count), out...  11 us
    unnamed x22, local copies, waits for them, and re-layouts  8.2 us
  transfers between devices with their start and end apart: 19, of which 12 were waited for; matrix products, arithmetic and copies ran while one was open for 2% of the time, Pallas kernels for 3%

profile of v2, /device:TPU:0, one launch (start us, length us, event | category | flops | bytes accessed | tf_op | source)
XLA Modules:
  0.0 164.7 jit_solution(8761869023309070911)
XLA Ops:
  0.0 1.5 constant_dynamic-slice_fusion
  1.5 3.1 %collective-permute-start = (bf16[3,256,256]{2,1,0:T(8,128)(2,1)S(1)}, bf16[3,256,256]{2,1,0:T(8,128)(2,1)S(1)}, u32[]{:S(2)}, u32[]{:S(2)}) collective-permute-start(bf16[3,256,256]{2,1,0:T(8,128)(2,1)S(1)} %get-tuple-element.14), channel_id=1, source_target_pairs={{0,8},{8,0},{16,24},{24,16},{1,9},{9,1},{17,25},{25,17},{2,10},{10... | collective-permute-start | bytes 1179656 | tf_op jit(solution)/shard_map/ppermute | solution.py:74
  4.6 2.6 %collective-permute-start.1 = (bf16[3,256,256]{2,1,0:T(8,128)(2,1)S(1)}, bf16[3,256,256]{2,1,0:T(8,128)(2,1)S(1)}, u32[]{:S(2)}, u32[]{:S(2)}) collective-permute-start(bf16[3,256,256]{2,1,0:T(8,128)(2,1)S(1)} %get-tuple-element.16), channel_id=1, source_target_pairs={{0,16},{8,24},{16,0},{24,8},{1,17},{9,25},{17,1},{25,9},{2,18},{10... | collective-permute-start | bytes 1179656 | tf_op jit(solution)/shard_map/ppermute | solution.py:74
  7.2 1.7 %collective-permute-start.3 = (bf16[3,256,256]{2,1,0:T(8,128)(2,1)S(1)}, bf16[3,256,256]{2,1,0:T(8,128)(2,1)S(1)}, u32[]{:S(2)}, u32[]{:S(2)}) collective-permute-start(bf16[3,256,256]{2,1,0:T(8,128)(2,1)S(1)} %get-tuple-element.15.refs_0_), channel_id=1, source_target_pairs={{0,4},{4,0},{1,5},{5,1},{2,6},{6,2},{3,7},{7,3},{8,12},{12,8},{9,1... | collective-permute-start | bytes 1179656 | tf_op jit(solution)/shard_map/ppermute | solution.py:74
  8.9 12.4 %collective-permute-done.refs_1_ = bf16[3,256,256]{2,1,0:T(8,128)(2,1)S(1)} collective-permute-done((bf16[3,256,256]{2,1,0:T(8,128)(2,1)S(1)}, bf16[3,256,256]{2,1,0:T(8,128)(2,1)S(1)}, u32[]{:S(2)}, u32[]{:S(2)}) %collective-permute-start) | collective-permute-done | bytes 393248 | tf_op jit(solution)/shard_map/ppermute | solution.py:74
  21.4 1.7 %collective-permute-start.4 = (bf16[3,256,256]{2,1,0:T(8,128)(2,1)S(1)}, bf16[3,256,256]{2,1,0:T(8,128)(2,1)S(1)}, u32[]{:S(2)}, u32[]{:S(2)}) collective-permute-start(bf16[3,256,256]{2,1,0:T(8,128)(2,1)S(1)} %collective-permute-done.refs_1_), channel_id=1, source_target_pairs={{0,4},{4,0},{1,5},{5,1},{2,6},{6,2},{3,7},{7,3},{8,12},{12,8},{9,1... | collective-permute-start | bytes 1179656 | tf_op jit(solution)/shard_map/ppermute | solution.py:74
  23.0 11.3 %collective-permute-done.1.refs_2_ = bf16[3,256,256]{2,1,0:T(8,128)(2,1)S(1)} collective-permute-done((bf16[3,256,256]{2,1,0:T(8,128)(2,1)S(1)}, bf16[3,256,256]{2,1,0:T(8,128)(2,1)S(1)}, u32[]{:S(2)}, u32[]{:S(2)}) %collective-permute-start.1) | collective-permute-done | bytes 393248 | tf_op jit(solution)/shard_map/ppermute | solution.py:74
  34.4 1.5 collective-permute-start.5
  35.9 0.0 collective-permute-done.2.refs_3_
  35.9 0.5 collective-permute-start.6
  36.4 0.1 pad_add_fusion
  36.5 0.1 copy.6
  36.6 0.1 reshape.27.pairs
  36.7 0.1 pad_add_fusion.2.position
  36.7 0.0 collective-permute-done.3.refs_4_
  36.7 0.0 collective-permute-done.4.refs_5_
  36.8 0.0 copy-start
  36.8 0.7 copy-done
  37.5 6.8 %collective-permute-done.5.refs_6_ = bf16[3,256,256]{2,1,0:T(8,128)(2,1)S(1)} collective-permute-done((bf16[3,256,256]{2,1,0:T(8,128)(2,1)S(1)}, bf16[3,256,256]{2,1,0:T(8,128)(2,1)S(1)}, u32[]{:S(2)}, u32[]{:S(2)}) %collective-permute-start.5) | collective-permute-done | bytes 393248 | tf_op jit(solution)/shard_map/ppermute | solution.py:74
  44.3 0.7 copy-done.3
  45.0 3.5 %collective-permute-done.6.refs_7_ = bf16[3,256,256]{2,1,0:T(8,128)(2,1)S(1)} collective-permute-done((bf16[3,256,256]{2,1,0:T(8,128)(2,1)S(1)}, bf16[3,256,256]{2,1,0:T(8,128)(2,1)S(1)}, u32[]{:S(2)}, u32[]{:S(2)}) %collective-permute-start.6) | collective-permute-done | bytes 393248 | tf_op jit(solution)/shard_map/ppermute | solution.py:74
  48.5 0.7 copy-done.6
  49.2 1.0 copy-done.1
  50.2 1.0 copy-done.4
  51.2 1.0 copy-done.7
  52.2 6.3 %partial_tiles.2 = (f32[2,10,64,256]{3,2,1,0:T(8,128)S(1)}, f32[2,10,64,256]{3,2,1,0:T(8,128)}) custom-call(s32[4]{0:T(128)S(1)} %pad_add_fusion.2.position, s32[20]{0:T(128)S(1)} %reshape.27.pairs, bf16[3,256,256]{2,1,0:T(8,128)(2,1)S(1)} %get-tuple-element.15.refs_0_, bf16[3,256,256]{2,1,0:T(8,128)(2,1)S(1)} %collective-permute-done.refs_1_, ...), custom_call_target="tpu_custom_call" | custom-call | flops 1006632960 | bytes 4194304 | tf_op jit(solution)/shard_map/partial_tiles/pallas_call | solution.py:98
  58.6 0.1 collective-permute-start.7
  58.6 0.1 slice_bitcast_fusion.4
  58.7 0.1 pad_add_fusion.1
  58.8 0.1 copy.7
  58.9 0.1 reshape.28.pairs
  59.0 1.0 copy-done.2
  60.0 1.0 copy-done.5
  61.0 1.0 copy-done.8
  62.0 4.6 %partial_tiles.3 = (f32[2,8,64,256]{3,2,1,0:T(8,128)S(1)}, f32[2,8,64,256]{3,2,1,0:T(8,128)S(1)}) custom-call(s32[4]{0:T(128)S(1)} %pad_add_fusion.2.position, s32[16]{0:T(128)S(1)} %reshape.28.pairs, bf16[3,256,256]{2,1,0:T(8,128)(2,1)S(1)} %get-tuple-element.15.refs_0_, bf16[3,256,256]{2,1,0:T(8,128)(2,1)S(1)} %collective-permute-done.refs_1_, ...), custom_call_target="tpu_custom_call" | custom-call | flops 805306368 | bytes 4194304 | tf_op jit(solution)/shard_map/partial_tiles/pallas_call | solution.py:98
  66.6 0.6 collective-permute-start.13
  67.2 1.5 add.90
  68.7 1.4 collective-permute-start.8
  70.1 0.2 add.94
  70.3 0.8 collective-permute-start.14
  71.1 15.3 %collective-permute-done.8 = f32[10,64,256]{2,1,0:T(8,128)S(1)} collective-permute-done((f32[10,64,256]{2,1,0:T(8,128)S(1)}, f32[10,64,256]{2,1,0:T(8,128)S(1)}, u32[]{:S(2)}, u32[]{:S(2)}) %collective-permute-start.8) | collective-permute-done | bytes 655392 | tf_op jit(solution)/shard_map/ppermute | solution.py:74
  86.4 0.1 fusion
  86.5 3.2 %collective-permute-start.9 = (f32[5,64,256]{2,1,0:T(8,128)S(1)}, f32[5,64,256]{2,1,0:T(8,128)S(1)}, u32[]{:S(2)}, u32[]{:S(2)}) collective-permute-start(f32[5,64,256]{2,1,0:T(8,128)S(1)} %slice.77), channel_id=1, source_target_pairs={{0,8},{8,0},{16,24},{24,16},{1,9},{9,1},{17,25},{25,17},{2,10},{10... | collective-permute-start | bytes 983048 | tf_op jit(solution)/shard_map/ppermute | solution.py:74
  89.7 6.9 %collective-permute-done.14 = f32[8,64,256]{2,1,0:T(8,128)S(1)} collective-permute-done((f32[8,64,256]{2,1,0:T(8,128)S(1)}, f32[8,64,256]{2,1,0:T(8,128)S(1)}, u32[]{:S(2)}, u32[]{:S(2)}) %collective-permute-start.14) | collective-permute-done | bytes 524320 | tf_op jit(solution)/shard_map/ppermute | solution.py:74
  96.7 0.1 fusion.1
  96.8 3.2 %collective-permute-start.15 = (f32[4,64,256]{2,1,0:T(8,128)S(1)}, f32[4,64,256]{2,1,0:T(8,128)S(1)}, u32[]{:S(2)}, u32[]{:S(2)}) collective-permute-start(f32[4,64,256]{2,1,0:T(8,128)S(1)} %slice.81), channel_id=1, source_target_pairs={{0,8},{8,0},{16,24},{24,16},{1,9},{9,1},{17,25},{25,17},{2,10},{10... | collective-permute-start | bytes 786440 | tf_op jit(solution)/shard_map/ppermute | solution.py:74
  100.1 1.1 collective-permute-start.10
  101.2 9.9 %collective-permute-done.15 = f32[4,64,256]{2,1,0:T(8,128)S(1)} collective-permute-done((f32[4,64,256]{2,1,0:T(8,128)S(1)}, f32[4,64,256]{2,1,0:T(8,128)S(1)}, u32[]{:S(2)}, u32[]{:S(2)}) %collective-permute-start.15) | collective-permute-done | bytes 262176 | tf_op jit(solution)/shard_map/ppermute | solution.py:74
  111.1 0.1 collective-permute-start.16
  111.2 12.7 %collective-permute-done.10 = f32[5,64,256]{2,1,0:T(8,128)S(1)} collective-permute-done((f32[5,64,256]{2,1,0:T(8,128)S(1)}, f32[5,64,256]{2,1,0:T(8,128)S(1)}, u32[]{:S(2)}, u32[]{:S(2)}) %collective-permute-start.10) | collective-permute-done | bytes 327712 | tf_op jit(solution)/shard_map/ppermute | solution.py:74
  123.9 0.0 copy-start.9
  123.9 0.1 collective-permute-start.11
  124.1 3.8 %collective-permute-done.16 = f32[4,64,256]{2,1,0:T(8,128)S(1)} collective-permute-done((f32[4,64,256]{2,1,0:T(8,128)S(1)}, f32[4,64,256]{2,1,0:T(8,128)S(1)}, u32[]{:S(2)}, u32[]{:S(2)}) %collective-permute-start.16) | collective-permute-done | bytes 262176 | tf_op jit(solution)/shard_map/ppermute | solution.py:74
  128.0 0.1 collective-permute-start.17
  128.1 6.9 %collective-permute-done.11 = f32[5,64,256]{2,1,0:T(8,128)S(1)} collective-permute-done((f32[5,64,256]{2,1,0:T(8,128)S(1)}, f32[5,64,256]{2,1,0:T(8,128)S(1)}, u32[]{:S(2)}, u32[]{:S(2)}) %collective-permute-start.11) | collective-permute-done | bytes 327712 | tf_op jit(solution)/shard_map/ppermute | solution.py:74
  134.9 0.1 fusion.7
  135.0 1.6 collective-permute-start.12
  136.6 3.8 %collective-permute-done.17 = f32[4,64,256]{2,1,0:T(8,128)S(1)} collective-permute-done((f32[4,64,256]{2,1,0:T(8,128)S(1)}, f32[4,64,256]{2,1,0:T(8,128)S(1)}, u32[]{:S(2)}, u32[]{:S(2)}) %collective-permute-start.17) | collective-permute-done | bytes 262176 | tf_op jit(solution)/shard_map/ppermute | solution.py:74
  140.5 0.1 fusion.6
  140.5 1.6 collective-permute-start.18
  142.2 20.7 %collective-permute-done.18 = f32[2,4,64,256]{3,2,1,0:T(8,128)S(1)} collective-permute-done((f32[2,4,64,256]{3,2,1,0:T(8,128)S(1)}, f32[2,4,64,256]{3,2,1,0:T(8,128)S(1)}, u32[]{:S(2)}, u32[]{:S(2)}) %collective-permute-start.18) | collective-permute-done | bytes 524320 | tf_op jit(solution)/shard_map/ppermute | solution.py:74
  162.9 0.3 maximum_maximum_fusion
  163.2 0.6 gather_fusion
  163.8 0.9 bitcast_select_fusion
  (29 shorter events, 0.4 us)
Async XLA Ops:
  0.0 8.9 %copy-start.10 = (s32[2,2,9,2]{2,3,1,0:T(2,128)S(1)}, s32[2,2,9,2]{2,3,1,0:T(2,128)}, u32[]{:S(2)}) copy-start(s32[2,2,9,2]{2,3,1,0:T(2,128)} %constant.84.clone) | copy-start | bytes 868
  1.5 19.9 %collective-permute-start = (bf16[3,256,256]{2,1,0:T(8,128)(2,1)S(1)}, bf16[3,256,256]{2,1,0:T(8,128)(2,1)S(1)}, u32[]{:S(2)}, u32[]{:S(2)}) collective-permute-start(bf16[3,256,256]{2,1,0:T(8,128)(2,1)S(1)} %get-tuple-element.14), channel_id=1, source_target_pairs={{0,8},{8,0},{16,24},{24,16},{1,9},{9,1},{17,25},{25,17},{2,10},{10... | collective-permute-start | bytes 1179656 | tf_op jit(solution)/shard_map/ppermute | solution.py:74
  4.6 29.8 %collective-permute-start.1 = (bf16[3,256,256]{2,1,0:T(8,128)(2,1)S(1)}, bf16[3,256,256]{2,1,0:T(8,128)(2,1)S(1)}, u32[]{:S(2)}, u32[]{:S(2)}) collective-permute-start(bf16[3,256,256]{2,1,0:T(8,128)(2,1)S(1)} %get-tuple-element.16), channel_id=1, source_target_pairs={{0,16},{8,24},{16,0},{24,8},{1,17},{9,25},{17,1},{25,9},{2,18},{10... | collective-permute-start | bytes 1179656 | tf_op jit(solution)/shard_map/ppermute | solution.py:74
  7.2 28.7 %collective-permute-start.2 = (bf16[3,256,256]{2,1,0:T(8,128)(2,1)S(1)}, bf16[3,256,256]{2,1,0:T(8,128)(2,1)S(1)}, u32[]{:S(2)}, u32[]{:S(2)}) collective-permute-start(bf16[3,256,256]{2,1,0:T(8,128)(2,1)S(1)} %get-tuple-element.13), channel_id=1, source_target_pairs={{0,24},{8,16},{16,8},{24,0},{1,25},{9,17},{17,9},{25,1},{2,26},{10... | collective-permute-start | bytes 1179656 | tf_op jit(solution)/shard_map/ppermute | solution.py:74
  7.2 29.6 %collective-permute-start.3 = (bf16[3,256,256]{2,1,0:T(8,128)(2,1)S(1)}, bf16[3,256,256]{2,1,0:T(8,128)(2,1)S(1)}, u32[]{:S(2)}, u32[]{:S(2)}) collective-permute-start(bf16[3,256,256]{2,1,0:T(8,128)(2,1)S(1)} %get-tuple-element.15.refs_0_), channel_id=1, source_target_pairs={{0,4},{4,0},{1,5},{5,1},{2,6},{6,2},{3,7},{7,3},{8,12},{12,8},{9,1... | collective-permute-start | bytes 1179656 | tf_op jit(solution)/shard_map/ppermute | solution.py:74
  21.4 15.4 %collective-permute-start.4 = (bf16[3,256,256]{2,1,0:T(8,128)(2,1)S(1)}, bf16[3,256,256]{2,1,0:T(8,128)(2,1)S(1)}, u32[]{:S(2)}, u32[]{:S(2)}) collective-permute-start(bf16[3,256,256]{2,1,0:T(8,128)(2,1)S(1)} %collective-permute-done.refs_1_), channel_id=1, source_target_pairs={{0,4},{4,0},{1,5},{5,1},{2,6},{6,2},{3,7},{7,3},{8,12},{12,8},{9,1... | collective-permute-start | bytes 1179656 | tf_op jit(solution)/shard_map/ppermute | solution.py:74
  34.4 9.9 %collective-permute-start.5 = (bf16[3,256,256]{2,1,0:T(8,128)(2,1)S(1)}, bf16[3,256,256]{2,1,0:T(8,128)(2,1)S(1)}, u32[]{:S(2)}, u32[]{:S(2)}) collective-permute-start(bf16[3,256,256]{2,1,0:T(8,128)(2,1)S(1)} %collective-permute-done.1.refs_2_), channel_id=1, source_target_pairs={{0,4},{4,0},{1,5},{5,1},{2,6},{6,2},{3,7},{7,3},{8,12},{12,8},{9,1... | collective-permute-start | bytes 1179656 | tf_op jit(solution)/shard_map/ppermute | solution.py:74
  35.9 12.6 %collective-permute-start.6 = (bf16[3,256,256]{2,1,0:T(8,128)(2,1)S(1)}, bf16[3,256,256]{2,1,0:T(8,128)(2,1)S(1)}, u32[]{:S(2)}, u32[]{:S(2)}) collective-permute-start(bf16[3,256,256]{2,1,0:T(8,128)(2,1)S(1)} %collective-permute-done.2.refs_3_), channel_id=1, source_target_pairs={{0,4},{4,0},{1,5},{5,1},{2,6},{6,2},{3,7},{7,3},{8,12},{12,8},{9,1... | collective-permute-start | bytes 1179656 | tf_op jit(solution)/shard_map/ppermute | solution.py:74
  36.8 0.8 copy-start
  44.3 0.7 copy-start.3
  48.5 0.7 copy-start.6
  49.2 1.0 copy-start.1
  50.2 1.0 copy-start.4
  51.2 1.0 copy-start.7
  58.6 8.6 %collective-permute-start.7 = (f32[2,10,64,256]{3,2,1,0:T(8,128)}, f32[2,10,64,256]{3,2,1,0:T(8,128)}, u32[]{:S(2)}, u32[]{:S(2)}) collective-permute-start(f32[2,10,64,256]{3,2,1,0:T(8,128)} %get-tuple-element.10), channel_id=1, source_target_pairs={{0,1},{1,0},{2,3},{3,2},{4,5},{5,4},{6,7},{7,6},{8,9},{9,8},{10,11... | collective-permute-start | bytes 3932168 | tf_op jit(solution)/shard_map/ppermute | solution.py:74
  59.0 1.0 copy-start.2
  60.0 1.0 copy-start.5
  61.0 1.0 copy-start.8
  66.6 3.5 %collective-permute-start.13 = (f32[2,8,64,256]{3,2,1,0:T(8,128)S(1)}, f32[2,8,64,256]{3,2,1,0:T(8,128)S(1)}, u32[]{:S(2)}, u32[]{:S(2)}) collective-permute-start(f32[2,8,64,256]{3,2,1,0:T(8,128)S(1)} %get-tuple-element.12), channel_id=1, source_target_pairs={{0,1},{1,0},{2,3},{3,2},{4,5},{5,4},{6,7},{7,6},{8,9},{9,8},{10,11... | collective-permute-start | bytes 3145736 | tf_op jit(solution)/shard_map/ppermute | solution.py:74
  68.7 17.7 %collective-permute-start.8 = (f32[10,64,256]{2,1,0:T(8,128)S(1)}, f32[10,64,256]{2,1,0:T(8,128)S(1)}, u32[]{:S(2)}, u32[]{:S(2)}) collective-permute-start(f32[10,64,256]{2,1,0:T(8,128)S(1)} %slice_bitcast_fusion), channel_id=1, source_target_pairs={{0,2},{2,0},{1,3},{3,1},{4,6},{6,4},{5,7},{7,5},{8,10},{10,8},{9,1... | collective-permute-start | bytes 1966088 | tf_op jit(solution)/shard_map/ppermute | solution.py:74
  70.3 26.3 %collective-permute-start.14 = (f32[8,64,256]{2,1,0:T(8,128)S(1)}, f32[8,64,256]{2,1,0:T(8,128)S(1)}, u32[]{:S(2)}, u32[]{:S(2)}) collective-permute-start(f32[8,64,256]{2,1,0:T(8,128)S(1)} %slice_bitcast_fusion.2), channel_id=1, source_target_pairs={{0,2},{2,0},{1,3},{3,1},{4,6},{6,4},{5,7},{7,5},{8,10},{10,8},{9,1... | collective-permute-start | bytes 1572872 | tf_op jit(solution)/shard_map/ppermute | solution.py:74
  86.5 13.5 %collective-permute-start.9 = (f32[5,64,256]{2,1,0:T(8,128)S(1)}, f32[5,64,256]{2,1,0:T(8,128)S(1)}, u32[]{:S(2)}, u32[]{:S(2)}) collective-permute-start(f32[5,64,256]{2,1,0:T(8,128)S(1)} %slice.77), channel_id=1, source_target_pairs={{0,8},{8,0},{16,24},{24,16},{1,9},{9,1},{17,25},{25,17},{2,10},{10... | collective-permute-start | bytes 983048 | tf_op jit(solution)/shard_map/ppermute | solution.py:74
  96.8 14.2 %collective-permute-start.15 = (f32[4,64,256]{2,1,0:T(8,128)S(1)}, f32[4,64,256]{2,1,0:T(8,128)S(1)}, u32[]{:S(2)}, u32[]{:S(2)}) collective-permute-start(f32[4,64,256]{2,1,0:T(8,128)S(1)} %slice.81), channel_id=1, source_target_pairs={{0,8},{8,0},{16,24},{24,16},{1,9},{9,1},{17,25},{25,17},{2,10},{10... | collective-permute-start | bytes 786440 | tf_op jit(solution)/shard_map/ppermute | solution.py:74
  100.1 23.8 %collective-permute-start.10 = (f32[5,64,256]{2,1,0:T(8,128)S(1)}, f32[5,64,256]{2,1,0:T(8,128)S(1)}, u32[]{:S(2)}, u32[]{:S(2)}) collective-permute-start(f32[5,64,256]{2,1,0:T(8,128)S(1)} %slice_add_fusion), channel_id=1, source_target_pairs={{0,16},{8,24},{16,0},{24,8},{1,17},{9,25},{17,1},{25,9},{2,18},{10... | collective-permute-start | bytes 983048 | tf_op jit(solution)/shard_map/ppermute | solution.py:74
  111.1 16.9 %collective-permute-start.16 = (f32[4,64,256]{2,1,0:T(8,128)S(1)}, f32[4,64,256]{2,1,0:T(8,128)S(1)}, u32[]{:S(2)}, u32[]{:S(2)}) collective-permute-start(f32[4,64,256]{2,1,0:T(8,128)S(1)} %slice_add_fusion.1), channel_id=1, source_target_pairs={{0,16},{8,24},{16,0},{24,8},{1,17},{9,25},{17,1},{25,9},{2,18},{10... | collective-permute-start | bytes 786440 | tf_op jit(solution)/shard_map/ppermute | solution.py:74
  123.9 18.2 %copy-start.9 = (s32[1,10,2]{1,2,0:T(2,128)S(1)}, s32[1,10,2]{1,2,0:T(2,128)}, u32[]{:S(2)}) copy-start(s32[1,10,2]{1,2,0:T(2,128)} %param.4) | copy-start | bytes 244
  123.9 11.0 %collective-permute-start.11 = (f32[5,64,256]{2,1,0:T(8,128)S(1)}, f32[5,64,256]{2,1,0:T(8,128)S(1)}, u32[]{:S(2)}, u32[]{:S(2)}) collective-permute-start(f32[5,64,256]{2,1,0:T(8,128)S(1)} %add_multiply_fusion), channel_id=1, source_target_pairs={{0,8},{8,0},{16,24},{24,16},{1,9},{9,1},{17,25},{25,17},{2,10},{10... | collective-permute-start | bytes 983048 | tf_op jit(solution)/shard_map/ppermute | solution.py:74
  128.0 12.5 %collective-permute-start.17 = (f32[4,64,256]{2,1,0:T(8,128)S(1)}, f32[4,64,256]{2,1,0:T(8,128)S(1)}, u32[]{:S(2)}, u32[]{:S(2)}) collective-permute-start(f32[4,64,256]{2,1,0:T(8,128)S(1)} %add_multiply_fusion.1), channel_id=1, source_target_pairs={{0,8},{8,0},{16,24},{24,16},{1,9},{9,1},{17,25},{25,17},{2,10},{10... | collective-permute-start | bytes 786440 | tf_op jit(solution)/shard_map/ppermute | solution.py:74
  135.0 27.9 %collective-permute-start.12 = (f32[2,5,64,256]{3,2,1,0:T(8,128)S(1)}, f32[2,5,64,256]{3,2,1,0:T(8,128)S(1)}, u32[]{:S(2)}, u32[]{:S(2)}) collective-permute-start(f32[2,5,64,256]{3,2,1,0:T(8,128)S(1)} %get-tuple-element.18), channel_id=1, source_target_pairs={{0,4},{4,0},{1,5},{5,1},{2,6},{6,2},{3,7},{7,3},{8,12},{12,8},{9,1... | collective-permute-start | bytes 1966088 | tf_op jit(solution)/shard_map/ppermute | solution.py:74
  140.5 22.4 %collective-permute-start.18 = (f32[2,4,64,256]{3,2,1,0:T(8,128)S(1)}, f32[2,4,64,256]{3,2,1,0:T(8,128)S(1)}, u32[]{:S(2)}, u32[]{:S(2)}) collective-permute-start(f32[2,4,64,256]{3,2,1,0:T(8,128)S(1)} %get-tuple-element.20), channel_id=1, source_target_pairs={{0,4},{4,0},{1,5},{5,1},{2,6},{6,2},{3,7},{7,3},{8,12},{12,8},{9,1... | collective-permute-start | bytes 1572872 | tf_op jit(solution)/shard_map/ppermute | solution.py:74

commit v3 on v1

v3 whole, which is shorter than its diff:
```python
import functools
import math

import jax
import jax.numpy as jnp
import numpy as np
from jax import lax
from jax.experimental import pallas as pl
from jax.experimental.pallas import tpu as pltpu
from jax.sharding import Mesh, PartitionSpec as P

VMEM_LIMIT = 48 * 2**20


def tile_lists(block_count):
    rows, cols = np.triu_indices(block_count)
    return np.stack([rows, cols], axis=1).reshape(2, 2, -1, 2)


def multiply_tiles(scalars, first_pair, blocks, keep_ref, send_ref, x_first):
    x, core = scalars[2], scalars[3]
    group_size = keep_ref.shape[2]
    rows_dev = keep_ref.shape[3]
    part_count = blocks.shape[1] // rows_dev

    def one_slot(slot, carry):
        for low in range(2):
            where = first_pair + 2 * (low * group_size + slot)
            tile = lax.dot_general(
                blocks[scalars[where]],
                blocks[scalars[where + 1]],
                (((1,), (1,)), ((), ())),
                preferred_element_type=jnp.float32,
            )
            parts = [tile[part * rows_dev : (part + 1) * rows_dev] for part in range(part_count)]
            for step in range(part_count // 2):
                even, odd = parts[2 * step], parts[2 * step + 1]
                target = x ^ step
                place = (target, low) if x_first else (low, target)
                keep_ref[place[0], place[1], slot] = jnp.where(core == 0, even, odd)
                send_ref[place[0], place[1], slot] = jnp.where(core == 0, odd, even)
        return carry

    lax.fori_loop(0, group_size, one_slot, 0)


def first_kernel(chunk_count, first_pair, scalars, *refs):
    chunks = refs[: 2 * chunk_count]
    blocks, keep_ref, send_ref = refs[2 * chunk_count :]
    z, y = scalars[0], scalars[1]
    components, _, cells = chunks[0].shape
    for index, chunk in enumerate(chunks):
        other, step = divmod(index, chunk_count)
        block = (z ^ step) * 2 + (y ^ other)
        for component in range(components):
            blocks[block, :, component * cells : (component + 1) * cells] = chunk[component]
    multiply_tiles(scalars, first_pair, blocks, keep_ref, send_ref, True)


def second_kernel(first_pair, scalars, blocks, keep_ref, send_ref):
    multiply_tiles(scalars, first_pair, blocks, keep_ref, send_ref, False)


def per_device(z_count, y_count, x_count, core_count, snapshots, tile_table):
    components, block_size, cells_dev = snapshots.shape
    block_count = z_count * y_count
    space_count = x_count * core_count
    rows_dev = block_size // space_count
    scale_factor = 1.0 / math.sqrt(components * cells_dev * space_count)
    z, y, x, core = (lax.axis_index(name) for name in ("z", "y", "x", "core"))
    low_bit = z & 1
    cells = cells_dev // z_count

    def swap(value, axis, bits):
        size = lax.axis_size(axis)
        return lax.ppermute(value, axis, [(i, i ^ bits) for i in range(size)])

    lists = tile_lists(block_count)
    quarter = lists.shape[2]
    sizes = (quarter - quarter // 2, quarter // 2)
    ordered = np.stack(
        [
            np.concatenate(
                [
                    lists[of_y, of_bit ^ flip, cut].reshape(-1)
                    for cut in (slice(0, sizes[0]), slice(sizes[0], quarter))
                    for flip in range(2)
                ]
            )
            for of_y in range(2)
            for of_bit in range(2)
        ]
    ).astype(np.int32)
    pairs = lax.dynamic_index_in_dim(jnp.asarray(ordered), y * 2 + low_bit, 0, keepdims=False)
    scalars = jnp.concatenate([jnp.stack([z, y, x, core]).astype(jnp.int32), pairs])

    def part(step):
        return lax.dynamic_slice_in_dim(snapshots, (z ^ step) * cells, cells, 2)

    parts = [part(step) for step in range(z_count)]
    own = [parts[0]]
    for step in range(1, z_count):
        piece = parts[step]
        if step >= 3:
            piece, own[step - 2] = lax.optimization_barrier((piece, own[step - 2]))
        own.append(swap(piece, "z", step))
    chunks = own + [swap(piece, "y", 1) for piece in own]

    def sums_shape(size, x_first):
        lead = (x_count, 2) if x_first else (2, x_count)
        return jax.ShapeDtypeStruct((*lead, size, rows_dev, block_size), jnp.float32)

    def call(kernel, size, out_shape, operands, name):
        vmem = pl.BlockSpec(memory_space=pltpu.VMEM)
        return pl.pallas_call(
            kernel,
            out_shape=out_shape,
            in_specs=[pl.BlockSpec(memory_space=pltpu.SMEM)] + [vmem] * len(operands),
            out_specs=[vmem] * len(out_shape),
            compiler_params=pltpu.CompilerParams(vmem_limit_bytes=VMEM_LIMIT),
            cost_estimate=pl.CostEstimate(
                flops=4 * size * block_size * block_size * components * cells,
                bytes_accessed=4 * 2**20,
                transcendentals=0,
            ),
            name=name,
        )(scalars, *operands)

    blocks_shape = jax.ShapeDtypeStruct(
        (block_count, block_size, components * cells), jnp.bfloat16
    )
    blocks, keep_a, send_a = call(
        functools.partial(first_kernel, z_count, 4),
        sizes[0],
        [blocks_shape] + [sums_shape(sizes[0], True)] * 2,
        chunks,
        "tiles_first",
    )
    keep_b, send_b = call(
        functools.partial(second_kernel, 4 + 4 * sizes[0]),
        sizes[1],
        [sums_shape(sizes[1], False)] * 2,
        [blocks],
        "tiles_second",
    )

    def over_x(value):
        total = value[0]
        for step in range(1, x_count):
            total = total + swap(value[step], "x", step)
        return total

    def over_low_bit(value):
        return value[0] + swap(value[1], "z", 1)

    def over_high_bits(value):
        bits = 2
        while bits < z_count:
            value = value + swap(value, "z", bits)
            bits *= 2
        return value * scale_factor

    total_a = keep_a + swap(send_a, "core", 1)
    total_b = keep_b + swap(send_b, "core", 1)
    held_a = over_high_bits(over_low_bit(over_x(total_a)))
    held_b = over_high_bits(over_x(over_low_bit(total_b)))

    column_a = jnp.stack([held_a, swap(held_a, "z", 1)])
    column_b = jnp.stack([held_b, swap(held_b, "y", 1)])
    whole_a = jnp.stack([column_a, swap(column_a, "y", 1)])
    whole_b = jnp.stack([column_b, swap(column_b, "z", 1)])
    flat = jnp.concatenate(
        [part.reshape(-1, rows_dev, block_size) for part in (whole_a, whole_b)]
    )

    table = tile_table[0]
    row_block = table[:, 0]
    col_block = table[:, 1]
    valid = row_block >= 0
    first = jnp.maximum(row_block, 0)
    second = jnp.maximum(col_block, 0)
    pair = first * block_count - (first * (first - 1)) // 2 + second - first
    of_list, slot = pair // quarter, pair % quarter
    off_y, off_bit = (of_list // 2) ^ y, (of_list % 2) ^ low_bit
    place_a = (off_y * 2 + off_bit) * sizes[0] + slot
    place_b = 4 * sizes[0] + (off_bit * 2 + off_y) * sizes[1] + slot - sizes[0]
    result = flat[jnp.where(slot < sizes[0], place_a, place_b)]
    result = jnp.where(valid[:, None, None], result, jnp.zeros_like(result))
    return result[None]


def solution(mesh):
    tm, space = mesh.shape["tm"], mesh.shape["space"]
    sizes = (tm // 2, 2, space // 2, 2)
    grid = Mesh(mesh.devices.reshape(sizes), ("z", "y", "x", "core"))
    in_specs = (P(None, ("z", "y"), ("x", "core")), P(("z", "y"), None, None))
    out_specs = P(("z", "y"), None, ("x", "core"), None)
    return jax.shard_map(
        functools.partial(per_device, *sizes),
        mesh=grid,
        in_specs=in_specs,
        out_specs=out_specs,
        check_vma=False,
    )
```

time: 245 us -> 150 us (0.61)
  blocking collectives: 55.3 us -> 0 us
  waiting for transfers between devices: 155 us -> 112 us
  starting transfers between devices: 0.04 us -> 23.3 us
  between operations: 13.5 us -> 0.18 us
  local copies, waits for them, and re-layouts: 13.9 us -> 4.86 us
  Pallas kernels: 0 us -> 6.49 us
  matrix products: 5 us -> 0 us
    ppermute x0 -> x19, waiting for transfers between devices: none -> 112 us  [swap(): return lax.ppermute(value, axis, [(i, i ^ bits) for i in range(size)])]
    psum x1 -> x0, waiting for transfers between devices: 108 us -> none  [per_device(): summed = lax.psum(pairs, 'tm') * scale_factor]
    all_to_all x1 -> x0, blocking collectives: 55.3 us -> none  [per_device(): lax.all_to_all(snapshots, 'tm', split_axis=2, concat_axis=1, tiled=True)]
    all_gather x1 -> x0, waiting for transfers between devices: 46.3 us -> none  [per_device(): deep = lax.all_gather(mixed, 'space', axis=2, tiled=True)]
    ppermute x0 -> x19, starting transfers between devices: none -> 23.3 us  [swap(): return lax.ppermute(value, axis, [(i, i ^ bits) for i in range(size)])]
    pallas_call x0 -> x2, Pallas kernels: none -> 6.49 us  [call(): pl.pallas_call(kernel, out_shape=out_shape, in_specs=[pl.BlockSpec(memory...]
    dot_general x1 -> x0, matrix products: 5 us -> none  [per_device(): jnp.einsum('kaic,kbjc->abij', mine, blocks, preferred_element_type=jnp.fl...]
    gather x2 -> x1, local copies, waits for them, and re-layouts: 5.07 us -> 0.59 us  [per_device(): result = flat[jnp.where(slot < sizes[0], place_a, place_b)]]
  transfers between devices with their start and end apart: 2 -> 19, of which waited for: 2 -> 18; matrix products, arithmetic and copies ran while one was open for 0% -> 1% of each run, Pallas kernels for 0% -> 0%
where the time goes in v3:
time: 150 us; the launch traced here: 149 us
  waiting for transfers between devices  112 us (75%)
  starting transfers between devices  23.3 us (16%)
  Pallas kernels  6.49 us (4%)
  local copies, waits for them, and re-layouts  4.86 us (3%)
  other arithmetic  2.34 us (2%)
    ppermute x19, waiting for transfers between devices, swap(): return lax.ppermute(value, axis, [(i, i ^ bits) for i in range(size)])  112 us
    ppermute x19, starting transfers between devices, swap(): return lax.ppermute(value, axis, [(i, i ^ bits) for i in range(size)])  23.3 us
    pallas_call x2, Pallas kernels, call(): pl.pallas_call(kernel, out_shape=out_shape, in_specs=[pl.BlockSpec(memory...  6.49 us
  transfers between devices with their start and end apart: 19, of which 18 were waited for; matrix products, arithmetic and copies ran while one was open for 1% of the time, Pallas kernels for 0%

profile of v3, /device:TPU:0, one launch (start us, length us, event | category | flops | bytes accessed | tf_op | source)
XLA Modules:
  0.0 149.4 jit_solution(6952689897306065634)
XLA Ops:
  0.0 1.5 constant_dynamic-slice_fusion
  1.5 3.1 %collective-permute-start = (bf16[3,256,256]{2,1,0:T(8,128)(2,1)S(1)}, bf16[3,256,256]{2,1,0:T(8,128)(2,1)S(1)}, u32[]{:S(2)}, u32[]{:S(2)}) collective-permute-start(bf16[3,256,256]{2,1,0:T(8,128)(2,1)S(1)} %get-tuple-element.22), channel_id=1, source_target_pairs={{0,8},{8,0},{16,24},{24,16},{1,9},{9,1},{17,25},{25,17},{2,10},{10... | collective-permute-start | bytes 1179656 | tf_op jit(solution)/shard_map/ppermute | solution.py:76
  4.6 2.6 %collective-permute-start.1 = (bf16[3,256,256]{2,1,0:T(8,128)(2,1)S(1)}, bf16[3,256,256]{2,1,0:T(8,128)(2,1)S(1)}, u32[]{:S(2)}, u32[]{:S(2)}) collective-permute-start(bf16[3,256,256]{2,1,0:T(8,128)(2,1)S(1)} %get-tuple-element.19), channel_id=1, source_target_pairs={{0,16},{8,24},{16,0},{24,8},{1,17},{9,25},{17,1},{25,9},{2,18},{10... | collective-permute-start | bytes 1179656 | tf_op jit(solution)/shard_map/ppermute | solution.py:76
  7.2 14.8 %collective-permute-done.refs_1_ = bf16[3,256,256]{2,1,0:T(8,128)(2,1)S(1)} collective-permute-done((bf16[3,256,256]{2,1,0:T(8,128)(2,1)S(1)}, bf16[3,256,256]{2,1,0:T(8,128)(2,1)S(1)}, u32[]{:S(2)}, u32[]{:S(2)}) %collective-permute-start) | collective-permute-done | bytes 393248 | tf_op jit(solution)/shard_map/ppermute | solution.py:76
  22.0 2.6 %collective-permute-start.2 = (bf16[3,256,256]{2,1,0:T(8,128)(2,1)S(1)}, bf16[3,256,256]{2,1,0:T(8,128)(2,1)S(1)}, u32[]{:S(2)}, u32[]{:S(2)}) collective-permute-start(bf16[3,256,256]{2,1,0:T(8,128)(2,1)S(1)} %get-tuple-element.13), channel_id=1, source_target_pairs={{0,24},{8,16},{16,8},{24,0},{1,25},{9,17},{17,9},{25,1},{2,26},{10... | collective-permute-start | bytes 1179656 | tf_op jit(solution)/shard_map/ppermute | solution.py:76
  24.6 1.5 %collective-permute-start.3 = (bf16[3,256,256]{2,1,0:T(8,128)(2,1)S(1)}, bf16[3,256,256]{2,1,0:T(8,128)(2,1)S(1)}, u32[]{:S(2)}, u32[]{:S(2)}) collective-permute-start(bf16[3,256,256]{2,1,0:T(8,128)(2,1)S(1)} %get-tuple-element.21.refs_0_), channel_id=1, source_target_pairs={{0,4},{4,0},{1,5},{5,1},{2,6},{6,2},{3,7},{7,3},{8,12},{12,8},{9,1... | collective-permute-start | bytes 1179656 | tf_op jit(solution)/shard_map/ppermute | solution.py:76
  26.2 0.5 collective-permute-start.4
  26.7 0.0 collective-permute-done.1.refs_2_
  26.7 1.5 %collective-permute-start.5 = (bf16[3,256,256]{2,1,0:T(8,128)(2,1)S(1)}, bf16[3,256,256]{2,1,0:T(8,128)(2,1)S(1)}, u32[]{:S(2)}, u32[]{:S(2)}) collective-permute-start(bf16[3,256,256]{2,1,0:T(8,128)(2,1)S(1)} %collective-permute-done.1.refs_2_), channel_id=1, source_target_pairs={{0,4},{4,0},{1,5},{5,1},{2,6},{6,2},{3,7},{7,3},{8,12},{12,8},{9,1... | collective-permute-start | bytes 1179656 | tf_op jit(solution)/shard_map/ppermute | solution.py:76
  28.2 6.0 %collective-permute-done.2.refs_3_ = bf16[3,256,256]{2,1,0:T(8,128)(2,1)S(1)} collective-permute-done((bf16[3,256,256]{2,1,0:T(8,128)(2,1)S(1)}, bf16[3,256,256]{2,1,0:T(8,128)(2,1)S(1)}, u32[]{:S(2)}, u32[]{:S(2)}) %collective-permute-start.2) | collective-permute-done | bytes 393248 | tf_op jit(solution)/shard_map/ppermute | solution.py:76
  34.2 1.4 collective-permute-start.6
  35.6 0.7 fusion.4
  36.2 0.1 concatenate.6.scalars
  36.3 0.3 collective-permute-done.3.refs_4_
  36.7 8.4 %collective-permute-done.4.refs_5_ = bf16[3,256,256]{2,1,0:T(8,128)(2,1)S(1)} collective-permute-done((bf16[3,256,256]{2,1,0:T(8,128)(2,1)S(1)}, bf16[3,256,256]{2,1,0:T(8,128)(2,1)S(1)}, u32[]{:S(2)}, u32[]{:S(2)}) %collective-permute-start.4) | collective-permute-done | bytes 393248 | tf_op jit(solution)/shard_map/ppermute | solution.py:76
  45.1 8.4 %collective-permute-done.5.refs_6_ = bf16[3,256,256]{2,1,0:T(8,128)(2,1)S(1)} collective-permute-done((bf16[3,256,256]{2,1,0:T(8,128)(2,1)S(1)}, bf16[3,256,256]{2,1,0:T(8,128)(2,1)S(1)}, u32[]{:S(2)}, u32[]{:S(2)}) %collective-permute-start.5) | collective-permute-done | bytes 393248 | tf_op jit(solution)/shard_map/ppermute | solution.py:76
  53.5 6.1 %collective-permute-done.6.refs_7_ = bf16[3,256,256]{2,1,0:T(8,128)(2,1)S(1)} collective-permute-done((bf16[3,256,256]{2,1,0:T(8,128)(2,1)S(1)}, bf16[3,256,256]{2,1,0:T(8,128)(2,1)S(1)}, u32[]{:S(2)}, u32[]{:S(2)}) %collective-permute-start.6) | collective-permute-done | bytes 393248 | tf_op jit(solution)/shard_map/ppermute | solution.py:76
  59.6 4.3 %tiles_first.1 = (bf16[8,256,768]{2,1,0:T(8,128)(2,1)}, f32[2,2,5,64,256]{4,3,2,1,0:T(8,128)S(1)}, f32[2,2,5,64,256]{4,3,2,1,0:T(8,128)S(1)}) custom-call(s32[40]{0:T(128)S(1)} %concatenate.6.scalars, bf16[3,256,256]{2,1,0:T(8,128)(2,1)S(1)} %get-tuple-element.21.refs_0_, bf16[3,256,256]{2,1,0:T(8,128)(2,1)S(1)} %collective-permute-done.refs_1_, ...), custom_call_target="tpu_custom_call" | custom-call | flops 1006632960 | bytes 4194304 | tf_op jit(solution)/shard_map/tiles_first/pallas_call | solution.py:115
  63.9 0.0 copy-start
  63.9 1.9 %copy-done = bf16[8,256,768]{2,1,0:T(8,128)(2,1)S(1)} copy-done((bf16[8,256,768]{2,1,0:T(8,128)(2,1)S(1)}, bf16[8,256,768]{2,1,0:T(8,128)(2,1)}, u32[]{:S(2)}) %copy-start) | copy-done | bytes 3145752
  65.8 2.2 %tiles_second.1 = (f32[2,2,4,64,256]{4,3,2,1,0:T(8,128)S(1)}, f32[2,2,4,64,256]{4,3,2,1,0:T(8,128)S(1)}) custom-call(s32[40]{0:T(128)S(1)} %concatenate.6.scalars, bf16[8,256,768]{2,1,0:T(8,128)(2,1)S(1)} %copy-done), custom_call_target="tpu_custom_call" | custom-call | flops 805306368 | bytes 4194304 | tf_op jit(solution)/shard_map/tiles_second/pallas_call | solution.py:115
  68.0 0.1 collective-permute-start.13
  68.1 0.5 collective-permute-start.7
  68.6 2.1 %collective-permute-done.13 = f32[2,2,4,64,256]{4,3,2,1,0:T(8,128)S(1)} collective-permute-done((f32[2,2,4,64,256]{4,3,2,1,0:T(8,128)S(1)}, f32[2,2,4,64,256]{4,3,2,1,0:T(8,128)S(1)}, u32[]{:S(2)}, u32[]{:S(2)}) %collective-permute-start.13) | collective-permute-done | bytes 1048608 | tf_op jit(solution)/shard_map/ppermute | solution.py:76
  70.7 0.1 add.103
  70.9 0.1 collective-permute-start.14
  71.0 1.6 %collective-permute-done.7 = f32[2,2,5,64,256]{4,3,2,1,0:T(8,128)S(1)} collective-permute-done((f32[2,2,5,64,256]{4,3,2,1,0:T(8,128)S(1)}, f32[2,2,5,64,256]{4,3,2,1,0:T(8,128)S(1)}, u32[]{:S(2)}, u32[]{:S(2)}) %collective-permute-start.7) | collective-permute-done | bytes 1310752 | tf_op jit(solution)/shard_map/ppermute | solution.py:76
  72.6 0.2 add.99
  72.9 1.6 %collective-permute-start.8 = (f32[2,5,64,256]{3,2,1,0:T(8,128)S(1)}, f32[2,5,64,256]{3,2,1,0:T(8,128)S(1)}, u32[]{:S(2)}, u32[]{:S(2)}) collective-permute-start(f32[2,5,64,256]{3,2,1,0:T(8,128)S(1)} %slice_bitcast_fusion), channel_id=1, source_target_pairs={{0,2},{2,0},{1,3},{3,1},{4,6},{6,4},{5,7},{7,5},{8,10},{10,8},{9,1... | collective-permute-start | bytes 1966088 | tf_op jit(solution)/shard_map/ppermute | solution.py:76
  74.4 10.5 %collective-permute-done.14 = f32[2,4,64,256]{3,2,1,0:T(8,128)S(1)} collective-permute-done((f32[2,4,64,256]{3,2,1,0:T(8,128)S(1)}, f32[2,4,64,256]{3,2,1,0:T(8,128)S(1)}, u32[]{:S(2)}, u32[]{:S(2)}) %collective-permute-start.14) | collective-permute-done | bytes 524320 | tf_op jit(solution)/shard_map/ppermute | solution.py:76
  85.0 0.1 fusion.1
  85.1 1.6 %collective-permute-start.15 = (f32[4,64,256]{2,1,0:T(8,128)S(1)}, f32[4,64,256]{2,1,0:T(8,128)S(1)}, u32[]{:S(2)}, u32[]{:S(2)}) collective-permute-start(f32[4,64,256]{2,1,0:T(8,128)S(1)} %slice_bitcast_fusion.6), channel_id=1, source_target_pairs={{0,2},{2,0},{1,3},{3,1},{4,6},{6,4},{5,7},{7,5},{8,10},{10,8},{9,1... | collective-permute-start | bytes 786440 | tf_op jit(solution)/shard_map/ppermute | solution.py:76
  86.6 3.9 %collective-permute-done.8 = f32[2,5,64,256]{3,2,1,0:T(8,128)S(1)} collective-permute-done((f32[2,5,64,256]{3,2,1,0:T(8,128)S(1)}, f32[2,5,64,256]{3,2,1,0:T(8,128)S(1)}, u32[]{:S(2)}, u32[]{:S(2)}) %collective-permute-start.8) | collective-permute-done | bytes 655392 | tf_op jit(solution)/shard_map/ppermute | solution.py:76
  90.5 0.1 fusion
  90.6 0.5 collective-permute-start.9
  91.2 4.2 %collective-permute-done.15 = f32[4,64,256]{2,1,0:T(8,128)S(1)} collective-permute-done((f32[4,64,256]{2,1,0:T(8,128)S(1)}, f32[4,64,256]{2,1,0:T(8,128)S(1)}, u32[]{:S(2)}, u32[]{:S(2)}) %collective-permute-start.15) | collective-permute-done | bytes 262176 | tf_op jit(solution)/shard_map/ppermute | solution.py:76
  95.4 0.2 collective-permute-start.16
  95.6 3.8 %collective-permute-done.9 = f32[5,64,256]{2,1,0:T(8,128)S(1)} collective-permute-done((f32[5,64,256]{2,1,0:T(8,128)S(1)}, f32[5,64,256]{2,1,0:T(8,128)S(1)}, u32[]{:S(2)}, u32[]{:S(2)}) %collective-permute-start.9) | collective-permute-done | bytes 327712 | tf_op jit(solution)/shard_map/ppermute | solution.py:76
  99.5 0.8 collective-permute-start.10
  100.3 16.7 %collective-permute-done.16 = f32[4,64,256]{2,1,0:T(8,128)S(1)} collective-permute-done((f32[4,64,256]{2,1,0:T(8,128)S(1)}, f32[4,64,256]{2,1,0:T(8,128)S(1)}, u32[]{:S(2)}, u32[]{:S(2)}) %collective-permute-start.16) | collective-permute-done | bytes 262176 | tf_op jit(solution)/shard_map/ppermute | solution.py:76
  117.0 1.4 collective-permute-start.17
  118.5 4.7 %collective-permute-done.10 = f32[5,64,256]{2,1,0:T(8,128)S(1)} collective-permute-done((f32[5,64,256]{2,1,0:T(8,128)S(1)}, f32[5,64,256]{2,1,0:T(8,128)S(1)}, u32[]{:S(2)}, u32[]{:S(2)}) %collective-permute-start.10) | collective-permute-done | bytes 327712 | tf_op jit(solution)/shard_map/ppermute | solution.py:76
  123.2 0.1 collective-permute-start.11
  123.3 0.4 collective-permute-done.17
  123.7 0.1 fusion.7
  123.8 0.0 copy-start.1
  123.8 1.7 %collective-permute-start.18 = (f32[2,4,64,256]{3,2,1,0:T(8,128)S(1)}, f32[2,4,64,256]{3,2,1,0:T(8,128)S(1)}, u32[]{:S(2)}, u32[]{:S(2)}) collective-permute-start(f32[2,4,64,256]{3,2,1,0:T(8,128)S(1)} %get-tuple-element.26), channel_id=1, source_target_pairs={{0,8},{8,0},{16,24},{24,16},{1,9},{9,1},{17,25},{25,17},{2,10},{10... | collective-permute-start | bytes 1572872 | tf_op jit(solution)/shard_map/ppermute | solution.py:76
  125.5 8.4 %collective-permute-done.11 = f32[5,64,256]{2,1,0:T(8,128)S(1)} collective-permute-done((f32[5,64,256]{2,1,0:T(8,128)S(1)}, f32[5,64,256]{2,1,0:T(8,128)S(1)}, u32[]{:S(2)}, u32[]{:S(2)}) %collective-permute-start.11) | collective-permute-done | bytes 327712 | tf_op jit(solution)/shard_map/ppermute | solution.py:76
  133.9 0.1 fusion.8
  134.1 1.6 %collective-permute-start.12 = (f32[2,5,64,256]{3,2,1,0:T(8,128)S(1)}, f32[2,5,64,256]{3,2,1,0:T(8,128)S(1)}, u32[]{:S(2)}, u32[]{:S(2)}) collective-permute-start(f32[2,5,64,256]{3,2,1,0:T(8,128)S(1)} %get-tuple-element.24), channel_id=1, source_target_pairs={{0,4},{4,0},{1,5},{5,1},{2,6},{6,2},{3,7},{7,3},{8,12},{12,8},{9,1... | collective-permute-start | bytes 1966088 | tf_op jit(solution)/shard_map/ppermute | solution.py:76
  135.6 0.0 copy-done.1
  135.7 7.7 %collective-permute-done.18 = f32[2,4,64,256]{3,2,1,0:T(8,128)S(1)} collective-permute-done((f32[2,4,64,256]{3,2,1,0:T(8,128)S(1)}, f32[2,4,64,256]{3,2,1,0:T(8,128)S(1)}, u32[]{:S(2)}, u32[]{:S(2)}) %collective-permute-start.18) | collective-permute-done | bytes 524320 | tf_op jit(solution)/shard_map/ppermute | solution.py:76
  143.4 0.1 pad_maximum_fusion.2
  143.5 3.9 %collective-permute-done.12 = f32[2,5,64,256]{3,2,1,0:T(8,128)S(1)} collective-permute-done((f32[2,5,64,256]{3,2,1,0:T(8,128)S(1)}, f32[2,5,64,256]{3,2,1,0:T(8,128)S(1)}, u32[]{:S(2)}, u32[]{:S(2)}) %collective-permute-start.12) | collective-permute-done | bytes 655392 | tf_op jit(solution)/shard_map/ppermute | solution.py:76
  147.4 0.1 pad_maximum_fusion.1
  147.5 0.3 pad_maximum_fusion
  147.8 0.6 gather_fusion
  148.4 0.9 bitcast_select_fusion
  (11 shorter events, 0.4 us)
Async XLA Ops:
  1.5 20.5 %collective-permute-start = (bf16[3,256,256]{2,1,0:T(8,128)(2,1)S(1)}, bf16[3,256,256]{2,1,0:T(8,128)(2,1)S(1)}, u32[]{:S(2)}, u32[]{:S(2)}) collective-permute-start(bf16[3,256,256]{2,1,0:T(8,128)(2,1)S(1)} %get-tuple-element.22), channel_id=1, source_target_pairs={{0,8},{8,0},{16,24},{24,16},{1,9},{9,1},{17,25},{25,17},{2,10},{10... | collective-permute-start | bytes 1179656 | tf_op jit(solution)/shard_map/ppermute | solution.py:76
  4.6 22.1 %collective-permute-start.1 = (bf16[3,256,256]{2,1,0:T(8,128)(2,1)S(1)}, bf16[3,256,256]{2,1,0:T(8,128)(2,1)S(1)}, u32[]{:S(2)}, u32[]{:S(2)}) collective-permute-start(bf16[3,256,256]{2,1,0:T(8,128)(2,1)S(1)} %get-tuple-element.19), channel_id=1, source_target_pairs={{0,16},{8,24},{16,0},{24,8},{1,17},{9,25},{17,1},{25,9},{2,18},{10... | collective-permute-start | bytes 1179656 | tf_op jit(solution)/shard_map/ppermute | solution.py:76
  22.0 12.2 %collective-permute-start.2 = (bf16[3,256,256]{2,1,0:T(8,128)(2,1)S(1)}, bf16[3,256,256]{2,1,0:T(8,128)(2,1)S(1)}, u32[]{:S(2)}, u32[]{:S(2)}) collective-permute-start(bf16[3,256,256]{2,1,0:T(8,128)(2,1)S(1)} %get-tuple-element.13), channel_id=1, source_target_pairs={{0,24},{8,16},{16,8},{24,0},{1,25},{9,17},{17,9},{25,1},{2,26},{10... | collective-permute-start | bytes 1179656 | tf_op jit(solution)/shard_map/ppermute | solution.py:76
  24.6 12.1 %collective-permute-start.3 = (bf16[3,256,256]{2,1,0:T(8,128)(2,1)S(1)}, bf16[3,256,256]{2,1,0:T(8,128)(2,1)S(1)}, u32[]{:S(2)}, u32[]{:S(2)}) collective-permute-start(bf16[3,256,256]{2,1,0:T(8,128)(2,1)S(1)} %get-tuple-element.21.refs_0_), channel_id=1, source_target_pairs={{0,4},{4,0},{1,5},{5,1},{2,6},{6,2},{3,7},{7,3},{8,12},{12,8},{9,1... | collective-permute-start | bytes 1179656 | tf_op jit(solution)/shard_map/ppermute | solution.py:76
  26.2 19.0 %collective-permute-start.4 = (bf16[3,256,256]{2,1,0:T(8,128)(2,1)S(1)}, bf16[3,256,256]{2,1,0:T(8,128)(2,1)S(1)}, u32[]{:S(2)}, u32[]{:S(2)}) collective-permute-start(bf16[3,256,256]{2,1,0:T(8,128)(2,1)S(1)} %collective-permute-done.refs_1_), channel_id=1, source_target_pairs={{0,4},{4,0},{1,5},{5,1},{2,6},{6,2},{3,7},{7,3},{8,12},{12,8},{9,1... | collective-permute-start | bytes 1179656 | tf_op jit(solution)/shard_map/ppermute | solution.py:76
  26.7 26.9 %collective-permute-start.5 = (bf16[3,256,256]{2,1,0:T(8,128)(2,1)S(1)}, bf16[3,256,256]{2,1,0:T(8,128)(2,1)S(1)}, u32[]{:S(2)}, u32[]{:S(2)}) collective-permute-start(bf16[3,256,256]{2,1,0:T(8,128)(2,1)S(1)} %collective-permute-done.1.refs_2_), channel_id=1, source_target_pairs={{0,4},{4,0},{1,5},{5,1},{2,6},{6,2},{3,7},{7,3},{8,12},{12,8},{9,1... | collective-permute-start | bytes 1179656 | tf_op jit(solution)/shard_map/ppermute | solution.py:76
  34.2 25.4 %collective-permute-start.6 = (bf16[3,256,256]{2,1,0:T(8,128)(2,1)S(1)}, bf16[3,256,256]{2,1,0:T(8,128)(2,1)S(1)}, u32[]{:S(2)}, u32[]{:S(2)}) collective-permute-start(bf16[3,256,256]{2,1,0:T(8,128)(2,1)S(1)} %collective-permute-done.2.refs_3_), channel_id=1, source_target_pairs={{0,4},{4,0},{1,5},{5,1},{2,6},{6,2},{3,7},{7,3},{8,12},{12,8},{9,1... | collective-permute-start | bytes 1179656 | tf_op jit(solution)/shard_map/ppermute | solution.py:76
  63.9 1.9 %copy-start = (bf16[8,256,768]{2,1,0:T(8,128)(2,1)S(1)}, bf16[8,256,768]{2,1,0:T(8,128)(2,1)}, u32[]{:S(2)}) copy-start(bf16[8,256,768]{2,1,0:T(8,128)(2,1)} %get-tuple-element.16.blocks) | copy-start | bytes 9437188
  68.0 2.7 %collective-permute-start.13 = (f32[2,2,4,64,256]{4,3,2,1,0:T(8,128)S(1)}, f32[2,2,4,64,256]{4,3,2,1,0:T(8,128)S(1)}, u32[]{:S(2)}, u32[]{:S(2)}) collective-permute-start(f32[2,2,4,64,256]{4,3,2,1,0:T(8,128)S(1)} %get-tuple-element.18), channel_id=1, source_target_pairs={{0,1},{1,0},{2,3},{3,2},{4,5},{5,4},{6,7},{7,6},{8,9},{9,8},{10,11... | collective-permute-start | bytes 3145736 | tf_op jit(solution)/shard_map/ppermute | solution.py:76
  68.1 4.5 %collective-permute-start.7 = (f32[2,2,5,64,256]{4,3,2,1,0:T(8,128)S(1)}, f32[2,2,5,64,256]{4,3,2,1,0:T(8,128)S(1)}, u32[]{:S(2)}, u32[]{:S(2)}) collective-permute-start(f32[2,2,5,64,256]{4,3,2,1,0:T(8,128)S(1)} %get-tuple-element.15), channel_id=1, source_target_pairs={{0,1},{1,0},{2,3},{3,2},{4,5},{5,4},{6,7},{7,6},{8,9},{9,8},{10,11... | collective-permute-start | bytes 3932168 | tf_op jit(solution)/shard_map/ppermute | solution.py:76
  70.9 14.0 %collective-permute-start.14 = (f32[2,4,64,256]{3,2,1,0:T(8,128)S(1)}, f32[2,4,64,256]{3,2,1,0:T(8,128)S(1)}, u32[]{:S(2)}, u32[]{:S(2)}) collective-permute-start(f32[2,4,64,256]{3,2,1,0:T(8,128)S(1)} %slice_bitcast_fusion.2), channel_id=1, source_target_pairs={{0,8},{8,0},{16,24},{24,16},{1,9},{9,1},{17,25},{25,17},{2,10},{10... | collective-permute-start | bytes 1572872 | tf_op jit(solution)/shard_map/ppermute | solution.py:76
  72.9 17.6 %collective-permute-start.8 = (f32[2,5,64,256]{3,2,1,0:T(8,128)S(1)}, f32[2,5,64,256]{3,2,1,0:T(8,128)S(1)}, u32[]{:S(2)}, u32[]{:S(2)}) collective-permute-start(f32[2,5,64,256]{3,2,1,0:T(8,128)S(1)} %slice_bitcast_fusion), channel_id=1, source_target_pairs={{0,2},{2,0},{1,3},{3,1},{4,6},{6,4},{5,7},{7,5},{8,10},{10,8},{9,1... | collective-permute-start | bytes 1966088 | tf_op jit(solution)/shard_map/ppermute | solution.py:76
  85.1 10.3 %collective-permute-start.15 = (f32[4,64,256]{2,1,0:T(8,128)S(1)}, f32[4,64,256]{2,1,0:T(8,128)S(1)}, u32[]{:S(2)}, u32[]{:S(2)}) collective-permute-start(f32[4,64,256]{2,1,0:T(8,128)S(1)} %slice_bitcast_fusion.6), channel_id=1, source_target_pairs={{0,2},{2,0},{1,3},{3,1},{4,6},{6,4},{5,7},{7,5},{8,10},{10,8},{9,1... | collective-permute-start | bytes 786440 | tf_op jit(solution)/shard_map/ppermute | solution.py:76
  90.6 8.8 %collective-permute-start.9 = (f32[5,64,256]{2,1,0:T(8,128)S(1)}, f32[5,64,256]{2,1,0:T(8,128)S(1)}, u32[]{:S(2)}, u32[]{:S(2)}) collective-permute-start(f32[5,64,256]{2,1,0:T(8,128)S(1)} %slice_bitcast_fusion.4), channel_id=1, source_target_pairs={{0,8},{8,0},{16,24},{24,16},{1,9},{9,1},{17,25},{25,17},{2,10},{10... | collective-permute-start | bytes 983048 | tf_op jit(solution)/shard_map/ppermute | solution.py:76
  95.4 21.6 %collective-permute-start.16 = (f32[4,64,256]{2,1,0:T(8,128)S(1)}, f32[4,64,256]{2,1,0:T(8,128)S(1)}, u32[]{:S(2)}, u32[]{:S(2)}) collective-permute-start(f32[4,64,256]{2,1,0:T(8,128)S(1)} %fusion.3), channel_id=1, source_target_pairs={{0,16},{8,24},{16,0},{24,8},{1,17},{9,25},{17,1},{25,9},{2,18},{10... | collective-permute-start | bytes 786440 | tf_op jit(solution)/shard_map/ppermute | solution.py:76
  99.5 23.7 %collective-permute-start.10 = (f32[5,64,256]{2,1,0:T(8,128)S(1)}, f32[5,64,256]{2,1,0:T(8,128)S(1)}, u32[]{:S(2)}, u32[]{:S(2)}) collective-permute-start(f32[5,64,256]{2,1,0:T(8,128)S(1)} %fusion.2), channel_id=1, source_target_pairs={{0,16},{8,24},{16,0},{24,8},{1,17},{9,25},{17,1},{25,9},{2,18},{10... | collective-permute-start | bytes 983048 | tf_op jit(solution)/shard_map/ppermute | solution.py:76
  117.0 6.7 %collective-permute-start.17 = (f32[4,64,256]{2,1,0:T(8,128)S(1)}, f32[4,64,256]{2,1,0:T(8,128)S(1)}, u32[]{:S(2)}, u32[]{:S(2)}) collective-permute-start(f32[4,64,256]{2,1,0:T(8,128)S(1)} %add_multiply_fusion.1), channel_id=1, source_target_pairs={{0,4},{4,0},{1,5},{5,1},{2,6},{6,2},{3,7},{7,3},{8,12},{12,8},{9,1... | collective-permute-start | bytes 786440 | tf_op jit(solution)/shard_map/ppermute | solution.py:76
  123.2 10.7 %collective-permute-start.11 = (f32[5,64,256]{2,1,0:T(8,128)S(1)}, f32[5,64,256]{2,1,0:T(8,128)S(1)}, u32[]{:S(2)}, u32[]{:S(2)}) collective-permute-start(f32[5,64,256]{2,1,0:T(8,128)S(1)} %add_multiply_fusion), channel_id=1, source_target_pairs={{0,8},{8,0},{16,24},{24,16},{1,9},{9,1},{17,25},{25,17},{2,10},{10... | collective-permute-start | bytes 983048 | tf_op jit(solution)/shard_map/ppermute | solution.py:76
  123.8 11.8 %copy-start.1 = (s32[1,10,2]{1,2,0:T(2,128)S(1)}, s32[1,10,2]{1,2,0:T(2,128)}, u32[]{:S(2)}) copy-start(s32[1,10,2]{1,2,0:T(2,128)} %param.4) | copy-start | bytes 244
  123.8 19.6 %collective-permute-start.18 = (f32[2,4,64,256]{3,2,1,0:T(8,128)S(1)}, f32[2,4,64,256]{3,2,1,0:T(8,128)S(1)}, u32[]{:S(2)}, u32[]{:S(2)}) collective-permute-start(f32[2,4,64,256]{3,2,1,0:T(8,128)S(1)} %get-tuple-element.26), channel_id=1, source_target_pairs={{0,8},{8,0},{16,24},{24,16},{1,9},{9,1},{17,25},{25,17},{2,10},{10... | collective-permute-start | bytes 1572872 | tf_op jit(solution)/shard_map/ppermute | solution.py:76
  134.1 13.4 %collective-permute-start.12 = (f32[2,5,64,256]{3,2,1,0:T(8,128)S(1)}, f32[2,5,64,256]{3,2,1,0:T(8,128)S(1)}, u32[]{:S(2)}, u32[]{:S(2)}) collective-permute-start(f32[2,5,64,256]{3,2,1,0:T(8,128)S(1)} %get-tuple-element.24), channel_id=1, source_target_pairs={{0,4},{4,0},{1,5},{5,1},{2,6},{6,2},{3,7},{7,3},{8,12},{12,8},{9,1... | collective-permute-start | bytes 1966088 | tf_op jit(solution)/shard_map/ppermute | solution.py:76

commit v4 on v3

--- a/solution.py
+++ b/solution.py
@@ -9,12 +9,17 @@
 from jax.experimental.pallas import tpu as pltpu
 from jax.sharding import Mesh, PartitionSpec as P
 
-VMEM_LIMIT = 48 * 2**20
+VMEM_LIMIT = 24 * 2**20
+X_FIRST = (True, False, True, False)
 
 
 def tile_lists(block_count):
     rows, cols = np.triu_indices(block_count)
     return np.stack([rows, cols], axis=1).reshape(2, 2, -1, 2)
+
+
+def group_sizes(quarter):
+    return [len(piece) for piece in np.array_split(np.arange(quarter), len(X_FIRST))][::-1]
 
 
 def multiply_tiles(scalars, first_pair, blocks, keep_ref, send_ref, x_first):
@@ -44,21 +49,28 @@
     lax.fori_loop(0, group_size, one_slot, 0)
 
 
-def first_kernel(chunk_count, first_pair, scalars, *refs):
-    chunks = refs[: 2 * chunk_count]
-    blocks, keep_ref, send_ref = refs[2 * chunk_count :]
+def multiply_groups(scalars, first_pair, x_first, blocks, outs):
+    for index, first in enumerate(x_first):
+        keep_ref, send_ref = outs[2 * index : 2 * index + 2]
+        multiply_tiles(scalars, first_pair, blocks, keep_ref, send_ref, first)
+        first_pair += 4 * keep_ref.shape[2]
+
+
+def first_kernel(layout, first_pair, x_first, scalars, *refs):
+    pieces = refs[: len(layout)]
+    blocks = refs[len(layout)]
     z, y = scalars[0], scalars[1]
-    components, _, cells = chunks[0].shape
-    for index, chunk in enumerate(chunks):
-        other, step = divmod(index, chunk_count)
+    for (step, other, component), piece in zip(layout, pieces):
         block = (z ^ step) * 2 + (y ^ other)
-        for component in range(components):
-            blocks[block, :, component * cells : (component + 1) * cells] = chunk[component]
-    multiply_tiles(scalars, first_pair, blocks, keep_ref, send_ref, True)
-
-
-def second_kernel(first_pair, scalars, blocks, keep_ref, send_ref):
-    multiply_tiles(scalars, first_pair, blocks, keep_ref, send_ref, False)
+        cells = piece.shape[2]
+        for index in range(piece.shape[0]):
+            start = (component + index) * cells
+            blocks[block, :, start : start + cells] = piece[index]
+    multiply_groups(scalars, first_pair, x_first, blocks, refs[len(layout) + 1 :])
+
+
+def second_kernel(first_pair, x_first, scalars, blocks, *outs):
+    multiply_groups(scalars, first_pair, x_first, blocks, outs)
 
 
 def per_device(z_count, y_count, x_count, core_count, snapshots, tile_table):
@@ -75,15 +87,19 @@
         size = lax.axis_size(axis)
         return lax.ppermute(value, axis, [(i, i ^ bits) for i in range(size)])
 
+    def after(value, earlier):
+        return lax.optimization_barrier((value, earlier))
+
     lists = tile_lists(block_count)
     quarter = lists.shape[2]
-    sizes = (quarter - quarter // 2, quarter // 2)
+    sizes = group_sizes(quarter)
+    starts = np.cumsum([0] + sizes)
     ordered = np.stack(
         [
             np.concatenate(
                 [
-                    lists[of_y, of_bit ^ flip, cut].reshape(-1)
-                    for cut in (slice(0, sizes[0]), slice(sizes[0], quarter))
+                    lists[of_y, of_bit ^ flip, start : start + size].reshape(-1)
+                    for start, size in zip(starts, sizes)
                     for flip in range(2)
                 ]
             )
@@ -97,14 +113,20 @@
     def part(step):
         return lax.dynamic_slice_in_dim(snapshots, (z ^ step) * cells, cells, 2)
 
-    parts = [part(step) for step in range(z_count)]
-    own = [parts[0]]
-    for step in range(1, z_count):
-        piece = parts[step]
-        if step >= 3:
-            piece, own[step - 2] = lax.optimization_barrier((piece, own[step - 2]))
-        own.append(swap(piece, "z", step))
-    chunks = own + [swap(piece, "y", 1) for piece in own]
+    pieces = {(0, 0): part(0)}
+    far = range(2, z_count)
+    parts = {step: part(step) for step in far}
+    for component in range(components):
+        for step in far:
+            piece = parts[step][component : component + 1]
+            if component > 0:
+                piece, pieces[step, component - 1] = after(piece, pieces[step, component - 1])
+            pieces[step, component] = swap(piece, "z", step)
+        if component == 0:
+            pieces[1, 0] = swap(part(1), "z", 1)
+    layout = [(step, 0, component) for step, component in pieces]
+    layout += [(step, 1, component) for step, component in pieces]
+    chunks = list(pieces.values()) + [swap(piece, "y", 1) for piece in pieces.values()]
 
     def sums_shape(size, x_first):
         lead = (x_count, 2) if x_first else (2, x_count)
@@ -126,20 +148,21 @@
             name=name,
         )(scalars, *operands)
 
+    shapes = [sums_shape(size, first) for size, first in zip(sizes, X_FIRST) for _ in range(2)]
     blocks_shape = jax.ShapeDtypeStruct(
         (block_count, block_size, components * cells), jnp.bfloat16
     )
-    blocks, keep_a, send_a = call(
-        functools.partial(first_kernel, z_count, 4),
-        sizes[0],
-        [blocks_shape] + [sums_shape(sizes[0], True)] * 2,
+    blocks, *sums = call(
+        functools.partial(first_kernel, layout, 4, X_FIRST[:2]),
+        sizes[0] + sizes[1],
+        [blocks_shape] + shapes[:4],
         chunks,
         "tiles_first",
     )
-    keep_b, send_b = call(
-        functools.partial(second_kernel, 4 + 4 * sizes[0]),
-        sizes[1],
-        [sums_shape(sizes[1], False)] * 2,
+    sums += call(
+        functools.partial(second_kernel, 4 + 4 * (sizes[0] + sizes[1]), X_FIRST[2:]),
+        sizes[2] + sizes[3],
+        shapes[4:],
         [blocks],
         "tiles_second",
     )
@@ -160,18 +183,20 @@
             bits *= 2
         return value * scale_factor
 
-    total_a = keep_a + swap(send_a, "core", 1)
-    total_b = keep_b + swap(send_b, "core", 1)
-    held_a = over_high_bits(over_low_bit(over_x(total_a)))
-    held_b = over_high_bits(over_x(over_low_bit(total_b)))
-
-    column_a = jnp.stack([held_a, swap(held_a, "z", 1)])
-    column_b = jnp.stack([held_b, swap(held_b, "y", 1)])
-    whole_a = jnp.stack([column_a, swap(column_a, "y", 1)])
-    whole_b = jnp.stack([column_b, swap(column_b, "z", 1)])
-    flat = jnp.concatenate(
-        [part.reshape(-1, rows_dev, block_size) for part in (whole_a, whole_b)]
-    )
+    flat = []
+    for index, first in enumerate(X_FIRST):
+        keep, send = sums[2 * index : 2 * index + 2]
+        total = keep + swap(send, "core", 1)
+        if first:
+            held = over_high_bits(over_low_bit(over_x(total)))
+            pair = jnp.stack([held, swap(held, "z", 1)])
+            whole = jnp.stack([pair, swap(pair, "y", 1)])
+        else:
+            held = over_high_bits(over_x(over_low_bit(total)))
+            pair = jnp.stack([held, swap(held, "y", 1)])
+            whole = jnp.stack([pair, swap(pair, "z", 1)])
+        flat.append(whole.reshape(-1, rows_dev, block_size))
+    flat = jnp.concatenate(flat)
 
     table = tile_table[0]
     row_block = table[:, 0]
@@ -182,9 +207,12 @@
     pair = first * block_count - (first * (first - 1)) // 2 + second - first
     of_list, slot = pair // quarter, pair % quarter
     off_y, off_bit = (of_list // 2) ^ y, (of_list % 2) ^ low_bit
-    place_a = (off_y * 2 + off_bit) * sizes[0] + slot
-    place_b = 4 * sizes[0] + (off_bit * 2 + off_y) * sizes[1] + slot - sizes[0]
-    result = flat[jnp.where(slot < sizes[0], place_a, place_b)]
+    place = jnp.zeros_like(slot)
+    for start, size, first in zip(starts, sizes, X_FIRST):
+        off = off_y * 2 + off_bit if first else off_bit * 2 + off_y
+        here = 4 * int(start) + off * size + slot - int(start)
+        place = jnp.where((slot >= int(start)) & (slot < int(start) + size), here, place)
+    result = flat[place]
     result = jnp.where(valid[:, None, None], result, jnp.zeros_like(result))
     return result[None]
 

time: 150 us -> 132 us (0.88)
  waiting for transfers between devices: 112 us -> 55.8 us
  starting transfers between devices: 23.3 us -> 64.5 us
    ppermute x19 -> x39, waiting for transfers between devices: 112 us -> 55.8 us  [swap(): return lax.ppermute(value, axis, [(i, i ^ bits) for i in range(size)])]
    ppermute x19 -> x39, starting transfers between devices: 23.3 us -> 64.5 us  [swap(): return lax.ppermute(value, axis, [(i, i ^ bits) for i in range(size)])]
    unnamed x4 -> x2, local copies, waits for them, and re-layouts: 1.9 us -> 0.01 us
  transfers between devices with their start and end apart: 19 -> 39, of which waited for: 18 -> 16; matrix products, arithmetic and copies ran while one was open for 1% -> 2% of each run, Pallas kernels for 0% -> 2%
where the time goes in v4:
time: 132 us
  starting transfers between devices  64.5 us (49%)
  waiting for transfers between devices  55.8 us (42%)
  Pallas kernels  5.06 us (4%)
  local copies, waits for them, and re-layouts  3.94 us (3%)
  other arithmetic  2.19 us (2%)
    ppermute x39, starting transfers between devices, swap(): return lax.ppermute(value, axis, [(i, i ^ bits) for i in range(size)])  64.5 us
    ppermute x39, waiting for transfers between devices, swap(): return lax.ppermute(value, axis, [(i, i ^ bits) for i in range(size)])  55.8 us
    pallas_call x2, Pallas kernels, call(): pl.pallas_call(kernel, out_shape=out_shape, in_specs=[pl.BlockSpec(memory...  5.06 us
  transfers between devices with their start and end apart: 39, of which 16 were waited for; matrix products, arithmetic and copies ran while one was open for 2% of the time, Pallas kernels for 2%

profile of v4, /device:TPU:0, one launch (start us, length us, event | category | flops | bytes accessed | tf_op | source)
XLA Modules:
  0.0 131.8 jit_solution(2542931494289089253)
XLA Ops:
  0.0 1.2 constant_dynamic-slice_fusion.4
  1.2 3.1 %collective-permute-start.2 = (bf16[3,256,256]{2,1,0:T(8,128)(2,1)S(1)}, bf16[3,256,256]{2,1,0:T(8,128)(2,1)S(1)}, u32[]{:S(2)}, u32[]{:S(2)}) collective-permute-start(bf16[3,256,256]{2,1,0:T(8,128)(2,1)S(1)} %get-tuple-element.45), channel_id=1, source_target_pairs={{0,8},{8,0},{16,24},{24,16},{1,9},{9,1},{17,25},{25,17},{2,10},{10... | collective-permute-start | bytes 1179656 | tf_op jit(solution)/shard_map/ppermute | solution.py:88
  4.3 1.3 constant_dynamic-slice_fusion.5
  5.5 2.5 %collective-permute-start.1 = (bf16[1,256,256]{2,1,0:T(8,128)(2,1)S(1)}, bf16[1,256,256]{2,1,0:T(8,128)(2,1)S(1)}, u32[]{:S(2)}, u32[]{:S(2)}) collective-permute-start(bf16[1,256,256]{2,1,0:T(8,128)(2,1)S(1)} %get-tuple-element.40), channel_id=1, source_target_pairs={{0,24},{8,16},{16,8},{24,0},{1,25},{9,17},{17,9},{25,1},{2,26},{10... | collective-permute-start | bytes 393224 | tf_op jit(solution)/shard_map/ppermute | solution.py:88
  8.1 0.2 collective-permute-start
  8.3 11.4 %collective-permute-done.1.refs_2_ = bf16[1,256,256]{2,1,0:T(8,128)(2,1)S(1)} collective-permute-done((bf16[1,256,256]{2,1,0:T(8,128)(2,1)S(1)}, bf16[1,256,256]{2,1,0:T(8,128)(2,1)S(1)}, u32[]{:S(2)}, u32[]{:S(2)}) %collective-permute-start.1) | collective-permute-done | bytes 131104 | tf_op jit(solution)/shard_map/ppermute | solution.py:88
  19.6 1.4 %collective-permute-start.4 = (bf16[1,256,256]{2,1,0:T(8,128)(2,1)S(1)}, bf16[1,256,256]{2,1,0:T(8,128)(2,1)S(1)}, u32[]{:S(2)}, u32[]{:S(2)}) collective-permute-start(bf16[1,256,256]{2,1,0:T(8,128)(2,1)S(1)} %get-tuple-element.26), channel_id=1, source_target_pairs={{0,24},{8,16},{16,8},{24,0},{1,25},{9,17},{17,9},{25,1},{2,26},{10... | collective-permute-start | bytes 393224 | tf_op jit(solution)/shard_map/ppermute | solution.py:88
  21.0 0.8 collective-permute-start.3
  21.7 1.5 %collective-permute-start.9 = (bf16[1,256,256]{2,1,0:T(8,128)(2,1)S(1)}, bf16[1,256,256]{2,1,0:T(8,128)(2,1)S(1)}, u32[]{:S(2)}, u32[]{:S(2)}) collective-permute-start(bf16[1,256,256]{2,1,0:T(8,128)(2,1)S(1)} %collective-permute-done.1.refs_2_), channel_id=1, source_target_pairs={{0,4},{4,0},{1,5},{5,1},{2,6},{6,2},{3,7},{7,3},{8,12},{12,8},{9,1... | collective-permute-start | bytes 393224 | tf_op jit(solution)/shard_map/ppermute | solution.py:88
  23.3 0.5 collective-permute-start.8
  23.8 2.8 %collective-permute-done.4.refs_5_ = bf16[1,256,256]{2,1,0:T(8,128)(2,1)S(1)} collective-permute-done((bf16[1,256,256]{2,1,0:T(8,128)(2,1)S(1)}, bf16[1,256,256]{2,1,0:T(8,128)(2,1)S(1)}, u32[]{:S(2)}, u32[]{:S(2)}) %collective-permute-start.4) | collective-permute-done | bytes 131104 | tf_op jit(solution)/shard_map/ppermute | solution.py:88
  26.6 1.5 %collective-permute-start.7 = (bf16[3,256,256]{2,1,0:T(8,128)(2,1)S(1)}, bf16[3,256,256]{2,1,0:T(8,128)(2,1)S(1)}, u32[]{:S(2)}, u32[]{:S(2)}) collective-permute-start(bf16[3,256,256]{2,1,0:T(8,128)(2,1)S(1)} %get-tuple-element.46.refs_0_), channel_id=1, source_target_pairs={{0,4},{4,0},{1,5},{5,1},{2,6},{6,2},{3,7},{7,3},{8,12},{12,8},{9,1... | collective-permute-start | bytes 1179656 | tf_op jit(solution)/shard_map/ppermute | solution.py:88
  28.1 0.5 collective-permute-start.10
  28.6 1.1 collective-permute-done.3.refs_4_
  29.7 6.7 %collective-permute-start.6 = (bf16[1,256,256]{2,1,0:T(8,128)(2,1)S(1)}, bf16[1,256,256]{2,1,0:T(8,128)(2,1)S(1)}, u32[]{:S(2)}, u32[]{:S(2)}) collective-permute-start(bf16[1,256,256]{2,1,0:T(8,128)(2,1)S(1)} %get-tuple-element.29), channel_id=1, source_target_pairs={{0,24},{8,16},{16,8},{24,0},{1,25},{9,17},{17,9},{25,1},{2,26},{10... | collective-permute-start | bytes 393224 | tf_op jit(solution)/shard_map/ppermute | solution.py:88
  36.4 4.5 %collective-permute-start.12 = (bf16[1,256,256]{2,1,0:T(8,128)(2,1)S(1)}, bf16[1,256,256]{2,1,0:T(8,128)(2,1)S(1)}, u32[]{:S(2)}, u32[]{:S(2)}) collective-permute-start(bf16[1,256,256]{2,1,0:T(8,128)(2,1)S(1)} %collective-permute-done.4.refs_5_), channel_id=1, source_target_pairs={{0,4},{4,0},{1,5},{5,1},{2,6},{6,2},{3,7},{7,3},{8,12},{12,8},{9,1... | collective-permute-start | bytes 393224 | tf_op jit(solution)/shard_map/ppermute | solution.py:88
  40.9 2.9 %collective-permute-start.11 = (bf16[1,256,256]{2,1,0:T(8,128)(2,1)S(1)}, bf16[1,256,256]{2,1,0:T(8,128)(2,1)S(1)}, u32[]{:S(2)}, u32[]{:S(2)}) collective-permute-start(bf16[1,256,256]{2,1,0:T(8,128)(2,1)S(1)} %collective-permute-done.3.refs_4_), channel_id=1, source_target_pairs={{0,4},{4,0},{1,5},{5,1},{2,6},{6,2},{3,7},{7,3},{8,12},{12,8},{9,1... | collective-permute-start | bytes 393224 | tf_op jit(solution)/shard_map/ppermute | solution.py:88
  43.8 6.8 %collective-permute-done.12.refs_13_ = bf16[1,256,256]{2,1,0:T(8,128)(2,1)S(1)} collective-permute-done((bf16[1,256,256]{2,1,0:T(8,128)(2,1)S(1)}, bf16[1,256,256]{2,1,0:T(8,128)(2,1)S(1)}, u32[]{:S(2)}, u32[]{:S(2)}) %collective-permute-start.12) | collective-permute-done | bytes 131104 | tf_op jit(solution)/shard_map/ppermute | solution.py:88
  50.6 1.5 %collective-permute-start.14 = (bf16[1,256,256]{2,1,0:T(8,128)(2,1)S(1)}, bf16[1,256,256]{2,1,0:T(8,128)(2,1)S(1)}, u32[]{:S(2)}, u32[]{:S(2)}) collective-permute-start(bf16[1,256,256]{2,1,0:T(8,128)(2,1)S(1)} %collective-permute-done.6.refs_7_), channel_id=1, source_target_pairs={{0,4},{4,0},{1,5},{5,1},{2,6},{6,2},{3,7},{7,3},{8,12},{12,8},{9,1... | collective-permute-start | bytes 393224 | tf_op jit(solution)/shard_map/ppermute | solution.py:88
  52.2 0.5 collective-permute-start.13
  52.7 0.7 fusion.9
  53.4 0.1 concatenate.6.scalars
  53.5 2.2 %collective-permute-done.14.refs_15_ = bf16[1,256,256]{2,1,0:T(8,128)(2,1)S(1)} collective-permute-done((bf16[1,256,256]{2,1,0:T(8,128)(2,1)S(1)}, bf16[1,256,256]{2,1,0:T(8,128)(2,1)S(1)}, u32[]{:S(2)}, u32[]{:S(2)}) %collective-permute-start.14) | collective-permute-done | bytes 131104 | tf_op jit(solution)/shard_map/ppermute | solution.py:88
  55.6 1.5 %collective-permute-done.13.refs_14_ = bf16[1,256,256]{2,1,0:T(8,128)(2,1)S(1)} collective-permute-done((bf16[1,256,256]{2,1,0:T(8,128)(2,1)S(1)}, bf16[1,256,256]{2,1,0:T(8,128)(2,1)S(1)}, u32[]{:S(2)}, u32[]{:S(2)}) %collective-permute-start.13) | collective-permute-done | bytes 131104 | tf_op jit(solution)/shard_map/ppermute | solution.py:88
  57.1 2.4 %tiles_first.1 = (bf16[8,256,768]{2,1,0:T(8,128)(2,1)S(1)}, f32[2,2,2,64,256]{4,3,2,1,0:T(8,128)S(1)}, f32[2,2,2,64,256]{4,3,2,1,0:T(8,128)S(1)}, f32[2,2,2,64,2...) custom-call(s32[40]{0:T(128)S(1)} %concatenate.6.scalars, bf16[3,256,256]{2,1,0:T(8,128)(2,1)S(1)} %get-tuple-element.46.refs_0_, ...), custom_call_target="tpu_custom_call" | custom-call | flops 805306368 | bytes 4194304 | tf_op jit(solution)/shard_map/tiles_first/pallas_call | solution.py:137
  59.7 0.6 collective-permute-start.21
  60.3 2.6 %tiles_second.1 = (f32[2,2,2,64,256]{4,3,2,1,0:T(8,128)S(1)}, f32[2,2,2,64,256]{4,3,2,1,0:T(8,128)S(1)}, f32[2,2,3,64,256]{4,3,2,1,0:T(8,128)S(1)}, f32[2,2,3,64,256]{4,3,2,1,0:T(8,128)S(1)}) custom-call(s32[40]{0:T(128)S(1)} %concatenate.6.scalars, bf16[8,256,768]{2,1,0:T(8,128)(2,1)S(1)} %get-tuple-element.34.blocks), custom_call_target="tpu_custom_call" | custom-call | flops 1006632960 | bytes 4194304 | tf_op jit(solution)/shard_map/tiles_second/pallas_call | solution.py:137
  62.9 0.1 collective-permute-start.27
  63.0 0.5 collective-permute-start.33
  63.6 1.6 %collective-permute-start.16 = (f32[2,2,64,256]{3,2,1,0:T(8,128)S(1)}, f32[2,2,64,256]{3,2,1,0:T(8,128)S(1)}, u32[]{:S(2)}, u32[]{:S(2)}) collective-permute-start(f32[2,2,64,256]{3,2,1,0:T(8,128)S(1)} %slice_bitcast_fusion.6), channel_id=1, source_target_pairs={{0,2},{2,0},{1,3},{3,1},{4,6},{6,4},{5,7},{7,5},{8,10},{10,8},{9,1... | collective-permute-start | bytes 786440 | tf_op jit(solution)/shard_map/ppermute | solution.py:88
  65.3 2.7 %collective-permute-start.22 = (f32[2,2,64,256]{3,2,1,0:T(8,128)S(1)}, f32[2,2,64,256]{3,2,1,0:T(8,128)S(1)}, u32[]{:S(2)}, u32[]{:S(2)}) collective-permute-start(f32[2,2,64,256]{3,2,1,0:T(8,128)S(1)} %slice_bitcast_fusion.4), channel_id=1, source_target_pairs={{0,8},{8,0},{16,24},{24,16},{1,9},{9,1},{17,25},{25,17},{2,10},{10... | collective-permute-start | bytes 786440 | tf_op jit(solution)/shard_map/ppermute | solution.py:88
  68.0 0.6 collective-permute-start.28
  68.6 4.2 %collective-permute-done.16 = f32[2,2,64,256]{3,2,1,0:T(8,128)S(1)} collective-permute-done((f32[2,2,64,256]{3,2,1,0:T(8,128)S(1)}, f32[2,2,64,256]{3,2,1,0:T(8,128)S(1)}, u32[]{:S(2)}, u32[]{:S(2)}) %collective-permute-start.16) | collective-permute-done | bytes 262176 | tf_op jit(solution)/shard_map/ppermute | solution.py:88
  72.9 2.7 %collective-permute-start.17 = (f32[2,64,256]{2,1,0:T(8,128)S(1)}, f32[2,64,256]{2,1,0:T(8,128)S(1)}, u32[]{:S(2)}, u32[]{:S(2)}) collective-permute-start(f32[2,64,256]{2,1,0:T(8,128)S(1)} %slice_bitcast_fusion.14), channel_id=1, source_target_pairs={{0,8},{8,0},{16,24},{24,16},{1,9},{9,1},{17,25},{25,17},{2,10},{10... | collective-permute-start | bytes 393224 | tf_op jit(solution)/shard_map/ppermute | solution.py:88
  75.6 1.6 %collective-permute-start.23 = (f32[2,64,256]{2,1,0:T(8,128)S(1)}, f32[2,64,256]{2,1,0:T(8,128)S(1)}, u32[]{:S(2)}, u32[]{:S(2)}) collective-permute-start(f32[2,64,256]{2,1,0:T(8,128)S(1)} %slice_bitcast_fusion.12), channel_id=1, source_target_pairs={{0,2},{2,0},{1,3},{3,1},{4,6},{6,4},{5,7},{7,5},{8,10},{10,8},{9,1... | collective-permute-start | bytes 393224 | tf_op jit(solution)/shard_map/ppermute | solution.py:88
  77.2 1.3 collective-permute-done.28
  78.5 2.7 %collective-permute-start.29 = (f32[2,64,256]{2,1,0:T(8,128)S(1)}, f32[2,64,256]{2,1,0:T(8,128)S(1)}, u32[]{:S(2)}, u32[]{:S(2)}) collective-permute-start(f32[2,64,256]{2,1,0:T(8,128)S(1)} %slice_bitcast_fusion.10), channel_id=1, source_target_pairs={{0,8},{8,0},{16,24},{24,16},{1,9},{9,1},{17,25},{25,17},{2,10},{10... | collective-permute-start | bytes 393224 | tf_op jit(solution)/shard_map/ppermute | solution.py:88
  81.2 0.1 add.157
  81.3 0.1 collective-permute-start.34
  81.4 3.5 %collective-permute-start.18 = (f32[2,64,256]{2,1,0:T(8,128)S(1)}, f32[2,64,256]{2,1,0:T(8,128)S(1)}, u32[]{:S(2)}, u32[]{:S(2)}) collective-permute-start(f32[2,64,256]{2,1,0:T(8,128)S(1)} %fusion.7), channel_id=1, source_target_pairs={{0,16},{8,24},{16,0},{24,8},{1,17},{9,25},{17,1},{25,9},{2,18},{10... | collective-permute-start | bytes 393224 | tf_op jit(solution)/shard_map/ppermute | solution.py:88
  85.0 0.1 collective-permute-start.24
  85.1 7.4 %collective-permute-done.29 = f32[2,64,256]{2,1,0:T(8,128)S(1)} collective-permute-done((f32[2,64,256]{2,1,0:T(8,128)S(1)}, f32[2,64,256]{2,1,0:T(8,128)S(1)}, u32[]{:S(2)}, u32[]{:S(2)}) %collective-permute-start.29) | collective-permute-done | bytes 131104 | tf_op jit(solution)/shard_map/ppermute | solution.py:88
  92.5 2.0 %collective-permute-start.30 = (f32[2,64,256]{2,1,0:T(8,128)S(1)}, f32[2,64,256]{2,1,0:T(8,128)S(1)}, u32[]{:S(2)}, u32[]{:S(2)}) collective-permute-start(f32[2,64,256]{2,1,0:T(8,128)S(1)} %fusion.5), channel_id=1, source_target_pairs={{0,16},{8,24},{16,0},{24,8},{1,17},{9,25},{17,1},{25,9},{2,18},{10... | collective-permute-start | bytes 393224 | tf_op jit(solution)/shard_map/ppermute | solution.py:88
  94.5 1.9 %collective-permute-done.18 = f32[2,64,256]{2,1,0:T(8,128)S(1)} collective-permute-done((f32[2,64,256]{2,1,0:T(8,128)S(1)}, f32[2,64,256]{2,1,0:T(8,128)S(1)}, u32[]{:S(2)}, u32[]{:S(2)}) %collective-permute-start.18) | collective-permute-done | bytes 131104 | tf_op jit(solution)/shard_map/ppermute | solution.py:88
  96.4 4.1 %collective-permute-start.19 = (f32[2,64,256]{2,1,0:T(8,128)S(1)}, f32[2,64,256]{2,1,0:T(8,128)S(1)}, u32[]{:S(2)}, u32[]{:S(2)}) collective-permute-start(f32[2,64,256]{2,1,0:T(8,128)S(1)} %add_multiply_fusion.3), channel_id=1, source_target_pairs={{0,8},{8,0},{16,24},{24,16},{1,9},{9,1},{17,25},{25,17},{2,10},{10... | collective-permute-start | bytes 393224 | tf_op jit(solution)/shard_map/ppermute | solution.py:88
  100.5 0.2 collective-permute-done.34
  100.8 1.6 %collective-permute-start.35 = (f32[3,64,256]{2,1,0:T(8,128)S(1)}, f32[3,64,256]{2,1,0:T(8,128)S(1)}, u32[]{:S(2)}, u32[]{:S(2)}) collective-permute-start(f32[3,64,256]{2,1,0:T(8,128)S(1)} %slice_bitcast_fusion.8), channel_id=1, source_target_pairs={{0,2},{2,0},{1,3},{3,1},{4,6},{6,4},{5,7},{7,5},{8,10},{10,8},{9,1... | collective-permute-start | bytes 589832 | tf_op jit(solution)/shard_map/ppermute | solution.py:88
  102.4 1.5 %collective-permute-start.25 = (f32[2,64,256]{2,1,0:T(8,128)S(1)}, f32[2,64,256]{2,1,0:T(8,128)S(1)}, u32[]{:S(2)}, u32[]{:S(2)}) collective-permute-start(f32[2,64,256]{2,1,0:T(8,128)S(1)} %add_multiply_fusion.2), channel_id=1, source_target_pairs={{0,4},{4,0},{1,5},{5,1},{2,6},{6,2},{3,7},{7,3},{8,12},{12,8},{9,1... | collective-permute-start | bytes 393224 | tf_op jit(solution)/shard_map/ppermute | solution.py:88
  103.8 2.7 %collective-permute-done.35 = f32[3,64,256]{2,1,0:T(8,128)S(1)} collective-permute-done((f32[3,64,256]{2,1,0:T(8,128)S(1)}, f32[3,64,256]{2,1,0:T(8,128)S(1)}, u32[]{:S(2)}, u32[]{:S(2)}) %collective-permute-start.35) | collective-permute-done | bytes 196640 | tf_op jit(solution)/shard_map/ppermute | solution.py:88
  106.5 2.4 %collective-permute-start.36 = (f32[3,64,256]{2,1,0:T(8,128)S(1)}, f32[3,64,256]{2,1,0:T(8,128)S(1)}, u32[]{:S(2)}, u32[]{:S(2)}) collective-permute-start(f32[3,64,256]{2,1,0:T(8,128)S(1)} %fusion.4), channel_id=1, source_target_pairs={{0,16},{8,24},{16,0},{24,8},{1,17},{9,25},{17,1},{25,9},{2,18},{10... | collective-permute-start | bytes 589832 | tf_op jit(solution)/shard_map/ppermute | solution.py:88
  108.9 2.5 %collective-permute-start.31 = (f32[2,64,256]{2,1,0:T(8,128)S(1)}, f32[2,64,256]{2,1,0:T(8,128)S(1)}, u32[]{:S(2)}, u32[]{:S(2)}) collective-permute-start(f32[2,64,256]{2,1,0:T(8,128)S(1)} %add_multiply_fusion.1), channel_id=1, source_target_pairs={{0,8},{8,0},{16,24},{24,16},{1,9},{9,1},{17,25},{25,17},{2,10},{10... | collective-permute-start | bytes 393224 | tf_op jit(solution)/shard_map/ppermute | solution.py:88
  111.5 1.5 %collective-permute-start.20 = (f32[2,2,64,256]{3,2,1,0:T(8,128)S(1)}, f32[2,2,64,256]{3,2,1,0:T(8,128)S(1)}, u32[]{:S(2)}, u32[]{:S(2)}) collective-permute-start(f32[2,2,64,256]{3,2,1,0:T(8,128)S(1)} %get-tuple-element.50), channel_id=1, source_target_pairs={{0,4},{4,0},{1,5},{5,1},{2,6},{6,2},{3,7},{7,3},{8,12},{12,8},{9,1... | collective-permute-start | bytes 786440 | tf_op jit(solution)/shard_map/ppermute | solution.py:88
  113.0 2.1 %collective-permute-done.36 = f32[3,64,256]{2,1,0:T(8,128)S(1)} collective-permute-done((f32[3,64,256]{2,1,0:T(8,128)S(1)}, f32[3,64,256]{2,1,0:T(8,128)S(1)}, u32[]{:S(2)}, u32[]{:S(2)}) %collective-permute-start.36) | collective-permute-done | bytes 196640 | tf_op jit(solution)/shard_map/ppermute | solution.py:88
  115.1 0.7 collective-permute-start.37
  115.8 2.7 %collective-permute-start.26 = (f32[2,2,64,256]{3,2,1,0:T(8,128)S(1)}, f32[2,2,64,256]{3,2,1,0:T(8,128)S(1)}, u32[]{:S(2)}, u32[]{:S(2)}) collective-permute-start(f32[2,2,64,256]{3,2,1,0:T(8,128)S(1)} %get-tuple-element.52), channel_id=1, source_target_pairs={{0,8},{8,0},{16,24},{24,16},{1,9},{9,1},{17,25},{25,17},{2,10},{10... | collective-permute-start | bytes 786440 | tf_op jit(solution)/shard_map/ppermute | solution.py:88
  118.5 0.1 collective-permute-start.32
  118.6 3.5 %collective-permute-done.37 = f32[3,64,256]{2,1,0:T(8,128)S(1)} collective-permute-done((f32[3,64,256]{2,1,0:T(8,128)S(1)}, f32[3,64,256]{2,1,0:T(8,128)S(1)}, u32[]{:S(2)}, u32[]{:S(2)}) %collective-permute-start.37) | collective-permute-done | bytes 196640 | tf_op jit(solution)/shard_map/ppermute | solution.py:88
  122.2 0.8 collective-permute-start.38
  123.1 1.9 %collective-permute-done.26 = f32[2,2,64,256]{3,2,1,0:T(8,128)S(1)} collective-permute-done((f32[2,2,64,256]{3,2,1,0:T(8,128)S(1)}, f32[2,2,64,256]{3,2,1,0:T(8,128)S(1)}, u32[]{:S(2)}, u32[]{:S(2)}) %collective-permute-start.26) | collective-permute-done | bytes 262176 | tf_op jit(solution)/shard_map/ppermute | solution.py:88
  125.1 4.9 %collective-permute-done.38 = f32[2,3,64,256]{3,2,1,0:T(8,128)S(1)} collective-permute-done((f32[2,3,64,256]{3,2,1,0:T(8,128)S(1)}, f32[2,3,64,256]{3,2,1,0:T(8,128)S(1)}, u32[]{:S(2)}, u32[]{:S(2)}) %collective-permute-start.38) | collective-permute-done | bytes 393248 | tf_op jit(solution)/shard_map/ppermute | solution.py:88
  130.0 0.1 pad_maximum_fusion.1
  130.1 0.2 pad_maximum_fusion
  130.3 0.6 gather_fusion
  130.8 0.9 bitcast_select_fusion
  (60 shorter events, 1.2 us)
Async XLA Ops:
  1.2 26.9 %collective-permute-start.2 = (bf16[3,256,256]{2,1,0:T(8,128)(2,1)S(1)}, bf16[3,256,256]{2,1,0:T(8,128)(2,1)S(1)}, u32[]{:S(2)}, u32[]{:S(2)}) collective-permute-start(bf16[3,256,256]{2,1,0:T(8,128)(2,1)S(1)} %get-tuple-element.45), channel_id=1, source_target_pairs={{0,8},{8,0},{16,24},{24,16},{1,9},{9,1},{17,25},{25,17},{2,10},{10... | collective-permute-start | bytes 1179656 | tf_op jit(solution)/shard_map/ppermute | solution.py:88
  4.3 55.4 %copy-start = (s32[1,10,2]{1,2,0:T(2,128)S(1)}, s32[1,10,2]{1,2,0:T(2,128)}, u32[]{:S(2)}) copy-start(s32[1,10,2]{1,2,0:T(2,128)} %param.4) | copy-start | bytes 244
  5.5 14.1 %collective-permute-start.1 = (bf16[1,256,256]{2,1,0:T(8,128)(2,1)S(1)}, bf16[1,256,256]{2,1,0:T(8,128)(2,1)S(1)}, u32[]{:S(2)}, u32[]{:S(2)}) collective-permute-start(bf16[1,256,256]{2,1,0:T(8,128)(2,1)S(1)} %get-tuple-element.40), channel_id=1, source_target_pairs={{0,24},{8,16},{16,8},{24,0},{1,25},{9,17},{17,9},{25,1},{2,26},{10... | collective-permute-start | bytes 393224 | tf_op jit(solution)/shard_map/ppermute | solution.py:88
  8.1 12.9 %collective-permute-start = (bf16[1,256,256]{2,1,0:T(8,128)(2,1)S(1)}, bf16[1,256,256]{2,1,0:T(8,128)(2,1)S(1)}, u32[]{:S(2)}, u32[]{:S(2)}) collective-permute-start(bf16[1,256,256]{2,1,0:T(8,128)(2,1)S(1)} %get-tuple-element.42), channel_id=1, source_target_pairs={{0,16},{8,24},{16,0},{24,8},{1,17},{9,25},{17,1},{25,9},{2,18},{10... | collective-permute-start | bytes 393224 | tf_op jit(solution)/shard_map/ppermute | solution.py:88
  19.6 7.0 %collective-permute-start.4 = (bf16[1,256,256]{2,1,0:T(8,128)(2,1)S(1)}, bf16[1,256,256]{2,1,0:T(8,128)(2,1)S(1)}, u32[]{:S(2)}, u32[]{:S(2)}) collective-permute-start(bf16[1,256,256]{2,1,0:T(8,128)(2,1)S(1)} %get-tuple-element.26), channel_id=1, source_target_pairs={{0,24},{8,16},{16,8},{24,0},{1,25},{9,17},{17,9},{25,1},{2,26},{10... | collective-permute-start | bytes 393224 | tf_op jit(solution)/shard_map/ppermute | solution.py:88
  21.0 8.7 %collective-permute-start.3 = (bf16[1,256,256]{2,1,0:T(8,128)(2,1)S(1)}, bf16[1,256,256]{2,1,0:T(8,128)(2,1)S(1)}, u32[]{:S(2)}, u32[]{:S(2)}) collective-permute-start(bf16[1,256,256]{2,1,0:T(8,128)(2,1)S(1)} %get-tuple-element.24), channel_id=1, source_target_pairs={{0,16},{8,24},{16,0},{24,8},{1,17},{9,25},{17,1},{25,9},{2,18},{10... | collective-permute-start | bytes 393224 | tf_op jit(solution)/shard_map/ppermute | solution.py:88
  21.7 14.7 %collective-permute-start.9 = (bf16[1,256,256]{2,1,0:T(8,128)(2,1)S(1)}, bf16[1,256,256]{2,1,0:T(8,128)(2,1)S(1)}, u32[]{:S(2)}, u32[]{:S(2)}) collective-permute-start(bf16[1,256,256]{2,1,0:T(8,128)(2,1)S(1)} %collective-permute-done.1.refs_2_), channel_id=1, source_target_pairs={{0,4},{4,0},{1,5},{5,1},{2,6},{6,2},{3,7},{7,3},{8,12},{12,8},{9,1... | collective-permute-start | bytes 393224 | tf_op jit(solution)/shard_map/ppermute | solution.py:88
  23.3 17.6 %collective-permute-start.8 = (bf16[1,256,256]{2,1,0:T(8,128)(2,1)S(1)}, bf16[1,256,256]{2,1,0:T(8,128)(2,1)S(1)}, u32[]{:S(2)}, u32[]{:S(2)}) collective-permute-start(bf16[1,256,256]{2,1,0:T(8,128)(2,1)S(1)} %collective-permute-done.refs_1_), channel_id=1, source_target_pairs={{0,4},{4,0},{1,5},{5,1},{2,6},{6,2},{3,7},{7,3},{8,12},{12,8},{9,1... | collective-permute-start | bytes 393224 | tf_op jit(solution)/shard_map/ppermute | solution.py:88
  26.6 26.9 %collective-permute-start.7 = (bf16[3,256,256]{2,1,0:T(8,128)(2,1)S(1)}, bf16[3,256,256]{2,1,0:T(8,128)(2,1)S(1)}, u32[]{:S(2)}, u32[]{:S(2)}) collective-permute-start(bf16[3,256,256]{2,1,0:T(8,128)(2,1)S(1)} %get-tuple-element.46.refs_0_), channel_id=1, source_target_pairs={{0,4},{4,0},{1,5},{5,1},{2,6},{6,2},{3,7},{7,3},{8,12},{12,8},{9,1... | collective-permute-start | bytes 1179656 | tf_op jit(solution)/shard_map/ppermute | solution.py:88
  28.1 29.0 %collective-permute-start.10 = (bf16[3,256,256]{2,1,0:T(8,128)(2,1)S(1)}, bf16[3,256,256]{2,1,0:T(8,128)(2,1)S(1)}, u32[]{:S(2)}, u32[]{:S(2)}) collective-permute-start(bf16[3,256,256]{2,1,0:T(8,128)(2,1)S(1)} %collective-permute-done.2.refs_3_), channel_id=1, source_target_pairs={{0,4},{4,0},{1,5},{5,1},{2,6},{6,2},{3,7},{7,3},{8,12},{12,8},{9,1... | collective-permute-start | bytes 1179656 | tf_op jit(solution)/shard_map/ppermute | solution.py:88
  29.7 11.2 %collective-permute-start.6 = (bf16[1,256,256]{2,1,0:T(8,128)(2,1)S(1)}, bf16[1,256,256]{2,1,0:T(8,128)(2,1)S(1)}, u32[]{:S(2)}, u32[]{:S(2)}) collective-permute-start(bf16[1,256,256]{2,1,0:T(8,128)(2,1)S(1)} %get-tuple-element.29), channel_id=1, source_target_pairs={{0,24},{8,16},{16,8},{24,0},{1,25},{9,17},{17,9},{25,1},{2,26},{10... | collective-permute-start | bytes 393224 | tf_op jit(solution)/shard_map/ppermute | solution.py:88
  36.4 14.2 %collective-permute-start.12 = (bf16[1,256,256]{2,1,0:T(8,128)(2,1)S(1)}, bf16[1,256,256]{2,1,0:T(8,128)(2,1)S(1)}, u32[]{:S(2)}, u32[]{:S(2)}) collective-permute-start(bf16[1,256,256]{2,1,0:T(8,128)(2,1)S(1)} %collective-permute-done.4.refs_5_), channel_id=1, source_target_pairs={{0,4},{4,0},{1,5},{5,1},{2,6},{6,2},{3,7},{7,3},{8,12},{12,8},{9,1... | collective-permute-start | bytes 393224 | tf_op jit(solution)/shard_map/ppermute | solution.py:88
  40.9 11.3 %collective-permute-start.5 = (bf16[1,256,256]{2,1,0:T(8,128)(2,1)S(1)}, bf16[1,256,256]{2,1,0:T(8,128)(2,1)S(1)}, u32[]{:S(2)}, u32[]{:S(2)}) collective-permute-start(bf16[1,256,256]{2,1,0:T(8,128)(2,1)S(1)} %get-tuple-element.28), channel_id=1, source_target_pairs={{0,16},{8,24},{16,0},{24,8},{1,17},{9,25},{17,1},{25,9},{2,18},{10... | collective-permute-start | bytes 393224 | tf_op jit(solution)/shard_map/ppermute | solution.py:88
  40.9 12.5 %collective-permute-start.11 = (bf16[1,256,256]{2,1,0:T(8,128)(2,1)S(1)}, bf16[1,256,256]{2,1,0:T(8,128)(2,1)S(1)}, u32[]{:S(2)}, u32[]{:S(2)}) collective-permute-start(bf16[1,256,256]{2,1,0:T(8,128)(2,1)S(1)} %collective-permute-done.3.refs_4_), channel_id=1, source_target_pairs={{0,4},{4,0},{1,5},{5,1},{2,6},{6,2},{3,7},{7,3},{8,12},{12,8},{9,1... | collective-permute-start | bytes 393224 | tf_op jit(solution)/shard_map/ppermute | solution.py:88
  50.6 5.0 %collective-permute-start.14 = (bf16[1,256,256]{2,1,0:T(8,128)(2,1)S(1)}, bf16[1,256,256]{2,1,0:T(8,128)(2,1)S(1)}, u32[]{:S(2)}, u32[]{:S(2)}) collective-permute-start(bf16[1,256,256]{2,1,0:T(8,128)(2,1)S(1)} %collective-permute-done.6.refs_7_), channel_id=1, source_target_pairs={{0,4},{4,0},{1,5},{5,1},{2,6},{6,2},{3,7},{7,3},{8,12},{12,8},{9,1... | collective-permute-start | bytes 393224 | tf_op jit(solution)/shard_map/ppermute | solution.py:88
  52.2 5.0 %collective-permute-start.13 = (bf16[1,256,256]{2,1,0:T(8,128)(2,1)S(1)}, bf16[1,256,256]{2,1,0:T(8,128)(2,1)S(1)}, u32[]{:S(2)}, u32[]{:S(2)}) collective-permute-start(bf16[1,256,256]{2,1,0:T(8,128)(2,1)S(1)} %collective-permute-done.5.refs_6_), channel_id=1, source_target_pairs={{0,4},{4,0},{1,5},{5,1},{2,6},{6,2},{3,7},{7,3},{8,12},{12,8},{9,1... | collective-permute-start | bytes 393224 | tf_op jit(solution)/shard_map/ppermute | solution.py:88
  59.6 3.9 %collective-permute-start.15 = (f32[2,2,2,64,256]{4,3,2,1,0:T(8,128)S(1)}, f32[2,2,2,64,256]{4,3,2,1,0:T(8,128)S(1)}, u32[]{:S(2)}, u32[]{:S(2)}) collective-permute-start(f32[2,2,2,64,256]{4,3,2,1,0:T(8,128)S(1)} %get-tuple-element.31), channel_id=1, source_target_pairs={{0,1},{1,0},{2,3},{3,2},{4,5},{5,4},{6,7},{7,6},{8,9},{9,8},{10,11... | collective-permute-start | bytes 1572872 | tf_op jit(solution)/shard_map/ppermute | solution.py:88
  59.7 5.4 %collective-permute-start.21 = (f32[2,2,2,64,256]{4,3,2,1,0:T(8,128)S(1)}, f32[2,2,2,64,256]{4,3,2,1,0:T(8,128)S(1)}, u32[]{:S(2)}, u32[]{:S(2)}) collective-permute-start(f32[2,2,2,64,256]{4,3,2,1,0:T(8,128)S(1)} %get-tuple-element.33), channel_id=1, source_target_pairs={{0,1},{1,0},{2,3},{3,2},{4,5},{5,4},{6,7},{7,6},{8,9},{9,8},{10,11... | collective-permute-start | bytes 1572872 | tf_op jit(solution)/shard_map/ppermute | solution.py:88
  62.9 5.0 %collective-permute-start.27 = (f32[2,2,2,64,256]{4,3,2,1,0:T(8,128)S(1)}, f32[2,2,2,64,256]{4,3,2,1,0:T(8,128)S(1)}, u32[]{:S(2)}, u32[]{:S(2)}) collective-permute-start(f32[2,2,2,64,256]{4,3,2,1,0:T(8,128)S(1)} %get-tuple-element.36), channel_id=1, source_target_pairs={{0,1},{1,0},{2,3},{3,2},{4,5},{5,4},{6,7},{7,6},{8,9},{9,8},{10,11... | collective-permute-start | bytes 1572872 | tf_op jit(solution)/shard_map/ppermute | solution.py:88
  63.0 18.2 %collective-permute-start.33 = (f32[2,2,3,64,256]{4,3,2,1,0:T(8,128)S(1)}, f32[2,2,3,64,256]{4,3,2,1,0:T(8,128)S(1)}, u32[]{:S(2)}, u32[]{:S(2)}) collective-permute-start(f32[2,2,3,64,256]{4,3,2,1,0:T(8,128)S(1)} %get-tuple-element.38), channel_id=1, source_target_pairs={{0,1},{1,0},{2,3},{3,2},{4,5},{5,4},{6,7},{7,6},{8,9},{9,8},{10,11... | collective-permute-start | bytes 2359304 | tf_op jit(solution)/shard_map/ppermute | solution.py:88
  63.6 9.2 %collective-permute-start.16 = (f32[2,2,64,256]{3,2,1,0:T(8,128)S(1)}, f32[2,2,64,256]{3,2,1,0:T(8,128)S(1)}, u32[]{:S(2)}, u32[]{:S(2)}) collective-permute-start(f32[2,2,64,256]{3,2,1,0:T(8,128)S(1)} %slice_bitcast_fusion.6), channel_id=1, source_target_pairs={{0,2},{2,0},{1,3},{3,1},{4,6},{6,4},{5,7},{7,5},{8,10},{10,8},{9,1... | collective-permute-start | bytes 786440 | tf_op jit(solution)/shard_map/ppermute | solution.py:88
  65.3 10.3 %collective-permute-start.22 = (f32[2,2,64,256]{3,2,1,0:T(8,128)S(1)}, f32[2,2,64,256]{3,2,1,0:T(8,128)S(1)}, u32[]{:S(2)}, u32[]{:S(2)}) collective-permute-start(f32[2,2,64,256]{3,2,1,0:T(8,128)S(1)} %slice_bitcast_fusion.4), channel_id=1, source_target_pairs={{0,8},{8,0},{16,24},{24,16},{1,9},{9,1},{17,25},{25,17},{2,10},{10... | collective-permute-start | bytes 786440 | tf_op jit(solution)/shard_map/ppermute | solution.py:88
  68.0 10.4 %collective-permute-start.28 = (f32[2,2,64,256]{3,2,1,0:T(8,128)S(1)}, f32[2,2,64,256]{3,2,1,0:T(8,128)S(1)}, u32[]{:S(2)}, u32[]{:S(2)}) collective-permute-start(f32[2,2,64,256]{3,2,1,0:T(8,128)S(1)} %slice_bitcast_fusion.2), channel_id=1, source_target_pairs={{0,2},{2,0},{1,3},{3,1},{4,6},{6,4},{5,7},{7,5},{8,10},{10,8},{9,1... | collective-permute-start | bytes 786440 | tf_op jit(solution)/shard_map/ppermute | solution.py:88
  72.9 8.5 %collective-permute-start.17 = (f32[2,64,256]{2,1,0:T(8,128)S(1)}, f32[2,64,256]{2,1,0:T(8,128)S(1)}, u32[]{:S(2)}, u32[]{:S(2)}) collective-permute-start(f32[2,64,256]{2,1,0:T(8,128)S(1)} %slice_bitcast_fusion.14), channel_id=1, source_target_pairs={{0,8},{8,0},{16,24},{24,16},{1,9},{9,1},{17,25},{25,17},{2,10},{10... | collective-permute-start | bytes 393224 | tf_op jit(solution)/shard_map/ppermute | solution.py:88
  75.6 9.3 %collective-permute-start.23 = (f32[2,64,256]{2,1,0:T(8,128)S(1)}, f32[2,64,256]{2,1,0:T(8,128)S(1)}, u32[]{:S(2)}, u32[]{:S(2)}) collective-permute-start(f32[2,64,256]{2,1,0:T(8,128)S(1)} %slice_bitcast_fusion.12), channel_id=1, source_target_pairs={{0,2},{2,0},{1,3},{3,1},{4,6},{6,4},{5,7},{7,5},{8,10},{10,8},{9,1... | collective-permute-start | bytes 393224 | tf_op jit(solution)/shard_map/ppermute | solution.py:88
  78.5 14.0 %collective-permute-start.29 = (f32[2,64,256]{2,1,0:T(8,128)S(1)}, f32[2,64,256]{2,1,0:T(8,128)S(1)}, u32[]{:S(2)}, u32[]{:S(2)}) collective-permute-start(f32[2,64,256]{2,1,0:T(8,128)S(1)} %slice_bitcast_fusion.10), channel_id=1, source_target_pairs={{0,8},{8,0},{16,24},{24,16},{1,9},{9,1},{17,25},{25,17},{2,10},{10... | collective-permute-start | bytes 393224 | tf_op jit(solution)/shard_map/ppermute | solution.py:88
  81.3 19.4 %collective-permute-start.34 = (f32[2,3,64,256]{3,2,1,0:T(8,128)S(1)}, f32[2,3,64,256]{3,2,1,0:T(8,128)S(1)}, u32[]{:S(2)}, u32[]{:S(2)}) collective-permute-start(f32[2,3,64,256]{3,2,1,0:T(8,128)S(1)} %slice_bitcast_fusion), channel_id=1, source_target_pairs={{0,8},{8,0},{16,24},{24,16},{1,9},{9,1},{17,25},{25,17},{2,10},{10... | collective-permute-start | bytes 1179656 | tf_op jit(solution)/shard_map/ppermute | solution.py:88
  81.4 14.9 %collective-permute-start.18 = (f32[2,64,256]{2,1,0:T(8,128)S(1)}, f32[2,64,256]{2,1,0:T(8,128)S(1)}, u32[]{:S(2)}, u32[]{:S(2)}) collective-permute-start(f32[2,64,256]{2,1,0:T(8,128)S(1)} %fusion.7), channel_id=1, source_target_pairs={{0,16},{8,24},{16,0},{24,8},{1,17},{9,25},{17,1},{25,9},{2,18},{10... | collective-permute-start | bytes 393224 | tf_op jit(solution)/shard_map/ppermute | solution.py:88
  85.0 17.3 %collective-permute-start.24 = (f32[2,64,256]{2,1,0:T(8,128)S(1)}, f32[2,64,256]{2,1,0:T(8,128)S(1)}, u32[]{:S(2)}, u32[]{:S(2)}) collective-permute-start(f32[2,64,256]{2,1,0:T(8,128)S(1)} %fusion.6), channel_id=1, source_target_pairs={{0,16},{8,24},{16,0},{24,8},{1,17},{9,25},{17,1},{25,9},{2,18},{10... | collective-permute-start | bytes 393224 | tf_op jit(solution)/shard_map/ppermute | solution.py:88
  92.5 16.4 %collective-permute-start.30 = (f32[2,64,256]{2,1,0:T(8,128)S(1)}, f32[2,64,256]{2,1,0:T(8,128)S(1)}, u32[]{:S(2)}, u32[]{:S(2)}) collective-permute-start(f32[2,64,256]{2,1,0:T(8,128)S(1)} %fusion.5), channel_id=1, source_target_pairs={{0,16},{8,24},{16,0},{24,8},{1,17},{9,25},{17,1},{25,9},{2,18},{10... | collective-permute-start | bytes 393224 | tf_op jit(solution)/shard_map/ppermute | solution.py:88
  96.4 15.1 %collective-permute-start.19 = (f32[2,64,256]{2,1,0:T(8,128)S(1)}, f32[2,64,256]{2,1,0:T(8,128)S(1)}, u32[]{:S(2)}, u32[]{:S(2)}) collective-permute-start(f32[2,64,256]{2,1,0:T(8,128)S(1)} %add_multiply_fusion.3), channel_id=1, source_target_pairs={{0,8},{8,0},{16,24},{24,16},{1,9},{9,1},{17,25},{25,17},{2,10},{10... | collective-permute-start | bytes 393224 | tf_op jit(solution)/shard_map/ppermute | solution.py:88
  100.8 5.7 %collective-permute-start.35 = (f32[3,64,256]{2,1,0:T(8,128)S(1)}, f32[3,64,256]{2,1,0:T(8,128)S(1)}, u32[]{:S(2)}, u32[]{:S(2)}) collective-permute-start(f32[3,64,256]{2,1,0:T(8,128)S(1)} %slice_bitcast_fusion.8), channel_id=1, source_target_pairs={{0,2},{2,0},{1,3},{3,1},{4,6},{6,4},{5,7},{7,5},{8,10},{10,8},{9,1... | collective-permute-start | bytes 589832 | tf_op jit(solution)/shard_map/ppermute | solution.py:88
  102.4 13.4 %collective-permute-start.25 = (f32[2,64,256]{2,1,0:T(8,128)S(1)}, f32[2,64,256]{2,1,0:T(8,128)S(1)}, u32[]{:S(2)}, u32[]{:S(2)}) collective-permute-start(f32[2,64,256]{2,1,0:T(8,128)S(1)} %add_multiply_fusion.2), channel_id=1, source_target_pairs={{0,4},{4,0},{1,5},{5,1},{2,6},{6,2},{3,7},{7,3},{8,12},{12,8},{9,1... | collective-permute-start | bytes 393224 | tf_op jit(solution)/shard_map/ppermute | solution.py:88
  106.5 8.5 %collective-permute-start.36 = (f32[3,64,256]{2,1,0:T(8,128)S(1)}, f32[3,64,256]{2,1,0:T(8,128)S(1)}, u32[]{:S(2)}, u32[]{:S(2)}) collective-permute-start(f32[3,64,256]{2,1,0:T(8,128)S(1)} %fusion.4), channel_id=1, source_target_pairs={{0,16},{8,24},{16,0},{24,8},{1,17},{9,25},{17,1},{25,9},{2,18},{10... | collective-permute-start | bytes 589832 | tf_op jit(solution)/shard_map/ppermute | solution.py:88
  108.9 9.6 %collective-permute-start.31 = (f32[2,64,256]{2,1,0:T(8,128)S(1)}, f32[2,64,256]{2,1,0:T(8,128)S(1)}, u32[]{:S(2)}, u32[]{:S(2)}) collective-permute-start(f32[2,64,256]{2,1,0:T(8,128)S(1)} %add_multiply_fusion.1), channel_id=1, source_target_pairs={{0,8},{8,0},{16,24},{24,16},{1,9},{9,1},{17,25},{25,17},{2,10},{10... | collective-permute-start | bytes 393224 | tf_op jit(solution)/shard_map/ppermute | solution.py:88
  111.5 11.5 %collective-permute-start.20 = (f32[2,2,64,256]{3,2,1,0:T(8,128)S(1)}, f32[2,2,64,256]{3,2,1,0:T(8,128)S(1)}, u32[]{:S(2)}, u32[]{:S(2)}) collective-permute-start(f32[2,2,64,256]{3,2,1,0:T(8,128)S(1)} %get-tuple-element.50), channel_id=1, source_target_pairs={{0,4},{4,0},{1,5},{5,1},{2,6},{6,2},{3,7},{7,3},{8,12},{12,8},{9,1... | collective-permute-start | bytes 786440 | tf_op jit(solution)/shard_map/ppermute | solution.py:88
  115.1 7.0 %collective-permute-start.37 = (f32[3,64,256]{2,1,0:T(8,128)S(1)}, f32[3,64,256]{2,1,0:T(8,128)S(1)}, u32[]{:S(2)}, u32[]{:S(2)}) collective-permute-start(f32[3,64,256]{2,1,0:T(8,128)S(1)} %add_multiply_fusion), channel_id=1, source_target_pairs={{0,4},{4,0},{1,5},{5,1},{2,6},{6,2},{3,7},{7,3},{8,12},{12,8},{9,1... | collective-permute-start | bytes 589832 | tf_op jit(solution)/shard_map/ppermute | solution.py:88
  115.8 9.2 %collective-permute-start.26 = (f32[2,2,64,256]{3,2,1,0:T(8,128)S(1)}, f32[2,2,64,256]{3,2,1,0:T(8,128)S(1)}, u32[]{:S(2)}, u32[]{:S(2)}) collective-permute-start(f32[2,2,64,256]{3,2,1,0:T(8,128)S(1)} %get-tuple-element.52), channel_id=1, source_target_pairs={{0,8},{8,0},{16,24},{24,16},{1,9},{9,1},{17,25},{25,17},{2,10},{10... | collective-permute-start | bytes 786440 | tf_op jit(solution)/shard_map/ppermute | solution.py:88
  118.5 6.5 %collective-permute-start.32 = (f32[2,2,64,256]{3,2,1,0:T(8,128)S(1)}, f32[2,2,64,256]{3,2,1,0:T(8,128)S(1)}, u32[]{:S(2)}, u32[]{:S(2)}) collective-permute-start(f32[2,2,64,256]{3,2,1,0:T(8,128)S(1)} %get-tuple-element.54), channel_id=1, source_target_pairs={{0,4},{4,0},{1,5},{5,1},{2,6},{6,2},{3,7},{7,3},{8,12},{12,8},{9,1... | collective-permute-start | bytes 786440 | tf_op jit(solution)/shard_map/ppermute | solution.py:88
  122.2 7.8 %collective-permute-start.38 = (f32[2,3,64,256]{3,2,1,0:T(8,128)S(1)}, f32[2,3,64,256]{3,2,1,0:T(8,128)S(1)}, u32[]{:S(2)}, u32[]{:S(2)}) collective-permute-start(f32[2,3,64,256]{3,2,1,0:T(8,128)S(1)} %get-tuple-element.48), channel_id=1, source_target_pairs={{0,8},{8,0},{16,24},{24,16},{1,9},{9,1},{17,25},{25,17},{2,10},{10... | collective-permute-start | bytes 1179656 | tf_op jit(solution)/shard_map/ppermute | solution.py:88

commit v5 on v4

--- a/solution.py
+++ b/solution.py
@@ -10,7 +10,7 @@
 from jax.sharding import Mesh, PartitionSpec as P
 
 VMEM_LIMIT = 24 * 2**20
-X_FIRST = (True, False, True, False)
+GROUPS = 4
 
 
 def tile_lists(block_count):
@@ -19,10 +19,11 @@
 
 
 def group_sizes(quarter):
-    return [len(piece) for piece in np.array_split(np.arange(quarter), len(X_FIRST))][::-1]
-
-
-def multiply_tiles(scalars, first_pair, blocks, keep_ref, send_ref, x_first):
+    sizes = [len(piece) for piece in np.array_split(np.arange(quarter), GROUPS)]
+    return sizes[1:-1] + sizes[:1] + sizes[-1:]
+
+
+def multiply_tiles(scalars, first_pair, blocks, keep_ref, send_ref):
     x, core = scalars[2], scalars[3]
     group_size = keep_ref.shape[2]
     rows_dev = keep_ref.shape[3]
@@ -41,22 +42,20 @@
             for step in range(part_count // 2):
                 even, odd = parts[2 * step], parts[2 * step + 1]
                 target = x ^ step
-                place = (target, low) if x_first else (low, target)
-                keep_ref[place[0], place[1], slot] = jnp.where(core == 0, even, odd)
-                send_ref[place[0], place[1], slot] = jnp.where(core == 0, odd, even)
+                keep_ref[target, low, slot] = jnp.where(core == 0, even, odd)
+                send_ref[target, low, slot] = jnp.where(core == 0, odd, even)
         return carry
 
     lax.fori_loop(0, group_size, one_slot, 0)
 
 
-def multiply_groups(scalars, first_pair, x_first, blocks, outs):
-    for index, first in enumerate(x_first):
-        keep_ref, send_ref = outs[2 * index : 2 * index + 2]
-        multiply_tiles(scalars, first_pair, blocks, keep_ref, send_ref, first)
+def multiply_groups(scalars, first_pair, blocks, outs):
+    for keep_ref, send_ref in zip(outs[::2], outs[1::2]):
+        multiply_tiles(scalars, first_pair, blocks, keep_ref, send_ref)
         first_pair += 4 * keep_ref.shape[2]
 
 
-def first_kernel(layout, first_pair, x_first, scalars, *refs):
+def first_kernel(layout, first_pair, scalars, *refs):
     pieces = refs[: len(layout)]
     blocks = refs[len(layout)]
     z, y = scalars[0], scalars[1]
@@ -66,11 +65,11 @@
         for index in range(piece.shape[0]):
             start = (component + index) * cells
             blocks[block, :, start : start + cells] = piece[index]
-    multiply_groups(scalars, first_pair, x_first, blocks, refs[len(layout) + 1 :])
-
-
-def second_kernel(first_pair, x_first, scalars, blocks, *outs):
-    multiply_groups(scalars, first_pair, x_first, blocks, outs)
+    multiply_groups(scalars, first_pair, blocks, refs[len(layout) + 1 :])
+
+
+def second_kernel(first_pair, scalars, blocks, *outs):
+    multiply_groups(scalars, first_pair, blocks, outs)
 
 
 def per_device(z_count, y_count, x_count, core_count, snapshots, tile_table):
@@ -114,23 +113,14 @@
         return lax.dynamic_slice_in_dim(snapshots, (z ^ step) * cells, cells, 2)
 
     pieces = {(0, 0): part(0)}
-    far = range(2, z_count)
-    parts = {step: part(step) for step in far}
-    for component in range(components):
-        for step in far:
-            piece = parts[step][component : component + 1]
-            if component > 0:
-                piece, pieces[step, component - 1] = after(piece, pieces[step, component - 1])
-            pieces[step, component] = swap(piece, "z", step)
-        if component == 0:
-            pieces[1, 0] = swap(part(1), "z", 1)
+    for step in range(1, z_count):
+        pieces[step, 0] = swap(part(step), "z", step)
     layout = [(step, 0, component) for step, component in pieces]
     layout += [(step, 1, component) for step, component in pieces]
     chunks = list(pieces.values()) + [swap(piece, "y", 1) for piece in pieces.values()]
 
-    def sums_shape(size, x_first):
-        lead = (x_count, 2) if x_first else (2, x_count)
-        return jax.ShapeDtypeStruct((*lead, size, rows_dev, block_size), jnp.float32)
+    def sums_shape(size):
+        return jax.ShapeDtypeStruct((x_count, 2, size, rows_dev, block_size), jnp.float32)
 
     def call(kernel, size, out_shape, operands, name):
         vmem = pl.BlockSpec(memory_space=pltpu.VMEM)
@@ -148,53 +138,45 @@
             name=name,
         )(scalars, *operands)
 
-    shapes = [sums_shape(size, first) for size, first in zip(sizes, X_FIRST) for _ in range(2)]
+    shapes = [sums_shape(size) for size in sizes for _ in range(2)]
     blocks_shape = jax.ShapeDtypeStruct(
         (block_count, block_size, components * cells), jnp.bfloat16
     )
     blocks, *sums = call(
-        functools.partial(first_kernel, layout, 4, X_FIRST[:2]),
+        functools.partial(first_kernel, layout, 4),
         sizes[0] + sizes[1],
         [blocks_shape] + shapes[:4],
         chunks,
         "tiles_first",
     )
     sums += call(
-        functools.partial(second_kernel, 4 + 4 * (sizes[0] + sizes[1]), X_FIRST[2:]),
+        functools.partial(second_kernel, 4 + 4 * (sizes[0] + sizes[1])),
         sizes[2] + sizes[3],
         shapes[4:],
         [blocks],
         "tiles_second",
     )
 
-    def over_x(value):
-        total = value[0]
+    flat = []
+    arrived = None
+    for index in range(GROUPS):
+        keep, send = sums[2 * index : 2 * index + 2]
+        total = keep + swap(send, "core", 1)
+        held = total[0]
         for step in range(1, x_count):
-            total = total + swap(value[step], "x", step)
-        return total
-
-    def over_low_bit(value):
-        return value[0] + swap(value[1], "z", 1)
-
-    def over_high_bits(value):
+            away = total[step]
+            if arrived is not None:
+                away, arrived = after(away, arrived)
+            arrived = swap(away, "x", step)
+            held = held + arrived
+        held = held[0] + swap(held[1], "z", 1)
         bits = 2
         while bits < z_count:
-            value = value + swap(value, "z", bits)
+            held = held + swap(held, "z", bits)
             bits *= 2
-        return value * scale_factor
-
-    flat = []
-    for index, first in enumerate(X_FIRST):
-        keep, send = sums[2 * index : 2 * index + 2]
-        total = keep + swap(send, "core", 1)
-        if first:
-            held = over_high_bits(over_low_bit(over_x(total)))
-            pair = jnp.stack([held, swap(held, "z", 1)])
-            whole = jnp.stack([pair, swap(pair, "y", 1)])
-        else:
-            held = over_high_bits(over_x(over_low_bit(total)))
-            pair = jnp.stack([held, swap(held, "y", 1)])
-            whole = jnp.stack([pair, swap(pair, "z", 1)])
+        held = held * scale_factor
+        pair = jnp.stack([held, swap(held, "z", 1)])
+        whole = jnp.stack([pair, swap(pair, "y", 1)])
         flat.append(whole.reshape(-1, rows_dev, block_size))
     flat = jnp.concatenate(flat)
 
@@ -208,8 +190,8 @@
     of_list, slot = pair // quarter, pair % quarter
     off_y, off_bit = (of_list // 2) ^ y, (of_list % 2) ^ low_bit
     place = jnp.zeros_like(slot)
-    for start, size, first in zip(starts, sizes, X_FIRST):
-        off = off_y * 2 + off_bit if first else off_bit * 2 + off_y
+    for start, size in zip(starts, sizes):
+        off = off_y * 2 + off_bit
         here = 4 * int(start) + off * size + slot - int(start)
         place = jnp.where((slot >= int(start)) & (slot < int(start) + size), here, place)
     result = flat[place]

time: 132 us -> 127 us (0.962)
  starting transfers between devices: 64.5 us -> 45 us
  waiting for transfers between devices: 55.8 us -> 71 us
    ppermute x39 -> x31, starting transfers between devices: 64.5 us -> 45 us  [swap(): return lax.ppermute(value, axis, [(i, i ^ bits) for i in range(size)])]
    ppermute x39 -> x31, waiting for transfers between devices: 55.8 us -> 71 us  [swap(): return lax.ppermute(value, axis, [(i, i ^ bits) for i in range(size)])]
  transfers between devices with their start and end apart: 39 -> 31, of which waited for: 16 -> 18; matrix products, arithmetic and copies ran while one was open for 2% -> 1% of each run, Pallas kernels for 2% -> 2%
where the time goes in v5:
time: 127 us
  waiting for transfers between devices  71 us (56%)
  starting transfers between devices  45 us (35%)
  Pallas kernels  5.06 us (4%)
  local copies, waits for them, and re-layouts  2.97 us (2%)
  other arithmetic  2.22 us (2%)
    ppermute x31, waiting for transfers between devices, swap(): return lax.ppermute(value, axis, [(i, i ^ bits) for i in range(size)])  71 us
    ppermute x31, starting transfers between devices, swap(): return lax.ppermute(value, axis, [(i, i ^ bits) for i in range(size)])  45 us
    pallas_call x2, Pallas kernels, call(): pl.pallas_call(kernel, out_shape=out_shape, in_specs=[pl.BlockSpec(memory...  5.06 us
  transfers between devices with their start and end apart: 31, of which 18 were waited for; matrix products, arithmetic and copies ran while one was open for 1% of the time, Pallas kernels for 2%

profile of v5, /device:TPU:0, one launch (start us, length us, event | category | flops | bytes accessed | tf_op | source)
XLA Modules:
  0.0 126.6 jit_solution(506150548232018087)
XLA Ops:
  0.0 1.5 %constant_dynamic-slice_fusion = (bf16[3,256,256]{2,1,0:T(8,128)(2,1)S(1)}, bf16[3,256,256]{2,1,0:T(8,128)(2,1)S(1)}, bf16[3,256,256]{2,1,0:T(8,128)(2,1)S(1)}, bf16[3,256,256]{2,1,0:T(8,128)(2,1)S(1)}) fusion(bf16[3,256,1024]{2,1,0:T(8,128)(2,1)} %param.3, s32[]{:T(128)S(6)} %select_n.78, s32[]{:T(128)S(6)} %select_n.76, s32[]{:T(128)S(6)} %select_n.75, ...), kind=kLoop, calls=%fused_computation.51 | loop fusion | bytes 3145744 | tf_op jit(solution)/shard_map/dynamic_slice | solution.py:113
  1.5 3.1 %collective-permute-start = (bf16[3,256,256]{2,1,0:T(8,128)(2,1)S(1)}, bf16[3,256,256]{2,1,0:T(8,128)(2,1)S(1)}, u32[]{:S(2)}, u32[]{:S(2)}) collective-permute-start(bf16[3,256,256]{2,1,0:T(8,128)(2,1)S(1)} %get-tuple-element.30), channel_id=1, source_target_pairs={{0,8},{8,0},{16,24},{24,16},{1,9},{9,1},{17,25},{25,17},{2,10},{10... | collective-permute-start | bytes 1179656 | tf_op jit(solution)/shard_map/ppermute | solution.py:87
  4.6 2.6 %collective-permute-start.1 = (bf16[3,256,256]{2,1,0:T(8,128)(2,1)S(1)}, bf16[3,256,256]{2,1,0:T(8,128)(2,1)S(1)}, u32[]{:S(2)}, u32[]{:S(2)}) collective-permute-start(bf16[3,256,256]{2,1,0:T(8,128)(2,1)S(1)} %get-tuple-element.32), channel_id=1, source_target_pairs={{0,16},{8,24},{16,0},{24,8},{1,17},{9,25},{17,1},{25,9},{2,18},{10... | collective-permute-start | bytes 1179656 | tf_op jit(solution)/shard_map/ppermute | solution.py:87
  7.2 1.7 %collective-permute-start.3 = (bf16[3,256,256]{2,1,0:T(8,128)(2,1)S(1)}, bf16[3,256,256]{2,1,0:T(8,128)(2,1)S(1)}, u32[]{:S(2)}, u32[]{:S(2)}) collective-permute-start(bf16[3,256,256]{2,1,0:T(8,128)(2,1)S(1)} %get-tuple-element.31.refs_0_), channel_id=1, source_target_pairs={{0,4},{4,0},{1,5},{5,1},{2,6},{6,2},{3,7},{7,3},{8,12},{12,8},{9,1... | collective-permute-start | bytes 1179656 | tf_op jit(solution)/shard_map/ppermute | solution.py:87
  8.9 12.4 %collective-permute-done.refs_1_ = bf16[3,256,256]{2,1,0:T(8,128)(2,1)S(1)} collective-permute-done((bf16[3,256,256]{2,1,0:T(8,128)(2,1)S(1)}, bf16[3,256,256]{2,1,0:T(8,128)(2,1)S(1)}, u32[]{:S(2)}, u32[]{:S(2)}) %collective-permute-start) | collective-permute-done | bytes 393248 | tf_op jit(solution)/shard_map/ppermute | solution.py:87
  21.3 1.7 %collective-permute-start.4 = (bf16[3,256,256]{2,1,0:T(8,128)(2,1)S(1)}, bf16[3,256,256]{2,1,0:T(8,128)(2,1)S(1)}, u32[]{:S(2)}, u32[]{:S(2)}) collective-permute-start(bf16[3,256,256]{2,1,0:T(8,128)(2,1)S(1)} %collective-permute-done.refs_1_), channel_id=1, source_target_pairs={{0,4},{4,0},{1,5},{5,1},{2,6},{6,2},{3,7},{7,3},{8,12},{12,8},{9,1... | collective-permute-start | bytes 1179656 | tf_op jit(solution)/shard_map/ppermute | solution.py:87
  23.0 11.3 %collective-permute-done.1.refs_2_ = bf16[3,256,256]{2,1,0:T(8,128)(2,1)S(1)} collective-permute-done((bf16[3,256,256]{2,1,0:T(8,128)(2,1)S(1)}, bf16[3,256,256]{2,1,0:T(8,128)(2,1)S(1)}, u32[]{:S(2)}, u32[]{:S(2)}) %collective-permute-start.1) | collective-permute-done | bytes 393248 | tf_op jit(solution)/shard_map/ppermute | solution.py:87
  34.4 1.5 %collective-permute-start.5 = (bf16[3,256,256]{2,1,0:T(8,128)(2,1)S(1)}, bf16[3,256,256]{2,1,0:T(8,128)(2,1)S(1)}, u32[]{:S(2)}, u32[]{:S(2)}) collective-permute-start(bf16[3,256,256]{2,1,0:T(8,128)(2,1)S(1)} %collective-permute-done.1.refs_2_), channel_id=1, source_target_pairs={{0,4},{4,0},{1,5},{5,1},{2,6},{6,2},{3,7},{7,3},{8,12},{12,8},{9,1... | collective-permute-start | bytes 1179656 | tf_op jit(solution)/shard_map/ppermute | solution.py:87
  35.9 0.5 collective-permute-start.6
  36.4 0.7 fusion.8
  37.1 0.1 concatenate.6.scalars
  37.2 7.1 %collective-permute-done.5.refs_6_ = bf16[3,256,256]{2,1,0:T(8,128)(2,1)S(1)} collective-permute-done((bf16[3,256,256]{2,1,0:T(8,128)(2,1)S(1)}, bf16[3,256,256]{2,1,0:T(8,128)(2,1)S(1)}, u32[]{:S(2)}, u32[]{:S(2)}) %collective-permute-start.5) | collective-permute-done | bytes 393248 | tf_op jit(solution)/shard_map/ppermute | solution.py:87
  44.3 4.2 %collective-permute-done.6.refs_7_ = bf16[3,256,256]{2,1,0:T(8,128)(2,1)S(1)} collective-permute-done((bf16[3,256,256]{2,1,0:T(8,128)(2,1)S(1)}, bf16[3,256,256]{2,1,0:T(8,128)(2,1)S(1)}, u32[]{:S(2)}, u32[]{:S(2)}) %collective-permute-start.6) | collective-permute-done | bytes 393248 | tf_op jit(solution)/shard_map/ppermute | solution.py:87
  48.5 2.4 %tiles_first.1 = (bf16[8,256,768]{2,1,0:T(8,128)(2,1)S(1)}, f32[2,2,2,64,256]{4,3,2,1,0:T(8,128)S(1)}, f32[2,2,2,64,256]{4,3,2,1,0:T(8,128)S(1)}, f32[2,2,2,64,2...) custom-call(s32[40]{0:T(128)S(1)} %concatenate.6.scalars, bf16[3,256,256]{2,1,0:T(8,128)(2,1)S(1)} %get-tuple-element.31.refs_0_, ...), custom_call_target="tpu_custom_call" | custom-call | flops 805306368 | bytes 4194304 | tf_op jit(solution)/shard_map/tiles_first/pallas_call | solution.py:127
  50.9 0.0 copy-start
  50.9 0.1 collective-permute-start.7
  51.0 0.5 collective-permute-start.13
  51.5 2.6 %tiles_second.1 = (f32[2,2,3,64,256]{4,3,2,1,0:T(8,128)S(1)}, f32[2,2,3,64,256]{4,3,2,1,0:T(8,128)S(1)}, f32[2,2,2,64,256]{4,3,2,1,0:T(8,128)S(1)}, f32[2,2,2,64,256]{4,3,2,1,0:T(8,128)S(1)}) custom-call(s32[40]{0:T(128)S(1)} %concatenate.6.scalars, bf16[8,256,768]{2,1,0:T(8,128)(2,1)S(1)} %get-tuple-element.22.blocks), custom_call_target="tpu_custom_call" | custom-call | flops 1006632960 | bytes 4194304 | tf_op jit(solution)/shard_map/tiles_second/pallas_call | solution.py:127
  54.2 0.1 collective-permute-start.25
  54.4 0.5 collective-permute-start.19
  54.8 0.1 add.142
  54.9 1.4 %collective-permute-start.8 = (f32[2,2,64,256]{3,2,1,0:T(8,128)S(1)}, f32[2,2,64,256]{3,2,1,0:T(8,128)S(1)}, u32[]{:S(2)}, u32[]{:S(2)}) collective-permute-start(f32[2,2,64,256]{3,2,1,0:T(8,128)S(1)} %slice_bitcast_fusion.6), channel_id=1, source_target_pairs={{0,2},{2,0},{1,3},{3,1},{4,6},{6,4},{5,7},{7,5},{8,10},{10,8},{9,1... | collective-permute-start | bytes 786440 | tf_op jit(solution)/shard_map/ppermute | solution.py:87
  56.4 0.1 add.146
  56.4 0.1 add.154
  56.6 6.8 %collective-permute-done.8 = f32[2,2,64,256]{3,2,1,0:T(8,128)S(1)} collective-permute-done((f32[2,2,64,256]{3,2,1,0:T(8,128)S(1)}, f32[2,2,64,256]{3,2,1,0:T(8,128)S(1)}, u32[]{:S(2)}, u32[]{:S(2)}) %collective-permute-start.8) | collective-permute-done | bytes 262176 | tf_op jit(solution)/shard_map/ppermute | solution.py:87
  63.4 3.2 %collective-permute-start.9 = (f32[2,64,256]{2,1,0:T(8,128)S(1)}, f32[2,64,256]{2,1,0:T(8,128)S(1)}, u32[]{:S(2)}, u32[]{:S(2)}) collective-permute-start(f32[2,64,256]{2,1,0:T(8,128)S(1)} %slice_bitcast_fusion.14), channel_id=1, source_target_pairs={{0,8},{8,0},{16,24},{24,16},{1,9},{9,1},{17,25},{25,17},{2,10},{10... | collective-permute-start | bytes 393224 | tf_op jit(solution)/shard_map/ppermute | solution.py:87
  66.6 1.5 %collective-permute-start.14 = (f32[2,2,64,256]{3,2,1,0:T(8,128)S(1)}, f32[2,2,64,256]{3,2,1,0:T(8,128)S(1)}, u32[]{:S(2)}, u32[]{:S(2)}) collective-permute-start(f32[2,2,64,256]{3,2,1,0:T(8,128)S(1)} %slice_bitcast_fusion.4), channel_id=1, source_target_pairs={{0,2},{2,0},{1,3},{3,1},{4,6},{6,4},{5,7},{7,5},{8,10},{10,8},{9,1... | collective-permute-start | bytes 786440 | tf_op jit(solution)/shard_map/ppermute | solution.py:87
  68.1 0.1 add.150
  68.2 1.3 %collective-permute-done.9 = f32[2,64,256]{2,1,0:T(8,128)S(1)} collective-permute-done((f32[2,64,256]{2,1,0:T(8,128)S(1)}, f32[2,64,256]{2,1,0:T(8,128)S(1)}, u32[]{:S(2)}, u32[]{:S(2)}) %collective-permute-start.9) | collective-permute-done | bytes 131104 | tf_op jit(solution)/shard_map/ppermute | solution.py:87
  69.5 3.1 %collective-permute-start.10 = (f32[2,64,256]{2,1,0:T(8,128)S(1)}, f32[2,64,256]{2,1,0:T(8,128)S(1)}, u32[]{:S(2)}, u32[]{:S(2)}) collective-permute-start(f32[2,64,256]{2,1,0:T(8,128)S(1)} %fusion.7), channel_id=1, source_target_pairs={{0,16},{8,24},{16,0},{24,8},{1,17},{9,25},{17,1},{25,9},{2,18},{10... | collective-permute-start | bytes 393224 | tf_op jit(solution)/shard_map/ppermute | solution.py:87
  72.6 1.1 collective-permute-done.14
  73.8 0.4 collective-permute-start.15
  74.2 1.9 %collective-permute-done.10 = f32[2,64,256]{2,1,0:T(8,128)S(1)} collective-permute-done((f32[2,64,256]{2,1,0:T(8,128)S(1)}, f32[2,64,256]{2,1,0:T(8,128)S(1)}, u32[]{:S(2)}, u32[]{:S(2)}) %collective-permute-start.10) | collective-permute-done | bytes 131104 | tf_op jit(solution)/shard_map/ppermute | solution.py:87
  76.1 2.8 %collective-permute-start.11 = (f32[2,64,256]{2,1,0:T(8,128)S(1)}, f32[2,64,256]{2,1,0:T(8,128)S(1)}, u32[]{:S(2)}, u32[]{:S(2)}) collective-permute-start(f32[2,64,256]{2,1,0:T(8,128)S(1)} %add_multiply_fusion.3), channel_id=1, source_target_pairs={{0,8},{8,0},{16,24},{24,16},{1,9},{9,1},{17,25},{25,17},{2,10},{10... | collective-permute-start | bytes 393224 | tf_op jit(solution)/shard_map/ppermute | solution.py:87
  78.9 1.5 %collective-permute-start.20 = (f32[2,3,64,256]{3,2,1,0:T(8,128)S(1)}, f32[2,3,64,256]{3,2,1,0:T(8,128)S(1)}, u32[]{:S(2)}, u32[]{:S(2)}) collective-permute-start(f32[2,3,64,256]{3,2,1,0:T(8,128)S(1)} %slice_bitcast_fusion), channel_id=1, source_target_pairs={{0,2},{2,0},{1,3},{3,1},{4,6},{6,4},{5,7},{7,5},{8,10},{10,8},{9,1... | collective-permute-start | bytes 1179656 | tf_op jit(solution)/shard_map/ppermute | solution.py:87
  80.4 1.3 %collective-permute-start.16 = (f32[2,64,256]{2,1,0:T(8,128)S(1)}, f32[2,64,256]{2,1,0:T(8,128)S(1)}, u32[]{:S(2)}, u32[]{:S(2)}) collective-permute-start(f32[2,64,256]{2,1,0:T(8,128)S(1)} %fusion.6), channel_id=1, source_target_pairs={{0,16},{8,24},{16,0},{24,8},{1,17},{9,25},{17,1},{25,9},{2,18},{10... | collective-permute-start | bytes 393224 | tf_op jit(solution)/shard_map/ppermute | solution.py:87
  81.8 0.9 collective-permute-done.11
  82.7 1.6 %collective-permute-start.12 = (f32[2,2,64,256]{3,2,1,0:T(8,128)S(1)}, f32[2,2,64,256]{3,2,1,0:T(8,128)S(1)}, u32[]{:S(2)}, u32[]{:S(2)}) collective-permute-start(f32[2,2,64,256]{3,2,1,0:T(8,128)S(1)} %get-tuple-element.36), channel_id=1, source_target_pairs={{0,4},{4,0},{1,5},{5,1},{2,6},{6,2},{3,7},{7,3},{8,12},{12,8},{9,1... | collective-permute-start | bytes 786440 | tf_op jit(solution)/shard_map/ppermute | solution.py:87
  84.3 3.3 %collective-permute-done.16 = f32[2,64,256]{2,1,0:T(8,128)S(1)} collective-permute-done((f32[2,64,256]{2,1,0:T(8,128)S(1)}, f32[2,64,256]{2,1,0:T(8,128)S(1)}, u32[]{:S(2)}, u32[]{:S(2)}) %collective-permute-start.16) | collective-permute-done | bytes 131104 | tf_op jit(solution)/shard_map/ppermute | solution.py:87
  87.7 0.1 collective-permute-start.17
  87.8 1.5 %collective-permute-start.26 = (f32[2,2,64,256]{3,2,1,0:T(8,128)S(1)}, f32[2,2,64,256]{3,2,1,0:T(8,128)S(1)}, u32[]{:S(2)}, u32[]{:S(2)}) collective-permute-start(f32[2,2,64,256]{3,2,1,0:T(8,128)S(1)} %slice_bitcast_fusion.2), channel_id=1, source_target_pairs={{0,2},{2,0},{1,3},{3,1},{4,6},{6,4},{5,7},{7,5},{8,10},{10,8},{9,1... | collective-permute-start | bytes 786440 | tf_op jit(solution)/shard_map/ppermute | solution.py:87
  89.3 0.1 fusion
  89.3 2.0 %collective-permute-start.21 = (f32[3,64,256]{2,1,0:T(8,128)S(1)}, f32[3,64,256]{2,1,0:T(8,128)S(1)}, u32[]{:S(2)}, u32[]{:S(2)}) collective-permute-start(f32[3,64,256]{2,1,0:T(8,128)S(1)} %slice_bitcast_fusion.8), channel_id=1, source_target_pairs={{0,8},{8,0},{16,24},{24,16},{1,9},{9,1},{17,25},{25,17},{2,10},{10... | collective-permute-start | bytes 589832 | tf_op jit(solution)/shard_map/ppermute | solution.py:87
  91.3 2.8 %collective-permute-done.26 = f32[2,2,64,256]{3,2,1,0:T(8,128)S(1)} collective-permute-done((f32[2,2,64,256]{3,2,1,0:T(8,128)S(1)}, f32[2,2,64,256]{3,2,1,0:T(8,128)S(1)}, u32[]{:S(2)}, u32[]{:S(2)}) %collective-permute-start.26) | collective-permute-done | bytes 262176 | tf_op jit(solution)/shard_map/ppermute | solution.py:87
  94.2 2.0 %collective-permute-start.27 = (f32[2,64,256]{2,1,0:T(8,128)S(1)}, f32[2,64,256]{2,1,0:T(8,128)S(1)}, u32[]{:S(2)}, u32[]{:S(2)}) collective-permute-start(f32[2,64,256]{2,1,0:T(8,128)S(1)} %slice_bitcast_fusion.10), channel_id=1, source_target_pairs={{0,8},{8,0},{16,24},{24,16},{1,9},{9,1},{17,25},{25,17},{2,10},{10... | collective-permute-start | bytes 393224 | tf_op jit(solution)/shard_map/ppermute | solution.py:87
  96.3 2.1 %collective-permute-done.21 = f32[3,64,256]{2,1,0:T(8,128)S(1)} collective-permute-done((f32[3,64,256]{2,1,0:T(8,128)S(1)}, f32[3,64,256]{2,1,0:T(8,128)S(1)}, u32[]{:S(2)}, u32[]{:S(2)}) %collective-permute-start.21) | collective-permute-done | bytes 196640 | tf_op jit(solution)/shard_map/ppermute | solution.py:87
  98.3 1.8 %collective-permute-start.22 = (f32[3,64,256]{2,1,0:T(8,128)S(1)}, f32[3,64,256]{2,1,0:T(8,128)S(1)}, u32[]{:S(2)}, u32[]{:S(2)}) collective-permute-start(f32[3,64,256]{2,1,0:T(8,128)S(1)} %fusion.4), channel_id=1, source_target_pairs={{0,16},{8,24},{16,0},{24,8},{1,17},{9,25},{17,1},{25,9},{2,18},{10... | collective-permute-start | bytes 589832 | tf_op jit(solution)/shard_map/ppermute | solution.py:87
  100.1 2.5 %collective-permute-start.28 = (f32[2,64,256]{2,1,0:T(8,128)S(1)}, f32[2,64,256]{2,1,0:T(8,128)S(1)}, u32[]{:S(2)}, u32[]{:S(2)}) collective-permute-start(f32[2,64,256]{2,1,0:T(8,128)S(1)} %fusion.5), channel_id=1, source_target_pairs={{0,16},{8,24},{16,0},{24,8},{1,17},{9,25},{17,1},{25,9},{2,18},{10... | collective-permute-start | bytes 393224 | tf_op jit(solution)/shard_map/ppermute | solution.py:87
  102.6 4.2 %collective-permute-done.22 = f32[3,64,256]{2,1,0:T(8,128)S(1)} collective-permute-done((f32[3,64,256]{2,1,0:T(8,128)S(1)}, f32[3,64,256]{2,1,0:T(8,128)S(1)}, u32[]{:S(2)}, u32[]{:S(2)}) %collective-permute-start.22) | collective-permute-done | bytes 196640 | tf_op jit(solution)/shard_map/ppermute | solution.py:87
  106.9 1.2 collective-permute-start.23
  108.0 1.9 %collective-permute-done.28 = f32[2,64,256]{2,1,0:T(8,128)S(1)} collective-permute-done((f32[2,64,256]{2,1,0:T(8,128)S(1)}, f32[2,64,256]{2,1,0:T(8,128)S(1)}, u32[]{:S(2)}, u32[]{:S(2)}) %collective-permute-start.28) | collective-permute-done | bytes 131104 | tf_op jit(solution)/shard_map/ppermute | solution.py:87
  109.9 0.1 collective-permute-start.29
  110.1 1.6 %collective-permute-start.18 = (f32[2,2,64,256]{3,2,1,0:T(8,128)S(1)}, f32[2,2,64,256]{3,2,1,0:T(8,128)S(1)}, u32[]{:S(2)}, u32[]{:S(2)}) collective-permute-start(f32[2,2,64,256]{3,2,1,0:T(8,128)S(1)} %get-tuple-element.38), channel_id=1, source_target_pairs={{0,4},{4,0},{1,5},{5,1},{2,6},{6,2},{3,7},{7,3},{8,12},{12,8},{9,1... | collective-permute-start | bytes 786440 | tf_op jit(solution)/shard_map/ppermute | solution.py:87
  111.6 1.0 collective-permute-done.23
  112.6 0.1 fusion.15
  112.7 1.6 %collective-permute-start.24 = (f32[2,3,64,256]{3,2,1,0:T(8,128)S(1)}, f32[2,3,64,256]{3,2,1,0:T(8,128)S(1)}, u32[]{:S(2)}, u32[]{:S(2)}) collective-permute-start(f32[2,3,64,256]{3,2,1,0:T(8,128)S(1)} %get-tuple-element.34), channel_id=1, source_target_pairs={{0,4},{4,0},{1,5},{5,1},{2,6},{6,2},{3,7},{7,3},{8,12},{12,8},{9,1... | collective-permute-start | bytes 1179656 | tf_op jit(solution)/shard_map/ppermute | solution.py:87
  114.3 0.7 collective-permute-done.29
  115.0 1.6 %collective-permute-start.30 = (f32[2,2,64,256]{3,2,1,0:T(8,128)S(1)}, f32[2,2,64,256]{3,2,1,0:T(8,128)S(1)}, u32[]{:S(2)}, u32[]{:S(2)}) collective-permute-start(f32[2,2,64,256]{3,2,1,0:T(8,128)S(1)} %get-tuple-element.40), channel_id=1, source_target_pairs={{0,4},{4,0},{1,5},{5,1},{2,6},{6,2},{3,7},{7,3},{8,12},{12,8},{9,1... | collective-permute-start | bytes 786440 | tf_op jit(solution)/shard_map/ppermute | solution.py:87
  116.6 1.0 collective-permute-done.18
  117.7 7.0 %collective-permute-done.30 = f32[2,2,64,256]{3,2,1,0:T(8,128)S(1)} collective-permute-done((f32[2,2,64,256]{3,2,1,0:T(8,128)S(1)}, f32[2,2,64,256]{3,2,1,0:T(8,128)S(1)}, u32[]{:S(2)}, u32[]{:S(2)}) %collective-permute-start.30) | collective-permute-done | bytes 262176 | tf_op jit(solution)/shard_map/ppermute | solution.py:87
  124.7 0.1 pad_maximum_fusion.1
  124.8 0.2 pad_maximum_fusion
  125.1 0.6 gather_fusion
  125.7 0.9 bitcast_select_fusion
  (43 shorter events, 0.7 us)
Async XLA Ops:
  1.5 19.9 %collective-permute-start = (bf16[3,256,256]{2,1,0:T(8,128)(2,1)S(1)}, bf16[3,256,256]{2,1,0:T(8,128)(2,1)S(1)}, u32[]{:S(2)}, u32[]{:S(2)}) collective-permute-start(bf16[3,256,256]{2,1,0:T(8,128)(2,1)S(1)} %get-tuple-element.30), channel_id=1, source_target_pairs={{0,8},{8,0},{16,24},{24,16},{1,9},{9,1},{17,25},{25,17},{2,10},{10... | collective-permute-start | bytes 1179656 | tf_op jit(solution)/shard_map/ppermute | solution.py:87
  4.6 29.8 %collective-permute-start.1 = (bf16[3,256,256]{2,1,0:T(8,128)(2,1)S(1)}, bf16[3,256,256]{2,1,0:T(8,128)(2,1)S(1)}, u32[]{:S(2)}, u32[]{:S(2)}) collective-permute-start(bf16[3,256,256]{2,1,0:T(8,128)(2,1)S(1)} %get-tuple-element.32), channel_id=1, source_target_pairs={{0,16},{8,24},{16,0},{24,8},{1,17},{9,25},{17,1},{25,9},{2,18},{10... | collective-permute-start | bytes 1179656 | tf_op jit(solution)/shard_map/ppermute | solution.py:87
  7.2 28.7 %collective-permute-start.2 = (bf16[3,256,256]{2,1,0:T(8,128)(2,1)S(1)}, bf16[3,256,256]{2,1,0:T(8,128)(2,1)S(1)}, u32[]{:S(2)}, u32[]{:S(2)}) collective-permute-start(bf16[3,256,256]{2,1,0:T(8,128)(2,1)S(1)} %get-tuple-element.29), channel_id=1, source_target_pairs={{0,24},{8,16},{16,8},{24,0},{1,25},{9,17},{17,9},{25,1},{2,26},{10... | collective-permute-start | bytes 1179656 | tf_op jit(solution)/shard_map/ppermute | solution.py:87
  7.2 30.0 %collective-permute-start.3 = (bf16[3,256,256]{2,1,0:T(8,128)(2,1)S(1)}, bf16[3,256,256]{2,1,0:T(8,128)(2,1)S(1)}, u32[]{:S(2)}, u32[]{:S(2)}) collective-permute-start(bf16[3,256,256]{2,1,0:T(8,128)(2,1)S(1)} %get-tuple-element.31.refs_0_), channel_id=1, source_target_pairs={{0,4},{4,0},{1,5},{5,1},{2,6},{6,2},{3,7},{7,3},{8,12},{12,8},{9,1... | collective-permute-start | bytes 1179656 | tf_op jit(solution)/shard_map/ppermute | solution.py:87
  21.3 15.8 %collective-permute-start.4 = (bf16[3,256,256]{2,1,0:T(8,128)(2,1)S(1)}, bf16[3,256,256]{2,1,0:T(8,128)(2,1)S(1)}, u32[]{:S(2)}, u32[]{:S(2)}) collective-permute-start(bf16[3,256,256]{2,1,0:T(8,128)(2,1)S(1)} %collective-permute-done.refs_1_), channel_id=1, source_target_pairs={{0,4},{4,0},{1,5},{5,1},{2,6},{6,2},{3,7},{7,3},{8,12},{12,8},{9,1... | collective-permute-start | bytes 1179656 | tf_op jit(solution)/shard_map/ppermute | solution.py:87
  34.4 9.9 %collective-permute-start.5 = (bf16[3,256,256]{2,1,0:T(8,128)(2,1)S(1)}, bf16[3,256,256]{2,1,0:T(8,128)(2,1)S(1)}, u32[]{:S(2)}, u32[]{:S(2)}) collective-permute-start(bf16[3,256,256]{2,1,0:T(8,128)(2,1)S(1)} %collective-permute-done.1.refs_2_), channel_id=1, source_target_pairs={{0,4},{4,0},{1,5},{5,1},{2,6},{6,2},{3,7},{7,3},{8,12},{12,8},{9,1... | collective-permute-start | bytes 1179656 | tf_op jit(solution)/shard_map/ppermute | solution.py:87
  35.9 12.6 %collective-permute-start.6 = (bf16[3,256,256]{2,1,0:T(8,128)(2,1)S(1)}, bf16[3,256,256]{2,1,0:T(8,128)(2,1)S(1)}, u32[]{:S(2)}, u32[]{:S(2)}) collective-permute-start(bf16[3,256,256]{2,1,0:T(8,128)(2,1)S(1)} %collective-permute-done.2.refs_3_), channel_id=1, source_target_pairs={{0,4},{4,0},{1,5},{5,1},{2,6},{6,2},{3,7},{7,3},{8,12},{12,8},{9,1... | collective-permute-start | bytes 1179656 | tf_op jit(solution)/shard_map/ppermute | solution.py:87
  50.9 3.4 %copy-start = (s32[1,10,2]{1,2,0:T(2,128)S(1)}, s32[1,10,2]{1,2,0:T(2,128)}, u32[]{:S(2)}) copy-start(s32[1,10,2]{1,2,0:T(2,128)} %param.4) | copy-start | bytes 244
  50.9 3.9 %collective-permute-start.7 = (f32[2,2,2,64,256]{4,3,2,1,0:T(8,128)S(1)}, f32[2,2,2,64,256]{4,3,2,1,0:T(8,128)S(1)}, u32[]{:S(2)}, u32[]{:S(2)}) collective-permute-start(f32[2,2,2,64,256]{4,3,2,1,0:T(8,128)S(1)} %get-tuple-element.18), channel_id=1, source_target_pairs={{0,1},{1,0},{2,3},{3,2},{4,5},{5,4},{6,7},{7,6},{8,9},{9,8},{10,11... | collective-permute-start | bytes 1572872 | tf_op jit(solution)/shard_map/ppermute | solution.py:87
  51.0 5.3 %collective-permute-start.13 = (f32[2,2,2,64,256]{4,3,2,1,0:T(8,128)S(1)}, f32[2,2,2,64,256]{4,3,2,1,0:T(8,128)S(1)}, u32[]{:S(2)}, u32[]{:S(2)}) collective-permute-start(f32[2,2,2,64,256]{4,3,2,1,0:T(8,128)S(1)} %get-tuple-element.20), channel_id=1, source_target_pairs={{0,1},{1,0},{2,3},{3,2},{4,5},{5,4},{6,7},{7,6},{8,9},{9,8},{10,11... | collective-permute-start | bytes 1572872 | tf_op jit(solution)/shard_map/ppermute | solution.py:87
  54.2 2.3 %collective-permute-start.25 = (f32[2,2,2,64,256]{4,3,2,1,0:T(8,128)S(1)}, f32[2,2,2,64,256]{4,3,2,1,0:T(8,128)S(1)}, u32[]{:S(2)}, u32[]{:S(2)}) collective-permute-start(f32[2,2,2,64,256]{4,3,2,1,0:T(8,128)S(1)} %get-tuple-element.27), channel_id=1, source_target_pairs={{0,1},{1,0},{2,3},{3,2},{4,5},{5,4},{6,7},{7,6},{8,9},{9,8},{10,11... | collective-permute-start | bytes 1572872 | tf_op jit(solution)/shard_map/ppermute | solution.py:87
  54.4 13.7 %collective-permute-start.19 = (f32[2,2,3,64,256]{4,3,2,1,0:T(8,128)S(1)}, f32[2,2,3,64,256]{4,3,2,1,0:T(8,128)S(1)}, u32[]{:S(2)}, u32[]{:S(2)}) collective-permute-start(f32[2,2,3,64,256]{4,3,2,1,0:T(8,128)S(1)} %get-tuple-element.24), channel_id=1, source_target_pairs={{0,1},{1,0},{2,3},{3,2},{4,5},{5,4},{6,7},{7,6},{8,9},{9,8},{10,11... | collective-permute-start | bytes 2359304 | tf_op jit(solution)/shard_map/ppermute | solution.py:87
  54.9 8.4 %collective-permute-start.8 = (f32[2,2,64,256]{3,2,1,0:T(8,128)S(1)}, f32[2,2,64,256]{3,2,1,0:T(8,128)S(1)}, u32[]{:S(2)}, u32[]{:S(2)}) collective-permute-start(f32[2,2,64,256]{3,2,1,0:T(8,128)S(1)} %slice_bitcast_fusion.6), channel_id=1, source_target_pairs={{0,2},{2,0},{1,3},{3,1},{4,6},{6,4},{5,7},{7,5},{8,10},{10,8},{9,1... | collective-permute-start | bytes 786440 | tf_op jit(solution)/shard_map/ppermute | solution.py:87
  63.4 6.2 %collective-permute-start.9 = (f32[2,64,256]{2,1,0:T(8,128)S(1)}, f32[2,64,256]{2,1,0:T(8,128)S(1)}, u32[]{:S(2)}, u32[]{:S(2)}) collective-permute-start(f32[2,64,256]{2,1,0:T(8,128)S(1)} %slice_bitcast_fusion.14), channel_id=1, source_target_pairs={{0,8},{8,0},{16,24},{24,16},{1,9},{9,1},{17,25},{25,17},{2,10},{10... | collective-permute-start | bytes 393224 | tf_op jit(solution)/shard_map/ppermute | solution.py:87
  66.6 7.2 %collective-permute-start.14 = (f32[2,2,64,256]{3,2,1,0:T(8,128)S(1)}, f32[2,2,64,256]{3,2,1,0:T(8,128)S(1)}, u32[]{:S(2)}, u32[]{:S(2)}) collective-permute-start(f32[2,2,64,256]{3,2,1,0:T(8,128)S(1)} %slice_bitcast_fusion.4), channel_id=1, source_target_pairs={{0,2},{2,0},{1,3},{3,1},{4,6},{6,4},{5,7},{7,5},{8,10},{10,8},{9,1... | collective-permute-start | bytes 786440 | tf_op jit(solution)/shard_map/ppermute | solution.py:87
  69.5 6.6 %collective-permute-start.10 = (f32[2,64,256]{2,1,0:T(8,128)S(1)}, f32[2,64,256]{2,1,0:T(8,128)S(1)}, u32[]{:S(2)}, u32[]{:S(2)}) collective-permute-start(f32[2,64,256]{2,1,0:T(8,128)S(1)} %fusion.7), channel_id=1, source_target_pairs={{0,16},{8,24},{16,0},{24,8},{1,17},{9,25},{17,1},{25,9},{2,18},{10... | collective-permute-start | bytes 393224 | tf_op jit(solution)/shard_map/ppermute | solution.py:87
  73.8 6.6 %collective-permute-start.15 = (f32[2,64,256]{2,1,0:T(8,128)S(1)}, f32[2,64,256]{2,1,0:T(8,128)S(1)}, u32[]{:S(2)}, u32[]{:S(2)}) collective-permute-start(f32[2,64,256]{2,1,0:T(8,128)S(1)} %slice_bitcast_fusion.12), channel_id=1, source_target_pairs={{0,8},{8,0},{16,24},{24,16},{1,9},{9,1},{17,25},{25,17},{2,10},{10... | collective-permute-start | bytes 393224 | tf_op jit(solution)/shard_map/ppermute | solution.py:87
  76.1 6.6 %collective-permute-start.11 = (f32[2,64,256]{2,1,0:T(8,128)S(1)}, f32[2,64,256]{2,1,0:T(8,128)S(1)}, u32[]{:S(2)}, u32[]{:S(2)}) collective-permute-start(f32[2,64,256]{2,1,0:T(8,128)S(1)} %add_multiply_fusion.3), channel_id=1, source_target_pairs={{0,8},{8,0},{16,24},{24,16},{1,9},{9,1},{17,25},{25,17},{2,10},{10... | collective-permute-start | bytes 393224 | tf_op jit(solution)/shard_map/ppermute | solution.py:87
  78.9 8.8 %collective-permute-start.20 = (f32[2,3,64,256]{3,2,1,0:T(8,128)S(1)}, f32[2,3,64,256]{3,2,1,0:T(8,128)S(1)}, u32[]{:S(2)}, u32[]{:S(2)}) collective-permute-start(f32[2,3,64,256]{3,2,1,0:T(8,128)S(1)} %slice_bitcast_fusion), channel_id=1, source_target_pairs={{0,2},{2,0},{1,3},{3,1},{4,6},{6,4},{5,7},{7,5},{8,10},{10,8},{9,1... | collective-permute-start | bytes 1179656 | tf_op jit(solution)/shard_map/ppermute | solution.py:87
  80.4 7.2 %collective-permute-start.16 = (f32[2,64,256]{2,1,0:T(8,128)S(1)}, f32[2,64,256]{2,1,0:T(8,128)S(1)}, u32[]{:S(2)}, u32[]{:S(2)}) collective-permute-start(f32[2,64,256]{2,1,0:T(8,128)S(1)} %fusion.6), channel_id=1, source_target_pairs={{0,16},{8,24},{16,0},{24,8},{1,17},{9,25},{17,1},{25,9},{2,18},{10... | collective-permute-start | bytes 393224 | tf_op jit(solution)/shard_map/ppermute | solution.py:87
  82.7 33.9 %collective-permute-start.12 = (f32[2,2,64,256]{3,2,1,0:T(8,128)S(1)}, f32[2,2,64,256]{3,2,1,0:T(8,128)S(1)}, u32[]{:S(2)}, u32[]{:S(2)}) collective-permute-start(f32[2,2,64,256]{3,2,1,0:T(8,128)S(1)} %get-tuple-element.36), channel_id=1, source_target_pairs={{0,4},{4,0},{1,5},{5,1},{2,6},{6,2},{3,7},{7,3},{8,12},{12,8},{9,1... | collective-permute-start | bytes 786440 | tf_op jit(solution)/shard_map/ppermute | solution.py:87
  87.7 22.3 %collective-permute-start.17 = (f32[2,64,256]{2,1,0:T(8,128)S(1)}, f32[2,64,256]{2,1,0:T(8,128)S(1)}, u32[]{:S(2)}, u32[]{:S(2)}) collective-permute-start(f32[2,64,256]{2,1,0:T(8,128)S(1)} %add_multiply_fusion.2), channel_id=1, source_target_pairs={{0,8},{8,0},{16,24},{24,16},{1,9},{9,1},{17,25},{25,17},{2,10},{10... | collective-permute-start | bytes 393224 | tf_op jit(solution)/shard_map/ppermute | solution.py:87
  87.8 6.4 %collective-permute-start.26 = (f32[2,2,64,256]{3,2,1,0:T(8,128)S(1)}, f32[2,2,64,256]{3,2,1,0:T(8,128)S(1)}, u32[]{:S(2)}, u32[]{:S(2)}) collective-permute-start(f32[2,2,64,256]{3,2,1,0:T(8,128)S(1)} %slice_bitcast_fusion.2), channel_id=1, source_target_pairs={{0,2},{2,0},{1,3},{3,1},{4,6},{6,4},{5,7},{7,5},{8,10},{10,8},{9,1... | collective-permute-start | bytes 786440 | tf_op jit(solution)/shard_map/ppermute | solution.py:87
  89.3 9.0 %collective-permute-start.21 = (f32[3,64,256]{2,1,0:T(8,128)S(1)}, f32[3,64,256]{2,1,0:T(8,128)S(1)}, u32[]{:S(2)}, u32[]{:S(2)}) collective-permute-start(f32[3,64,256]{2,1,0:T(8,128)S(1)} %slice_bitcast_fusion.8), channel_id=1, source_target_pairs={{0,8},{8,0},{16,24},{24,16},{1,9},{9,1},{17,25},{25,17},{2,10},{10... | collective-permute-start | bytes 589832 | tf_op jit(solution)/shard_map/ppermute | solution.py:87
  94.2 5.9 %collective-permute-start.27 = (f32[2,64,256]{2,1,0:T(8,128)S(1)}, f32[2,64,256]{2,1,0:T(8,128)S(1)}, u32[]{:S(2)}, u32[]{:S(2)}) collective-permute-start(f32[2,64,256]{2,1,0:T(8,128)S(1)} %slice_bitcast_fusion.10), channel_id=1, source_target_pairs={{0,8},{8,0},{16,24},{24,16},{1,9},{9,1},{17,25},{25,17},{2,10},{10... | collective-permute-start | bytes 393224 | tf_op jit(solution)/shard_map/ppermute | solution.py:87
  98.3 8.5 %collective-permute-start.22 = (f32[3,64,256]{2,1,0:T(8,128)S(1)}, f32[3,64,256]{2,1,0:T(8,128)S(1)}, u32[]{:S(2)}, u32[]{:S(2)}) collective-permute-start(f32[3,64,256]{2,1,0:T(8,128)S(1)} %fusion.4), channel_id=1, source_target_pairs={{0,16},{8,24},{16,0},{24,8},{1,17},{9,25},{17,1},{25,9},{2,18},{10... | collective-permute-start | bytes 589832 | tf_op jit(solution)/shard_map/ppermute | solution.py:87
  100.1 9.8 %collective-permute-start.28 = (f32[2,64,256]{2,1,0:T(8,128)S(1)}, f32[2,64,256]{2,1,0:T(8,128)S(1)}, u32[]{:S(2)}, u32[]{:S(2)}) collective-permute-start(f32[2,64,256]{2,1,0:T(8,128)S(1)} %fusion.5), channel_id=1, source_target_pairs={{0,16},{8,24},{16,0},{24,8},{1,17},{9,25},{17,1},{25,9},{2,18},{10... | collective-permute-start | bytes 393224 | tf_op jit(solution)/shard_map/ppermute | solution.py:87
  106.9 5.7 %collective-permute-start.23 = (f32[3,64,256]{2,1,0:T(8,128)S(1)}, f32[3,64,256]{2,1,0:T(8,128)S(1)}, u32[]{:S(2)}, u32[]{:S(2)}) collective-permute-start(f32[3,64,256]{2,1,0:T(8,128)S(1)} %add_multiply_fusion), channel_id=1, source_target_pairs={{0,8},{8,0},{16,24},{24,16},{1,9},{9,1},{17,25},{25,17},{2,10},{10... | collective-permute-start | bytes 589832 | tf_op jit(solution)/shard_map/ppermute | solution.py:87
  109.9 5.0 %collective-permute-start.29 = (f32[2,64,256]{2,1,0:T(8,128)S(1)}, f32[2,64,256]{2,1,0:T(8,128)S(1)}, u32[]{:S(2)}, u32[]{:S(2)}) collective-permute-start(f32[2,64,256]{2,1,0:T(8,128)S(1)} %add_multiply_fusion.1), channel_id=1, source_target_pairs={{0,8},{8,0},{16,24},{24,16},{1,9},{9,1},{17,25},{25,17},{2,10},{10... | collective-permute-start | bytes 393224 | tf_op jit(solution)/shard_map/ppermute | solution.py:87
  110.1 7.6 %collective-permute-start.18 = (f32[2,2,64,256]{3,2,1,0:T(8,128)S(1)}, f32[2,2,64,256]{3,2,1,0:T(8,128)S(1)}, u32[]{:S(2)}, u32[]{:S(2)}) collective-permute-start(f32[2,2,64,256]{3,2,1,0:T(8,128)S(1)} %get-tuple-element.38), channel_id=1, source_target_pairs={{0,4},{4,0},{1,5},{5,1},{2,6},{6,2},{3,7},{7,3},{8,12},{12,8},{9,1... | collective-permute-start | bytes 786440 | tf_op jit(solution)/shard_map/ppermute | solution.py:87
  112.7 12.1 %collective-permute-start.24 = (f32[2,3,64,256]{3,2,1,0:T(8,128)S(1)}, f32[2,3,64,256]{3,2,1,0:T(8,128)S(1)}, u32[]{:S(2)}, u32[]{:S(2)}) collective-permute-start(f32[2,3,64,256]{3,2,1,0:T(8,128)S(1)} %get-tuple-element.34), channel_id=1, source_target_pairs={{0,4},{4,0},{1,5},{5,1},{2,6},{6,2},{3,7},{7,3},{8,12},{12,8},{9,1... | collective-permute-start | bytes 1179656 | tf_op jit(solution)/shard_map/ppermute | solution.py:87
  115.0 9.7 %collective-permute-start.30 = (f32[2,2,64,256]{3,2,1,0:T(8,128)S(1)}, f32[2,2,64,256]{3,2,1,0:T(8,128)S(1)}, u32[]{:S(2)}, u32[]{:S(2)}) collective-permute-start(f32[2,2,64,256]{3,2,1,0:T(8,128)S(1)} %get-tuple-element.40), channel_id=1, source_target_pairs={{0,4},{4,0},{1,5},{5,1},{2,6},{6,2},{3,7},{7,3},{8,12},{12,8},{9,1... | collective-permute-start | bytes 786440 | tf_op jit(solution)/shard_map/ppermute | solution.py:87

commit v6 on v5

--- a/solution.py
+++ b/solution.py
@@ -10,7 +10,8 @@
 from jax.sharding import Mesh, PartitionSpec as P
 
 VMEM_LIMIT = 24 * 2**20
-GROUPS = 4
+GROUPS = 3
+CODE_TOP = 32767.0
 
 
 def tile_lists(block_count):
@@ -19,8 +20,7 @@
 
 
 def group_sizes(quarter):
-    sizes = [len(piece) for piece in np.array_split(np.arange(quarter), GROUPS)]
-    return sizes[1:-1] + sizes[:1] + sizes[-1:]
+    return [len(piece) for piece in np.array_split(np.arange(quarter), GROUPS)]
 
 
 def multiply_tiles(scalars, first_pair, blocks, keep_ref, send_ref):
@@ -85,9 +85,6 @@
     def swap(value, axis, bits):
         size = lax.axis_size(axis)
         return lax.ppermute(value, axis, [(i, i ^ bits) for i in range(size)])
-
-    def after(value, earlier):
-        return lax.optimization_barrier((value, earlier))
 
     lists = tile_lists(block_count)
     quarter = lists.shape[2]
@@ -144,41 +141,55 @@
     )
     blocks, *sums = call(
         functools.partial(first_kernel, layout, 4),
-        sizes[0] + sizes[1],
-        [blocks_shape] + shapes[:4],
+        sizes[0],
+        [blocks_shape] + shapes[:2],
         chunks,
         "tiles_first",
     )
     sums += call(
-        functools.partial(second_kernel, 4 + 4 * (sizes[0] + sizes[1])),
-        sizes[2] + sizes[3],
-        shapes[4:],
+        functools.partial(second_kernel, 4 + 4 * sizes[0]),
+        sum(sizes[1:]),
+        shapes[2:],
         [blocks],
         "tiles_second",
     )
 
-    flat = []
-    arrived = None
-    for index in range(GROUPS):
-        keep, send = sums[2 * index : 2 * index + 2]
+    def after(value, earlier):
+        return lax.optimization_barrier((value, earlier))[0]
+
+    groups = len(sizes)
+    low_arrived, y_arrived = [], []
+    codes, scales = [], []
+    for index, (keep, send) in enumerate(zip(sums[::2], sums[1::2])):
         total = keep + swap(send, "core", 1)
         held = total[0]
         for step in range(1, x_count):
-            away = total[step]
-            if arrived is not None:
-                away, arrived = after(away, arrived)
-            arrived = swap(away, "x", step)
-            held = held + arrived
-        held = held[0] + swap(held[1], "z", 1)
+            held = held + swap(total[step], "x", step)
+        away, held = held[1], held[0]
+        if index >= 2:
+            away = after(away, low_arrived[index - 2])
+        held = held + swap(away, "z", 1)
+        if index >= 2:
+            held = after(held, y_arrived[index - 2])
         bits = 2
         while bits < z_count:
             held = held + swap(held, "z", bits)
             bits *= 2
-        held = held * scale_factor
-        pair = jnp.stack([held, swap(held, "z", 1)])
-        whole = jnp.stack([pair, swap(pair, "y", 1)])
-        flat.append(whole.reshape(-1, rows_dev, block_size))
-    flat = jnp.concatenate(flat)
+        if index == groups - 1:
+            held = after(held, y_arrived[index - 1])
+        top = jnp.max(jnp.abs(held), axis=2)
+        factor = jnp.where(top > 0, CODE_TOP / top, 0.0)
+        code = jnp.round(held * factor[:, :, None])
+        code = jnp.clip(code, -CODE_TOP, CODE_TOP).astype(jnp.int16)
+        low_arrived.append(swap(code, "z", 1))
+        pair = jnp.stack([code, low_arrived[-1]])
+        y_arrived.append(swap(pair, "y", 1))
+        codes.append(jnp.stack([pair, y_arrived[-1]]).reshape(-1, rows_dev, block_size))
+        scales.append(top * (scale_factor / CODE_TOP))
+    codes = jnp.concatenate(codes)
+    scales = after(jnp.concatenate(scales), low_arrived[-1])
+    scales = jnp.stack([scales, swap(scales, "z", 1)])
+    scales = jnp.stack([scales, swap(scales, "y", 1)])
 
     table = tile_table[0]
     row_block = table[:, 0]
@@ -188,14 +199,14 @@
     second = jnp.maximum(col_block, 0)
     pair = first * block_count - (first * (first - 1)) // 2 + second - first
     of_list, slot = pair // quarter, pair % quarter
-    off_y, off_bit = (of_list // 2) ^ y, (of_list % 2) ^ low_bit
+    off = ((of_list // 2) ^ y) * 2 + ((of_list % 2) ^ low_bit)
     place = jnp.zeros_like(slot)
     for start, size in zip(starts, sizes):
-        off = off_y * 2 + off_bit
         here = 4 * int(start) + off * size + slot - int(start)
         place = jnp.where((slot >= int(start)) & (slot < int(start) + size), here, place)
-    result = flat[place]
-    result = jnp.where(valid[:, None, None], result, jnp.zeros_like(result))
+    scale = scales.reshape(-1, rows_dev)[off * quarter + slot]
+    scale = jnp.where(valid[:, None], scale, 0.0)
+    result = codes[place].astype(jnp.float32) * scale[:, :, None]
     return result[None]
 
 

time: 127 us -> 149 us (1.17)
  waiting for transfers between devices: 71 us -> 103 us
  starting transfers between devices: 45 us -> 33.7 us
    ppermute x31 -> x27, waiting for transfers between devices: 71 us -> 103 us  [swap(): return lax.ppermute(value, axis, [(i, i ^ bits) for i in range(size)])]
    ppermute x31 -> x27, starting transfers between devices: 45 us -> 33.7 us  [swap(): return lax.ppermute(value, axis, [(i, i ^ bits) for i in range(size)])]
  transfers between devices with their start and end apart: 31 -> 27, of which waited for: 18 -> 18; matrix products, arithmetic and copies ran while one was open for 1% -> 2% of each run, Pallas kernels for 2% -> 0%
where the time goes in v6:
time: 149 us; the launch traced here: 148 us
  waiting for transfers between devices  103 us (69%)
  starting transfers between devices  33.7 us (23%)
  Pallas kernels  5.07 us (3%)
  local copies, waits for them, and re-layouts  3.59 us (2%)
  other arithmetic  2.93 us (2%)
    ppermute x27, waiting for transfers between devices, swap(): return lax.ppermute(value, axis, [(i, i ^ bits) for i in range(size)])  103 us
    ppermute x27, starting transfers between devices, swap(): return lax.ppermute(value, axis, [(i, i ^ bits) for i in range(size)])  33.7 us
    pallas_call x2, Pallas kernels, call(): pl.pallas_call(kernel, out_shape=out_shape, in_specs=[pl.BlockSpec(memory...  5.07 us
  transfers between devices with their start and end apart: 27, of which 18 were waited for; matrix products, arithmetic and copies ran while one was open for 2% of the time, Pallas kernels for 0%

profile of v6, /device:TPU:0, one launch (start us, length us, event | category | flops | bytes accessed | tf_op | source)
XLA Modules:
  0.0 148.5 jit_solution(7808934033414376840)
XLA Ops:
  0.0 1.5 constant_dynamic-slice_fusion
  1.5 3.1 %collective-permute-start = (bf16[3,256,256]{2,1,0:T(8,128)(2,1)S(1)}, bf16[3,256,256]{2,1,0:T(8,128)(2,1)S(1)}, u32[]{:S(2)}, u32[]{:S(2)}) collective-permute-start(bf16[3,256,256]{2,1,0:T(8,128)(2,1)S(1)} %get-tuple-element.35), channel_id=1, source_target_pairs={{0,8},{8,0},{16,24},{24,16},{1,9},{9,1},{17,25},{25,17},{2,10},{10... | collective-permute-start | bytes 1179656 | tf_op jit(solution)/shard_map/ppermute | solution.py:87
  4.6 2.6 %collective-permute-start.1 = (bf16[3,256,256]{2,1,0:T(8,128)(2,1)S(1)}, bf16[3,256,256]{2,1,0:T(8,128)(2,1)S(1)}, u32[]{:S(2)}, u32[]{:S(2)}) collective-permute-start(bf16[3,256,256]{2,1,0:T(8,128)(2,1)S(1)} %get-tuple-element.37), channel_id=1, source_target_pairs={{0,16},{8,24},{16,0},{24,8},{1,17},{9,25},{17,1},{25,9},{2,18},{10... | collective-permute-start | bytes 1179656 | tf_op jit(solution)/shard_map/ppermute | solution.py:87
  7.2 1.7 %collective-permute-start.3 = (bf16[3,256,256]{2,1,0:T(8,128)(2,1)S(1)}, bf16[3,256,256]{2,1,0:T(8,128)(2,1)S(1)}, u32[]{:S(2)}, u32[]{:S(2)}) collective-permute-start(bf16[3,256,256]{2,1,0:T(8,128)(2,1)S(1)} %get-tuple-element.36.refs_0_), channel_id=1, source_target_pairs={{0,4},{4,0},{1,5},{5,1},{2,6},{6,2},{3,7},{7,3},{8,12},{12,8},{9,1... | collective-permute-start | bytes 1179656 | tf_op jit(solution)/shard_map/ppermute | solution.py:87
  8.9 12.4 %collective-permute-done.refs_1_ = bf16[3,256,256]{2,1,0:T(8,128)(2,1)S(1)} collective-permute-done((bf16[3,256,256]{2,1,0:T(8,128)(2,1)S(1)}, bf16[3,256,256]{2,1,0:T(8,128)(2,1)S(1)}, u32[]{:S(2)}, u32[]{:S(2)}) %collective-permute-start) | collective-permute-done | bytes 393248 | tf_op jit(solution)/shard_map/ppermute | solution.py:87
  21.3 1.7 %collective-permute-start.4 = (bf16[3,256,256]{2,1,0:T(8,128)(2,1)S(1)}, bf16[3,256,256]{2,1,0:T(8,128)(2,1)S(1)}, u32[]{:S(2)}, u32[]{:S(2)}) collective-permute-start(bf16[3,256,256]{2,1,0:T(8,128)(2,1)S(1)} %collective-permute-done.refs_1_), channel_id=1, source_target_pairs={{0,4},{4,0},{1,5},{5,1},{2,6},{6,2},{3,7},{7,3},{8,12},{12,8},{9,1... | collective-permute-start | bytes 1179656 | tf_op jit(solution)/shard_map/ppermute | solution.py:87
  23.0 11.3 %collective-permute-done.1.refs_2_ = bf16[3,256,256]{2,1,0:T(8,128)(2,1)S(1)} collective-permute-done((bf16[3,256,256]{2,1,0:T(8,128)(2,1)S(1)}, bf16[3,256,256]{2,1,0:T(8,128)(2,1)S(1)}, u32[]{:S(2)}, u32[]{:S(2)}) %collective-permute-start.1) | collective-permute-done | bytes 393248 | tf_op jit(solution)/shard_map/ppermute | solution.py:87
  34.4 1.5 %collective-permute-start.5 = (bf16[3,256,256]{2,1,0:T(8,128)(2,1)S(1)}, bf16[3,256,256]{2,1,0:T(8,128)(2,1)S(1)}, u32[]{:S(2)}, u32[]{:S(2)}) collective-permute-start(bf16[3,256,256]{2,1,0:T(8,128)(2,1)S(1)} %collective-permute-done.1.refs_2_), channel_id=1, source_target_pairs={{0,4},{4,0},{1,5},{5,1},{2,6},{6,2},{3,7},{7,3},{8,12},{12,8},{9,1... | collective-permute-start | bytes 1179656 | tf_op jit(solution)/shard_map/ppermute | solution.py:87
  35.9 0.5 collective-permute-start.6
  36.4 0.7 fusion.6
  37.1 0.1 concatenate.9.scalars
  37.2 7.1 %collective-permute-done.5.refs_6_ = bf16[3,256,256]{2,1,0:T(8,128)(2,1)S(1)} collective-permute-done((bf16[3,256,256]{2,1,0:T(8,128)(2,1)S(1)}, bf16[3,256,256]{2,1,0:T(8,128)(2,1)S(1)}, u32[]{:S(2)}, u32[]{:S(2)}) %collective-permute-start.5) | collective-permute-done | bytes 393248 | tf_op jit(solution)/shard_map/ppermute | solution.py:87
  44.3 4.2 %collective-permute-done.6.refs_7_ = bf16[3,256,256]{2,1,0:T(8,128)(2,1)S(1)} collective-permute-done((bf16[3,256,256]{2,1,0:T(8,128)(2,1)S(1)}, bf16[3,256,256]{2,1,0:T(8,128)(2,1)S(1)}, u32[]{:S(2)}, u32[]{:S(2)}) %collective-permute-start.6) | collective-permute-done | bytes 393248 | tf_op jit(solution)/shard_map/ppermute | solution.py:87
  48.5 2.0 %tiles_first.1 = (bf16[8,256,768]{2,1,0:T(8,128)(2,1)S(1)}, f32[2,2,3,64,256]{4,3,2,1,0:T(8,128)S(1)}, f32[2,2,3,64,256]{4,3,2,1,0:T(8,128)S(1)}) custom-call(s32[40]{0:T(128)S(1)} %concatenate.9.scalars, bf16[3,256,256]{2,1,0:T(8,128)(2,1)S(1)} %get-tuple-element.36.refs_0_, bf16[3,256,256]{2,1,0:T(8,128)(2,1)S(1)} %collective-permute-done.refs_1_, ...), custom_call_target="tpu_custom_call" | custom-call | flops 603979776 | bytes 4194304 | tf_op jit(solution)/shard_map/tiles_first/pallas_call | solution.py:124
  50.5 3.1 %tiles_second.1 = (f32[2,2,3,64,256]{4,3,2,1,0:T(8,128)S(1)}, f32[2,2,3,64,256]{4,3,2,1,0:T(8,128)S(1)}, f32[2,2,3,64,256]{4,3,2,1,0:T(8,128)S(1)}, f32[2,2,3,64,256]{4,3,2,1,0:T(8,128)S(1)}) custom-call(s32[40]{0:T(128)S(1)} %concatenate.9.scalars, bf16[8,256,768]{2,1,0:T(8,128)(2,1)S(1)} %get-tuple-element.18.blocks), custom_call_target="tpu_custom_call" | custom-call | flops 1207959552 | bytes 4194304 | tf_op jit(solution)/shard_map/tiles_second/pallas_call | solution.py:124
  53.6 0.1 collective-permute-start.13
  53.7 0.6 collective-permute-start.7
  54.3 0.1 collective-permute-start.19
  54.4 1.5 %collective-permute-done.13 = f32[2,2,3,64,256]{4,3,2,1,0:T(8,128)S(1)} collective-permute-done((f32[2,2,3,64,256]{4,3,2,1,0:T(8,128)S(1)}, f32[2,2,3,64,256]{4,3,2,1,0:T(8,128)S(1)}, u32[]{:S(2)}, u32[]{:S(2)}) %collective-permute-start.13) | collective-permute-done | bytes 786464 | tf_op jit(solution)/shard_map/ppermute | solution.py:87
  55.9 0.1 add.137
  56.1 1.4 collective-permute-start.14
  57.5 0.1 add.133
  57.6 1.0 collective-permute-start.8
  58.6 0.1 add.141
  58.8 1.2 collective-permute-start.20
  59.9 8.2 %collective-permute-done.14 = f32[2,3,64,256]{3,2,1,0:T(8,128)S(1)} collective-permute-done((f32[2,3,64,256]{3,2,1,0:T(8,128)S(1)}, f32[2,3,64,256]{3,2,1,0:T(8,128)S(1)}, u32[]{:S(2)}, u32[]{:S(2)}) %collective-permute-start.14) | collective-permute-done | bytes 393248 | tf_op jit(solution)/shard_map/ppermute | solution.py:87
  68.2 3.2 %collective-permute-start.15 = (f32[3,64,256]{2,1,0:T(8,128)S(1)}, f32[3,64,256]{2,1,0:T(8,128)S(1)}, u32[]{:S(2)}, u32[]{:S(2)}) collective-permute-start(f32[3,64,256]{2,1,0:T(8,128)S(1)} %slice_bitcast_fusion.8), channel_id=1, source_target_pairs={{0,8},{8,0},{16,24},{24,16},{1,9},{9,1},{17,25},{25,17},{2,10},{10... | collective-permute-start | bytes 589832 | tf_op jit(solution)/shard_map/ppermute | solution.py:87
  71.4 5.1 %collective-permute-done.8 = f32[2,3,64,256]{3,2,1,0:T(8,128)S(1)} collective-permute-done((f32[2,3,64,256]{3,2,1,0:T(8,128)S(1)}, f32[2,3,64,256]{3,2,1,0:T(8,128)S(1)}, u32[]{:S(2)}, u32[]{:S(2)}) %collective-permute-start.8) | collective-permute-done | bytes 393248 | tf_op jit(solution)/shard_map/ppermute | solution.py:87
  76.6 3.2 %collective-permute-start.9 = (f32[3,64,256]{2,1,0:T(8,128)S(1)}, f32[3,64,256]{2,1,0:T(8,128)S(1)}, u32[]{:S(2)}, u32[]{:S(2)}) collective-permute-start(f32[3,64,256]{2,1,0:T(8,128)S(1)} %slice_bitcast_fusion.10), channel_id=1, source_target_pairs={{0,8},{8,0},{16,24},{24,16},{1,9},{9,1},{17,25},{25,17},{2,10},{10... | collective-permute-start | bytes 589832 | tf_op jit(solution)/shard_map/ppermute | solution.py:87
  79.8 4.3 %collective-permute-done.20 = f32[2,3,64,256]{3,2,1,0:T(8,128)S(1)} collective-permute-done((f32[2,3,64,256]{3,2,1,0:T(8,128)S(1)}, f32[2,3,64,256]{3,2,1,0:T(8,128)S(1)}, u32[]{:S(2)}, u32[]{:S(2)}) %collective-permute-start.20) | collective-permute-done | bytes 393248 | tf_op jit(solution)/shard_map/ppermute | solution.py:87
  84.3 4.2 %collective-permute-start.16 = (f32[3,64,256]{2,1,0:T(8,128)S(1)}, f32[3,64,256]{2,1,0:T(8,128)S(1)}, u32[]{:S(2)}, u32[]{:S(2)}) collective-permute-start(f32[3,64,256]{2,1,0:T(8,128)S(1)} %fusion.4), channel_id=1, source_target_pairs={{0,16},{8,24},{16,0},{24,8},{1,17},{9,25},{17,1},{25,9},{2,18},{10... | collective-permute-start | bytes 589832 | tf_op jit(solution)/shard_map/ppermute | solution.py:87
  88.5 0.1 collective-permute-start.10
  88.6 13.9 %collective-permute-done.16 = f32[3,64,256]{2,1,0:T(8,128)S(1)} collective-permute-done((f32[3,64,256]{2,1,0:T(8,128)S(1)}, f32[3,64,256]{2,1,0:T(8,128)S(1)}, u32[]{:S(2)}, u32[]{:S(2)}) %collective-permute-start.16) | collective-permute-done | bytes 196640 | tf_op jit(solution)/shard_map/ppermute | solution.py:87
  102.5 0.1 abs_reduce_fusion.1
  102.6 2.9 %collective-permute-done.10 = f32[3,64,256]{2,1,0:T(8,128)S(1)} collective-permute-done((f32[3,64,256]{2,1,0:T(8,128)S(1)}, f32[3,64,256]{2,1,0:T(8,128)S(1)}, u32[]{:S(2)}, u32[]{:S(2)}) %collective-permute-start.10) | collective-permute-done | bytes 196640 | tf_op jit(solution)/shard_map/ppermute | solution.py:87
  105.5 0.1 abs_reduce_fusion.2
  105.6 0.1 fusion.17
  105.7 0.1 clamp_convert_fusion.1
  105.8 0.1 collective-permute-start.17
  105.9 0.1 clamp_convert_fusion.2
  106.0 2.1 %collective-permute-start.11 = (s16[3,64,256]{2,1,0:T(8,128)(2,1)S(1)}, s16[3,64,256]{2,1,0:T(8,128)(2,1)S(1)}, u32[]{:S(2)}, u32[]{:S(2)}) collective-permute-start(s16[3,64,256]{2,1,0:T(8,128)(2,1)S(1)} %clamp_convert_fusion.2), channel_id=1, source_target_pairs={{0,8},{8,0},{16,24},{24,16},{1,9},{9,1},{17,25},{25,17},{2,10},{10... | collective-permute-start | bytes 294920 | tf_op jit(solution)/shard_map/ppermute | solution.py:87
  108.1 0.1 fusion.18
  108.2 3.4 %collective-permute-done.11 = s16[3,64,256]{2,1,0:T(8,128)(2,1)S(1)} collective-permute-done((s16[3,64,256]{2,1,0:T(8,128)(2,1)S(1)}, s16[3,64,256]{2,1,0:T(8,128)(2,1)S(1)}, u32[]{:S(2)}, u32[]{:S(2)}) %collective-permute-start.11) | collective-permute-done | bytes 98336 | tf_op jit(solution)/shard_map/ppermute | solution.py:87
  111.6 1.1 collective-permute-start.21
  112.8 1.6 %collective-permute-start.18 = (s16[2,3,64,256]{3,2,1,0:T(8,128)(2,1)S(1)}, s16[2,3,64,256]{3,2,1,0:T(8,128)(2,1)S(1)}, u32[]{:S(2)}, u32[]{:S(2)}) collective-permute-start(s16[2,3,64,256]{3,2,1,0:T(8,128)(2,1)S(1)} %get-tuple-element.41), channel_id=1, source_target_pairs={{0,4},{4,0},{1,5},{5,1},{2,6},{6,2},{3,7},{7,3},{8,12},{12,8},{9,1... | collective-permute-start | bytes 589832 | tf_op jit(solution)/shard_map/ppermute | solution.py:87
  114.4 0.6 collective-permute-start.12
  115.0 2.3 %collective-permute-done.21 = f32[3,64,256]{2,1,0:T(8,128)S(1)} collective-permute-done((f32[3,64,256]{2,1,0:T(8,128)S(1)}, f32[3,64,256]{2,1,0:T(8,128)S(1)}, u32[]{:S(2)}, u32[]{:S(2)}) %collective-permute-start.21) | collective-permute-done | bytes 196640 | tf_op jit(solution)/shard_map/ppermute | solution.py:87
  117.3 4.9 %collective-permute-done.12 = s16[2,3,64,256]{3,2,1,0:T(8,128)(2,1)S(1)} collective-permute-done((s16[2,3,64,256]{3,2,1,0:T(8,128)(2,1)S(1)}, s16[2,3,64,256]{3,2,1,0:T(8,128)(2,1)S(1)}, u32[]{:S(2)}, u32[]{:S(2)}) %collective-permute-start.12) | collective-permute-done | bytes 196640 | tf_op jit(solution)/shard_map/ppermute | solution.py:87
  122.3 8.5 %collective-permute-done.22 = f32[3,64,256]{2,1,0:T(8,128)S(1)} collective-permute-done((f32[3,64,256]{2,1,0:T(8,128)S(1)}, f32[3,64,256]{2,1,0:T(8,128)S(1)}, u32[]{:S(2)}, u32[]{:S(2)}) %collective-permute-start.22) | collective-permute-done | bytes 196640 | tf_op jit(solution)/shard_map/ppermute | solution.py:87
  130.8 0.1 abs_reduce_fusion
  130.9 0.1 clamp_convert_fusion
  131.0 0.1 collective-permute-start.23
  131.1 4.6 %collective-permute-done.23 = s16[3,64,256]{2,1,0:T(8,128)(2,1)S(1)} collective-permute-done((s16[3,64,256]{2,1,0:T(8,128)(2,1)S(1)}, s16[3,64,256]{2,1,0:T(8,128)(2,1)S(1)}, u32[]{:S(2)}, u32[]{:S(2)}) %collective-permute-start.23) | collective-permute-done | bytes 98336 | tf_op jit(solution)/shard_map/ppermute | solution.py:87
  135.7 0.1 fusion.16
  135.8 3.5 %collective-permute-done.25 = f32[9,64]{1,0:T(8,128)S(1)} collective-permute-done((f32[9,64]{1,0:T(8,128)S(1)}, f32[9,64]{1,0:T(8,128)S(1)}, u32[]{:S(2)}, u32[]{:S(2)}) %collective-permute-start.25) | collective-permute-done | bytes 2336 | tf_op jit(solution)/shard_map/ppermute | solution.py:87
  139.3 1.5 %collective-permute-start.26 = (f32[2,9,64]{2,1,0:T(8,128)S(1)}, f32[2,9,64]{2,1,0:T(8,128)S(1)}, u32[]{:S(2)}, u32[]{:S(2)}) collective-permute-start(f32[2,9,64]{2,1,0:T(8,128)S(1)} %get-tuple-element.45), channel_id=1, source_target_pairs={{0,4},{4,0},{1,5},{5,1},{2,6},{6,2},{3,7},{7,3},{8,12},{12,8},{9,1... | collective-permute-start | bytes 13832 | tf_op jit(solution)/shard_map/ppermute | solution.py:87
  140.9 0.6 collective-permute-start.24
  141.5 1.6 %collective-permute-done.26 = f32[2,9,64]{2,1,0:T(8,128)S(1)} collective-permute-done((f32[2,9,64]{2,1,0:T(8,128)S(1)}, f32[2,9,64]{2,1,0:T(8,128)S(1)}, u32[]{:S(2)}, u32[]{:S(2)}) %collective-permute-start.26) | collective-permute-done | bytes 4640 | tf_op jit(solution)/shard_map/ppermute | solution.py:87
  143.1 0.6 gather_fusion.1
  143.7 0.1 broadcast_select_fusion
  143.7 2.9 %collective-permute-done.24 = s16[2,3,64,256]{3,2,1,0:T(8,128)(2,1)S(1)} collective-permute-done((s16[2,3,64,256]{3,2,1,0:T(8,128)(2,1)S(1)}, s16[2,3,64,256]{3,2,1,0:T(8,128)(2,1)S(1)}, u32[]{:S(2)}, u32[]{:S(2)}) %collective-permute-start.24) | collective-permute-done | bytes 196640 | tf_op jit(solution)/shard_map/ppermute | solution.py:87
  146.7 0.1 pad_add_fusion
  146.8 0.6 gather_fusion
  147.5 1.0 convert_multiply_fusion
  (44 shorter events, 0.7 us)
Async XLA Ops:
  1.5 19.9 %collective-permute-start = (bf16[3,256,256]{2,1,0:T(8,128)(2,1)S(1)}, bf16[3,256,256]{2,1,0:T(8,128)(2,1)S(1)}, u32[]{:S(2)}, u32[]{:S(2)}) collective-permute-start(bf16[3,256,256]{2,1,0:T(8,128)(2,1)S(1)} %get-tuple-element.35), channel_id=1, source_target_pairs={{0,8},{8,0},{16,24},{24,16},{1,9},{9,1},{17,25},{25,17},{2,10},{10... | collective-permute-start | bytes 1179656 | tf_op jit(solution)/shard_map/ppermute | solution.py:87
  4.6 29.8 %collective-permute-start.1 = (bf16[3,256,256]{2,1,0:T(8,128)(2,1)S(1)}, bf16[3,256,256]{2,1,0:T(8,128)(2,1)S(1)}, u32[]{:S(2)}, u32[]{:S(2)}) collective-permute-start(bf16[3,256,256]{2,1,0:T(8,128)(2,1)S(1)} %get-tuple-element.37), channel_id=1, source_target_pairs={{0,16},{8,24},{16,0},{24,8},{1,17},{9,25},{17,1},{25,9},{2,18},{10... | collective-permute-start | bytes 1179656 | tf_op jit(solution)/shard_map/ppermute | solution.py:87
  7.2 28.7 %collective-permute-start.2 = (bf16[3,256,256]{2,1,0:T(8,128)(2,1)S(1)}, bf16[3,256,256]{2,1,0:T(8,128)(2,1)S(1)}, u32[]{:S(2)}, u32[]{:S(2)}) collective-permute-start(bf16[3,256,256]{2,1,0:T(8,128)(2,1)S(1)} %get-tuple-element.34), channel_id=1, source_target_pairs={{0,24},{8,16},{16,8},{24,0},{1,25},{9,17},{17,9},{25,1},{2,26},{10... | collective-permute-start | bytes 1179656 | tf_op jit(solution)/shard_map/ppermute | solution.py:87
  7.2 30.0 %collective-permute-start.3 = (bf16[3,256,256]{2,1,0:T(8,128)(2,1)S(1)}, bf16[3,256,256]{2,1,0:T(8,128)(2,1)S(1)}, u32[]{:S(2)}, u32[]{:S(2)}) collective-permute-start(bf16[3,256,256]{2,1,0:T(8,128)(2,1)S(1)} %get-tuple-element.36.refs_0_), channel_id=1, source_target_pairs={{0,4},{4,0},{1,5},{5,1},{2,6},{6,2},{3,7},{7,3},{8,12},{12,8},{9,1... | collective-permute-start | bytes 1179656 | tf_op jit(solution)/shard_map/ppermute | solution.py:87
  21.3 15.8 %collective-permute-start.4 = (bf16[3,256,256]{2,1,0:T(8,128)(2,1)S(1)}, bf16[3,256,256]{2,1,0:T(8,128)(2,1)S(1)}, u32[]{:S(2)}, u32[]{:S(2)}) collective-permute-start(bf16[3,256,256]{2,1,0:T(8,128)(2,1)S(1)} %collective-permute-done.refs_1_), channel_id=1, source_target_pairs={{0,4},{4,0},{1,5},{5,1},{2,6},{6,2},{3,7},{7,3},{8,12},{12,8},{9,1... | collective-permute-start | bytes 1179656 | tf_op jit(solution)/shard_map/ppermute | solution.py:87
  34.4 9.9 %collective-permute-start.5 = (bf16[3,256,256]{2,1,0:T(8,128)(2,1)S(1)}, bf16[3,256,256]{2,1,0:T(8,128)(2,1)S(1)}, u32[]{:S(2)}, u32[]{:S(2)}) collective-permute-start(bf16[3,256,256]{2,1,0:T(8,128)(2,1)S(1)} %collective-permute-done.1.refs_2_), channel_id=1, source_target_pairs={{0,4},{4,0},{1,5},{5,1},{2,6},{6,2},{3,7},{7,3},{8,12},{12,8},{9,1... | collective-permute-start | bytes 1179656 | tf_op jit(solution)/shard_map/ppermute | solution.py:87
  35.9 12.6 %collective-permute-start.6 = (bf16[3,256,256]{2,1,0:T(8,128)(2,1)S(1)}, bf16[3,256,256]{2,1,0:T(8,128)(2,1)S(1)}, u32[]{:S(2)}, u32[]{:S(2)}) collective-permute-start(bf16[3,256,256]{2,1,0:T(8,128)(2,1)S(1)} %collective-permute-done.2.refs_3_), channel_id=1, source_target_pairs={{0,4},{4,0},{1,5},{5,1},{2,6},{6,2},{3,7},{7,3},{8,12},{12,8},{9,1... | collective-permute-start | bytes 1179656 | tf_op jit(solution)/shard_map/ppermute | solution.py:87
  50.5 3.2 %copy-start = (s32[1,10,2]{1,2,0:T(2,128)S(1)}, s32[1,10,2]{1,2,0:T(2,128)}, u32[]{:S(2)}) copy-start(s32[1,10,2]{1,2,0:T(2,128)} %param.4) | copy-start | bytes 244
  53.6 2.4 %collective-permute-start.13 = (f32[2,2,3,64,256]{4,3,2,1,0:T(8,128)S(1)}, f32[2,2,3,64,256]{4,3,2,1,0:T(8,128)S(1)}, u32[]{:S(2)}, u32[]{:S(2)}) collective-permute-start(f32[2,2,3,64,256]{4,3,2,1,0:T(8,128)S(1)} %get-tuple-element.20), channel_id=1, source_target_pairs={{0,1},{1,0},{2,3},{3,2},{4,5},{5,4},{6,7},{7,6},{8,9},{9,8},{10,11... | collective-permute-start | bytes 2359304 | tf_op jit(solution)/shard_map/ppermute | solution.py:87
  53.7 3.8 %collective-permute-start.7 = (f32[2,2,3,64,256]{4,3,2,1,0:T(8,128)S(1)}, f32[2,2,3,64,256]{4,3,2,1,0:T(8,128)S(1)}, u32[]{:S(2)}, u32[]{:S(2)}) collective-permute-start(f32[2,2,3,64,256]{4,3,2,1,0:T(8,128)S(1)} %get-tuple-element.17), channel_id=1, source_target_pairs={{0,1},{1,0},{2,3},{3,2},{4,5},{5,4},{6,7},{7,6},{8,9},{9,8},{10,11... | collective-permute-start | bytes 2359304 | tf_op jit(solution)/shard_map/ppermute | solution.py:87
  54.3 4.3 %collective-permute-start.19 = (f32[2,2,3,64,256]{4,3,2,1,0:T(8,128)S(1)}, f32[2,2,3,64,256]{4,3,2,1,0:T(8,128)S(1)}, u32[]{:S(2)}, u32[]{:S(2)}) collective-permute-start(f32[2,2,3,64,256]{4,3,2,1,0:T(8,128)S(1)} %get-tuple-element.22), channel_id=1, source_target_pairs={{0,1},{1,0},{2,3},{3,2},{4,5},{5,4},{6,7},{7,6},{8,9},{9,8},{10,11... | collective-permute-start | bytes 2359304 | tf_op jit(solution)/shard_map/ppermute | solution.py:87
  56.1 12.0 %collective-permute-start.14 = (f32[2,3,64,256]{3,2,1,0:T(8,128)S(1)}, f32[2,3,64,256]{3,2,1,0:T(8,128)S(1)}, u32[]{:S(2)}, u32[]{:S(2)}) collective-permute-start(f32[2,3,64,256]{3,2,1,0:T(8,128)S(1)} %slice_bitcast_fusion.2), channel_id=1, source_target_pairs={{0,2},{2,0},{1,3},{3,1},{4,6},{6,4},{5,7},{7,5},{8,10},{10,8},{9,1... | collective-permute-start | bytes 1179656 | tf_op jit(solution)/shard_map/ppermute | solution.py:87
  57.6 18.9 %collective-permute-start.8 = (f32[2,3,64,256]{3,2,1,0:T(8,128)S(1)}, f32[2,3,64,256]{3,2,1,0:T(8,128)S(1)}, u32[]{:S(2)}, u32[]{:S(2)}) collective-permute-start(f32[2,3,64,256]{3,2,1,0:T(8,128)S(1)} %slice_bitcast_fusion.4), channel_id=1, source_target_pairs={{0,2},{2,0},{1,3},{3,1},{4,6},{6,4},{5,7},{7,5},{8,10},{10,8},{9,1... | collective-permute-start | bytes 1179656 | tf_op jit(solution)/shard_map/ppermute | solution.py:87
  58.8 25.4 %collective-permute-start.20 = (f32[2,3,64,256]{3,2,1,0:T(8,128)S(1)}, f32[2,3,64,256]{3,2,1,0:T(8,128)S(1)}, u32[]{:S(2)}, u32[]{:S(2)}) collective-permute-start(f32[2,3,64,256]{3,2,1,0:T(8,128)S(1)} %slice_bitcast_fusion), channel_id=1, source_target_pairs={{0,2},{2,0},{1,3},{3,1},{4,6},{6,4},{5,7},{7,5},{8,10},{10,8},{9,1... | collective-permute-start | bytes 1179656 | tf_op jit(solution)/shard_map/ppermute | solution.py:87
  68.2 16.1 %collective-permute-start.15 = (f32[3,64,256]{2,1,0:T(8,128)S(1)}, f32[3,64,256]{2,1,0:T(8,128)S(1)}, u32[]{:S(2)}, u32[]{:S(2)}) collective-permute-start(f32[3,64,256]{2,1,0:T(8,128)S(1)} %slice_bitcast_fusion.8), channel_id=1, source_target_pairs={{0,8},{8,0},{16,24},{24,16},{1,9},{9,1},{17,25},{25,17},{2,10},{10... | collective-permute-start | bytes 589832 | tf_op jit(solution)/shard_map/ppermute | solution.py:87
  76.6 11.9 %collective-permute-start.9 = (f32[3,64,256]{2,1,0:T(8,128)S(1)}, f32[3,64,256]{2,1,0:T(8,128)S(1)}, u32[]{:S(2)}, u32[]{:S(2)}) collective-permute-start(f32[3,64,256]{2,1,0:T(8,128)S(1)} %slice_bitcast_fusion.10), channel_id=1, source_target_pairs={{0,8},{8,0},{16,24},{24,16},{1,9},{9,1},{17,25},{25,17},{2,10},{10... | collective-permute-start | bytes 589832 | tf_op jit(solution)/shard_map/ppermute | solution.py:87
  84.3 18.2 %collective-permute-start.16 = (f32[3,64,256]{2,1,0:T(8,128)S(1)}, f32[3,64,256]{2,1,0:T(8,128)S(1)}, u32[]{:S(2)}, u32[]{:S(2)}) collective-permute-start(f32[3,64,256]{2,1,0:T(8,128)S(1)} %fusion.4), channel_id=1, source_target_pairs={{0,16},{8,24},{16,0},{24,8},{1,17},{9,25},{17,1},{25,9},{2,18},{10... | collective-permute-start | bytes 589832 | tf_op jit(solution)/shard_map/ppermute | solution.py:87
  88.5 17.0 %collective-permute-start.10 = (f32[3,64,256]{2,1,0:T(8,128)S(1)}, f32[3,64,256]{2,1,0:T(8,128)S(1)}, u32[]{:S(2)}, u32[]{:S(2)}) collective-permute-start(f32[3,64,256]{2,1,0:T(8,128)S(1)} %fusion.5), channel_id=1, source_target_pairs={{0,16},{8,24},{16,0},{24,8},{1,17},{9,25},{17,1},{25,9},{2,18},{10... | collective-permute-start | bytes 589832 | tf_op jit(solution)/shard_map/ppermute | solution.py:87
  105.8 6.9 %collective-permute-start.17 = (s16[3,64,256]{2,1,0:T(8,128)(2,1)S(1)}, s16[3,64,256]{2,1,0:T(8,128)(2,1)S(1)}, u32[]{:S(2)}, u32[]{:S(2)}) collective-permute-start(s16[3,64,256]{2,1,0:T(8,128)(2,1)S(1)} %clamp_convert_fusion.1), channel_id=1, source_target_pairs={{0,8},{8,0},{16,24},{24,16},{1,9},{9,1},{17,25},{25,17},{2,10},{10... | collective-permute-start | bytes 294920 | tf_op jit(solution)/shard_map/ppermute | solution.py:87
  106.0 5.6 %collective-permute-start.11 = (s16[3,64,256]{2,1,0:T(8,128)(2,1)S(1)}, s16[3,64,256]{2,1,0:T(8,128)(2,1)S(1)}, u32[]{:S(2)}, u32[]{:S(2)}) collective-permute-start(s16[3,64,256]{2,1,0:T(8,128)(2,1)S(1)} %clamp_convert_fusion.2), channel_id=1, source_target_pairs={{0,8},{8,0},{16,24},{24,16},{1,9},{9,1},{17,25},{25,17},{2,10},{10... | collective-permute-start | bytes 294920 | tf_op jit(solution)/shard_map/ppermute | solution.py:87
  111.6 5.7 %collective-permute-start.21 = (f32[3,64,256]{2,1,0:T(8,128)S(1)}, f32[3,64,256]{2,1,0:T(8,128)S(1)}, u32[]{:S(2)}, u32[]{:S(2)}) collective-permute-start(f32[3,64,256]{2,1,0:T(8,128)S(1)} %slice_bitcast_fusion.6), channel_id=1, source_target_pairs={{0,8},{8,0},{16,24},{24,16},{1,9},{9,1},{17,25},{25,17},{2,10},{10... | collective-permute-start | bytes 589832 | tf_op jit(solution)/shard_map/ppermute | solution.py:87
  112.8 9.5 %collective-permute-start.18 = (s16[2,3,64,256]{3,2,1,0:T(8,128)(2,1)S(1)}, s16[2,3,64,256]{3,2,1,0:T(8,128)(2,1)S(1)}, u32[]{:S(2)}, u32[]{:S(2)}) collective-permute-start(s16[2,3,64,256]{3,2,1,0:T(8,128)(2,1)S(1)} %get-tuple-element.41), channel_id=1, source_target_pairs={{0,4},{4,0},{1,5},{5,1},{2,6},{6,2},{3,7},{7,3},{8,12},{12,8},{9,1... | collective-permute-start | bytes 589832 | tf_op jit(solution)/shard_map/ppermute | solution.py:87
  114.4 7.8 %collective-permute-start.12 = (s16[2,3,64,256]{3,2,1,0:T(8,128)(2,1)S(1)}, s16[2,3,64,256]{3,2,1,0:T(8,128)(2,1)S(1)}, u32[]{:S(2)}, u32[]{:S(2)}) collective-permute-start(s16[2,3,64,256]{3,2,1,0:T(8,128)(2,1)S(1)} %get-tuple-element.39), channel_id=1, source_target_pairs={{0,4},{4,0},{1,5},{5,1},{2,6},{6,2},{3,7},{7,3},{8,12},{12,8},{9,1... | collective-permute-start | bytes 589832 | tf_op jit(solution)/shard_map/ppermute | solution.py:87
  122.2 8.5 %collective-permute-start.22 = (f32[3,64,256]{2,1,0:T(8,128)S(1)}, f32[3,64,256]{2,1,0:T(8,128)S(1)}, u32[]{:S(2)}, u32[]{:S(2)}) collective-permute-start(f32[3,64,256]{2,1,0:T(8,128)S(1)} %fusion.3), channel_id=1, source_target_pairs={{0,16},{8,24},{16,0},{24,8},{1,17},{9,25},{17,1},{25,9},{2,18},{10... | collective-permute-start | bytes 589832 | tf_op jit(solution)/shard_map/ppermute | solution.py:87
  131.0 4.7 %collective-permute-start.23 = (s16[3,64,256]{2,1,0:T(8,128)(2,1)S(1)}, s16[3,64,256]{2,1,0:T(8,128)(2,1)S(1)}, u32[]{:S(2)}, u32[]{:S(2)}) collective-permute-start(s16[3,64,256]{2,1,0:T(8,128)(2,1)S(1)} %clamp_convert_fusion), channel_id=1, source_target_pairs={{0,8},{8,0},{16,24},{24,16},{1,9},{9,1},{17,25},{25,17},{2,10},{10... | collective-permute-start | bytes 294920 | tf_op jit(solution)/shard_map/ppermute | solution.py:87
  135.7 3.7 %collective-permute-start.25 = (f32[9,64]{1,0:T(8,128)S(1)}, f32[9,64]{1,0:T(8,128)S(1)}, u32[]{:S(2)}, u32[]{:S(2)}) collective-permute-start(f32[9,64]{1,0:T(8,128)S(1)} %pad_maximum_fusion.2), channel_id=1, source_target_pairs={{0,8},{8,0},{16,24},{24,16},{1,9},{9,1},{17,25},{25,17},{2,10},{10... | collective-permute-start | bytes 6920 | tf_op jit(solution)/shard_map/ppermute | solution.py:87
  139.3 3.7 %collective-permute-start.26 = (f32[2,9,64]{2,1,0:T(8,128)S(1)}, f32[2,9,64]{2,1,0:T(8,128)S(1)}, u32[]{:S(2)}, u32[]{:S(2)}) collective-permute-start(f32[2,9,64]{2,1,0:T(8,128)S(1)} %get-tuple-element.45), channel_id=1, source_target_pairs={{0,4},{4,0},{1,5},{5,1},{2,6},{6,2},{3,7},{7,3},{8,12},{12,8},{9,1... | collective-permute-start | bytes 13832 | tf_op jit(solution)/shard_map/ppermute | solution.py:87
  140.9 5.7 %collective-permute-start.24 = (s16[2,3,64,256]{3,2,1,0:T(8,128)(2,1)S(1)}, s16[2,3,64,256]{3,2,1,0:T(8,128)(2,1)S(1)}, u32[]{:S(2)}, u32[]{:S(2)}) collective-permute-start(s16[2,3,64,256]{3,2,1,0:T(8,128)(2,1)S(1)} %get-tuple-element.43), channel_id=1, source_target_pairs={{0,4},{4,0},{1,5},{5,1},{2,6},{6,2},{3,7},{7,3},{8,12},{12,8},{9,1... | collective-permute-start | bytes 589832 | tf_op jit(solution)/shard_map/ppermute | solution.py:87

commit v7 on v6

--- a/solution.py
+++ b/solution.py
@@ -11,6 +11,7 @@
 
 VMEM_LIMIT = 24 * 2**20
 GROUPS = 3
+ORDER = ((0, 0), (1, 0), (0, 1), (1, 1), (2, 0), (0, 2), (1, 2), (2, 1), (2, 2))
 CODE_TOP = 32767.0
 
 
@@ -70,6 +71,24 @@
 
 def second_kernel(first_pair, scalars, blocks, *outs):
     multiply_groups(scalars, first_pair, blocks, outs)
+
+
+def split_sum_kernel(left, right, *outs):
+    for index, out in enumerate(outs):
+        out[...] = left[index] + right[index]
+
+
+def sum_kernel(left, right, out):
+    out[...] = left[...] + right[...]
+
+
+def code_kernel(scale_factor, left, right, code, scale):
+    total = left[...] + right[...]
+    top = jnp.max(jnp.abs(total), axis=2, keepdims=True)
+    factor = jnp.where(top > 0, CODE_TOP / top, 0.0)
+    rounded = jnp.clip(jnp.round(total * factor), -CODE_TOP, CODE_TOP)
+    code[...] = rounded.astype(jnp.int32).astype(jnp.int16)
+    scale[...] = jnp.max(jnp.abs(total), axis=2) * (scale_factor / CODE_TOP)
 
 
 def per_device(z_count, y_count, x_count, core_count, snapshots, tile_table):
@@ -154,42 +173,70 @@
         "tiles_second",
     )
 
-    def after(value, earlier):
-        return lax.optimization_barrier((value, earlier))[0]
-
-    groups = len(sizes)
-    low_arrived, y_arrived = [], []
-    codes, scales = [], []
-    for index, (keep, send) in enumerate(zip(sums[::2], sums[1::2])):
-        total = keep + swap(send, "core", 1)
-        held = total[0]
-        for step in range(1, x_count):
-            held = held + swap(total[step], "x", step)
-        away, held = held[1], held[0]
-        if index >= 2:
-            away = after(away, low_arrived[index - 2])
-        held = held + swap(away, "z", 1)
-        if index >= 2:
-            held = after(held, y_arrived[index - 2])
+    last = []
+
+    def step_call(kernel, out_shape, *operands, name):
+        operands = lax.optimization_barrier((*operands, *last))[: len(operands)]
+        vmem = pl.BlockSpec(memory_space=pltpu.VMEM)
+        outs = pl.pallas_call(
+            kernel,
+            out_shape=out_shape,
+            in_specs=[vmem] * len(operands),
+            out_specs=[vmem] * len(out_shape),
+            compiler_params=pltpu.CompilerParams(vmem_limit_bytes=VMEM_LIMIT),
+            name=name,
+        )(*operands)
+        last[:] = outs[:1]
+        return outs
+
+    def float_shape(*shape):
+        return jax.ShapeDtypeStruct((*shape, rows_dev, block_size), jnp.float32)
+
+    def sum_core(index):
+        keep, send = sums[2 * index], swap(sums[2 * index + 1], "core", 1)
+        shapes = [float_shape(2, sizes[index])] * x_count
+        mine, *away = step_call(split_sum_kernel, shapes, keep, send, name="sum_core")
+        return mine, [swap(value, "x", step + 1) for step, value in enumerate(away)]
+
+    def sum_x(index, mine, arrived):
+        for value in arrived[:-1]:
+            (mine,) = step_call(
+                sum_kernel, [float_shape(2, sizes[index])], mine, value, name="sum_x"
+            )
+        shapes = [float_shape(sizes[index])] * 2
+        mine, away = step_call(split_sum_kernel, shapes, mine, arrived[-1], name="sum_x")
+        return mine, swap(away, "z", 1)
+
+    def sum_low(index, mine, arrived):
+        (mine,) = step_call(sum_kernel, [float_shape(sizes[index])], mine, arrived, name="sum_z")
         bits = 2
-        while bits < z_count:
-            held = held + swap(held, "z", bits)
+        while 2 * bits < z_count:
+            (mine,) = step_call(
+                sum_kernel, [float_shape(sizes[index])], mine, swap(mine, "z", bits), name="sum_z"
+            )
             bits *= 2
-        if index == groups - 1:
-            held = after(held, y_arrived[index - 1])
-        top = jnp.max(jnp.abs(held), axis=2)
-        factor = jnp.where(top > 0, CODE_TOP / top, 0.0)
-        code = jnp.round(held * factor[:, :, None])
-        code = jnp.clip(code, -CODE_TOP, CODE_TOP).astype(jnp.int16)
-        low_arrived.append(swap(code, "z", 1))
-        pair = jnp.stack([code, low_arrived[-1]])
-        y_arrived.append(swap(pair, "y", 1))
-        codes.append(jnp.stack([pair, y_arrived[-1]]).reshape(-1, rows_dev, block_size))
-        scales.append(top * (scale_factor / CODE_TOP))
-    codes = jnp.concatenate(codes)
-    scales = after(jnp.concatenate(scales), low_arrived[-1])
-    scales = jnp.stack([scales, swap(scales, "z", 1)])
-    scales = jnp.stack([scales, swap(scales, "y", 1)])
+        return mine, swap(mine, "z", bits)
+
+    def sum_high(index, mine, arrived):
+        shapes = [
+            jax.ShapeDtypeStruct((sizes[index], rows_dev, block_size), jnp.int16),
+            jax.ShapeDtypeStruct((sizes[index], rows_dev), jnp.float32),
+        ]
+        kernel = functools.partial(code_kernel, scale_factor)
+        code, scale = step_call(kernel, shapes, mine, arrived, name="finish")
+        return to_owners(code), scale
+
+    def to_owners(value):
+        both = [(i, i ^ (y_count + 1)) for i in range(block_count)]
+        over_both = lax.ppermute(value, ("z", "y"), both)
+        return [value, swap(value, "z", 1), swap(value, "y", 1), over_both]
+
+    stages = [sum_x, sum_low, sum_high]
+    state = [sum_core(index) for index in range(len(sizes))]
+    for stage, index in ORDER:
+        state[index] = stages[stage](index, *state[index])
+    codes = jnp.concatenate([part for parts, _ in state for part in parts])
+    scales = jnp.concatenate(to_owners(jnp.concatenate([scale for _, scale in state])))
 
     table = tile_table[0]
     row_block = table[:, 0]
@@ -204,7 +251,7 @@
     for start, size in zip(starts, sizes):
         here = 4 * int(start) + off * size + slot - int(start)
         place = jnp.where((slot >= int(start)) & (slot < int(start) + size), here, place)
-    scale = scales.reshape(-1, rows_dev)[off * quarter + slot]
+    scale = scales[off * quarter + slot]
     scale = jnp.where(valid[:, None], scale, 0.0)
     result = codes[place].astype(jnp.float32) * scale[:, :, None]
     return result[None]

time: 149 us -> 126 us (0.85)
  waiting for transfers between devices: 103 us -> 72.5 us
  starting transfers between devices: 33.7 us -> 42.2 us
  other arithmetic: 2.93 us -> 1.15 us
    ppermute x27, waiting for transfers between devices: 103 us -> 61.7 us  [swap(): return lax.ppermute(value, axis, [(i, i ^ bits) for i in range(size)])]
    ppermute x0 -> x4, waiting for transfers between devices: none -> 10.8 us  [to_owners(): over_both = lax.ppermute(value, ('z', 'y'), both)]
    ppermute x0 -> x4, starting transfers between devices: none -> 5.18 us  [to_owners(): over_both = lax.ppermute(value, ('z', 'y'), both)]
    ppermute x27, starting transfers between devices: 33.7 us -> 37 us  [swap(): return lax.ppermute(value, axis, [(i, i ^ bits) for i in range(size)])]
  transfers between devices with their start and end apart: 27 -> 31, of which waited for: 18 -> 17; matrix products, arithmetic and copies ran while one was open for 2% -> 2% of each run, Pallas kernels for 0% -> 3%
where the time goes in v7:
time: 126 us
  waiting for transfers between devices  72.5 us (58%)
  starting transfers between devices  42.2 us (33%)
  Pallas kernels  5.93 us (5%)
  local copies, waits for them, and re-layouts  4 us (3%)
    ppermute x27, waiting for transfers between devices, swap(): return lax.ppermute(value, axis, [(i, i ^ bits) for i in range(size)])  61.7 us
    ppermute x27, starting transfers between devices, swap(): return lax.ppermute(value, axis, [(i, i ^ bits) for i in range(size)])  37 us
    ppermute x4, waiting for transfers between devices, to_owners(): over_both = lax.ppermute(value, ('z', 'y'), both)  10.8 us
    ppermute x4, starting transfers between devices, to_owners(): over_both = lax.ppermute(value, ('z', 'y'), both)  5.18 us
    pallas_call x2, Pallas kernels, call(): pl.pallas_call(kernel, out_shape=out_shape, in_specs=[pl.BlockSpec(memory...  5.06 us
  transfers between devices with their start and end apart: 31, of which 17 were waited for; matrix products, arithmetic and copies ran while one was open for 2% of the time, Pallas kernels for 3%

profile of v7, /device:TPU:0, one launch (start us, length us, event | category | flops | bytes accessed | tf_op | source)
XLA Modules:
  0.0 125.9 jit_solution(2309048503199669375)
XLA Ops:
  0.0 1.5 %constant_dynamic-slice_fusion = (bf16[3,256,256]{2,1,0:T(8,128)(2,1)S(1)}, bf16[3,256,256]{2,1,0:T(8,128)(2,1)S(1)}, bf16[3,256,256]{2,1,0:T(8,128)(2,1)S(1)}, bf16[3,256,256]{2,1,0:T(8,128)(2,1)S(1)}) fusion(bf16[3,256,1024]{2,1,0:T(8,128)(2,1)} %param.3, s32[]{:T(128)S(6)} %select_n.80, s32[]{:T(128)S(6)} %select_n.78, s32[]{:T(128)S(6)} %select_n.77, ...), kind=kLoop, calls=%fused_computation.30 | loop fusion | bytes 3145744 | tf_op jit(solution)/shard_map/dynamic_slice | solution.py:129
  1.5 3.1 %collective-permute-start = (bf16[3,256,256]{2,1,0:T(8,128)(2,1)S(1)}, bf16[3,256,256]{2,1,0:T(8,128)(2,1)S(1)}, u32[]{:S(2)}, u32[]{:S(2)}) collective-permute-start(bf16[3,256,256]{2,1,0:T(8,128)(2,1)S(1)} %get-tuple-element.107), channel_id=1, source_target_pairs={{0,8},{8,0},{16,24},{24,16},{1,9},{9,1},{17,25},{25,17},{2,10},{10... | collective-permute-start | bytes 1179656 | tf_op jit(solution)/shard_map/ppermute | solution.py:106
  4.6 2.6 %collective-permute-start.1 = (bf16[3,256,256]{2,1,0:T(8,128)(2,1)S(1)}, bf16[3,256,256]{2,1,0:T(8,128)(2,1)S(1)}, u32[]{:S(2)}, u32[]{:S(2)}) collective-permute-start(bf16[3,256,256]{2,1,0:T(8,128)(2,1)S(1)} %get-tuple-element.109), channel_id=1, source_target_pairs={{0,16},{8,24},{16,0},{24,8},{1,17},{9,25},{17,1},{25,9},{2,18},{10... | collective-permute-start | bytes 1179656 | tf_op jit(solution)/shard_map/ppermute | solution.py:106
  7.2 1.7 %collective-permute-start.3 = (bf16[3,256,256]{2,1,0:T(8,128)(2,1)S(1)}, bf16[3,256,256]{2,1,0:T(8,128)(2,1)S(1)}, u32[]{:S(2)}, u32[]{:S(2)}) collective-permute-start(bf16[3,256,256]{2,1,0:T(8,128)(2,1)S(1)} %get-tuple-element.108.refs_0_), channel_id=1, source_target_pairs={{0,4},{4,0},{1,5},{5,1},{2,6},{6,2},{3,7},{7,3},{8,12},{12,8},{9,1... | collective-permute-start | bytes 1179656 | tf_op jit(solution)/shard_map/ppermute | solution.py:106
  8.9 12.4 %collective-permute-done.refs_1_ = bf16[3,256,256]{2,1,0:T(8,128)(2,1)S(1)} collective-permute-done((bf16[3,256,256]{2,1,0:T(8,128)(2,1)S(1)}, bf16[3,256,256]{2,1,0:T(8,128)(2,1)S(1)}, u32[]{:S(2)}, u32[]{:S(2)}) %collective-permute-start) | collective-permute-done | bytes 393248 | tf_op jit(solution)/shard_map/ppermute | solution.py:106
  21.3 1.7 %collective-permute-start.4 = (bf16[3,256,256]{2,1,0:T(8,128)(2,1)S(1)}, bf16[3,256,256]{2,1,0:T(8,128)(2,1)S(1)}, u32[]{:S(2)}, u32[]{:S(2)}) collective-permute-start(bf16[3,256,256]{2,1,0:T(8,128)(2,1)S(1)} %collective-permute-done.refs_1_), channel_id=1, source_target_pairs={{0,4},{4,0},{1,5},{5,1},{2,6},{6,2},{3,7},{7,3},{8,12},{12,8},{9,1... | collective-permute-start | bytes 1179656 | tf_op jit(solution)/shard_map/ppermute | solution.py:106
  23.0 11.3 %collective-permute-done.1.refs_2_ = bf16[3,256,256]{2,1,0:T(8,128)(2,1)S(1)} collective-permute-done((bf16[3,256,256]{2,1,0:T(8,128)(2,1)S(1)}, bf16[3,256,256]{2,1,0:T(8,128)(2,1)S(1)}, u32[]{:S(2)}, u32[]{:S(2)}) %collective-permute-start.1) | collective-permute-done | bytes 393248 | tf_op jit(solution)/shard_map/ppermute | solution.py:106
  34.4 1.5 %collective-permute-start.5 = (bf16[3,256,256]{2,1,0:T(8,128)(2,1)S(1)}, bf16[3,256,256]{2,1,0:T(8,128)(2,1)S(1)}, u32[]{:S(2)}, u32[]{:S(2)}) collective-permute-start(bf16[3,256,256]{2,1,0:T(8,128)(2,1)S(1)} %collective-permute-done.1.refs_2_), channel_id=1, source_target_pairs={{0,4},{4,0},{1,5},{5,1},{2,6},{6,2},{3,7},{7,3},{8,12},{12,8},{9,1... | collective-permute-start | bytes 1179656 | tf_op jit(solution)/shard_map/ppermute | solution.py:106
  35.9 0.5 collective-permute-start.6
  36.4 0.7 fusion
  37.1 0.1 concatenate.13.scalars
  37.2 7.1 %collective-permute-done.5.refs_6_ = bf16[3,256,256]{2,1,0:T(8,128)(2,1)S(1)} collective-permute-done((bf16[3,256,256]{2,1,0:T(8,128)(2,1)S(1)}, bf16[3,256,256]{2,1,0:T(8,128)(2,1)S(1)}, u32[]{:S(2)}, u32[]{:S(2)}) %collective-permute-start.5) | collective-permute-done | bytes 393248 | tf_op jit(solution)/shard_map/ppermute | solution.py:106
  44.3 4.2 %collective-permute-done.6.refs_7_ = bf16[3,256,256]{2,1,0:T(8,128)(2,1)S(1)} collective-permute-done((bf16[3,256,256]{2,1,0:T(8,128)(2,1)S(1)}, bf16[3,256,256]{2,1,0:T(8,128)(2,1)S(1)}, u32[]{:S(2)}, u32[]{:S(2)}) %collective-permute-start.6) | collective-permute-done | bytes 393248 | tf_op jit(solution)/shard_map/ppermute | solution.py:106
  48.5 2.0 %tiles_first.1 = (bf16[8,256,768]{2,1,0:T(8,128)(2,1)S(1)}, f32[2,2,3,64,256]{4,3,2,1,0:T(8,128)S(1)}, f32[2,2,3,64,256]{4,3,2,1,0:T(8,128)S(1)}) custom-call(s32[40]{0:T(128)S(1)} %concatenate.13.scalars, bf16[3,256,256]{2,1,0:T(8,128)(2,1)S(1)} %get-tuple-element.108.refs_0_, bf16[3,256,256]{2,1,0:T(8,128)(2,1)S(1)} %collective-permute-done.refs_1_, ...), custom_call_target="tpu_custom_call" | custom-call | flops 603979776 | bytes 4194304 | tf_op jit(solution)/shard_map/tiles_first/pallas_call | solution.py:143
  50.5 0.1 collective-permute-start.7
  50.6 3.1 %tiles_second.1 = (f32[2,2,3,64,256]{4,3,2,1,0:T(8,128)S(1)}, f32[2,2,3,64,256]{4,3,2,1,0:T(8,128)S(1)}, f32[2,2,3,64,256]{4,3,2,1,0:T(8,128)S(1)}, f32[2,2,3,64,256]{4,3,2,1,0:T(8,128)S(1)}) custom-call(s32[40]{0:T(128)S(1)} %concatenate.13.scalars, bf16[8,256,768]{2,1,0:T(8,128)(2,1)S(1)} %get-tuple-element.60.blocks), custom_call_target="tpu_custom_call" | custom-call | flops 1207959552 | bytes 4194304 | tf_op jit(solution)/shard_map/tiles_second/pallas_call | solution.py:143
  53.7 0.6 collective-permute-start.10
  54.2 0.1 collective-permute-start.9
  54.3 0.1 sum_core.3
  54.4 1.4 %collective-permute-start.8 = (f32[2,3,64,256]{3,2,1,0:T(8,128)S(1)}, f32[2,3,64,256]{3,2,1,0:T(8,128)S(1)}, u32[]{:S(2)}, u32[]{:S(2)}) collective-permute-start(f32[2,3,64,256]{3,2,1,0:T(8,128)S(1)} %get-tuple-element.59), channel_id=1, source_target_pairs={{0,2},{2,0},{1,3},{3,1},{4,6},{6,4},{5,7},{7,5},{8,10},{10,8},{9,1... | collective-permute-start | bytes 1179656 | tf_op jit(solution)/shard_map/ppermute | solution.py:106
  55.8 0.3 collective-permute-done.10.right
  56.1 0.1 sum_core.4
  56.2 1.4 %collective-permute-start.13 = (f32[2,3,64,256]{3,2,1,0:T(8,128)S(1)}, f32[2,3,64,256]{3,2,1,0:T(8,128)S(1)}, u32[]{:S(2)}, u32[]{:S(2)}) collective-permute-start(f32[2,3,64,256]{3,2,1,0:T(8,128)S(1)} %get-tuple-element.77), channel_id=1, source_target_pairs={{0,2},{2,0},{1,3},{3,1},{4,6},{6,4},{5,7},{7,5},{8,10},{10,8},{9,1... | collective-permute-start | bytes 1179656 | tf_op jit(solution)/shard_map/ppermute | solution.py:106
  57.7 0.1 sum_core.5
  57.8 1.0 collective-permute-start.19
  58.8 7.6 %collective-permute-done.8.right = f32[2,3,64,256]{3,2,1,0:T(8,128)S(1)} collective-permute-done((f32[2,3,64,256]{3,2,1,0:T(8,128)S(1)}, f32[2,3,64,256]{3,2,1,0:T(8,128)S(1)}, u32[]{:S(2)}, u32[]{:S(2)}) %collective-permute-start.8) | collective-permute-done | bytes 393248 | tf_op jit(solution)/shard_map/ppermute | solution.py:106
  66.4 0.1 sum_x.3
  66.4 3.2 %collective-permute-start.11 = (f32[3,64,256]{2,1,0:T(8,128)S(1)}, f32[3,64,256]{2,1,0:T(8,128)S(1)}, u32[]{:S(2)}, u32[]{:S(2)}) collective-permute-start(f32[3,64,256]{2,1,0:T(8,128)S(1)} %get-tuple-element.74), channel_id=1, source_target_pairs={{0,8},{8,0},{16,24},{24,16},{1,9},{9,1},{17,25},{25,17},{2,10},{10... | collective-permute-start | bytes 589832 | tf_op jit(solution)/shard_map/ppermute | solution.py:106
  69.7 4.3 %collective-permute-done.11.right = f32[3,64,256]{2,1,0:T(8,128)S(1)} collective-permute-done((f32[3,64,256]{2,1,0:T(8,128)S(1)}, f32[3,64,256]{2,1,0:T(8,128)S(1)}, u32[]{:S(2)}, u32[]{:S(2)}) %collective-permute-start.11) | collective-permute-done | bytes 196640 | tf_op jit(solution)/shard_map/ppermute | solution.py:106
  73.9 2.8 %collective-permute-start.12 = (f32[3,64,256]{2,1,0:T(8,128)S(1)}, f32[3,64,256]{2,1,0:T(8,128)S(1)}, u32[]{:S(2)}, u32[]{:S(2)}) collective-permute-start(f32[3,64,256]{2,1,0:T(8,128)S(1)} %sum_z.3.left), channel_id=1, source_target_pairs={{0,16},{8,24},{16,0},{24,8},{1,17},{9,25},{17,1},{25,9},{2,18},{10... | collective-permute-start | bytes 589832 | tf_op jit(solution)/shard_map/ppermute | solution.py:106
  76.8 1.2 collective-permute-start.14
  78.1 7.5 %collective-permute-done.14.right = f32[3,64,256]{2,1,0:T(8,128)S(1)} collective-permute-done((f32[3,64,256]{2,1,0:T(8,128)S(1)}, f32[3,64,256]{2,1,0:T(8,128)S(1)}, u32[]{:S(2)}, u32[]{:S(2)}) %collective-permute-start.14) | collective-permute-done | bytes 196640 | tf_op jit(solution)/shard_map/ppermute | solution.py:106
  85.6 0.1 finish.3
  85.7 0.7 collective-permute-start.15
  86.4 1.5 %collective-permute-start.16 = (s16[3,64,256]{2,1,0:T(8,128)(2,1)S(1)}, s16[3,64,256]{2,1,0:T(8,128)(2,1)S(1)}, u32[]{:S(2)}, u32[]{:S(2)}) collective-permute-start(s16[3,64,256]{2,1,0:T(8,128)(2,1)S(1)} %get-tuple-element.86), channel_id=1, source_target_pairs={{0,4},{4,0},{1,5},{5,1},{2,6},{6,2},{3,7},{7,3},{8,12},{12,8},{9,1... | collective-permute-start | bytes 294920 | tf_op jit(solution)/shard_map/ppermute | solution.py:106
  87.9 1.3 %collective-permute-start.17 = (s16[3,64,256]{2,1,0:T(8,128)(2,1)S(1)}, s16[3,64,256]{2,1,0:T(8,128)(2,1)S(1)}, u32[]{:S(2)}, u32[]{:S(2)}) collective-permute-start(s16[3,64,256]{2,1,0:T(8,128)(2,1)S(1)} %get-tuple-element.86), channel_id=1, source_target_pairs={{0,12},{4,8},{8,4},{12,0},{16,28},{20,24},{24,20},{28,16},{1,13},{... | collective-permute-start | bytes 294920 | tf_op jit(solution)/shard_map/ppermute | solution.py:231
  89.3 1.1 collective-permute-start.18
  90.4 2.0 %collective-permute-start.20 = (f32[3,64,256]{2,1,0:T(8,128)S(1)}, f32[3,64,256]{2,1,0:T(8,128)S(1)}, u32[]{:S(2)}, u32[]{:S(2)}) collective-permute-start(f32[3,64,256]{2,1,0:T(8,128)S(1)} %get-tuple-element.91), channel_id=1, source_target_pairs={{0,8},{8,0},{16,24},{24,16},{1,9},{9,1},{17,25},{25,17},{2,10},{10... | collective-permute-start | bytes 589832 | tf_op jit(solution)/shard_map/ppermute | solution.py:106
  92.4 0.4 collective-permute-done.15
  92.9 5.2 %collective-permute-done.17 = s16[3,64,256]{2,1,0:T(8,128)(2,1)S(1)} collective-permute-done((s16[3,64,256]{2,1,0:T(8,128)(2,1)S(1)}, s16[3,64,256]{2,1,0:T(8,128)(2,1)S(1)}, u32[]{:S(2)}, u32[]{:S(2)}) %collective-permute-start.17) | collective-permute-done | bytes 98336 | tf_op jit(solution)/shard_map/ppermute | solution.py:231
  98.1 1.8 %collective-permute-done.20.right = f32[3,64,256]{2,1,0:T(8,128)S(1)} collective-permute-done((f32[3,64,256]{2,1,0:T(8,128)S(1)}, f32[3,64,256]{2,1,0:T(8,128)S(1)}, u32[]{:S(2)}, u32[]{:S(2)}) %collective-permute-start.20) | collective-permute-done | bytes 196640 | tf_op jit(solution)/shard_map/ppermute | solution.py:106
  99.9 0.1 finish.4
  100.1 1.0 collective-permute-start.21
  101.1 1.5 %collective-permute-start.22 = (s16[3,64,256]{2,1,0:T(8,128)(2,1)S(1)}, s16[3,64,256]{2,1,0:T(8,128)(2,1)S(1)}, u32[]{:S(2)}, u32[]{:S(2)}) collective-permute-start(s16[3,64,256]{2,1,0:T(8,128)(2,1)S(1)} %get-tuple-element.96), channel_id=1, source_target_pairs={{0,4},{4,0},{1,5},{5,1},{2,6},{6,2},{3,7},{7,3},{8,12},{12,8},{9,1... | collective-permute-start | bytes 294920 | tf_op jit(solution)/shard_map/ppermute | solution.py:106
  102.6 1.0 collective-permute-start.23
  103.6 2.0 %collective-permute-start.24 = (f32[3,64,256]{2,1,0:T(8,128)S(1)}, f32[3,64,256]{2,1,0:T(8,128)S(1)}, u32[]{:S(2)}, u32[]{:S(2)}) collective-permute-start(f32[3,64,256]{2,1,0:T(8,128)S(1)} %sum_z.5.left), channel_id=1, source_target_pairs={{0,16},{8,24},{16,0},{24,8},{1,17},{9,25},{17,1},{25,9},{2,18},{10... | collective-permute-start | bytes 589832 | tf_op jit(solution)/shard_map/ppermute | solution.py:106
  105.7 3.2 %collective-permute-done.23 = s16[3,64,256]{2,1,0:T(8,128)(2,1)S(1)} collective-permute-done((s16[3,64,256]{2,1,0:T(8,128)(2,1)S(1)}, s16[3,64,256]{2,1,0:T(8,128)(2,1)S(1)}, u32[]{:S(2)}, u32[]{:S(2)}) %collective-permute-start.23) | collective-permute-done | bytes 98336 | tf_op jit(solution)/shard_map/ppermute | solution.py:231
  108.9 4.2 %collective-permute-done.24.right = f32[3,64,256]{2,1,0:T(8,128)S(1)} collective-permute-done((f32[3,64,256]{2,1,0:T(8,128)S(1)}, f32[3,64,256]{2,1,0:T(8,128)S(1)}, u32[]{:S(2)}, u32[]{:S(2)}) %collective-permute-start.24) | collective-permute-done | bytes 196640 | tf_op jit(solution)/shard_map/ppermute | solution.py:106
  113.2 0.1 finish.5
  113.3 0.1 collective-permute-start.25
  113.4 1.6 %collective-permute-start.26 = (s16[3,64,256]{2,1,0:T(8,128)(2,1)S(1)}, s16[3,64,256]{2,1,0:T(8,128)(2,1)S(1)}, u32[]{:S(2)}, u32[]{:S(2)}) collective-permute-start(s16[3,64,256]{2,1,0:T(8,128)(2,1)S(1)} %get-tuple-element.99), channel_id=1, source_target_pairs={{0,4},{4,0},{1,5},{5,1},{2,6},{6,2},{3,7},{7,3},{8,12},{12,8},{9,1... | collective-permute-start | bytes 294920 | tf_op jit(solution)/shard_map/ppermute | solution.py:106
  115.0 2.0 %collective-permute-start.28 = (f32[9,64]{1,0:T(8,128)S(1)}, f32[9,64]{1,0:T(8,128)S(1)}, u32[]{:S(2)}, u32[]{:S(2)}) collective-permute-start(f32[9,64]{1,0:T(8,128)S(1)} %pad_maximum_fusion), channel_id=1, source_target_pairs={{0,8},{8,0},{16,24},{24,16},{1,9},{9,1},{17,25},{25,17},{2,10},{10... | collective-permute-start | bytes 6920 | tf_op jit(solution)/shard_map/ppermute | solution.py:106
  117.0 0.5 collective-permute-start.29
  117.5 1.1 collective-permute-start.30
  118.6 0.2 collective-permute-done.28
  118.8 1.8 %collective-permute-start.27 = (s16[3,64,256]{2,1,0:T(8,128)(2,1)S(1)}, s16[3,64,256]{2,1,0:T(8,128)(2,1)S(1)}, u32[]{:S(2)}, u32[]{:S(2)}) collective-permute-start(s16[3,64,256]{2,1,0:T(8,128)(2,1)S(1)} %get-tuple-element.99), channel_id=1, source_target_pairs={{0,12},{4,8},{8,4},{12,0},{16,28},{20,24},{24,20},{28,16},{1,13},{... | collective-permute-start | bytes 294920 | tf_op jit(solution)/shard_map/ppermute | solution.py:231
  120.6 0.2 collective-permute-done.29
  120.8 1.2 collective-permute-done.30
  122.0 0.5 concatenate.16
  122.5 0.6 gather_fusion.1
  123.1 0.1 broadcast_select_fusion
  123.2 1.1 collective-permute-done.27
  124.3 0.6 gather_fusion
  125.0 1.0 convert_multiply_fusion
  (40 shorter events, 0.4 us)
Async XLA Ops:
  1.5 19.9 %collective-permute-start = (bf16[3,256,256]{2,1,0:T(8,128)(2,1)S(1)}, bf16[3,256,256]{2,1,0:T(8,128)(2,1)S(1)}, u32[]{:S(2)}, u32[]{:S(2)}) collective-permute-start(bf16[3,256,256]{2,1,0:T(8,128)(2,1)S(1)} %get-tuple-element.107), channel_id=1, source_target_pairs={{0,8},{8,0},{16,24},{24,16},{1,9},{9,1},{17,25},{25,17},{2,10},{10... | collective-permute-start | bytes 1179656 | tf_op jit(solution)/shard_map/ppermute | solution.py:106
  4.6 29.8 %collective-permute-start.1 = (bf16[3,256,256]{2,1,0:T(8,128)(2,1)S(1)}, bf16[3,256,256]{2,1,0:T(8,128)(2,1)S(1)}, u32[]{:S(2)}, u32[]{:S(2)}) collective-permute-start(bf16[3,256,256]{2,1,0:T(8,128)(2,1)S(1)} %get-tuple-element.109), channel_id=1, source_target_pairs={{0,16},{8,24},{16,0},{24,8},{1,17},{9,25},{17,1},{25,9},{2,18},{10... | collective-permute-start | bytes 1179656 | tf_op jit(solution)/shard_map/ppermute | solution.py:106
  7.2 28.7 %collective-permute-start.2 = (bf16[3,256,256]{2,1,0:T(8,128)(2,1)S(1)}, bf16[3,256,256]{2,1,0:T(8,128)(2,1)S(1)}, u32[]{:S(2)}, u32[]{:S(2)}) collective-permute-start(bf16[3,256,256]{2,1,0:T(8,128)(2,1)S(1)} %get-tuple-element.106), channel_id=1, source_target_pairs={{0,24},{8,16},{16,8},{24,0},{1,25},{9,17},{17,9},{25,1},{2,26},{10... | collective-permute-start | bytes 1179656 | tf_op jit(solution)/shard_map/ppermute | solution.py:106
  7.2 30.0 %collective-permute-start.3 = (bf16[3,256,256]{2,1,0:T(8,128)(2,1)S(1)}, bf16[3,256,256]{2,1,0:T(8,128)(2,1)S(1)}, u32[]{:S(2)}, u32[]{:S(2)}) collective-permute-start(bf16[3,256,256]{2,1,0:T(8,128)(2,1)S(1)} %get-tuple-element.108.refs_0_), channel_id=1, source_target_pairs={{0,4},{4,0},{1,5},{5,1},{2,6},{6,2},{3,7},{7,3},{8,12},{12,8},{9,1... | collective-permute-start | bytes 1179656 | tf_op jit(solution)/shard_map/ppermute | solution.py:106
  21.3 15.8 %collective-permute-start.4 = (bf16[3,256,256]{2,1,0:T(8,128)(2,1)S(1)}, bf16[3,256,256]{2,1,0:T(8,128)(2,1)S(1)}, u32[]{:S(2)}, u32[]{:S(2)}) collective-permute-start(bf16[3,256,256]{2,1,0:T(8,128)(2,1)S(1)} %collective-permute-done.refs_1_), channel_id=1, source_target_pairs={{0,4},{4,0},{1,5},{5,1},{2,6},{6,2},{3,7},{7,3},{8,12},{12,8},{9,1... | collective-permute-start | bytes 1179656 | tf_op jit(solution)/shard_map/ppermute | solution.py:106
  34.4 9.9 %collective-permute-start.5 = (bf16[3,256,256]{2,1,0:T(8,128)(2,1)S(1)}, bf16[3,256,256]{2,1,0:T(8,128)(2,1)S(1)}, u32[]{:S(2)}, u32[]{:S(2)}) collective-permute-start(bf16[3,256,256]{2,1,0:T(8,128)(2,1)S(1)} %collective-permute-done.1.refs_2_), channel_id=1, source_target_pairs={{0,4},{4,0},{1,5},{5,1},{2,6},{6,2},{3,7},{7,3},{8,12},{12,8},{9,1... | collective-permute-start | bytes 1179656 | tf_op jit(solution)/shard_map/ppermute | solution.py:106
  35.9 12.6 %collective-permute-start.6 = (bf16[3,256,256]{2,1,0:T(8,128)(2,1)S(1)}, bf16[3,256,256]{2,1,0:T(8,128)(2,1)S(1)}, u32[]{:S(2)}, u32[]{:S(2)}) collective-permute-start(bf16[3,256,256]{2,1,0:T(8,128)(2,1)S(1)} %collective-permute-done.2.refs_3_), channel_id=1, source_target_pairs={{0,4},{4,0},{1,5},{5,1},{2,6},{6,2},{3,7},{7,3},{8,12},{12,8},{9,1... | collective-permute-start | bytes 1179656 | tf_op jit(solution)/shard_map/ppermute | solution.py:106
  50.5 3.8 %collective-permute-start.7 = (f32[2,2,3,64,256]{4,3,2,1,0:T(8,128)S(1)}, f32[2,2,3,64,256]{4,3,2,1,0:T(8,128)S(1)}, u32[]{:S(2)}, u32[]{:S(2)}) collective-permute-start(f32[2,2,3,64,256]{4,3,2,1,0:T(8,128)S(1)} %get-tuple-element.55), channel_id=1, source_target_pairs={{0,1},{1,0},{2,3},{3,2},{4,5},{5,4},{6,7},{7,6},{8,9},{9,8},{10,11... | collective-permute-start | bytes 2359304 | tf_op jit(solution)/shard_map/ppermute | solution.py:106
  53.7 2.1 %copy-start = (s32[1,10,2]{1,2,0:T(2,128)S(1)}, s32[1,10,2]{1,2,0:T(2,128)}, u32[]{:S(2)}) copy-start(s32[1,10,2]{1,2,0:T(2,128)} %param.4) | copy-start | bytes 244
  53.7 2.5 %collective-permute-start.10 = (f32[2,2,3,64,256]{4,3,2,1,0:T(8,128)S(1)}, f32[2,2,3,64,256]{4,3,2,1,0:T(8,128)S(1)}, u32[]{:S(2)}, u32[]{:S(2)}) collective-permute-start(f32[2,2,3,64,256]{4,3,2,1,0:T(8,128)S(1)} %get-tuple-element.64), channel_id=1, source_target_pairs={{0,1},{1,0},{2,3},{3,2},{4,5},{5,4},{6,7},{7,6},{8,9},{9,8},{10,11... | collective-permute-start | bytes 2359304 | tf_op jit(solution)/shard_map/ppermute | solution.py:106
  54.2 3.4 %collective-permute-start.9 = (f32[2,2,3,64,256]{4,3,2,1,0:T(8,128)S(1)}, f32[2,2,3,64,256]{4,3,2,1,0:T(8,128)S(1)}, u32[]{:S(2)}, u32[]{:S(2)}) collective-permute-start(f32[2,2,3,64,256]{4,3,2,1,0:T(8,128)S(1)} %get-tuple-element.62), channel_id=1, source_target_pairs={{0,1},{1,0},{2,3},{3,2},{4,5},{5,4},{6,7},{7,6},{8,9},{9,8},{10,11... | collective-permute-start | bytes 2359304 | tf_op jit(solution)/shard_map/ppermute | solution.py:106
  54.4 12.0 %collective-permute-start.8 = (f32[2,3,64,256]{3,2,1,0:T(8,128)S(1)}, f32[2,3,64,256]{3,2,1,0:T(8,128)S(1)}, u32[]{:S(2)}, u32[]{:S(2)}) collective-permute-start(f32[2,3,64,256]{3,2,1,0:T(8,128)S(1)} %get-tuple-element.59), channel_id=1, source_target_pairs={{0,2},{2,0},{1,3},{3,1},{4,6},{6,4},{5,7},{7,5},{8,10},{10,8},{9,1... | collective-permute-start | bytes 1179656 | tf_op jit(solution)/shard_map/ppermute | solution.py:106
  56.2 20.5 %collective-permute-start.13 = (f32[2,3,64,256]{3,2,1,0:T(8,128)S(1)}, f32[2,3,64,256]{3,2,1,0:T(8,128)S(1)}, u32[]{:S(2)}, u32[]{:S(2)}) collective-permute-start(f32[2,3,64,256]{3,2,1,0:T(8,128)S(1)} %get-tuple-element.77), channel_id=1, source_target_pairs={{0,2},{2,0},{1,3},{3,1},{4,6},{6,4},{5,7},{7,5},{8,10},{10,8},{9,1... | collective-permute-start | bytes 1179656 | tf_op jit(solution)/shard_map/ppermute | solution.py:106
  57.8 32.6 %collective-permute-start.19 = (f32[2,3,64,256]{3,2,1,0:T(8,128)S(1)}, f32[2,3,64,256]{3,2,1,0:T(8,128)S(1)}, u32[]{:S(2)}, u32[]{:S(2)}) collective-permute-start(f32[2,3,64,256]{3,2,1,0:T(8,128)S(1)} %get-tuple-element.87), channel_id=1, source_target_pairs={{0,2},{2,0},{1,3},{3,1},{4,6},{6,4},{5,7},{7,5},{8,10},{10,8},{9,1... | collective-permute-start | bytes 1179656 | tf_op jit(solution)/shard_map/ppermute | solution.py:106
  66.4 7.5 %collective-permute-start.11 = (f32[3,64,256]{2,1,0:T(8,128)S(1)}, f32[3,64,256]{2,1,0:T(8,128)S(1)}, u32[]{:S(2)}, u32[]{:S(2)}) collective-permute-start(f32[3,64,256]{2,1,0:T(8,128)S(1)} %get-tuple-element.74), channel_id=1, source_target_pairs={{0,8},{8,0},{16,24},{24,16},{1,9},{9,1},{17,25},{25,17},{2,10},{10... | collective-permute-start | bytes 589832 | tf_op jit(solution)/shard_map/ppermute | solution.py:106
  73.9 11.6 %collective-permute-start.12 = (f32[3,64,256]{2,1,0:T(8,128)S(1)}, f32[3,64,256]{2,1,0:T(8,128)S(1)}, u32[]{:S(2)}, u32[]{:S(2)}) collective-permute-start(f32[3,64,256]{2,1,0:T(8,128)S(1)} %sum_z.3.left), channel_id=1, source_target_pairs={{0,16},{8,24},{16,0},{24,8},{1,17},{9,25},{17,1},{25,9},{2,18},{10... | collective-permute-start | bytes 589832 | tf_op jit(solution)/shard_map/ppermute | solution.py:106
  76.8 8.7 %collective-permute-start.14 = (f32[3,64,256]{2,1,0:T(8,128)S(1)}, f32[3,64,256]{2,1,0:T(8,128)S(1)}, u32[]{:S(2)}, u32[]{:S(2)}) collective-permute-start(f32[3,64,256]{2,1,0:T(8,128)S(1)} %get-tuple-element.81), channel_id=1, source_target_pairs={{0,8},{8,0},{16,24},{24,16},{1,9},{9,1},{17,25},{25,17},{2,10},{10... | collective-permute-start | bytes 589832 | tf_op jit(solution)/shard_map/ppermute | solution.py:106
  85.7 7.1 %collective-permute-start.15 = (s16[3,64,256]{2,1,0:T(8,128)(2,1)S(1)}, s16[3,64,256]{2,1,0:T(8,128)(2,1)S(1)}, u32[]{:S(2)}, u32[]{:S(2)}) collective-permute-start(s16[3,64,256]{2,1,0:T(8,128)(2,1)S(1)} %get-tuple-element.86), channel_id=1, source_target_pairs={{0,8},{8,0},{16,24},{24,16},{1,9},{9,1},{17,25},{25,17},{2,10},{10... | collective-permute-start | bytes 294920 | tf_op jit(solution)/shard_map/ppermute | solution.py:106
  86.4 6.4 %collective-permute-start.16 = (s16[3,64,256]{2,1,0:T(8,128)(2,1)S(1)}, s16[3,64,256]{2,1,0:T(8,128)(2,1)S(1)}, u32[]{:S(2)}, u32[]{:S(2)}) collective-permute-start(s16[3,64,256]{2,1,0:T(8,128)(2,1)S(1)} %get-tuple-element.86), channel_id=1, source_target_pairs={{0,4},{4,0},{1,5},{5,1},{2,6},{6,2},{3,7},{7,3},{8,12},{12,8},{9,1... | collective-permute-start | bytes 294920 | tf_op jit(solution)/shard_map/ppermute | solution.py:106
  87.9 10.1 %collective-permute-start.17 = (s16[3,64,256]{2,1,0:T(8,128)(2,1)S(1)}, s16[3,64,256]{2,1,0:T(8,128)(2,1)S(1)}, u32[]{:S(2)}, u32[]{:S(2)}) collective-permute-start(s16[3,64,256]{2,1,0:T(8,128)(2,1)S(1)} %get-tuple-element.86), channel_id=1, source_target_pairs={{0,12},{4,8},{8,4},{12,0},{16,28},{20,24},{24,20},{28,16},{1,13},{... | collective-permute-start | bytes 294920 | tf_op jit(solution)/shard_map/ppermute | solution.py:231
  89.3 10.6 %collective-permute-start.18 = (f32[3,64,256]{2,1,0:T(8,128)S(1)}, f32[3,64,256]{2,1,0:T(8,128)S(1)}, u32[]{:S(2)}, u32[]{:S(2)}) collective-permute-start(f32[3,64,256]{2,1,0:T(8,128)S(1)} %sum_z.4.left), channel_id=1, source_target_pairs={{0,16},{8,24},{16,0},{24,8},{1,17},{9,25},{17,1},{25,9},{2,18},{10... | collective-permute-start | bytes 589832 | tf_op jit(solution)/shard_map/ppermute | solution.py:106
  90.4 9.5 %collective-permute-start.20 = (f32[3,64,256]{2,1,0:T(8,128)S(1)}, f32[3,64,256]{2,1,0:T(8,128)S(1)}, u32[]{:S(2)}, u32[]{:S(2)}) collective-permute-start(f32[3,64,256]{2,1,0:T(8,128)S(1)} %get-tuple-element.91), channel_id=1, source_target_pairs={{0,8},{8,0},{16,24},{24,16},{1,9},{9,1},{17,25},{25,17},{2,10},{10... | collective-permute-start | bytes 589832 | tf_op jit(solution)/shard_map/ppermute | solution.py:106
  100.1 5.6 %collective-permute-start.21 = (s16[3,64,256]{2,1,0:T(8,128)(2,1)S(1)}, s16[3,64,256]{2,1,0:T(8,128)(2,1)S(1)}, u32[]{:S(2)}, u32[]{:S(2)}) collective-permute-start(s16[3,64,256]{2,1,0:T(8,128)(2,1)S(1)} %get-tuple-element.96), channel_id=1, source_target_pairs={{0,8},{8,0},{16,24},{24,16},{1,9},{9,1},{17,25},{25,17},{2,10},{10... | collective-permute-start | bytes 294920 | tf_op jit(solution)/shard_map/ppermute | solution.py:106
  101.1 4.6 %collective-permute-start.22 = (s16[3,64,256]{2,1,0:T(8,128)(2,1)S(1)}, s16[3,64,256]{2,1,0:T(8,128)(2,1)S(1)}, u32[]{:S(2)}, u32[]{:S(2)}) collective-permute-start(s16[3,64,256]{2,1,0:T(8,128)(2,1)S(1)} %get-tuple-element.96), channel_id=1, source_target_pairs={{0,4},{4,0},{1,5},{5,1},{2,6},{6,2},{3,7},{7,3},{8,12},{12,8},{9,1... | collective-permute-start | bytes 294920 | tf_op jit(solution)/shard_map/ppermute | solution.py:106
  102.6 6.3 %collective-permute-start.23 = (s16[3,64,256]{2,1,0:T(8,128)(2,1)S(1)}, s16[3,64,256]{2,1,0:T(8,128)(2,1)S(1)}, u32[]{:S(2)}, u32[]{:S(2)}) collective-permute-start(s16[3,64,256]{2,1,0:T(8,128)(2,1)S(1)} %get-tuple-element.96), channel_id=1, source_target_pairs={{0,12},{4,8},{8,4},{12,0},{16,28},{20,24},{24,20},{28,16},{1,13},{... | collective-permute-start | bytes 294920 | tf_op jit(solution)/shard_map/ppermute | solution.py:231
  103.6 9.5 %collective-permute-start.24 = (f32[3,64,256]{2,1,0:T(8,128)S(1)}, f32[3,64,256]{2,1,0:T(8,128)S(1)}, u32[]{:S(2)}, u32[]{:S(2)}) collective-permute-start(f32[3,64,256]{2,1,0:T(8,128)S(1)} %sum_z.5.left), channel_id=1, source_target_pairs={{0,16},{8,24},{16,0},{24,8},{1,17},{9,25},{17,1},{25,9},{2,18},{10... | collective-permute-start | bytes 589832 | tf_op jit(solution)/shard_map/ppermute | solution.py:106
  113.3 9.8 %collective-permute-start.25 = (s16[3,64,256]{2,1,0:T(8,128)(2,1)S(1)}, s16[3,64,256]{2,1,0:T(8,128)(2,1)S(1)}, u32[]{:S(2)}, u32[]{:S(2)}) collective-permute-start(s16[3,64,256]{2,1,0:T(8,128)(2,1)S(1)} %get-tuple-element.99), channel_id=1, source_target_pairs={{0,8},{8,0},{16,24},{24,16},{1,9},{9,1},{17,25},{25,17},{2,10},{10... | collective-permute-start | bytes 294920 | tf_op jit(solution)/shard_map/ppermute | solution.py:106
  113.4 9.8 %collective-permute-start.26 = (s16[3,64,256]{2,1,0:T(8,128)(2,1)S(1)}, s16[3,64,256]{2,1,0:T(8,128)(2,1)S(1)}, u32[]{:S(2)}, u32[]{:S(2)}) collective-permute-start(s16[3,64,256]{2,1,0:T(8,128)(2,1)S(1)} %get-tuple-element.99), channel_id=1, source_target_pairs={{0,4},{4,0},{1,5},{5,1},{2,6},{6,2},{3,7},{7,3},{8,12},{12,8},{9,1... | collective-permute-start | bytes 294920 | tf_op jit(solution)/shard_map/ppermute | solution.py:106
  115.0 3.8 %collective-permute-start.28 = (f32[9,64]{1,0:T(8,128)S(1)}, f32[9,64]{1,0:T(8,128)S(1)}, u32[]{:S(2)}, u32[]{:S(2)}) collective-permute-start(f32[9,64]{1,0:T(8,128)S(1)} %pad_maximum_fusion), channel_id=1, source_target_pairs={{0,8},{8,0},{16,24},{24,16},{1,9},{9,1},{17,25},{25,17},{2,10},{10... | collective-permute-start | bytes 6920 | tf_op jit(solution)/shard_map/ppermute | solution.py:106
  117.0 3.8 %collective-permute-start.29 = (f32[9,64]{1,0:T(8,128)S(1)}, f32[9,64]{1,0:T(8,128)S(1)}, u32[]{:S(2)}, u32[]{:S(2)}) collective-permute-start(f32[9,64]{1,0:T(8,128)S(1)} %pad_maximum_fusion), channel_id=1, source_target_pairs={{0,4},{4,0},{1,5},{5,1},{2,6},{6,2},{3,7},{7,3},{8,12},{12,8},{9,1... | collective-permute-start | bytes 6920 | tf_op jit(solution)/shard_map/ppermute | solution.py:106
  117.5 4.5 %collective-permute-start.30 = (f32[9,64]{1,0:T(8,128)S(1)}, f32[9,64]{1,0:T(8,128)S(1)}, u32[]{:S(2)}, u32[]{:S(2)}) collective-permute-start(f32[9,64]{1,0:T(8,128)S(1)} %pad_maximum_fusion), channel_id=1, source_target_pairs={{0,12},{4,8},{8,4},{12,0},{16,28},{20,24},{24,20},{28,16},{1,13},{... | collective-permute-start | bytes 6920 | tf_op jit(solution)/shard_map/ppermute | solution.py:231
  118.8 5.5 %collective-permute-start.27 = (s16[3,64,256]{2,1,0:T(8,128)(2,1)S(1)}, s16[3,64,256]{2,1,0:T(8,128)(2,1)S(1)}, u32[]{:S(2)}, u32[]{:S(2)}) collective-permute-start(s16[3,64,256]{2,1,0:T(8,128)(2,1)S(1)} %get-tuple-element.99), channel_id=1, source_target_pairs={{0,12},{4,8},{8,4},{12,0},{16,28},{20,24},{24,20},{28,16},{1,13},{... | collective-permute-start | bytes 294920 | tf_op jit(solution)/shard_map/ppermute | solution.py:231

commit v8 on v7

--- a/solution.py
+++ b/solution.py
@@ -11,8 +11,14 @@
 
 VMEM_LIMIT = 24 * 2**20
 GROUPS = 3
-ORDER = ((0, 0), (1, 0), (0, 1), (1, 1), (2, 0), (0, 2), (1, 2), (2, 1), (2, 2))
+BATCHES = ((0, 1), (2,))
+ORDER = (
+    ("x", 0), ("low", 0), ("x", 1), ("high", 0), ("low", 1),
+    ("x", 2), ("low", 2), ("finish", BATCHES[0]), ("finish", BATCHES[1]),
+)
 CODE_TOP = 32767.0
+SCALE_ROWS = 16
+SCALE_STEPS = 8192.0
 
 
 def tile_lists(block_count):
@@ -82,13 +88,71 @@
     out[...] = left[...] + right[...]
 
 
-def code_kernel(scale_factor, left, right, code, scale):
-    total = left[...] + right[...]
-    top = jnp.max(jnp.abs(total), axis=2, keepdims=True)
-    factor = jnp.where(top > 0, CODE_TOP / top, 0.0)
-    rounded = jnp.clip(jnp.round(total * factor), -CODE_TOP, CODE_TOP)
-    code[...] = rounded.astype(jnp.int32).astype(jnp.int16)
-    scale[...] = jnp.max(jnp.abs(total), axis=2) * (scale_factor / CODE_TOP)
+def code_kernel(sizes, pairs, *refs):
+    code = refs[-1]
+    refs = list(refs[:-1])
+    rows, columns = refs[0].shape[1:]
+    header_rows = -(-sum(sizes) * rows // columns)
+    row_of = lax.broadcasted_iota(jnp.int32, (rows, columns), 0)
+    lane_of = lax.broadcasted_iota(jnp.int32, (rows, columns), 1)
+    place = lax.broadcasted_iota(jnp.int32, (SCALE_ROWS, columns), 0)
+    header = jnp.zeros((SCALE_ROWS, columns), jnp.float32)
+    slot = 0
+    for size, pair in zip(sizes, pairs):
+        terms = [refs.pop(0) for _ in range(pair)]
+        for index in range(size):
+            total = sum((term[index] for term in terms[1:]), terms[0][index])
+            top = jnp.max(jnp.abs(total), axis=1, keepdims=True)
+            filled = top > 0
+            exponent = jnp.log(jnp.where(filled, top, 1.0)) * (1.0 / math.log(2.0))
+            exponent = jnp.clip(jnp.floor(exponent), -120.0, 120.0)
+            power = jnp.exp(exponent * math.log(2.0))
+            steps = jnp.where(filled, jnp.ceil(top / power * SCALE_STEPS), 0.0)
+            scale = steps * power * (1.0 / SCALE_STEPS)
+            factor = jnp.where(filled, CODE_TOP / jnp.where(filled, scale, 1.0), 0.0)
+            rounded = jnp.clip(jnp.round(total * factor), -CODE_TOP, CODE_TOP)
+            start = SCALE_ROWS + slot * rows
+            code[start : start + rows, :] = rounded.astype(jnp.int32).astype(jnp.int16)
+            row, lane = divmod(slot * rows, columns)
+            diagonal = lane_of == row_of + lane
+            for at, value in ((row, exponent), (row + header_rows, steps)):
+                across = jnp.sum(jnp.where(diagonal, value, 0.0), axis=0, keepdims=True)
+                header += jnp.where(place == at, across, 0.0)
+            slot += 1
+    code[:SCALE_ROWS, :] = header.astype(jnp.int32).astype(jnp.int16)
+
+
+def place_kernel(factor, scalars, *refs):
+    out, codes, headers = refs[-3:]
+    slots, rows, columns = out.shape
+    at = 0
+    for index, part in enumerate(refs[:-3]):
+        count = part.shape[0] - SCALE_ROWS
+        start = index * SCALE_ROWS
+        headers[start : start + SCALE_ROWS, :] = (
+            part[:SCALE_ROWS, :].astype(jnp.int32).astype(jnp.float32)
+        )
+        codes[at : at + count, :] = part[SCALE_ROWS:, :]
+        at += count
+    row_of = lax.broadcasted_iota(jnp.int32, (rows, columns), 0)
+    lane_of = lax.broadcasted_iota(jnp.int32, (rows, columns), 1)
+
+    def one_slot(slot, carry):
+        tile, lane, exponent_row, steps_row, filled = (
+            scalars[kind * slots + slot] for kind in range(5)
+        )
+        exponent = headers[pl.ds(exponent_row, 1), :]
+        steps = headers[pl.ds(steps_row, 1), :]
+        scale = steps * jnp.exp(exponent * math.log(2.0)) * factor
+        scale = jnp.where(filled > 0, scale, 0.0)
+        column = jnp.sum(
+            jnp.where(lane_of == row_of + lane, scale, 0.0), axis=1, keepdims=True
+        )
+        code = codes[pl.ds(pl.multiple_of(tile * rows, rows), rows), :]
+        out[slot] = code.astype(jnp.int32).astype(jnp.float32) * column
+        return carry
+
+    lax.fori_loop(0, slots, one_slot, 0)
 
 
 def per_device(z_count, y_count, x_count, core_count, snapshots, tile_table):
@@ -184,6 +248,9 @@
             in_specs=[vmem] * len(operands),
             out_specs=[vmem] * len(out_shape),
             compiler_params=pltpu.CompilerParams(vmem_limit_bytes=VMEM_LIMIT),
+            cost_estimate=pl.CostEstimate(
+                flops=operands[0].size, bytes_accessed=0, transcendentals=0
+            ),
             name=name,
         )(*operands)
         last[:] = outs[:1]
@@ -217,43 +284,70 @@
             bits *= 2
         return mine, swap(mine, "z", bits)
 
-    def sum_high(index, mine, arrived):
-        shapes = [
-            jax.ShapeDtypeStruct((sizes[index], rows_dev, block_size), jnp.int16),
-            jax.ShapeDtypeStruct((sizes[index], rows_dev), jnp.float32),
-        ]
-        kernel = functools.partial(code_kernel, scale_factor)
-        code, scale = step_call(kernel, shapes, mine, arrived, name="finish")
-        return to_owners(code), scale
-
     def to_owners(value):
         both = [(i, i ^ (y_count + 1)) for i in range(block_count)]
         over_both = lax.ppermute(value, ("z", "y"), both)
         return [value, swap(value, "z", 1), swap(value, "y", 1), over_both]
 
-    stages = [sum_x, sum_low, sum_high]
-    state = [sum_core(index) for index in range(len(sizes))]
-    for stage, index in ORDER:
-        state[index] = stages[stage](index, *state[index])
-    codes = jnp.concatenate([part for parts, _ in state for part in parts])
-    scales = jnp.concatenate(to_owners(jnp.concatenate([scale for _, scale in state])))
+    parts = []
+    state = [sum_core(index) for index in range(GROUPS)]
+    for stage, which in ORDER:
+        if stage == "x":
+            state[which] = sum_x(which, *state[which])
+        elif stage == "low":
+            state[which] = sum_low(which, *state[which])
+        elif stage == "high":
+            state[which] = step_call(
+                sum_kernel, [float_shape(sizes[which])], *state[which], name="sum_high"
+            )
+        else:
+            counts = [sizes[index] for index in which]
+            shape = (SCALE_ROWS + sum(counts) * rows_dev, block_size)
+            kernel = functools.partial(code_kernel, counts, [len(state[i]) for i in which])
+            operands = [value for index in which for value in state[index]]
+            (code,) = step_call(
+                kernel, [jax.ShapeDtypeStruct(shape, jnp.int16)], *operands, name="finish"
+            )
+            parts += to_owners(code)
 
     table = tile_table[0]
     row_block = table[:, 0]
     col_block = table[:, 1]
-    valid = row_block >= 0
     first = jnp.maximum(row_block, 0)
     second = jnp.maximum(col_block, 0)
     pair = first * block_count - (first * (first - 1)) // 2 + second - first
     of_list, slot = pair // quarter, pair % quarter
     off = ((of_list // 2) ^ y) * 2 + ((of_list % 2) ^ low_bit)
-    place = jnp.zeros_like(slot)
-    for start, size in zip(starts, sizes):
-        here = 4 * int(start) + off * size + slot - int(start)
-        place = jnp.where((slot >= int(start)) & (slot < int(start) + size), here, place)
-    scale = scales[off * quarter + slot]
-    scale = jnp.where(valid[:, None], scale, 0.0)
-    result = codes[place].astype(jnp.float32) * scale[:, :, None]
+    tile, lane, exponent_row, steps_row = (jnp.zeros_like(slot) for _ in range(4))
+    for index, batch in enumerate(BATCHES):
+        start, end = int(starts[batch[0]]), int(starts[batch[-1] + 1])
+        inside = (slot >= start) & (slot < end)
+        header_rows = -(-(end - start) * rows_dev // block_size)
+        at = (slot - start) * rows_dev
+        top = (4 * index + off) * SCALE_ROWS + at // block_size
+        tile = jnp.where(inside, 4 * start + off * (end - start) + slot - start, tile)
+        lane = jnp.where(inside, at % block_size, lane)
+        exponent_row = jnp.where(inside, top, exponent_row)
+        steps_row = jnp.where(inside, top + header_rows, steps_row)
+    places = jnp.concatenate(
+        [tile, lane, exponent_row, steps_row, (row_block >= 0).astype(jnp.int32)]
+    )
+    vmem = pl.BlockSpec(memory_space=pltpu.VMEM)
+    result = pl.pallas_call(
+        functools.partial(place_kernel, scale_factor / (CODE_TOP * SCALE_STEPS)),
+        out_shape=float_shape(table.shape[0]),
+        in_specs=[pl.BlockSpec(memory_space=pltpu.SMEM)] + [vmem] * len(parts),
+        out_specs=vmem,
+        scratch_shapes=[
+            pltpu.VMEM((4 * quarter * rows_dev, block_size), jnp.int16),
+            pltpu.VMEM((len(parts) * SCALE_ROWS, block_size), jnp.float32),
+        ],
+        compiler_params=pltpu.CompilerParams(vmem_limit_bytes=VMEM_LIMIT),
+        cost_estimate=pl.CostEstimate(
+            flops=table.shape[0] * rows_dev * block_size, bytes_accessed=0, transcendentals=0
+        ),
+        name="place_tiles",
+    )(places, *parts)
     return result[None]
 
 

time: 126 us -> 120 us (0.952)
  starting transfers between devices: 42.2 us -> 30.3 us
  waiting for transfers between devices: 72.5 us -> 78.8 us
  Pallas kernels: 5.93 us -> 8.53 us
  local copies, waits for them, and re-layouts: 4 us -> 2.33 us
    ppermute x27 -> x23, waiting for transfers between devices: 61.7 us -> 74.8 us  [swap(): return lax.ppermute(value, axis, [(i, i ^ bits) for i in range(size)])]
    ppermute x27 -> x23, starting transfers between devices: 37 us -> 27.9 us  [swap(): return lax.ppermute(value, axis, [(i, i ^ bits) for i in range(size)])]
    ppermute x4 -> x2, waiting for transfers between devices: 10.8 us -> 3.96 us  [to_owners(): over_both = lax.ppermute(value, ('z', 'y'), both)]
    ppermute x4 -> x2, starting transfers between devices: 5.18 us -> 2.45 us  [to_owners(): over_both = lax.ppermute(value, ('z', 'y'), both)]
    pallas_call x0 -> x1, Pallas kernels: none -> 2.44 us  [per_device(): pl.pallas_call(functools.partial(place_kernel, scale_factor / (CODE_TOP *...]
  transfers between devices with their start and end apart: 31 -> 25, of which waited for: 17 -> 16; matrix products, arithmetic and copies ran while one was open for 2% -> 1% of each run, Pallas kernels for 3% -> 3%
where the time goes in v8:
time: 120 us
  waiting for transfers between devices  78.8 us (66%)
  starting transfers between devices  30.3 us (25%)
  Pallas kernels  8.53 us (7%)
  local copies, waits for them, and re-layouts  2.33 us (2%)
    ppermute x23, waiting for transfers between devices, swap(): return lax.ppermute(value, axis, [(i, i ^ bits) for i in range(size)])  74.8 us
    ppermute x23, starting transfers between devices, swap(): return lax.ppermute(value, axis, [(i, i ^ bits) for i in range(size)])  27.9 us
    pallas_call x2, Pallas kernels, call(): pl.pallas_call(kernel, out_shape=out_shape, in_specs=[pl.BlockSpec(memory...  5.06 us
    ppermute x2, waiting for transfers between devices, to_owners(): over_both = lax.ppermute(value, ('z', 'y'), both)  3.96 us
    ppermute x2, starting transfers between devices, to_owners(): over_both = lax.ppermute(value, ('z', 'y'), both)  2.45 us
    pallas_call x1, Pallas kernels, per_device(): pl.pallas_call(functools.partial(place_kernel, scale_factor / (CODE_TOP *...  2.44 us
  transfers between devices with their start and end apart: 25, of which 16 were waited for; matrix products, arithmetic and copies ran while one was open for 1% of the time, Pallas kernels for 3%

profile of v8, /device:TPU:0, one launch (start us, length us, event | category | flops | bytes accessed | tf_op | source)
XLA Modules:
  0.0 120.1 jit_solution(5855259218958314142)
XLA Ops:
  0.0 1.5 %constant_dynamic-slice_fusion = (bf16[3,256,256]{2,1,0:T(8,128)(2,1)S(1)}, bf16[3,256,256]{2,1,0:T(8,128)(2,1)S(1)}, bf16[3,256,256]{2,1,0:T(8,128)(2,1)S(1)}, bf16[3,256,256]{2,1,0:T(8,128)(2,1)S(1)}) fusion(bf16[3,256,1024]{2,1,0:T(8,128)(2,1)} %param.3, s32[]{:T(128)S(6)} %select_n.97, s32[]{:T(128)S(6)} %select_n.95, s32[]{:T(128)S(6)} %select_n.94, ...), kind=kLoop, calls=%fused_computation.12 | loop fusion | bytes 3145744 | tf_op jit(solution)/shard_map/dynamic_slice | solution.py:193
  1.5 5.1 %collective-permute-start.2 = (bf16[3,256,256]{2,1,0:T(8,128)(2,1)S(1)}, bf16[3,256,256]{2,1,0:T(8,128)(2,1)S(1)}, u32[]{:S(2)}, u32[]{:S(2)}) collective-permute-start(bf16[3,256,256]{2,1,0:T(8,128)(2,1)S(1)} %get-tuple-element.98), channel_id=1, source_target_pairs={{0,24},{8,16},{16,8},{24,0},{1,25},{9,17},{17,9},{25,1},{2,26},{10... | collective-permute-start | bytes 1179656 | tf_op jit(solution)/shard_map/ppermute | solution.py:170
  6.6 0.0 collective-permute-start
  6.6 0.6 collective-permute-start.1
  7.2 1.7 %collective-permute-start.3 = (bf16[3,256,256]{2,1,0:T(8,128)(2,1)S(1)}, bf16[3,256,256]{2,1,0:T(8,128)(2,1)S(1)}, u32[]{:S(2)}, u32[]{:S(2)}) collective-permute-start(bf16[3,256,256]{2,1,0:T(8,128)(2,1)S(1)} %get-tuple-element.100.refs_0_), channel_id=1, source_target_pairs={{0,4},{4,0},{1,5},{5,1},{2,6},{6,2},{3,7},{7,3},{8,12},{12,8},{9,1... | collective-permute-start | bytes 1179656 | tf_op jit(solution)/shard_map/ppermute | solution.py:170
  8.9 7.7 %collective-permute-done.2.refs_3_ = bf16[3,256,256]{2,1,0:T(8,128)(2,1)S(1)} collective-permute-done((bf16[3,256,256]{2,1,0:T(8,128)(2,1)S(1)}, bf16[3,256,256]{2,1,0:T(8,128)(2,1)S(1)}, u32[]{:S(2)}, u32[]{:S(2)}) %collective-permute-start.2) | collective-permute-done | bytes 393248 | tf_op jit(solution)/shard_map/ppermute | solution.py:170
  16.6 1.7 %collective-permute-start.6 = (bf16[3,256,256]{2,1,0:T(8,128)(2,1)S(1)}, bf16[3,256,256]{2,1,0:T(8,128)(2,1)S(1)}, u32[]{:S(2)}, u32[]{:S(2)}) collective-permute-start(bf16[3,256,256]{2,1,0:T(8,128)(2,1)S(1)} %collective-permute-done.2.refs_3_), channel_id=1, source_target_pairs={{0,4},{4,0},{1,5},{5,1},{2,6},{6,2},{3,7},{7,3},{8,12},{12,8},{9,1... | collective-permute-start | bytes 1179656 | tf_op jit(solution)/shard_map/ppermute | solution.py:170
  18.3 6.9 %collective-permute-done.refs_1_ = bf16[3,256,256]{2,1,0:T(8,128)(2,1)S(1)} collective-permute-done((bf16[3,256,256]{2,1,0:T(8,128)(2,1)S(1)}, bf16[3,256,256]{2,1,0:T(8,128)(2,1)S(1)}, u32[]{:S(2)}, u32[]{:S(2)}) %collective-permute-start) | collective-permute-done | bytes 393248 | tf_op jit(solution)/shard_map/ppermute | solution.py:170
  25.3 1.4 %collective-permute-start.4 = (bf16[3,256,256]{2,1,0:T(8,128)(2,1)S(1)}, bf16[3,256,256]{2,1,0:T(8,128)(2,1)S(1)}, u32[]{:S(2)}, u32[]{:S(2)}) collective-permute-start(bf16[3,256,256]{2,1,0:T(8,128)(2,1)S(1)} %collective-permute-done.refs_1_), channel_id=1, source_target_pairs={{0,4},{4,0},{1,5},{5,1},{2,6},{6,2},{3,7},{7,3},{8,12},{12,8},{9,1... | collective-permute-start | bytes 1179656 | tf_op jit(solution)/shard_map/ppermute | solution.py:170
  26.7 13.5 %collective-permute-done.1.refs_2_ = bf16[3,256,256]{2,1,0:T(8,128)(2,1)S(1)} collective-permute-done((bf16[3,256,256]{2,1,0:T(8,128)(2,1)S(1)}, bf16[3,256,256]{2,1,0:T(8,128)(2,1)S(1)}, u32[]{:S(2)}, u32[]{:S(2)}) %collective-permute-start.1) | collective-permute-done | bytes 393248 | tf_op jit(solution)/shard_map/ppermute | solution.py:170
  40.1 1.5 %collective-permute-start.5 = (bf16[3,256,256]{2,1,0:T(8,128)(2,1)S(1)}, bf16[3,256,256]{2,1,0:T(8,128)(2,1)S(1)}, u32[]{:S(2)}, u32[]{:S(2)}) collective-permute-start(bf16[3,256,256]{2,1,0:T(8,128)(2,1)S(1)} %collective-permute-done.1.refs_2_), channel_id=1, source_target_pairs={{0,4},{4,0},{1,5},{5,1},{2,6},{6,2},{3,7},{7,3},{8,12},{12,8},{9,1... | collective-permute-start | bytes 1179656 | tf_op jit(solution)/shard_map/ppermute | solution.py:170
  41.7 0.7 fusion.2
  42.3 0.1 concatenate.7.scalars
  42.4 0.0 collective-permute-done.3.refs_4_
  42.4 0.0 collective-permute-done.6.refs_7_
  42.4 0.0 collective-permute-done.4.refs_5_
  42.4 7.9 %collective-permute-done.5.refs_6_ = bf16[3,256,256]{2,1,0:T(8,128)(2,1)S(1)} collective-permute-done((bf16[3,256,256]{2,1,0:T(8,128)(2,1)S(1)}, bf16[3,256,256]{2,1,0:T(8,128)(2,1)S(1)}, u32[]{:S(2)}, u32[]{:S(2)}) %collective-permute-start.5) | collective-permute-done | bytes 393248 | tf_op jit(solution)/shard_map/ppermute | solution.py:170
  50.3 2.0 %tiles_first.1 = (bf16[8,256,768]{2,1,0:T(8,128)(2,1)S(1)}, f32[2,2,3,64,256]{4,3,2,1,0:T(8,128)S(1)}, f32[2,2,3,64,256]{4,3,2,1,0:T(8,128)S(1)}) custom-call(s32[40]{0:T(128)S(1)} %concatenate.7.scalars, bf16[3,256,256]{2,1,0:T(8,128)(2,1)S(1)} %get-tuple-element.100.refs_0_, bf16[3,256,256]{2,1,0:T(8,128)(2,1)S(1)} %collective-permute-done.refs_1_, ...), custom_call_target="tpu_custom_call" | custom-call | flops 603979776 | bytes 4194304 | tf_op jit(solution)/shard_map/tiles_first/pallas_call | solution.py:207
  52.3 0.1 collective-permute-start.7
  52.4 3.1 %tiles_second.1 = (f32[2,2,3,64,256]{4,3,2,1,0:T(8,128)S(1)}, f32[2,2,3,64,256]{4,3,2,1,0:T(8,128)S(1)}, f32[2,2,3,64,256]{4,3,2,1,0:T(8,128)S(1)}, f32[2,2,3,64,256]{4,3,2,1,0:T(8,128)S(1)}) custom-call(s32[40]{0:T(128)S(1)} %concatenate.7.scalars, bf16[8,256,768]{2,1,0:T(8,128)(2,1)S(1)} %get-tuple-element.55.blocks), custom_call_target="tpu_custom_call" | custom-call | flops 1207959552 | bytes 4194304 | tf_op jit(solution)/shard_map/tiles_second/pallas_call | solution.py:207
  55.5 0.6 collective-permute-start.10
  56.0 0.1 collective-permute-start.9
  56.1 0.0 collective-permute-done.7.right
  56.1 0.1 sum_core.3
  56.2 1.6 %collective-permute-start.8 = (f32[2,3,64,256]{3,2,1,0:T(8,128)S(1)}, f32[2,3,64,256]{3,2,1,0:T(8,128)S(1)}, u32[]{:S(2)}, u32[]{:S(2)}) collective-permute-start(f32[2,3,64,256]{3,2,1,0:T(8,128)S(1)} %get-tuple-element.54), channel_id=1, source_target_pairs={{0,2},{2,0},{1,3},{3,1},{4,6},{6,4},{5,7},{7,5},{8,10},{10,8},{9,1... | collective-permute-start | bytes 1179656 | tf_op jit(solution)/shard_map/ppermute | solution.py:170
  57.7 0.2 collective-permute-done.10.right
  57.9 0.1 sum_core.4
  58.0 1.6 %collective-permute-start.13 = (f32[2,3,64,256]{3,2,1,0:T(8,128)S(1)}, f32[2,3,64,256]{3,2,1,0:T(8,128)S(1)}, u32[]{:S(2)}, u32[]{:S(2)}) collective-permute-start(f32[2,3,64,256]{3,2,1,0:T(8,128)S(1)} %get-tuple-element.72), channel_id=1, source_target_pairs={{0,2},{2,0},{1,3},{3,1},{4,6},{6,4},{5,7},{7,5},{8,10},{10,8},{9,1... | collective-permute-start | bytes 1179656 | tf_op jit(solution)/shard_map/ppermute | solution.py:170
  59.6 0.0 collective-permute-done.9.right
  59.6 0.1 sum_core.5
  59.7 8.5 %collective-permute-done.8.right = f32[2,3,64,256]{3,2,1,0:T(8,128)S(1)} collective-permute-done((f32[2,3,64,256]{3,2,1,0:T(8,128)S(1)}, f32[2,3,64,256]{3,2,1,0:T(8,128)S(1)}, u32[]{:S(2)}, u32[]{:S(2)}) %collective-permute-start.8) | collective-permute-done | bytes 393248 | tf_op jit(solution)/shard_map/ppermute | solution.py:170
  68.2 0.1 sum_x.3
  68.2 0.6 collective-permute-start.11
  68.9 1.5 %collective-permute-start.16 = (f32[2,3,64,256]{3,2,1,0:T(8,128)S(1)}, f32[2,3,64,256]{3,2,1,0:T(8,128)S(1)}, u32[]{:S(2)}, u32[]{:S(2)}) collective-permute-start(f32[2,3,64,256]{3,2,1,0:T(8,128)S(1)} %get-tuple-element.81), channel_id=1, source_target_pairs={{0,2},{2,0},{1,3},{3,1},{4,6},{6,4},{5,7},{7,5},{8,10},{10,8},{9,1... | collective-permute-start | bytes 1179656 | tf_op jit(solution)/shard_map/ppermute | solution.py:170
  70.3 4.0 %collective-permute-done.11.right = f32[3,64,256]{2,1,0:T(8,128)S(1)} collective-permute-done((f32[3,64,256]{2,1,0:T(8,128)S(1)}, f32[3,64,256]{2,1,0:T(8,128)S(1)}, u32[]{:S(2)}, u32[]{:S(2)}) %collective-permute-start.11) | collective-permute-done | bytes 196640 | tf_op jit(solution)/shard_map/ppermute | solution.py:170
  74.3 1.5 %collective-permute-start.12 = (f32[3,64,256]{2,1,0:T(8,128)S(1)}, f32[3,64,256]{2,1,0:T(8,128)S(1)}, u32[]{:S(2)}, u32[]{:S(2)}) collective-permute-start(f32[3,64,256]{2,1,0:T(8,128)S(1)} %sum_z.3.left), channel_id=1, source_target_pairs={{0,16},{8,24},{16,0},{24,8},{1,17},{9,25},{17,1},{25,9},{2,18},{10... | collective-permute-start | bytes 589832 | tf_op jit(solution)/shard_map/ppermute | solution.py:170
  75.8 0.8 collective-permute-done.13.right
  76.6 0.7 collective-permute-start.14
  77.4 7.3 %collective-permute-done.12.right = f32[3,64,256]{2,1,0:T(8,128)S(1)} collective-permute-done((f32[3,64,256]{2,1,0:T(8,128)S(1)}, f32[3,64,256]{2,1,0:T(8,128)S(1)}, u32[]{:S(2)}, u32[]{:S(2)}) %collective-permute-start.12) | collective-permute-done | bytes 196640 | tf_op jit(solution)/shard_map/ppermute | solution.py:170
  84.7 2.0 %collective-permute-done.14.right = f32[3,64,256]{2,1,0:T(8,128)S(1)} collective-permute-done((f32[3,64,256]{2,1,0:T(8,128)S(1)}, f32[3,64,256]{2,1,0:T(8,128)S(1)}, u32[]{:S(2)}, u32[]{:S(2)}) %collective-permute-start.14) | collective-permute-done | bytes 196640 | tf_op jit(solution)/shard_map/ppermute | solution.py:170
  86.7 0.4 collective-permute-start.15
  87.2 0.0 collective-permute-done.16.right
  87.2 2.5 %collective-permute-start.17 = (f32[3,64,256]{2,1,0:T(8,128)S(1)}, f32[3,64,256]{2,1,0:T(8,128)S(1)}, u32[]{:S(2)}, u32[]{:S(2)}) collective-permute-start(f32[3,64,256]{2,1,0:T(8,128)S(1)} %get-tuple-element.85), channel_id=1, source_target_pairs={{0,8},{8,0},{16,24},{24,16},{1,9},{9,1},{17,25},{25,17},{2,10},{10... | collective-permute-start | bytes 589832 | tf_op jit(solution)/shard_map/ppermute | solution.py:170
  89.8 0.0 copy-done
  89.8 9.4 %collective-permute-done.17.right = f32[3,64,256]{2,1,0:T(8,128)S(1)} collective-permute-done((f32[3,64,256]{2,1,0:T(8,128)S(1)}, f32[3,64,256]{2,1,0:T(8,128)S(1)}, u32[]{:S(2)}, u32[]{:S(2)}) %collective-permute-start.17) | collective-permute-done | bytes 196640 | tf_op jit(solution)/shard_map/ppermute | solution.py:170
  99.2 0.1 collective-permute-start.21
  99.3 0.0 collective-permute-done.15.refs_2_
  99.3 0.3 finish.2.refs_0_
  99.6 2.0 %collective-permute-start.20 = (s16[400,256]{1,0:T(8,128)(2,1)S(1)}, s16[400,256]{1,0:T(8,128)(2,1)S(1)}, u32[]{:S(2)}, u32[]{:S(2)}) collective-permute-start(s16[400,256]{1,0:T(8,128)(2,1)S(1)} %finish.2.refs_0_), channel_id=1, source_target_pairs={{0,12},{4,8},{8,4},{12,0},{16,28},{20,24},{24,20},{28,16},{1,13},{... | collective-permute-start | bytes 614408 | tf_op jit(solution)/shard_map/ppermute | solution.py:289
  101.6 0.6 collective-permute-start.19
  102.2 1.1 collective-permute-start.18
  103.3 3.8 %collective-permute-done.21.refs_1_ = f32[3,64,256]{2,1,0:T(8,128)S(1)} collective-permute-done((f32[3,64,256]{2,1,0:T(8,128)S(1)}, f32[3,64,256]{2,1,0:T(8,128)S(1)}, u32[]{:S(2)}, u32[]{:S(2)}) %collective-permute-start.21) | collective-permute-done | bytes 196640 | tf_op jit(solution)/shard_map/ppermute | solution.py:170
  107.0 0.2 finish.3.refs_4_
  107.3 0.5 collective-permute-start.24
  107.8 1.2 collective-permute-start.23
  108.9 1.8 %collective-permute-done.20.refs_3_ = s16[400,256]{1,0:T(8,128)(2,1)S(1)} collective-permute-done((s16[400,256]{1,0:T(8,128)(2,1)S(1)}, s16[400,256]{1,0:T(8,128)(2,1)S(1)}, u32[]{:S(2)}, u32[]{:S(2)}) %collective-permute-start.20) | collective-permute-done | bytes 204832 | tf_op jit(solution)/shard_map/ppermute | solution.py:289
  110.8 1.8 %collective-permute-start.22 = (s16[208,256]{1,0:T(8,128)(2,1)S(1)}, s16[208,256]{1,0:T(8,128)(2,1)S(1)}, u32[]{:S(2)}, u32[]{:S(2)}) collective-permute-start(s16[208,256]{1,0:T(8,128)(2,1)S(1)} %finish.3.refs_4_), channel_id=1, source_target_pairs={{0,8},{8,0},{16,24},{24,16},{1,9},{9,1},{17,25},{25,17},{2,10},{10... | collective-permute-start | bytes 319496 | tf_op jit(solution)/shard_map/ppermute | solution.py:170
  112.6 0.1 concatenate.6.scalars
  112.6 0.0 collective-permute-done.19.refs_2_
  112.7 2.3 %collective-permute-done.18.refs_1_ = s16[400,256]{1,0:T(8,128)(2,1)S(1)} collective-permute-done((s16[400,256]{1,0:T(8,128)(2,1)S(1)}, s16[400,256]{1,0:T(8,128)(2,1)S(1)}, u32[]{:S(2)}, u32[]{:S(2)}) %collective-permute-start.18) | collective-permute-done | bytes 204832 | tf_op jit(solution)/shard_map/ppermute | solution.py:170
  114.9 2.1 %collective-permute-done.24.refs_7_ = s16[208,256]{1,0:T(8,128)(2,1)S(1)} collective-permute-done((s16[208,256]{1,0:T(8,128)(2,1)S(1)}, s16[208,256]{1,0:T(8,128)(2,1)S(1)}, u32[]{:S(2)}, u32[]{:S(2)}) %collective-permute-start.24) | collective-permute-done | bytes 106528 | tf_op jit(solution)/shard_map/ppermute | solution.py:289
  117.0 0.0 collective-permute-done.23.refs_6_
  117.1 0.7 collective-permute-done.22.refs_5_
  117.7 2.4 %place_tiles.1 = f32[10,64,256]{2,1,0:T(8,128)} custom-call(s32[50]{0:T(128)S(1)} %concatenate.6.scalars, s16[400,256]{1,0:T(8,128)(2,1)S(1)} %finish.2.refs_0_, s16[400,256]{1,0:T(8,128)(2,1)S(1)} %collective-permute-done.18.refs_1_, s16[400,256]{1,0:T(8,128)(2,1)S(1)} %collective-permute-done.19.refs_2_, ...), custom_call_target="tpu_custom_call" | custom-call | flops 163840 | tf_op jit(solution)/shard_map/place_tiles/pallas_call | solution.py:336
  (10 shorter events, 0.2 us)
Async XLA Ops:
  1.5 15.1 %collective-permute-start.2 = (bf16[3,256,256]{2,1,0:T(8,128)(2,1)S(1)}, bf16[3,256,256]{2,1,0:T(8,128)(2,1)S(1)}, u32[]{:S(2)}, u32[]{:S(2)}) collective-permute-start(bf16[3,256,256]{2,1,0:T(8,128)(2,1)S(1)} %get-tuple-element.98), channel_id=1, source_target_pairs={{0,24},{8,16},{16,8},{24,0},{1,25},{9,17},{17,9},{25,1},{2,26},{10... | collective-permute-start | bytes 1179656 | tf_op jit(solution)/shard_map/ppermute | solution.py:170
  6.6 18.7 %collective-permute-start = (bf16[3,256,256]{2,1,0:T(8,128)(2,1)S(1)}, bf16[3,256,256]{2,1,0:T(8,128)(2,1)S(1)}, u32[]{:S(2)}, u32[]{:S(2)}) collective-permute-start(bf16[3,256,256]{2,1,0:T(8,128)(2,1)S(1)} %get-tuple-element.99), channel_id=1, source_target_pairs={{0,8},{8,0},{16,24},{24,16},{1,9},{9,1},{17,25},{25,17},{2,10},{10... | collective-permute-start | bytes 1179656 | tf_op jit(solution)/shard_map/ppermute | solution.py:170
  6.6 33.5 %collective-permute-start.1 = (bf16[3,256,256]{2,1,0:T(8,128)(2,1)S(1)}, bf16[3,256,256]{2,1,0:T(8,128)(2,1)S(1)}, u32[]{:S(2)}, u32[]{:S(2)}) collective-permute-start(bf16[3,256,256]{2,1,0:T(8,128)(2,1)S(1)} %get-tuple-element.101), channel_id=1, source_target_pairs={{0,16},{8,24},{16,0},{24,8},{1,17},{9,25},{17,1},{25,9},{2,18},{10... | collective-permute-start | bytes 1179656 | tf_op jit(solution)/shard_map/ppermute | solution.py:170
  7.2 35.2 %collective-permute-start.3 = (bf16[3,256,256]{2,1,0:T(8,128)(2,1)S(1)}, bf16[3,256,256]{2,1,0:T(8,128)(2,1)S(1)}, u32[]{:S(2)}, u32[]{:S(2)}) collective-permute-start(bf16[3,256,256]{2,1,0:T(8,128)(2,1)S(1)} %get-tuple-element.100.refs_0_), channel_id=1, source_target_pairs={{0,4},{4,0},{1,5},{5,1},{2,6},{6,2},{3,7},{7,3},{8,12},{12,8},{9,1... | collective-permute-start | bytes 1179656 | tf_op jit(solution)/shard_map/ppermute | solution.py:170
  16.6 25.8 %collective-permute-start.6 = (bf16[3,256,256]{2,1,0:T(8,128)(2,1)S(1)}, bf16[3,256,256]{2,1,0:T(8,128)(2,1)S(1)}, u32[]{:S(2)}, u32[]{:S(2)}) collective-permute-start(bf16[3,256,256]{2,1,0:T(8,128)(2,1)S(1)} %collective-permute-done.2.refs_3_), channel_id=1, source_target_pairs={{0,4},{4,0},{1,5},{5,1},{2,6},{6,2},{3,7},{7,3},{8,12},{12,8},{9,1... | collective-permute-start | bytes 1179656 | tf_op jit(solution)/shard_map/ppermute | solution.py:170
  25.3 17.2 %collective-permute-start.4 = (bf16[3,256,256]{2,1,0:T(8,128)(2,1)S(1)}, bf16[3,256,256]{2,1,0:T(8,128)(2,1)S(1)}, u32[]{:S(2)}, u32[]{:S(2)}) collective-permute-start(bf16[3,256,256]{2,1,0:T(8,128)(2,1)S(1)} %collective-permute-done.refs_1_), channel_id=1, source_target_pairs={{0,4},{4,0},{1,5},{5,1},{2,6},{6,2},{3,7},{7,3},{8,12},{12,8},{9,1... | collective-permute-start | bytes 1179656 | tf_op jit(solution)/shard_map/ppermute | solution.py:170
  40.1 10.2 %collective-permute-start.5 = (bf16[3,256,256]{2,1,0:T(8,128)(2,1)S(1)}, bf16[3,256,256]{2,1,0:T(8,128)(2,1)S(1)}, u32[]{:S(2)}, u32[]{:S(2)}) collective-permute-start(bf16[3,256,256]{2,1,0:T(8,128)(2,1)S(1)} %collective-permute-done.1.refs_2_), channel_id=1, source_target_pairs={{0,4},{4,0},{1,5},{5,1},{2,6},{6,2},{3,7},{7,3},{8,12},{12,8},{9,1... | collective-permute-start | bytes 1179656 | tf_op jit(solution)/shard_map/ppermute | solution.py:170
  52.3 3.8 %collective-permute-start.7 = (f32[2,2,3,64,256]{4,3,2,1,0:T(8,128)S(1)}, f32[2,2,3,64,256]{4,3,2,1,0:T(8,128)S(1)}, u32[]{:S(2)}, u32[]{:S(2)}) collective-permute-start(f32[2,2,3,64,256]{4,3,2,1,0:T(8,128)S(1)} %get-tuple-element.50), channel_id=1, source_target_pairs={{0,1},{1,0},{2,3},{3,2},{4,5},{5,4},{6,7},{7,6},{8,9},{9,8},{10,11... | collective-permute-start | bytes 2359304 | tf_op jit(solution)/shard_map/ppermute | solution.py:170
  55.5 2.5 %collective-permute-start.10 = (f32[2,2,3,64,256]{4,3,2,1,0:T(8,128)S(1)}, f32[2,2,3,64,256]{4,3,2,1,0:T(8,128)S(1)}, u32[]{:S(2)}, u32[]{:S(2)}) collective-permute-start(f32[2,2,3,64,256]{4,3,2,1,0:T(8,128)S(1)} %get-tuple-element.59), channel_id=1, source_target_pairs={{0,1},{1,0},{2,3},{3,2},{4,5},{5,4},{6,7},{7,6},{8,9},{9,8},{10,11... | collective-permute-start | bytes 2359304 | tf_op jit(solution)/shard_map/ppermute | solution.py:170
  56.0 3.6 %collective-permute-start.9 = (f32[2,2,3,64,256]{4,3,2,1,0:T(8,128)S(1)}, f32[2,2,3,64,256]{4,3,2,1,0:T(8,128)S(1)}, u32[]{:S(2)}, u32[]{:S(2)}) collective-permute-start(f32[2,2,3,64,256]{4,3,2,1,0:T(8,128)S(1)} %get-tuple-element.57), channel_id=1, source_target_pairs={{0,1},{1,0},{2,3},{3,2},{4,5},{5,4},{6,7},{7,6},{8,9},{9,8},{10,11... | collective-permute-start | bytes 2359304 | tf_op jit(solution)/shard_map/ppermute | solution.py:170
  56.2 12.0 %collective-permute-start.8 = (f32[2,3,64,256]{3,2,1,0:T(8,128)S(1)}, f32[2,3,64,256]{3,2,1,0:T(8,128)S(1)}, u32[]{:S(2)}, u32[]{:S(2)}) collective-permute-start(f32[2,3,64,256]{3,2,1,0:T(8,128)S(1)} %get-tuple-element.54), channel_id=1, source_target_pairs={{0,2},{2,0},{1,3},{3,1},{4,6},{6,4},{5,7},{7,5},{8,10},{10,8},{9,1... | collective-permute-start | bytes 1179656 | tf_op jit(solution)/shard_map/ppermute | solution.py:170
  58.0 18.6 %collective-permute-start.13 = (f32[2,3,64,256]{3,2,1,0:T(8,128)S(1)}, f32[2,3,64,256]{3,2,1,0:T(8,128)S(1)}, u32[]{:S(2)}, u32[]{:S(2)}) collective-permute-start(f32[2,3,64,256]{3,2,1,0:T(8,128)S(1)} %get-tuple-element.72), channel_id=1, source_target_pairs={{0,2},{2,0},{1,3},{3,1},{4,6},{6,4},{5,7},{7,5},{8,10},{10,8},{9,1... | collective-permute-start | bytes 1179656 | tf_op jit(solution)/shard_map/ppermute | solution.py:170
  68.2 6.1 %collective-permute-start.11 = (f32[3,64,256]{2,1,0:T(8,128)S(1)}, f32[3,64,256]{2,1,0:T(8,128)S(1)}, u32[]{:S(2)}, u32[]{:S(2)}) collective-permute-start(f32[3,64,256]{2,1,0:T(8,128)S(1)} %get-tuple-element.69), channel_id=1, source_target_pairs={{0,8},{8,0},{16,24},{24,16},{1,9},{9,1},{17,25},{25,17},{2,10},{10... | collective-permute-start | bytes 589832 | tf_op jit(solution)/shard_map/ppermute | solution.py:170
  68.9 18.3 %collective-permute-start.16 = (f32[2,3,64,256]{3,2,1,0:T(8,128)S(1)}, f32[2,3,64,256]{3,2,1,0:T(8,128)S(1)}, u32[]{:S(2)}, u32[]{:S(2)}) collective-permute-start(f32[2,3,64,256]{3,2,1,0:T(8,128)S(1)} %get-tuple-element.81), channel_id=1, source_target_pairs={{0,2},{2,0},{1,3},{3,1},{4,6},{6,4},{5,7},{7,5},{8,10},{10,8},{9,1... | collective-permute-start | bytes 1179656 | tf_op jit(solution)/shard_map/ppermute | solution.py:170
  74.3 15.5 %copy-start = (s32[1,10,2]{1,2,0:T(2,128)S(1)}, s32[1,10,2]{1,2,0:T(2,128)}, u32[]{:S(2)}) copy-start(s32[1,10,2]{1,2,0:T(2,128)} %param.4) | copy-start | bytes 244
  74.3 10.4 %collective-permute-start.12 = (f32[3,64,256]{2,1,0:T(8,128)S(1)}, f32[3,64,256]{2,1,0:T(8,128)S(1)}, u32[]{:S(2)}, u32[]{:S(2)}) collective-permute-start(f32[3,64,256]{2,1,0:T(8,128)S(1)} %sum_z.3.left), channel_id=1, source_target_pairs={{0,16},{8,24},{16,0},{24,8},{1,17},{9,25},{17,1},{25,9},{2,18},{10... | collective-permute-start | bytes 589832 | tf_op jit(solution)/shard_map/ppermute | solution.py:170
  76.6 10.1 %collective-permute-start.14 = (f32[3,64,256]{2,1,0:T(8,128)S(1)}, f32[3,64,256]{2,1,0:T(8,128)S(1)}, u32[]{:S(2)}, u32[]{:S(2)}) collective-permute-start(f32[3,64,256]{2,1,0:T(8,128)S(1)} %get-tuple-element.78), channel_id=1, source_target_pairs={{0,8},{8,0},{16,24},{24,16},{1,9},{9,1},{17,25},{25,17},{2,10},{10... | collective-permute-start | bytes 589832 | tf_op jit(solution)/shard_map/ppermute | solution.py:170
  86.7 12.5 %collective-permute-start.15 = (f32[3,64,256]{2,1,0:T(8,128)S(1)}, f32[3,64,256]{2,1,0:T(8,128)S(1)}, u32[]{:S(2)}, u32[]{:S(2)}) collective-permute-start(f32[3,64,256]{2,1,0:T(8,128)S(1)} %sum_z.4.refs_1_), channel_id=1, source_target_pairs={{0,16},{8,24},{16,0},{24,8},{1,17},{9,25},{17,1},{25,9},{2,18},{10... | collective-permute-start | bytes 589832 | tf_op jit(solution)/shard_map/ppermute | solution.py:170
  87.2 12.0 %collective-permute-start.17 = (f32[3,64,256]{2,1,0:T(8,128)S(1)}, f32[3,64,256]{2,1,0:T(8,128)S(1)}, u32[]{:S(2)}, u32[]{:S(2)}) collective-permute-start(f32[3,64,256]{2,1,0:T(8,128)S(1)} %get-tuple-element.85), channel_id=1, source_target_pairs={{0,8},{8,0},{16,24},{24,16},{1,9},{9,1},{17,25},{25,17},{2,10},{10... | collective-permute-start | bytes 589832 | tf_op jit(solution)/shard_map/ppermute | solution.py:170
  99.2 7.8 %collective-permute-start.21 = (f32[3,64,256]{2,1,0:T(8,128)S(1)}, f32[3,64,256]{2,1,0:T(8,128)S(1)}, u32[]{:S(2)}, u32[]{:S(2)}) collective-permute-start(f32[3,64,256]{2,1,0:T(8,128)S(1)} %sum_z.5.refs_0_), channel_id=1, source_target_pairs={{0,16},{8,24},{16,0},{24,8},{1,17},{9,25},{17,1},{25,9},{2,18},{10... | collective-permute-start | bytes 589832 | tf_op jit(solution)/shard_map/ppermute | solution.py:170
  99.6 11.1 %collective-permute-start.20 = (s16[400,256]{1,0:T(8,128)(2,1)S(1)}, s16[400,256]{1,0:T(8,128)(2,1)S(1)}, u32[]{:S(2)}, u32[]{:S(2)}) collective-permute-start(s16[400,256]{1,0:T(8,128)(2,1)S(1)} %finish.2.refs_0_), channel_id=1, source_target_pairs={{0,12},{4,8},{8,4},{12,0},{16,28},{20,24},{24,20},{28,16},{1,13},{... | collective-permute-start | bytes 614408 | tf_op jit(solution)/shard_map/ppermute | solution.py:289
  101.6 11.0 %collective-permute-start.19 = (s16[400,256]{1,0:T(8,128)(2,1)S(1)}, s16[400,256]{1,0:T(8,128)(2,1)S(1)}, u32[]{:S(2)}, u32[]{:S(2)}) collective-permute-start(s16[400,256]{1,0:T(8,128)(2,1)S(1)} %finish.2.refs_0_), channel_id=1, source_target_pairs={{0,4},{4,0},{1,5},{5,1},{2,6},{6,2},{3,7},{7,3},{8,12},{12,8},{9,1... | collective-permute-start | bytes 614408 | tf_op jit(solution)/shard_map/ppermute | solution.py:170
  102.2 12.7 %collective-permute-start.18 = (s16[400,256]{1,0:T(8,128)(2,1)S(1)}, s16[400,256]{1,0:T(8,128)(2,1)S(1)}, u32[]{:S(2)}, u32[]{:S(2)}) collective-permute-start(s16[400,256]{1,0:T(8,128)(2,1)S(1)} %finish.2.refs_0_), channel_id=1, source_target_pairs={{0,8},{8,0},{16,24},{24,16},{1,9},{9,1},{17,25},{25,17},{2,10},{10... | collective-permute-start | bytes 614408 | tf_op jit(solution)/shard_map/ppermute | solution.py:170
  107.3 9.8 %collective-permute-start.24 = (s16[208,256]{1,0:T(8,128)(2,1)S(1)}, s16[208,256]{1,0:T(8,128)(2,1)S(1)}, u32[]{:S(2)}, u32[]{:S(2)}) collective-permute-start(s16[208,256]{1,0:T(8,128)(2,1)S(1)} %finish.3.refs_4_), channel_id=1, source_target_pairs={{0,12},{4,8},{8,4},{12,0},{16,28},{20,24},{24,20},{28,16},{1,13},{... | collective-permute-start | bytes 319496 | tf_op jit(solution)/shard_map/ppermute | solution.py:289
  107.8 9.3 %collective-permute-start.23 = (s16[208,256]{1,0:T(8,128)(2,1)S(1)}, s16[208,256]{1,0:T(8,128)(2,1)S(1)}, u32[]{:S(2)}, u32[]{:S(2)}) collective-permute-start(s16[208,256]{1,0:T(8,128)(2,1)S(1)} %finish.3.refs_4_), channel_id=1, source_target_pairs={{0,4},{4,0},{1,5},{5,1},{2,6},{6,2},{3,7},{7,3},{8,12},{12,8},{9,1... | collective-permute-start | bytes 319496 | tf_op jit(solution)/shard_map/ppermute | solution.py:170
  110.8 6.9 %collective-permute-start.22 = (s16[208,256]{1,0:T(8,128)(2,1)S(1)}, s16[208,256]{1,0:T(8,128)(2,1)S(1)}, u32[]{:S(2)}, u32[]{:S(2)}) collective-permute-start(s16[208,256]{1,0:T(8,128)(2,1)S(1)} %finish.3.refs_4_), channel_id=1, source_target_pairs={{0,8},{8,0},{16,24},{24,16},{1,9},{9,1},{17,25},{25,17},{2,10},{10... | collective-permute-start | bytes 319496 | tf_op jit(solution)/shard_map/ppermute | solution.py:170

commit v9 on v8

--- a/solution.py
+++ b/solution.py
@@ -13,8 +13,9 @@
 GROUPS = 3
 BATCHES = ((0, 1), (2,))
 ORDER = (
-    ("x", 0), ("low", 0), ("x", 1), ("high", 0), ("low", 1),
-    ("x", 2), ("low", 2), ("finish", BATCHES[0]), ("finish", BATCHES[1]),
+    ("tiles", None), ("core", 0), ("core", 1), ("core", 2),
+    ("x", 0), ("low", 0), ("x", 1), ("high", 0), ("low", 1), ("x", 2), ("high", 1), ("low", 2),
+    ("finish", BATCHES[0]), ("relay", None), ("finish", BATCHES[1]),
 )
 CODE_TOP = 32767.0
 SCALE_ROWS = 16
@@ -122,11 +123,17 @@
     code[:SCALE_ROWS, :] = header.astype(jnp.int32).astype(jnp.int16)
 
 
+def pair_kernel(own, arrived, out):
+    out[0] = own[...]
+    out[1] = arrived[...]
+
+
 def place_kernel(factor, scalars, *refs):
     out, codes, headers = refs[-3:]
     slots, rows, columns = out.shape
     at = 0
-    for index, part in enumerate(refs[:-3]):
+    parts = [part.at[index] for part in refs[:-3] for index in range(part.shape[0])]
+    for index, part in enumerate(parts):
         count = part.shape[0] - SCALE_ROWS
         start = index * SCALE_ROWS
         headers[start : start + SCALE_ROWS, :] = (
@@ -212,7 +219,7 @@
             compiler_params=pltpu.CompilerParams(vmem_limit_bytes=VMEM_LIMIT),
             cost_estimate=pl.CostEstimate(
                 flops=4 * size * block_size * block_size * components * cells,
-                bytes_accessed=4 * 2**20,
+                bytes_accessed=0,
                 transcendentals=0,
             ),
             name=name,
@@ -229,14 +236,6 @@
         chunks,
         "tiles_first",
     )
-    sums += call(
-        functools.partial(second_kernel, 4 + 4 * sizes[0]),
-        sum(sizes[1:]),
-        shapes[2:],
-        [blocks],
-        "tiles_second",
-    )
-
     last = []
 
     def step_call(kernel, out_shape, *operands, name):
@@ -260,7 +259,8 @@
         return jax.ShapeDtypeStruct((*shape, rows_dev, block_size), jnp.float32)
 
     def sum_core(index):
-        keep, send = sums[2 * index], swap(sums[2 * index + 1], "core", 1)
+        keep, send = sums[2 * index : 2 * index + 2]
+        send = swap(send, "core", 1)
         shapes = [float_shape(2, sizes[index])] * x_count
         mine, *away = step_call(split_sum_kernel, shapes, keep, send, name="sum_core")
         return mine, [swap(value, "x", step + 1) for step, value in enumerate(away)]
@@ -284,15 +284,20 @@
             bits *= 2
         return mine, swap(mine, "z", bits)
 
-    def to_owners(value):
-        both = [(i, i ^ (y_count + 1)) for i in range(block_count)]
-        over_both = lax.ppermute(value, ("z", "y"), both)
-        return [value, swap(value, "z", 1), swap(value, "y", 1), over_both]
-
     parts = []
-    state = [sum_core(index) for index in range(GROUPS)]
+    state = {}
     for stage, which in ORDER:
-        if stage == "x":
+        if stage == "core":
+            state[which] = sum_core(which)
+        elif stage == "tiles":
+            sums += call(
+                functools.partial(second_kernel, 4 + 4 * sizes[0]),
+                sum(sizes[1:]),
+                shapes[2:],
+                [blocks],
+                "tiles_second",
+            )
+        elif stage == "x":
             state[which] = sum_x(which, *state[which])
         elif stage == "low":
             state[which] = sum_low(which, *state[which])
@@ -300,7 +305,7 @@
             state[which] = step_call(
                 sum_kernel, [float_shape(sizes[which])], *state[which], name="sum_high"
             )
-        else:
+        elif stage == "finish":
             counts = [sizes[index] for index in which]
             shape = (SCALE_ROWS + sum(counts) * rows_dev, block_size)
             kernel = functools.partial(code_kernel, counts, [len(state[i]) for i in which])
@@ -308,7 +313,15 @@
             (code,) = step_call(
                 kernel, [jax.ShapeDtypeStruct(shape, jnp.int16)], *operands, name="finish"
             )
-            parts += to_owners(code)
+            over_z = swap(code, "z", 1)
+            if which == BATCHES[-1]:
+                both = [(i, i ^ (y_count + 1)) for i in range(block_count)]
+                over_both = lax.ppermute(code, ("z", "y"), both)
+                parts += [part[None] for part in (code, over_z, swap(code, "y", 1), over_both)]
+        else:
+            shape = jax.ShapeDtypeStruct((2, *code.shape), code.dtype)
+            (pair,) = step_call(pair_kernel, [shape], code, over_z, name="pair")
+            parts += [pair, swap(pair, "y", 1)]
 
     table = tile_table[0]
     row_block = table[:, 0]
@@ -340,7 +353,7 @@
         out_specs=vmem,
         scratch_shapes=[
             pltpu.VMEM((4 * quarter * rows_dev, block_size), jnp.int16),
-            pltpu.VMEM((len(parts) * SCALE_ROWS, block_size), jnp.float32),
+            pltpu.VMEM((4 * len(BATCHES) * SCALE_ROWS, block_size), jnp.float32),
         ],
         compiler_params=pltpu.CompilerParams(vmem_limit_bytes=VMEM_LIMIT),
         cost_estimate=pl.CostEstimate(

time: 120 us -> 126 us (1.050)
  waiting for transfers between devices: 78.8 us -> 84.3 us
    ppermute x23, waiting for transfers between devices: 74.8 us -> 82.2 us  [swap(): return lax.ppermute(value, axis, [(i, i ^ bits) for i in range(size)])]
    ppermute x23, starting transfers between devices: 27.9 us -> 29.9 us  [swap(): return lax.ppermute(value, axis, [(i, i ^ bits) for i in range(size)])]
    ppermute x2 -> x1, waiting for transfers between devices: 3.96 us -> 2.14 us  [per_device(): over_both = lax.ppermute(code, ('z', 'y'), both)]
    ppermute x2 -> x1, starting transfers between devices: 2.45 us -> 0.65 us  [per_device(): over_both = lax.ppermute(code, ('z', 'y'), both)]
  transfers between devices with their start and end apart: 25 -> 24, of which waited for: 16 -> 16; matrix products, arithmetic and copies ran while one was open for 1% -> 1% of each run, Pallas kernels for 3% -> 3%
where the time goes in v9:
time: 126 us
  waiting for transfers between devices  84.3 us (67%)
  starting transfers between devices  30.5 us (24%)
  Pallas kernels  8.58 us (7%)
  local copies, waits for them, and re-layouts  2.33 us (2%)
    ppermute x23, waiting for transfers between devices, swap(): return lax.ppermute(value, axis, [(i, i ^ bits) for i in range(size)])  82.2 us
    ppermute x23, starting transfers between devices, swap(): return lax.ppermute(value, axis, [(i, i ^ bits) for i in range(size)])  29.9 us
    pallas_call x2, Pallas kernels, call(): pl.pallas_call(kernel, out_shape=out_shape, in_specs=[pl.BlockSpec(memory...  5.06 us
  transfers between devices with their start and end apart: 24, of which 16 were waited for; matrix products, arithmetic and copies ran while one was open for 1% of the time, Pallas kernels for 3%

profile of v9, /device:TPU:0, one launch (start us, length us, event | category | flops | bytes accessed | tf_op | source)
XLA Modules:
  0.0 125.9 jit_solution(2387090796965265186)
XLA Ops:
  0.0 1.5 %constant_dynamic-slice_fusion = (bf16[3,256,256]{2,1,0:T(8,128)(2,1)S(1)}, bf16[3,256,256]{2,1,0:T(8,128)(2,1)S(1)}, bf16[3,256,256]{2,1,0:T(8,128)(2,1)S(1)}, bf16[3,256,256]{2,1,0:T(8,128)(2,1)S(1)}) fusion(bf16[3,256,1024]{2,1,0:T(8,128)(2,1)} %param.3, s32[]{:T(128)S(6)} %select_n.97, s32[]{:T(128)S(6)} %select_n.95, s32[]{:T(128)S(6)} %select_n.94, ...), kind=kLoop, calls=%fused_computation.12 | loop fusion | bytes 3145744 | tf_op jit(solution)/shard_map/dynamic_slice | solution.py:200
  1.5 5.1 %collective-permute-start.2 = (bf16[3,256,256]{2,1,0:T(8,128)(2,1)S(1)}, bf16[3,256,256]{2,1,0:T(8,128)(2,1)S(1)}, u32[]{:S(2)}, u32[]{:S(2)}) collective-permute-start(bf16[3,256,256]{2,1,0:T(8,128)(2,1)S(1)} %get-tuple-element.104), channel_id=1, source_target_pairs={{0,24},{8,16},{16,8},{24,0},{1,25},{9,17},{17,9},{25,1},{2,26},{10... | collective-permute-start | bytes 1179656 | tf_op jit(solution)/shard_map/ppermute | solution.py:177
  6.6 0.0 collective-permute-start
  6.6 0.6 collective-permute-start.1
  7.2 1.7 %collective-permute-start.3 = (bf16[3,256,256]{2,1,0:T(8,128)(2,1)S(1)}, bf16[3,256,256]{2,1,0:T(8,128)(2,1)S(1)}, u32[]{:S(2)}, u32[]{:S(2)}) collective-permute-start(bf16[3,256,256]{2,1,0:T(8,128)(2,1)S(1)} %get-tuple-element.106.refs_0_), channel_id=1, source_target_pairs={{0,4},{4,0},{1,5},{5,1},{2,6},{6,2},{3,7},{7,3},{8,12},{12,8},{9,1... | collective-permute-start | bytes 1179656 | tf_op jit(solution)/shard_map/ppermute | solution.py:177
  8.9 7.7 %collective-permute-done.2.refs_3_ = bf16[3,256,256]{2,1,0:T(8,128)(2,1)S(1)} collective-permute-done((bf16[3,256,256]{2,1,0:T(8,128)(2,1)S(1)}, bf16[3,256,256]{2,1,0:T(8,128)(2,1)S(1)}, u32[]{:S(2)}, u32[]{:S(2)}) %collective-permute-start.2) | collective-permute-done | bytes 393248 | tf_op jit(solution)/shard_map/ppermute | solution.py:177
  16.6 1.7 %collective-permute-start.6 = (bf16[3,256,256]{2,1,0:T(8,128)(2,1)S(1)}, bf16[3,256,256]{2,1,0:T(8,128)(2,1)S(1)}, u32[]{:S(2)}, u32[]{:S(2)}) collective-permute-start(bf16[3,256,256]{2,1,0:T(8,128)(2,1)S(1)} %collective-permute-done.2.refs_3_), channel_id=1, source_target_pairs={{0,4},{4,0},{1,5},{5,1},{2,6},{6,2},{3,7},{7,3},{8,12},{12,8},{9,1... | collective-permute-start | bytes 1179656 | tf_op jit(solution)/shard_map/ppermute | solution.py:177
  18.3 6.9 %collective-permute-done.refs_1_ = bf16[3,256,256]{2,1,0:T(8,128)(2,1)S(1)} collective-permute-done((bf16[3,256,256]{2,1,0:T(8,128)(2,1)S(1)}, bf16[3,256,256]{2,1,0:T(8,128)(2,1)S(1)}, u32[]{:S(2)}, u32[]{:S(2)}) %collective-permute-start) | collective-permute-done | bytes 393248 | tf_op jit(solution)/shard_map/ppermute | solution.py:177
  25.3 1.4 %collective-permute-start.4 = (bf16[3,256,256]{2,1,0:T(8,128)(2,1)S(1)}, bf16[3,256,256]{2,1,0:T(8,128)(2,1)S(1)}, u32[]{:S(2)}, u32[]{:S(2)}) collective-permute-start(bf16[3,256,256]{2,1,0:T(8,128)(2,1)S(1)} %collective-permute-done.refs_1_), channel_id=1, source_target_pairs={{0,4},{4,0},{1,5},{5,1},{2,6},{6,2},{3,7},{7,3},{8,12},{12,8},{9,1... | collective-permute-start | bytes 1179656 | tf_op jit(solution)/shard_map/ppermute | solution.py:177
  26.7 13.5 %collective-permute-done.1.refs_2_ = bf16[3,256,256]{2,1,0:T(8,128)(2,1)S(1)} collective-permute-done((bf16[3,256,256]{2,1,0:T(8,128)(2,1)S(1)}, bf16[3,256,256]{2,1,0:T(8,128)(2,1)S(1)}, u32[]{:S(2)}, u32[]{:S(2)}) %collective-permute-start.1) | collective-permute-done | bytes 393248 | tf_op jit(solution)/shard_map/ppermute | solution.py:177
  40.1 1.5 %collective-permute-start.5 = (bf16[3,256,256]{2,1,0:T(8,128)(2,1)S(1)}, bf16[3,256,256]{2,1,0:T(8,128)(2,1)S(1)}, u32[]{:S(2)}, u32[]{:S(2)}) collective-permute-start(bf16[3,256,256]{2,1,0:T(8,128)(2,1)S(1)} %collective-permute-done.1.refs_2_), channel_id=1, source_target_pairs={{0,4},{4,0},{1,5},{5,1},{2,6},{6,2},{3,7},{7,3},{8,12},{12,8},{9,1... | collective-permute-start | bytes 1179656 | tf_op jit(solution)/shard_map/ppermute | solution.py:177
  41.7 0.7 fusion.2
  42.3 0.1 concatenate.7.scalars
  42.4 0.0 collective-permute-done.3.refs_4_
  42.4 0.0 collective-permute-done.6.refs_7_
  42.4 0.0 collective-permute-done.4.refs_5_
  42.4 7.9 %collective-permute-done.5.refs_6_ = bf16[3,256,256]{2,1,0:T(8,128)(2,1)S(1)} collective-permute-done((bf16[3,256,256]{2,1,0:T(8,128)(2,1)S(1)}, bf16[3,256,256]{2,1,0:T(8,128)(2,1)S(1)}, u32[]{:S(2)}, u32[]{:S(2)}) %collective-permute-start.5) | collective-permute-done | bytes 393248 | tf_op jit(solution)/shard_map/ppermute | solution.py:177
  50.3 2.0 %tiles_first.1 = (bf16[8,256,768]{2,1,0:T(8,128)(2,1)S(1)}, f32[2,2,3,64,256]{4,3,2,1,0:T(8,128)S(1)}, f32[2,2,3,64,256]{4,3,2,1,0:T(8,128)S(1)}) custom-call(s32[40]{0:T(128)S(1)} %concatenate.7.scalars, bf16[3,256,256]{2,1,0:T(8,128)(2,1)S(1)} %get-tuple-element.106.refs_0_, bf16[3,256,256]{2,1,0:T(8,128)(2,1)S(1)} %collective-permute-done.refs_1_, ...), custom_call_target="tpu_custom_call" | custom-call | flops 603979776 | tf_op jit(solution)/shard_map/tiles_first/pallas_call | solution.py:214
  52.3 0.1 collective-permute-start.7
  52.4 3.1 %tiles_second.1 = (f32[2,2,3,64,256]{4,3,2,1,0:T(8,128)S(1)}, f32[2,2,3,64,256]{4,3,2,1,0:T(8,128)S(1)}, f32[2,2,3,64,256]{4,3,2,1,0:T(8,128)S(1)}, f32[2,2,3,64,256]{4,3,2,1,0:T(8,128)S(1)}) custom-call(s32[40]{0:T(128)S(1)} %concatenate.7.scalars, bf16[8,256,768]{2,1,0:T(8,128)(2,1)S(1)} %get-tuple-element.58.blocks), custom_call_target="tpu_custom_call" | custom-call | flops 1207959552 | tf_op jit(solution)/shard_map/tiles_second/pallas_call | solution.py:214
  55.5 0.6 collective-permute-start.10
  56.0 0.1 collective-permute-start.9
  56.1 0.0 collective-permute-done.7.right
  56.1 0.1 sum_core.3
  56.2 1.6 %collective-permute-start.8 = (f32[2,3,64,256]{3,2,1,0:T(8,128)S(1)}, f32[2,3,64,256]{3,2,1,0:T(8,128)S(1)}, u32[]{:S(2)}, u32[]{:S(2)}) collective-permute-start(f32[2,3,64,256]{3,2,1,0:T(8,128)S(1)} %get-tuple-element.57), channel_id=1, source_target_pairs={{0,2},{2,0},{1,3},{3,1},{4,6},{6,4},{5,7},{7,5},{8,10},{10,8},{9,1... | collective-permute-start | bytes 1179656 | tf_op jit(solution)/shard_map/ppermute | solution.py:177
  57.7 0.2 collective-permute-done.10.right
  57.9 0.1 sum_core.4
  58.0 1.6 %collective-permute-start.13 = (f32[2,3,64,256]{3,2,1,0:T(8,128)S(1)}, f32[2,3,64,256]{3,2,1,0:T(8,128)S(1)}, u32[]{:S(2)}, u32[]{:S(2)}) collective-permute-start(f32[2,3,64,256]{3,2,1,0:T(8,128)S(1)} %get-tuple-element.75), channel_id=1, source_target_pairs={{0,2},{2,0},{1,3},{3,1},{4,6},{6,4},{5,7},{7,5},{8,10},{10,8},{9,1... | collective-permute-start | bytes 1179656 | tf_op jit(solution)/shard_map/ppermute | solution.py:177
  59.6 0.0 collective-permute-done.9.right
  59.6 0.1 sum_core.5
  59.7 8.5 %collective-permute-done.8.right = f32[2,3,64,256]{3,2,1,0:T(8,128)S(1)} collective-permute-done((f32[2,3,64,256]{3,2,1,0:T(8,128)S(1)}, f32[2,3,64,256]{3,2,1,0:T(8,128)S(1)}, u32[]{:S(2)}, u32[]{:S(2)}) %collective-permute-start.8) | collective-permute-done | bytes 393248 | tf_op jit(solution)/shard_map/ppermute | solution.py:177
  68.2 0.1 sum_x.3
  68.2 0.6 collective-permute-start.11
  68.9 1.5 %collective-permute-start.16 = (f32[2,3,64,256]{3,2,1,0:T(8,128)S(1)}, f32[2,3,64,256]{3,2,1,0:T(8,128)S(1)}, u32[]{:S(2)}, u32[]{:S(2)}) collective-permute-start(f32[2,3,64,256]{3,2,1,0:T(8,128)S(1)} %get-tuple-element.84), channel_id=1, source_target_pairs={{0,2},{2,0},{1,3},{3,1},{4,6},{6,4},{5,7},{7,5},{8,10},{10,8},{9,1... | collective-permute-start | bytes 1179656 | tf_op jit(solution)/shard_map/ppermute | solution.py:177
  70.3 4.0 %collective-permute-done.11.right = f32[3,64,256]{2,1,0:T(8,128)S(1)} collective-permute-done((f32[3,64,256]{2,1,0:T(8,128)S(1)}, f32[3,64,256]{2,1,0:T(8,128)S(1)}, u32[]{:S(2)}, u32[]{:S(2)}) %collective-permute-start.11) | collective-permute-done | bytes 196640 | tf_op jit(solution)/shard_map/ppermute | solution.py:177
  74.3 1.5 %collective-permute-start.12 = (f32[3,64,256]{2,1,0:T(8,128)S(1)}, f32[3,64,256]{2,1,0:T(8,128)S(1)}, u32[]{:S(2)}, u32[]{:S(2)}) collective-permute-start(f32[3,64,256]{2,1,0:T(8,128)S(1)} %sum_z.3.left), channel_id=1, source_target_pairs={{0,16},{8,24},{16,0},{24,8},{1,17},{9,25},{17,1},{25,9},{2,18},{10... | collective-permute-start | bytes 589832 | tf_op jit(solution)/shard_map/ppermute | solution.py:177
  75.8 0.8 collective-permute-done.13.right
  76.6 0.7 collective-permute-start.14
  77.4 7.3 %collective-permute-done.12.right = f32[3,64,256]{2,1,0:T(8,128)S(1)} collective-permute-done((f32[3,64,256]{2,1,0:T(8,128)S(1)}, f32[3,64,256]{2,1,0:T(8,128)S(1)}, u32[]{:S(2)}, u32[]{:S(2)}) %collective-permute-start.12) | collective-permute-done | bytes 196640 | tf_op jit(solution)/shard_map/ppermute | solution.py:177
  84.7 0.0 copy-start
  84.8 2.0 %collective-permute-done.14.right = f32[3,64,256]{2,1,0:T(8,128)S(1)} collective-permute-done((f32[3,64,256]{2,1,0:T(8,128)S(1)}, f32[3,64,256]{2,1,0:T(8,128)S(1)}, u32[]{:S(2)}, u32[]{:S(2)}) %collective-permute-start.14) | collective-permute-done | bytes 196640 | tf_op jit(solution)/shard_map/ppermute | solution.py:177
  86.7 0.4 collective-permute-start.15
  87.2 0.0 collective-permute-done.16.right
  87.2 2.5 %collective-permute-start.17 = (f32[3,64,256]{2,1,0:T(8,128)S(1)}, f32[3,64,256]{2,1,0:T(8,128)S(1)}, u32[]{:S(2)}, u32[]{:S(2)}) collective-permute-start(f32[3,64,256]{2,1,0:T(8,128)S(1)} %get-tuple-element.90), channel_id=1, source_target_pairs={{0,8},{8,0},{16,24},{24,16},{1,9},{9,1},{17,25},{25,17},{2,10},{10... | collective-permute-start | bytes 589832 | tf_op jit(solution)/shard_map/ppermute | solution.py:177
  89.8 8.1 %collective-permute-done.15.right = f32[3,64,256]{2,1,0:T(8,128)S(1)} collective-permute-done((f32[3,64,256]{2,1,0:T(8,128)S(1)}, f32[3,64,256]{2,1,0:T(8,128)S(1)}, u32[]{:S(2)}, u32[]{:S(2)}) %collective-permute-start.15) | collective-permute-done | bytes 196640 | tf_op jit(solution)/shard_map/ppermute | solution.py:177
  97.9 0.2 collective-permute-done.17.right
  98.1 0.3 finish.2.own
  98.5 0.1 collective-permute-start.18
  98.5 0.0 copy-done
  98.6 2.1 %collective-permute-start.20 = (f32[3,64,256]{2,1,0:T(8,128)S(1)}, f32[3,64,256]{2,1,0:T(8,128)S(1)}, u32[]{:S(2)}, u32[]{:S(2)}) collective-permute-start(f32[3,64,256]{2,1,0:T(8,128)S(1)} %sum_z.5.refs_0_), channel_id=1, source_target_pairs={{0,16},{8,24},{16,0},{24,8},{1,17},{9,25},{17,1},{25,9},{2,18},{10... | collective-permute-start | bytes 589832 | tf_op jit(solution)/shard_map/ppermute | solution.py:177
  100.7 7.8 %collective-permute-done.18.arrived = s16[400,256]{1,0:T(8,128)(2,1)S(1)} collective-permute-done((s16[400,256]{1,0:T(8,128)(2,1)S(1)}, s16[400,256]{1,0:T(8,128)(2,1)S(1)}, u32[]{:S(2)}, u32[]{:S(2)}) %collective-permute-start.18) | collective-permute-done | bytes 204832 | tf_op jit(solution)/shard_map/ppermute | solution.py:177
  108.6 1.6 %collective-permute-start.19 = (s16[2,400,256]{2,1,0:T(8,128)(2,1)S(1)}, s16[2,400,256]{2,1,0:T(8,128)(2,1)S(1)}, u32[]{:S(2)}, u32[]{:S(2)}) collective-permute-start(s16[2,400,256]{2,1,0:T(8,128)(2,1)S(1)} %pair.1.refs_0_), channel_id=1, source_target_pairs={{0,4},{4,0},{1,5},{5,1},{2,6},{6,2},{3,7},{7,3},{8,12},{12,8},{9,1... | collective-permute-start | bytes 1228808 | tf_op jit(solution)/shard_map/ppermute | solution.py:177
  110.2 0.2 collective-permute-done.20.refs_1_
  110.4 0.2 finish.3
  110.6 0.7 collective-permute-start.23
  111.2 1.0 collective-permute-start.22
  112.2 1.9 %collective-permute-start.21 = (s16[208,256]{1,0:T(8,128)(2,1)S(1)}, s16[208,256]{1,0:T(8,128)(2,1)S(1)}, u32[]{:S(2)}, u32[]{:S(2)}) collective-permute-start(s16[208,256]{1,0:T(8,128)(2,1)S(1)} %finish.3), channel_id=1, source_target_pairs={{0,8},{8,0},{16,24},{24,16},{1,9},{9,1},{17,25},{25,17},{2,10},{10... | collective-permute-start | bytes 319496 | tf_op jit(solution)/shard_map/ppermute | solution.py:177
  114.1 0.1 concatenate.6.scalars
  114.2 2.1 %collective-permute-done.23 = s16[208,256]{1,0:T(8,128)(2,1)S(1)} collective-permute-done((s16[208,256]{1,0:T(8,128)(2,1)S(1)}, s16[208,256]{1,0:T(8,128)(2,1)S(1)}, u32[]{:S(2)}, u32[]{:S(2)}) %collective-permute-start.23) | collective-permute-done | bytes 106528 | tf_op jit(solution)/shard_map/ppermute | solution.py:319
  116.4 7.1 %collective-permute-done.22 = s16[208,256]{1,0:T(8,128)(2,1)S(1)} collective-permute-done((s16[208,256]{1,0:T(8,128)(2,1)S(1)}, s16[208,256]{1,0:T(8,128)(2,1)S(1)}, u32[]{:S(2)}, u32[]{:S(2)}) %collective-permute-start.22) | collective-permute-done | bytes 106528 | tf_op jit(solution)/shard_map/ppermute | solution.py:177
  123.5 0.0 collective-permute-done.21
  123.5 0.0 collective-permute-done.19.refs_1_
  123.5 2.4 %place_tiles.1 = f32[10,64,256]{2,1,0:T(8,128)} custom-call(s32[50]{0:T(128)S(1)} %concatenate.6.scalars, s16[2,400,256]{2,1,0:T(8,128)(2,1)S(1)} %pair.1.refs_0_, s16[2,400,256]{2,1,0:T(8,128)(2,1)S(1)} %collective-permute-done.19.refs_1_, s16[1,208,256]{2,1,0:T(8,128)(2,1)S(1)} %bitcast.28, s16[1,208,256]{2,1,0:T(8,128)(2,1)S(1)} %bitcast.31, ...), custom_call_target="tpu_custom_call" | custom-call | flops 163840 | tf_op jit(solution)/shard_map/place_tiles/pallas_call | solution.py:349
  (11 shorter events, 0.3 us)
Async XLA Ops:
  1.5 15.1 %collective-permute-start.2 = (bf16[3,256,256]{2,1,0:T(8,128)(2,1)S(1)}, bf16[3,256,256]{2,1,0:T(8,128)(2,1)S(1)}, u32[]{:S(2)}, u32[]{:S(2)}) collective-permute-start(bf16[3,256,256]{2,1,0:T(8,128)(2,1)S(1)} %get-tuple-element.104), channel_id=1, source_target_pairs={{0,24},{8,16},{16,8},{24,0},{1,25},{9,17},{17,9},{25,1},{2,26},{10... | collective-permute-start | bytes 1179656 | tf_op jit(solution)/shard_map/ppermute | solution.py:177
  6.6 18.7 %collective-permute-start = (bf16[3,256,256]{2,1,0:T(8,128)(2,1)S(1)}, bf16[3,256,256]{2,1,0:T(8,128)(2,1)S(1)}, u32[]{:S(2)}, u32[]{:S(2)}) collective-permute-start(bf16[3,256,256]{2,1,0:T(8,128)(2,1)S(1)} %get-tuple-element.105), channel_id=1, source_target_pairs={{0,8},{8,0},{16,24},{24,16},{1,9},{9,1},{17,25},{25,17},{2,10},{10... | collective-permute-start | bytes 1179656 | tf_op jit(solution)/shard_map/ppermute | solution.py:177
  6.6 33.5 %collective-permute-start.1 = (bf16[3,256,256]{2,1,0:T(8,128)(2,1)S(1)}, bf16[3,256,256]{2,1,0:T(8,128)(2,1)S(1)}, u32[]{:S(2)}, u32[]{:S(2)}) collective-permute-start(bf16[3,256,256]{2,1,0:T(8,128)(2,1)S(1)} %get-tuple-element.107), channel_id=1, source_target_pairs={{0,16},{8,24},{16,0},{24,8},{1,17},{9,25},{17,1},{25,9},{2,18},{10... | collective-permute-start | bytes 1179656 | tf_op jit(solution)/shard_map/ppermute | solution.py:177
  7.2 35.2 %collective-permute-start.3 = (bf16[3,256,256]{2,1,0:T(8,128)(2,1)S(1)}, bf16[3,256,256]{2,1,0:T(8,128)(2,1)S(1)}, u32[]{:S(2)}, u32[]{:S(2)}) collective-permute-start(bf16[3,256,256]{2,1,0:T(8,128)(2,1)S(1)} %get-tuple-element.106.refs_0_), channel_id=1, source_target_pairs={{0,4},{4,0},{1,5},{5,1},{2,6},{6,2},{3,7},{7,3},{8,12},{12,8},{9,1... | collective-permute-start | bytes 1179656 | tf_op jit(solution)/shard_map/ppermute | solution.py:177
  16.6 25.8 %collective-permute-start.6 = (bf16[3,256,256]{2,1,0:T(8,128)(2,1)S(1)}, bf16[3,256,256]{2,1,0:T(8,128)(2,1)S(1)}, u32[]{:S(2)}, u32[]{:S(2)}) collective-permute-start(bf16[3,256,256]{2,1,0:T(8,128)(2,1)S(1)} %collective-permute-done.2.refs_3_), channel_id=1, source_target_pairs={{0,4},{4,0},{1,5},{5,1},{2,6},{6,2},{3,7},{7,3},{8,12},{12,8},{9,1... | collective-permute-start | bytes 1179656 | tf_op jit(solution)/shard_map/ppermute | solution.py:177
  25.3 17.2 %collective-permute-start.4 = (bf16[3,256,256]{2,1,0:T(8,128)(2,1)S(1)}, bf16[3,256,256]{2,1,0:T(8,128)(2,1)S(1)}, u32[]{:S(2)}, u32[]{:S(2)}) collective-permute-start(bf16[3,256,256]{2,1,0:T(8,128)(2,1)S(1)} %collective-permute-done.refs_1_), channel_id=1, source_target_pairs={{0,4},{4,0},{1,5},{5,1},{2,6},{6,2},{3,7},{7,3},{8,12},{12,8},{9,1... | collective-permute-start | bytes 1179656 | tf_op jit(solution)/shard_map/ppermute | solution.py:177
  40.1 10.2 %collective-permute-start.5 = (bf16[3,256,256]{2,1,0:T(8,128)(2,1)S(1)}, bf16[3,256,256]{2,1,0:T(8,128)(2,1)S(1)}, u32[]{:S(2)}, u32[]{:S(2)}) collective-permute-start(bf16[3,256,256]{2,1,0:T(8,128)(2,1)S(1)} %collective-permute-done.1.refs_2_), channel_id=1, source_target_pairs={{0,4},{4,0},{1,5},{5,1},{2,6},{6,2},{3,7},{7,3},{8,12},{12,8},{9,1... | collective-permute-start | bytes 1179656 | tf_op jit(solution)/shard_map/ppermute | solution.py:177
  52.3 3.8 %collective-permute-start.7 = (f32[2,2,3,64,256]{4,3,2,1,0:T(8,128)S(1)}, f32[2,2,3,64,256]{4,3,2,1,0:T(8,128)S(1)}, u32[]{:S(2)}, u32[]{:S(2)}) collective-permute-start(f32[2,2,3,64,256]{4,3,2,1,0:T(8,128)S(1)} %get-tuple-element.53), channel_id=1, source_target_pairs={{0,1},{1,0},{2,3},{3,2},{4,5},{5,4},{6,7},{7,6},{8,9},{9,8},{10,11... | collective-permute-start | bytes 2359304 | tf_op jit(solution)/shard_map/ppermute | solution.py:177
  55.5 2.5 %collective-permute-start.10 = (f32[2,2,3,64,256]{4,3,2,1,0:T(8,128)S(1)}, f32[2,2,3,64,256]{4,3,2,1,0:T(8,128)S(1)}, u32[]{:S(2)}, u32[]{:S(2)}) collective-permute-start(f32[2,2,3,64,256]{4,3,2,1,0:T(8,128)S(1)} %get-tuple-element.62), channel_id=1, source_target_pairs={{0,1},{1,0},{2,3},{3,2},{4,5},{5,4},{6,7},{7,6},{8,9},{9,8},{10,11... | collective-permute-start | bytes 2359304 | tf_op jit(solution)/shard_map/ppermute | solution.py:177
  56.0 3.6 %collective-permute-start.9 = (f32[2,2,3,64,256]{4,3,2,1,0:T(8,128)S(1)}, f32[2,2,3,64,256]{4,3,2,1,0:T(8,128)S(1)}, u32[]{:S(2)}, u32[]{:S(2)}) collective-permute-start(f32[2,2,3,64,256]{4,3,2,1,0:T(8,128)S(1)} %get-tuple-element.60), channel_id=1, source_target_pairs={{0,1},{1,0},{2,3},{3,2},{4,5},{5,4},{6,7},{7,6},{8,9},{9,8},{10,11... | collective-permute-start | bytes 2359304 | tf_op jit(solution)/shard_map/ppermute | solution.py:177
  56.2 12.0 %collective-permute-start.8 = (f32[2,3,64,256]{3,2,1,0:T(8,128)S(1)}, f32[2,3,64,256]{3,2,1,0:T(8,128)S(1)}, u32[]{:S(2)}, u32[]{:S(2)}) collective-permute-start(f32[2,3,64,256]{3,2,1,0:T(8,128)S(1)} %get-tuple-element.57), channel_id=1, source_target_pairs={{0,2},{2,0},{1,3},{3,1},{4,6},{6,4},{5,7},{7,5},{8,10},{10,8},{9,1... | collective-permute-start | bytes 1179656 | tf_op jit(solution)/shard_map/ppermute | solution.py:177
  58.0 18.6 %collective-permute-start.13 = (f32[2,3,64,256]{3,2,1,0:T(8,128)S(1)}, f32[2,3,64,256]{3,2,1,0:T(8,128)S(1)}, u32[]{:S(2)}, u32[]{:S(2)}) collective-permute-start(f32[2,3,64,256]{3,2,1,0:T(8,128)S(1)} %get-tuple-element.75), channel_id=1, source_target_pairs={{0,2},{2,0},{1,3},{3,1},{4,6},{6,4},{5,7},{7,5},{8,10},{10,8},{9,1... | collective-permute-start | bytes 1179656 | tf_op jit(solution)/shard_map/ppermute | solution.py:177
  68.2 6.1 %collective-permute-start.11 = (f32[3,64,256]{2,1,0:T(8,128)S(1)}, f32[3,64,256]{2,1,0:T(8,128)S(1)}, u32[]{:S(2)}, u32[]{:S(2)}) collective-permute-start(f32[3,64,256]{2,1,0:T(8,128)S(1)} %get-tuple-element.72), channel_id=1, source_target_pairs={{0,8},{8,0},{16,24},{24,16},{1,9},{9,1},{17,25},{25,17},{2,10},{10... | collective-permute-start | bytes 589832 | tf_op jit(solution)/shard_map/ppermute | solution.py:177
  68.9 18.3 %collective-permute-start.16 = (f32[2,3,64,256]{3,2,1,0:T(8,128)S(1)}, f32[2,3,64,256]{3,2,1,0:T(8,128)S(1)}, u32[]{:S(2)}, u32[]{:S(2)}) collective-permute-start(f32[2,3,64,256]{3,2,1,0:T(8,128)S(1)} %get-tuple-element.84), channel_id=1, source_target_pairs={{0,2},{2,0},{1,3},{3,1},{4,6},{6,4},{5,7},{7,5},{8,10},{10,8},{9,1... | collective-permute-start | bytes 1179656 | tf_op jit(solution)/shard_map/ppermute | solution.py:177
  74.3 10.4 %collective-permute-start.12 = (f32[3,64,256]{2,1,0:T(8,128)S(1)}, f32[3,64,256]{2,1,0:T(8,128)S(1)}, u32[]{:S(2)}, u32[]{:S(2)}) collective-permute-start(f32[3,64,256]{2,1,0:T(8,128)S(1)} %sum_z.3.left), channel_id=1, source_target_pairs={{0,16},{8,24},{16,0},{24,8},{1,17},{9,25},{17,1},{25,9},{2,18},{10... | collective-permute-start | bytes 589832 | tf_op jit(solution)/shard_map/ppermute | solution.py:177
  76.6 10.1 %collective-permute-start.14 = (f32[3,64,256]{2,1,0:T(8,128)S(1)}, f32[3,64,256]{2,1,0:T(8,128)S(1)}, u32[]{:S(2)}, u32[]{:S(2)}) collective-permute-start(f32[3,64,256]{2,1,0:T(8,128)S(1)} %get-tuple-element.81), channel_id=1, source_target_pairs={{0,8},{8,0},{16,24},{24,16},{1,9},{9,1},{17,25},{25,17},{2,10},{10... | collective-permute-start | bytes 589832 | tf_op jit(solution)/shard_map/ppermute | solution.py:177
  84.7 13.8 %copy-start = (s32[1,10,2]{1,2,0:T(2,128)S(1)}, s32[1,10,2]{1,2,0:T(2,128)}, u32[]{:S(2)}) copy-start(s32[1,10,2]{1,2,0:T(2,128)} %param.4) | copy-start | bytes 244
  86.7 11.1 %collective-permute-start.15 = (f32[3,64,256]{2,1,0:T(8,128)S(1)}, f32[3,64,256]{2,1,0:T(8,128)S(1)}, u32[]{:S(2)}, u32[]{:S(2)}) collective-permute-start(f32[3,64,256]{2,1,0:T(8,128)S(1)} %sum_z.4.left), channel_id=1, source_target_pairs={{0,16},{8,24},{16,0},{24,8},{1,17},{9,25},{17,1},{25,9},{2,18},{10... | collective-permute-start | bytes 589832 | tf_op jit(solution)/shard_map/ppermute | solution.py:177
  87.2 10.9 %collective-permute-start.17 = (f32[3,64,256]{2,1,0:T(8,128)S(1)}, f32[3,64,256]{2,1,0:T(8,128)S(1)}, u32[]{:S(2)}, u32[]{:S(2)}) collective-permute-start(f32[3,64,256]{2,1,0:T(8,128)S(1)} %get-tuple-element.90), channel_id=1, source_target_pairs={{0,8},{8,0},{16,24},{24,16},{1,9},{9,1},{17,25},{25,17},{2,10},{10... | collective-permute-start | bytes 589832 | tf_op jit(solution)/shard_map/ppermute | solution.py:177
  98.5 10.1 %collective-permute-start.18 = (s16[400,256]{1,0:T(8,128)(2,1)S(1)}, s16[400,256]{1,0:T(8,128)(2,1)S(1)}, u32[]{:S(2)}, u32[]{:S(2)}) collective-permute-start(s16[400,256]{1,0:T(8,128)(2,1)S(1)} %finish.2.own), channel_id=1, source_target_pairs={{0,8},{8,0},{16,24},{24,16},{1,9},{9,1},{17,25},{25,17},{2,10},{10... | collective-permute-start | bytes 614408 | tf_op jit(solution)/shard_map/ppermute | solution.py:177
  98.6 11.8 %collective-permute-start.20 = (f32[3,64,256]{2,1,0:T(8,128)S(1)}, f32[3,64,256]{2,1,0:T(8,128)S(1)}, u32[]{:S(2)}, u32[]{:S(2)}) collective-permute-start(f32[3,64,256]{2,1,0:T(8,128)S(1)} %sum_z.5.refs_0_), channel_id=1, source_target_pairs={{0,16},{8,24},{16,0},{24,8},{1,17},{9,25},{17,1},{25,9},{2,18},{10... | collective-permute-start | bytes 589832 | tf_op jit(solution)/shard_map/ppermute | solution.py:177
  108.6 14.9 %collective-permute-start.19 = (s16[2,400,256]{2,1,0:T(8,128)(2,1)S(1)}, s16[2,400,256]{2,1,0:T(8,128)(2,1)S(1)}, u32[]{:S(2)}, u32[]{:S(2)}) collective-permute-start(s16[2,400,256]{2,1,0:T(8,128)(2,1)S(1)} %pair.1.refs_0_), channel_id=1, source_target_pairs={{0,4},{4,0},{1,5},{5,1},{2,6},{6,2},{3,7},{7,3},{8,12},{12,8},{9,1... | collective-permute-start | bytes 1228808 | tf_op jit(solution)/shard_map/ppermute | solution.py:177
  110.6 5.8 %collective-permute-start.23 = (s16[208,256]{1,0:T(8,128)(2,1)S(1)}, s16[208,256]{1,0:T(8,128)(2,1)S(1)}, u32[]{:S(2)}, u32[]{:S(2)}) collective-permute-start(s16[208,256]{1,0:T(8,128)(2,1)S(1)} %finish.3), channel_id=1, source_target_pairs={{0,12},{4,8},{8,4},{12,0},{16,28},{20,24},{24,20},{28,16},{1,13},{... | collective-permute-start | bytes 319496 | tf_op jit(solution)/shard_map/ppermute | solution.py:319
  111.2 12.3 %collective-permute-start.22 = (s16[208,256]{1,0:T(8,128)(2,1)S(1)}, s16[208,256]{1,0:T(8,128)(2,1)S(1)}, u32[]{:S(2)}, u32[]{:S(2)}) collective-permute-start(s16[208,256]{1,0:T(8,128)(2,1)S(1)} %finish.3), channel_id=1, source_target_pairs={{0,4},{4,0},{1,5},{5,1},{2,6},{6,2},{3,7},{7,3},{8,12},{12,8},{9,1... | collective-permute-start | bytes 319496 | tf_op jit(solution)/shard_map/ppermute | solution.py:177
  112.2 11.3 %collective-permute-start.21 = (s16[208,256]{1,0:T(8,128)(2,1)S(1)}, s16[208,256]{1,0:T(8,128)(2,1)S(1)}, u32[]{:S(2)}, u32[]{:S(2)}) collective-permute-start(s16[208,256]{1,0:T(8,128)(2,1)S(1)} %finish.3), channel_id=1, source_target_pairs={{0,8},{8,0},{16,24},{24,16},{1,9},{9,1},{17,25},{25,17},{2,10},{10... | collective-permute-start | bytes 319496 | tf_op jit(solution)/shard_map/ppermute | solution.py:177

commit v10 on v8

--- a/solution.py
+++ b/solution.py
@@ -9,15 +9,17 @@
 from jax.experimental.pallas import tpu as pltpu
 from jax.sharding import Mesh, PartitionSpec as P
 
+Z = ("z_high", "z_low")
 VMEM_LIMIT = 24 * 2**20
 GROUPS = 3
-BATCHES = ((0, 1), (2,))
+BATCHES = ((0,), (1,), (2,))
 ORDER = (
-    ("x", 0), ("low", 0), ("x", 1), ("high", 0), ("low", 1),
-    ("x", 2), ("low", 2), ("finish", BATCHES[0]), ("finish", BATCHES[1]),
+    ("x", 0), ("low", 0), ("x", 1), ("finish", BATCHES[0]), ("low", 1),
+    ("x", 2), ("high", 1), ("low", 2),
+    ("finish", BATCHES[1]), ("finish", BATCHES[2]),
 )
 CODE_TOP = 32767.0
-SCALE_ROWS = 16
+SCALE_ROWS = 8
 SCALE_STEPS = 8192.0
 
 
@@ -111,27 +113,27 @@
             scale = steps * power * (1.0 / SCALE_STEPS)
             factor = jnp.where(filled, CODE_TOP / jnp.where(filled, scale, 1.0), 0.0)
             rounded = jnp.clip(jnp.round(total * factor), -CODE_TOP, CODE_TOP)
-            start = SCALE_ROWS + slot * rows
-            code[start : start + rows, :] = rounded.astype(jnp.int32).astype(jnp.int16)
+            rounded = rounded.astype(jnp.int32)
+            start, half = SCALE_ROWS + slot * (rows // 2), rows // 2
+            code[start : start + half, :] = (rounded[:half] << 16) | (rounded[half:] & 0xFFFF)
             row, lane = divmod(slot * rows, columns)
             diagonal = lane_of == row_of + lane
             for at, value in ((row, exponent), (row + header_rows, steps)):
                 across = jnp.sum(jnp.where(diagonal, value, 0.0), axis=0, keepdims=True)
                 header += jnp.where(place == at, across, 0.0)
             slot += 1
-    code[:SCALE_ROWS, :] = header.astype(jnp.int32).astype(jnp.int16)
+    code[:SCALE_ROWS, :] = header.astype(jnp.int32)
 
 
 def place_kernel(factor, scalars, *refs):
     out, codes, headers = refs[-3:]
     slots, rows, columns = out.shape
     at = 0
-    for index, part in enumerate(refs[:-3]):
+    parts = [part.at[index] for part in refs[:-3] for index in range(part.shape[0])]
+    for index, part in enumerate(parts):
         count = part.shape[0] - SCALE_ROWS
         start = index * SCALE_ROWS
-        headers[start : start + SCALE_ROWS, :] = (
-            part[:SCALE_ROWS, :].astype(jnp.int32).astype(jnp.float32)
-        )
+        headers[start : start + SCALE_ROWS, :] = part[:SCALE_ROWS, :].astype(jnp.float32)
         codes[at : at + count, :] = part[SCALE_ROWS:, :]
         at += count
     row_of = lax.broadcasted_iota(jnp.int32, (rows, columns), 0)
@@ -148,8 +150,10 @@
         column = jnp.sum(
             jnp.where(lane_of == row_of + lane, scale, 0.0), axis=1, keepdims=True
         )
-        code = codes[pl.ds(pl.multiple_of(tile * rows, rows), rows), :]
-        out[slot] = code.astype(jnp.int32).astype(jnp.float32) * column
+        half = rows // 2
+        code = codes[pl.ds(pl.multiple_of(tile * half, half), half), :]
+        out[slot, :half] = (code >> 16).astype(jnp.float32) * column[:half]
+        out[slot, half:] = ((code << 16) >> 16).astype(jnp.float32) * column[half:]
         return carry
 
     lax.fori_loop(0, slots, one_slot, 0)
@@ -161,8 +165,8 @@
     space_count = x_count * core_count
     rows_dev = block_size // space_count
     scale_factor = 1.0 / math.sqrt(components * cells_dev * space_count)
-    z, y, x, core = (lax.axis_index(name) for name in ("z", "y", "x", "core"))
-    low_bit = z & 1
+    low_bit, y, x, core = (lax.axis_index(name) for name in ("z_low", "y", "x", "core"))
+    z = lax.axis_index(Z)
     cells = cells_dev // z_count
 
     def swap(value, axis, bits):
@@ -194,7 +198,7 @@
 
     pieces = {(0, 0): part(0)}
     for step in range(1, z_count):
-        pieces[step, 0] = swap(part(step), "z", step)
+        pieces[step, 0] = swap(part(step), Z, step)
     layout = [(step, 0, component) for step, component in pieces]
     layout += [(step, 1, component) for step, component in pieces]
     chunks = list(pieces.values()) + [swap(piece, "y", 1) for piece in pieces.values()]
@@ -212,7 +216,7 @@
             compiler_params=pltpu.CompilerParams(vmem_limit_bytes=VMEM_LIMIT),
             cost_estimate=pl.CostEstimate(
                 flops=4 * size * block_size * block_size * components * cells,
-                bytes_accessed=4 * 2**20,
+                bytes_accessed=0,
                 transcendentals=0,
             ),
             name=name,
@@ -272,22 +276,25 @@
             )
         shapes = [float_shape(sizes[index])] * 2
         mine, away = step_call(split_sum_kernel, shapes, mine, arrived[-1], name="sum_x")
-        return mine, swap(away, "z", 1)
+        return mine, swap(away, Z, 1)
 
     def sum_low(index, mine, arrived):
         (mine,) = step_call(sum_kernel, [float_shape(sizes[index])], mine, arrived, name="sum_z")
         bits = 2
         while 2 * bits < z_count:
             (mine,) = step_call(
-                sum_kernel, [float_shape(sizes[index])], mine, swap(mine, "z", bits), name="sum_z"
+                sum_kernel, [float_shape(sizes[index])], mine, swap(mine, Z, bits), name="sum_z"
             )
             bits *= 2
-        return mine, swap(mine, "z", bits)
-
-    def to_owners(value):
+        return mine, swap(mine, Z, bits)
+
+    def to_owners(value, last_batch):
+        if not last_batch:
+            return [lax.all_gather(value, ("z_low", "y"))]
         both = [(i, i ^ (y_count + 1)) for i in range(block_count)]
-        over_both = lax.ppermute(value, ("z", "y"), both)
-        return [value, swap(value, "z", 1), swap(value, "y", 1), over_both]
+        over_both = lax.ppermute(value, (*Z, "y"), both)
+        parts = [value, swap(value, Z, 1), swap(value, "y", 1), over_both]
+        return [part[None] for part in parts]
 
     parts = []
     state = [sum_core(index) for index in range(GROUPS)]
@@ -302,13 +309,13 @@
             )
         else:
             counts = [sizes[index] for index in which]
-            shape = (SCALE_ROWS + sum(counts) * rows_dev, block_size)
+            shape = (SCALE_ROWS + sum(counts) * rows_dev // 2, block_size)
             kernel = functools.partial(code_kernel, counts, [len(state[i]) for i in which])
             operands = [value for index in which for value in state[index]]
             (code,) = step_call(
-                kernel, [jax.ShapeDtypeStruct(shape, jnp.int16)], *operands, name="finish"
-            )
-            parts += to_owners(code)
+                kernel, [jax.ShapeDtypeStruct(shape, jnp.int32)], *operands, name="finish"
+            )
+            parts += to_owners(code, which == BATCHES[-1])
 
     table = tile_table[0]
     row_block = table[:, 0]
@@ -317,9 +324,12 @@
     second = jnp.maximum(col_block, 0)
     pair = first * block_count - (first * (first - 1)) // 2 + second - first
     of_list, slot = pair // quarter, pair % quarter
-    off = ((of_list // 2) ^ y) * 2 + ((of_list % 2) ^ low_bit)
+    of_y, of_bit = of_list // 2, of_list % 2
     tile, lane, exponent_row, steps_row = (jnp.zeros_like(slot) for _ in range(4))
     for index, batch in enumerate(BATCHES):
+        off = of_bit * 2 + of_y
+        if batch == BATCHES[-1]:
+            off = (of_y ^ y) * 2 + (of_bit ^ low_bit)
         start, end = int(starts[batch[0]]), int(starts[batch[-1] + 1])
         inside = (slot >= start) & (slot < end)
         header_rows = -(-(end - start) * rows_dev // block_size)
@@ -339,8 +349,8 @@
         in_specs=[pl.BlockSpec(memory_space=pltpu.SMEM)] + [vmem] * len(parts),
         out_specs=vmem,
         scratch_shapes=[
-            pltpu.VMEM((4 * quarter * rows_dev, block_size), jnp.int16),
-            pltpu.VMEM((len(parts) * SCALE_ROWS, block_size), jnp.float32),
+            pltpu.VMEM((4 * quarter * rows_dev // 2, block_size), jnp.int32),
+            pltpu.VMEM((4 * len(BATCHES) * SCALE_ROWS, block_size), jnp.float32),
         ],
         compiler_params=pltpu.CompilerParams(vmem_limit_bytes=VMEM_LIMIT),
         cost_estimate=pl.CostEstimate(
@@ -354,9 +364,9 @@
 def solution(mesh):
     tm, space = mesh.shape["tm"], mesh.shape["space"]
     sizes = (tm // 2, 2, space // 2, 2)
-    grid = Mesh(mesh.devices.reshape(sizes), ("z", "y", "x", "core"))
-    in_specs = (P(None, ("z", "y"), ("x", "core")), P(("z", "y"), None, None))
-    out_specs = P(("z", "y"), None, ("x", "core"), None)
+    grid = Mesh(mesh.devices.reshape((tm // 4, 2, *sizes[1:])), (*Z, "y", "x", "core"))
+    in_specs = (P(None, (*Z, "y"), ("x", "core")), P((*Z, "y"), None, None))
+    out_specs = P((*Z, "y"), None, ("x", "core"), None)
     return jax.shard_map(
         functools.partial(per_device, *sizes),
         mesh=grid,

time: 120 us -> 133 us (1.11)
  blocking collectives: 0 us -> 28.1 us
  waiting for transfers between devices: 78.8 us -> 67.3 us
  starting transfers between devices: 30.3 us -> 26.5 us
    all_gather x0 -> x2, blocking collectives: none -> 28.1 us  [to_owners(): return [lax.all_gather(value, ('z_low', 'y'))]]
    ppermute x23 -> x21, waiting for transfers between devices: 74.8 us -> 67.3 us  [swap(): return lax.ppermute(value, axis, [(i, i ^ bits) for i in range(size)])]
    ppermute x2 -> x1, waiting for transfers between devices: 3.96 us -> 0.01 us  [to_owners(): over_both = lax.ppermute(value, (*Z, 'y'), both)]
    ppermute x23 -> x21, starting transfers between devices: 27.9 us -> 24.1 us  [swap(): return lax.ppermute(value, axis, [(i, i ^ bits) for i in range(size)])]
  transfers between devices with their start and end apart: 25 -> 22, of which waited for: 16 -> 12; matrix products, arithmetic and copies ran while one was open for 1% -> 1% of each run, Pallas kernels for 3% -> 3%
where the time goes in v10:
time: 133 us
  waiting for transfers between devices  67.3 us (51%)
  blocking collectives  28.1 us (21%)
  starting transfers between devices  26.5 us (20%)
  Pallas kernels  8.61 us (6%)
  local copies, waits for them, and re-layouts  2.33 us (2%)
    ppermute x21, waiting for transfers between devices, swap(): return lax.ppermute(value, axis, [(i, i ^ bits) for i in range(size)])  67.3 us
    all_gather x2, blocking collectives, to_owners(): return [lax.all_gather(value, ('z_low', 'y'))]  28.1 us
    ppermute x21, starting transfers between devices, swap(): return lax.ppermute(value, axis, [(i, i ^ bits) for i in range(size)])  24.1 us
    pallas_call x2, Pallas kernels, call(): pl.pallas_call(kernel, out_shape=out_shape, in_specs=[pl.BlockSpec(memory...  5.06 us
  transfers between devices with their start and end apart: 22, of which 12 were waited for; matrix products, arithmetic and copies ran while one was open for 1% of the time, Pallas kernels for 3%

profile of v10, /device:TPU:0, one launch (start us, length us, event | category | flops | bytes accessed | tf_op | source)
XLA Modules:
  0.0 133.1 jit_solution(12922597673436877396)
XLA Ops:
  0.0 1.5 %constant_dynamic-slice_fusion = (bf16[3,256,256]{2,1,0:T(8,128)(2,1)S(1)}, bf16[3,256,256]{2,1,0:T(8,128)(2,1)S(1)}, bf16[3,256,256]{2,1,0:T(8,128)(2,1)S(1)}, bf16[3,256,256]{2,1,0:T(8,128)(2,1)S(1)}) fusion(bf16[3,256,1024]{2,1,0:T(8,128)(2,1)} %param.3, s32[]{:T(128)S(6)} %select_n.122, s32[]{:T(128)S(6)} %select_n.120, s32[]{:T(128)S(6)} %select_n.119, ...), kind=kLoop, calls=%fused_computation.15 | loop fusion | bytes 3145744 | tf_op jit(solution)/shard_map/dynamic_slice | solution.py:197
  1.5 5.1 %collective-permute-start.2 = (bf16[3,256,256]{2,1,0:T(8,128)(2,1)S(1)}, bf16[3,256,256]{2,1,0:T(8,128)(2,1)S(1)}, u32[]{:S(2)}, u32[]{:S(2)}) collective-permute-start(bf16[3,256,256]{2,1,0:T(8,128)(2,1)S(1)} %get-tuple-element.104), channel_id=1, source_target_pairs={{0,24},{8,16},{16,8},{24,0},{1,25},{9,17},{17,9},{25,1},{2,26},{10... | collective-permute-start | bytes 1179656 | tf_op jit(solution)/shard_map/ppermute | solution.py:174
  6.6 0.0 collective-permute-start
  6.6 0.6 collective-permute-start.1
  7.2 1.7 %collective-permute-start.3 = (bf16[3,256,256]{2,1,0:T(8,128)(2,1)S(1)}, bf16[3,256,256]{2,1,0:T(8,128)(2,1)S(1)}, u32[]{:S(2)}, u32[]{:S(2)}) collective-permute-start(bf16[3,256,256]{2,1,0:T(8,128)(2,1)S(1)} %get-tuple-element.106.refs_0_), channel_id=1, source_target_pairs={{0,4},{4,0},{1,5},{5,1},{2,6},{6,2},{3,7},{7,3},{8,12},{12,8},{9,1... | collective-permute-start | bytes 1179656 | tf_op jit(solution)/shard_map/ppermute | solution.py:174
  8.9 7.7 %collective-permute-done.2.refs_3_ = bf16[3,256,256]{2,1,0:T(8,128)(2,1)S(1)} collective-permute-done((bf16[3,256,256]{2,1,0:T(8,128)(2,1)S(1)}, bf16[3,256,256]{2,1,0:T(8,128)(2,1)S(1)}, u32[]{:S(2)}, u32[]{:S(2)}) %collective-permute-start.2) | collective-permute-done | bytes 393248 | tf_op jit(solution)/shard_map/ppermute | solution.py:174
  16.6 1.7 %collective-permute-start.6 = (bf16[3,256,256]{2,1,0:T(8,128)(2,1)S(1)}, bf16[3,256,256]{2,1,0:T(8,128)(2,1)S(1)}, u32[]{:S(2)}, u32[]{:S(2)}) collective-permute-start(bf16[3,256,256]{2,1,0:T(8,128)(2,1)S(1)} %collective-permute-done.2.refs_3_), channel_id=1, source_target_pairs={{0,4},{4,0},{1,5},{5,1},{2,6},{6,2},{3,7},{7,3},{8,12},{12,8},{9,1... | collective-permute-start | bytes 1179656 | tf_op jit(solution)/shard_map/ppermute | solution.py:174
  18.3 6.9 %collective-permute-done.refs_1_ = bf16[3,256,256]{2,1,0:T(8,128)(2,1)S(1)} collective-permute-done((bf16[3,256,256]{2,1,0:T(8,128)(2,1)S(1)}, bf16[3,256,256]{2,1,0:T(8,128)(2,1)S(1)}, u32[]{:S(2)}, u32[]{:S(2)}) %collective-permute-start) | collective-permute-done | bytes 393248 | tf_op jit(solution)/shard_map/ppermute | solution.py:174
  25.3 1.4 %collective-permute-start.4 = (bf16[3,256,256]{2,1,0:T(8,128)(2,1)S(1)}, bf16[3,256,256]{2,1,0:T(8,128)(2,1)S(1)}, u32[]{:S(2)}, u32[]{:S(2)}) collective-permute-start(bf16[3,256,256]{2,1,0:T(8,128)(2,1)S(1)} %collective-permute-done.refs_1_), channel_id=1, source_target_pairs={{0,4},{4,0},{1,5},{5,1},{2,6},{6,2},{3,7},{7,3},{8,12},{12,8},{9,1... | collective-permute-start | bytes 1179656 | tf_op jit(solution)/shard_map/ppermute | solution.py:174
  26.7 13.5 %collective-permute-done.1.refs_2_ = bf16[3,256,256]{2,1,0:T(8,128)(2,1)S(1)} collective-permute-done((bf16[3,256,256]{2,1,0:T(8,128)(2,1)S(1)}, bf16[3,256,256]{2,1,0:T(8,128)(2,1)S(1)}, u32[]{:S(2)}, u32[]{:S(2)}) %collective-permute-start.1) | collective-permute-done | bytes 393248 | tf_op jit(solution)/shard_map/ppermute | solution.py:174
  40.1 1.5 %collective-permute-start.5 = (bf16[3,256,256]{2,1,0:T(8,128)(2,1)S(1)}, bf16[3,256,256]{2,1,0:T(8,128)(2,1)S(1)}, u32[]{:S(2)}, u32[]{:S(2)}) collective-permute-start(bf16[3,256,256]{2,1,0:T(8,128)(2,1)S(1)} %collective-permute-done.1.refs_2_), channel_id=1, source_target_pairs={{0,4},{4,0},{1,5},{5,1},{2,6},{6,2},{3,7},{7,3},{8,12},{12,8},{9,1... | collective-permute-start | bytes 1179656 | tf_op jit(solution)/shard_map/ppermute | solution.py:174
  41.7 0.7 fusion.3
  42.3 0.1 concatenate.7.scalars
  42.4 0.0 collective-permute-done.3.refs_4_
  42.4 0.0 collective-permute-done.6.refs_7_
  42.4 0.0 collective-permute-done.4.refs_5_
  42.4 7.9 %collective-permute-done.5.refs_6_ = bf16[3,256,256]{2,1,0:T(8,128)(2,1)S(1)} collective-permute-done((bf16[3,256,256]{2,1,0:T(8,128)(2,1)S(1)}, bf16[3,256,256]{2,1,0:T(8,128)(2,1)S(1)}, u32[]{:S(2)}, u32[]{:S(2)}) %collective-permute-start.5) | collective-permute-done | bytes 393248 | tf_op jit(solution)/shard_map/ppermute | solution.py:174
  50.3 2.0 %tiles_first.1 = (bf16[8,256,768]{2,1,0:T(8,128)(2,1)S(1)}, f32[2,2,3,64,256]{4,3,2,1,0:T(8,128)S(1)}, f32[2,2,3,64,256]{4,3,2,1,0:T(8,128)S(1)}) custom-call(s32[40]{0:T(128)S(1)} %concatenate.7.scalars, bf16[3,256,256]{2,1,0:T(8,128)(2,1)S(1)} %get-tuple-element.106.refs_0_, bf16[3,256,256]{2,1,0:T(8,128)(2,1)S(1)} %collective-permute-done.refs_1_, ...), custom_call_target="tpu_custom_call" | custom-call | flops 603979776 | tf_op jit(solution)/shard_map/tiles_first/pallas_call | solution.py:211
  52.3 0.1 collective-permute-start.7
  52.4 3.1 %tiles_second.1 = (f32[2,2,3,64,256]{4,3,2,1,0:T(8,128)S(1)}, f32[2,2,3,64,256]{4,3,2,1,0:T(8,128)S(1)}, f32[2,2,3,64,256]{4,3,2,1,0:T(8,128)S(1)}, f32[2,2,3,64,256]{4,3,2,1,0:T(8,128)S(1)}) custom-call(s32[40]{0:T(128)S(1)} %concatenate.7.scalars, bf16[8,256,768]{2,1,0:T(8,128)(2,1)S(1)} %get-tuple-element.55.blocks), custom_call_target="tpu_custom_call" | custom-call | flops 1207959552 | tf_op jit(solution)/shard_map/tiles_second/pallas_call | solution.py:211
  55.5 0.6 collective-permute-start.10
  56.0 0.1 collective-permute-start.9
  56.1 0.0 collective-permute-done.7.right
  56.1 0.0 copy-start
  56.1 0.1 sum_core.3
  56.2 1.6 %collective-permute-start.8 = (f32[2,3,64,256]{3,2,1,0:T(8,128)S(1)}, f32[2,3,64,256]{3,2,1,0:T(8,128)S(1)}, u32[]{:S(2)}, u32[]{:S(2)}) collective-permute-start(f32[2,3,64,256]{3,2,1,0:T(8,128)S(1)} %get-tuple-element.54), channel_id=1, source_target_pairs={{0,2},{2,0},{1,3},{3,1},{4,6},{6,4},{5,7},{7,5},{8,10},{10,8},{9,1... | collective-permute-start | bytes 1179656 | tf_op jit(solution)/shard_map/ppermute | solution.py:174
  57.7 0.2 collective-permute-done.10.right
  57.9 0.1 sum_core.4
  58.0 1.6 %collective-permute-start.13 = (f32[2,3,64,256]{3,2,1,0:T(8,128)S(1)}, f32[2,3,64,256]{3,2,1,0:T(8,128)S(1)}, u32[]{:S(2)}, u32[]{:S(2)}) collective-permute-start(f32[2,3,64,256]{3,2,1,0:T(8,128)S(1)} %get-tuple-element.72), channel_id=1, source_target_pairs={{0,2},{2,0},{1,3},{3,1},{4,6},{6,4},{5,7},{7,5},{8,10},{10,8},{9,1... | collective-permute-start | bytes 1179656 | tf_op jit(solution)/shard_map/ppermute | solution.py:174
  59.6 0.0 copy-done
  59.6 0.0 collective-permute-done.9.right
  59.6 0.1 sum_core.5
  59.7 1.0 collective-permute-start.16
  60.7 7.5 %collective-permute-done.8.right = f32[2,3,64,256]{3,2,1,0:T(8,128)S(1)} collective-permute-done((f32[2,3,64,256]{3,2,1,0:T(8,128)S(1)}, f32[2,3,64,256]{3,2,1,0:T(8,128)S(1)}, u32[]{:S(2)}, u32[]{:S(2)}) %collective-permute-start.8) | collective-permute-done | bytes 393248 | tf_op jit(solution)/shard_map/ppermute | solution.py:174
  68.2 0.6 collective-permute-start.11
  68.9 5.4 %collective-permute-done.11.right = f32[3,64,256]{2,1,0:T(8,128)S(1)} collective-permute-done((f32[3,64,256]{2,1,0:T(8,128)S(1)}, f32[3,64,256]{2,1,0:T(8,128)S(1)}, u32[]{:S(2)}, u32[]{:S(2)}) %collective-permute-start.11) | collective-permute-done | bytes 196640 | tf_op jit(solution)/shard_map/ppermute | solution.py:174
  74.3 1.5 %collective-permute-start.12 = (f32[3,64,256]{2,1,0:T(8,128)S(1)}, f32[3,64,256]{2,1,0:T(8,128)S(1)}, u32[]{:S(2)}, u32[]{:S(2)}) collective-permute-start(f32[3,64,256]{2,1,0:T(8,128)S(1)} %sum_z.3.refs_0_), channel_id=1, source_target_pairs={{0,16},{8,24},{16,0},{24,8},{1,17},{9,25},{17,1},{25,9},{2,18},{10... | collective-permute-start | bytes 589832 | tf_op jit(solution)/shard_map/ppermute | solution.py:174
  75.8 0.8 collective-permute-done.13.right
  76.6 0.7 collective-permute-start.14
  77.4 7.3 %collective-permute-done.12.refs_1_ = f32[3,64,256]{2,1,0:T(8,128)S(1)} collective-permute-done((f32[3,64,256]{2,1,0:T(8,128)S(1)}, f32[3,64,256]{2,1,0:T(8,128)S(1)}, u32[]{:S(2)}, u32[]{:S(2)}) %collective-permute-start.12) | collective-permute-done | bytes 196640 | tf_op jit(solution)/shard_map/ppermute | solution.py:174
  84.7 0.2 finish.3
  84.9 1.8 %collective-permute-done.14.right = f32[3,64,256]{2,1,0:T(8,128)S(1)} collective-permute-done((f32[3,64,256]{2,1,0:T(8,128)S(1)}, f32[3,64,256]{2,1,0:T(8,128)S(1)}, u32[]{:S(2)}, u32[]{:S(2)}) %collective-permute-start.14) | collective-permute-done | bytes 196640 | tf_op jit(solution)/shard_map/ppermute | solution.py:174
  86.7 0.4 collective-permute-start.15
  87.2 0.0 collective-permute-done.16.right
  87.2 2.5 %collective-permute-start.17 = (f32[3,64,256]{2,1,0:T(8,128)S(1)}, f32[3,64,256]{2,1,0:T(8,128)S(1)}, u32[]{:S(2)}, u32[]{:S(2)}) collective-permute-start(f32[3,64,256]{2,1,0:T(8,128)S(1)} %get-tuple-element.87), channel_id=1, source_target_pairs={{0,8},{8,0},{16,24},{24,16},{1,9},{9,1},{17,25},{25,17},{2,10},{10... | collective-permute-start | bytes 589832 | tf_op jit(solution)/shard_map/ppermute | solution.py:174
  89.8 8.0 %collective-permute-done.15.right = f32[3,64,256]{2,1,0:T(8,128)S(1)} collective-permute-done((f32[3,64,256]{2,1,0:T(8,128)S(1)}, f32[3,64,256]{2,1,0:T(8,128)S(1)}, u32[]{:S(2)}, u32[]{:S(2)}) %collective-permute-start.15) | collective-permute-done | bytes 196640 | tf_op jit(solution)/shard_map/ppermute | solution.py:174
  97.8 0.2 collective-permute-done.17.right
  98.1 0.3 collective-permute-start.18
  98.4 0.1 concatenate.6.scalars
  98.5 14.7 %all-gather = s32[416,256]{1,0:T(8,128)S(1)} all-gather(s32[104,256]{1,0:T(8,128)S(1)} %finish.3), channel_id=2, replica_groups=mesh['z_high'=2,'z_low'=2,'y'=2,'x'=2,'core'=2] {'z_low','y'}, dimensions={0}, use_global_device_ids=true | all-gather | bytes 532480 | tf_op jit(solution)/shard_map/all_gather | solution.py:293
  113.2 0.2 finish.4
  113.4 0.0 collective-permute-done.18.refs_1_
  113.4 0.2 finish.5
  113.6 2.5 %collective-permute-start.21 = (s32[104,256]{1,0:T(8,128)S(1)}, s32[104,256]{1,0:T(8,128)S(1)}, u32[]{:S(2)}, u32[]{:S(2)}) collective-permute-start(s32[104,256]{1,0:T(8,128)S(1)} %finish.5), channel_id=1, source_target_pairs={{0,12},{4,8},{8,4},{12,0},{16,28},{20,24},{24,20},{28,16},{1,13},{... | collective-permute-start | bytes 319496 | tf_op jit(solution)/shard_map/ppermute | solution.py:295
  116.1 0.5 collective-permute-start.20
  116.6 0.6 collective-permute-start.19
  117.2 13.5 %all-gather.1 = s32[416,256]{1,0:T(8,128)S(1)} all-gather(s32[104,256]{1,0:T(8,128)S(1)} %finish.4), channel_id=3, replica_groups=mesh['z_high'=2,'z_low'=2,'y'=2,'x'=2,'core'=2] {'z_low','y'}, dimensions={0}, use_global_device_ids=true | all-gather | bytes 532480 | tf_op jit(solution)/shard_map/all_gather | solution.py:293
  130.6 0.0 collective-permute-done.21
  130.7 0.0 collective-permute-done.20
  130.7 0.0 collective-permute-done.19
  130.7 2.4 %place_tiles.1 = f32[10,64,256]{2,1,0:T(8,128)} custom-call(s32[50]{0:T(128)S(1)} %concatenate.6.scalars, s32[4,104,256]{2,1,0:T(8,128)S(1)} %bitcast.32, s32[4,104,256]{2,1,0:T(8,128)S(1)} %bitcast.33, s32[1,104,256]{2,1,0:T(8,128)S(1)} %bitcast.34, s32[1,104,256]{2,1,0:T(8,128)S(1)} %bitcast.37, s32[1,104,256]{2,1,0:T(8,128)S(1)} %bitcast.36, ...), custom_call_target="tpu_custom_call" | custom-call | flops 163840 | tf_op jit(solution)/shard_map/place_tiles/pallas_call | solution.py:346
  (12 shorter events, 0.3 us)
Async XLA Ops:
  1.5 15.1 %collective-permute-start.2 = (bf16[3,256,256]{2,1,0:T(8,128)(2,1)S(1)}, bf16[3,256,256]{2,1,0:T(8,128)(2,1)S(1)}, u32[]{:S(2)}, u32[]{:S(2)}) collective-permute-start(bf16[3,256,256]{2,1,0:T(8,128)(2,1)S(1)} %get-tuple-element.104), channel_id=1, source_target_pairs={{0,24},{8,16},{16,8},{24,0},{1,25},{9,17},{17,9},{25,1},{2,26},{10... | collective-permute-start | bytes 1179656 | tf_op jit(solution)/shard_map/ppermute | solution.py:174
  6.6 18.7 %collective-permute-start = (bf16[3,256,256]{2,1,0:T(8,128)(2,1)S(1)}, bf16[3,256,256]{2,1,0:T(8,128)(2,1)S(1)}, u32[]{:S(2)}, u32[]{:S(2)}) collective-permute-start(bf16[3,256,256]{2,1,0:T(8,128)(2,1)S(1)} %get-tuple-element.105), channel_id=1, source_target_pairs={{0,8},{8,0},{16,24},{24,16},{1,9},{9,1},{17,25},{25,17},{2,10},{10... | collective-permute-start | bytes 1179656 | tf_op jit(solution)/shard_map/ppermute | solution.py:174
  6.6 33.5 %collective-permute-start.1 = (bf16[3,256,256]{2,1,0:T(8,128)(2,1)S(1)}, bf16[3,256,256]{2,1,0:T(8,128)(2,1)S(1)}, u32[]{:S(2)}, u32[]{:S(2)}) collective-permute-start(bf16[3,256,256]{2,1,0:T(8,128)(2,1)S(1)} %get-tuple-element.107), channel_id=1, source_target_pairs={{0,16},{8,24},{16,0},{24,8},{1,17},{9,25},{17,1},{25,9},{2,18},{10... | collective-permute-start | bytes 1179656 | tf_op jit(solution)/shard_map/ppermute | solution.py:174
  7.2 35.2 %collective-permute-start.3 = (bf16[3,256,256]{2,1,0:T(8,128)(2,1)S(1)}, bf16[3,256,256]{2,1,0:T(8,128)(2,1)S(1)}, u32[]{:S(2)}, u32[]{:S(2)}) collective-permute-start(bf16[3,256,256]{2,1,0:T(8,128)(2,1)S(1)} %get-tuple-element.106.refs_0_), channel_id=1, source_target_pairs={{0,4},{4,0},{1,5},{5,1},{2,6},{6,2},{3,7},{7,3},{8,12},{12,8},{9,1... | collective-permute-start | bytes 1179656 | tf_op jit(solution)/shard_map/ppermute | solution.py:174
  16.6 25.8 %collective-permute-start.6 = (bf16[3,256,256]{2,1,0:T(8,128)(2,1)S(1)}, bf16[3,256,256]{2,1,0:T(8,128)(2,1)S(1)}, u32[]{:S(2)}, u32[]{:S(2)}) collective-permute-start(bf16[3,256,256]{2,1,0:T(8,128)(2,1)S(1)} %collective-permute-done.2.refs_3_), channel_id=1, source_target_pairs={{0,4},{4,0},{1,5},{5,1},{2,6},{6,2},{3,7},{7,3},{8,12},{12,8},{9,1... | collective-permute-start | bytes 1179656 | tf_op jit(solution)/shard_map/ppermute | solution.py:174
  25.3 17.2 %collective-permute-start.4 = (bf16[3,256,256]{2,1,0:T(8,128)(2,1)S(1)}, bf16[3,256,256]{2,1,0:T(8,128)(2,1)S(1)}, u32[]{:S(2)}, u32[]{:S(2)}) collective-permute-start(bf16[3,256,256]{2,1,0:T(8,128)(2,1)S(1)} %collective-permute-done.refs_1_), channel_id=1, source_target_pairs={{0,4},{4,0},{1,5},{5,1},{2,6},{6,2},{3,7},{7,3},{8,12},{12,8},{9,1... | collective-permute-start | bytes 1179656 | tf_op jit(solution)/shard_map/ppermute | solution.py:174
  40.1 10.2 %collective-permute-start.5 = (bf16[3,256,256]{2,1,0:T(8,128)(2,1)S(1)}, bf16[3,256,256]{2,1,0:T(8,128)(2,1)S(1)}, u32[]{:S(2)}, u32[]{:S(2)}) collective-permute-start(bf16[3,256,256]{2,1,0:T(8,128)(2,1)S(1)} %collective-permute-done.1.refs_2_), channel_id=1, source_target_pairs={{0,4},{4,0},{1,5},{5,1},{2,6},{6,2},{3,7},{7,3},{8,12},{12,8},{9,1... | collective-permute-start | bytes 1179656 | tf_op jit(solution)/shard_map/ppermute | solution.py:174
  52.3 3.8 %collective-permute-start.7 = (f32[2,2,3,64,256]{4,3,2,1,0:T(8,128)S(1)}, f32[2,2,3,64,256]{4,3,2,1,0:T(8,128)S(1)}, u32[]{:S(2)}, u32[]{:S(2)}) collective-permute-start(f32[2,2,3,64,256]{4,3,2,1,0:T(8,128)S(1)} %get-tuple-element.50), channel_id=1, source_target_pairs={{0,1},{1,0},{2,3},{3,2},{4,5},{5,4},{6,7},{7,6},{8,9},{9,8},{10,11... | collective-permute-start | bytes 2359304 | tf_op jit(solution)/shard_map/ppermute | solution.py:174
  55.5 2.5 %collective-permute-start.10 = (f32[2,2,3,64,256]{4,3,2,1,0:T(8,128)S(1)}, f32[2,2,3,64,256]{4,3,2,1,0:T(8,128)S(1)}, u32[]{:S(2)}, u32[]{:S(2)}) collective-permute-start(f32[2,2,3,64,256]{4,3,2,1,0:T(8,128)S(1)} %get-tuple-element.59), channel_id=1, source_target_pairs={{0,1},{1,0},{2,3},{3,2},{4,5},{5,4},{6,7},{7,6},{8,9},{9,8},{10,11... | collective-permute-start | bytes 2359304 | tf_op jit(solution)/shard_map/ppermute | solution.py:174
  56.0 3.6 %collective-permute-start.9 = (f32[2,2,3,64,256]{4,3,2,1,0:T(8,128)S(1)}, f32[2,2,3,64,256]{4,3,2,1,0:T(8,128)S(1)}, u32[]{:S(2)}, u32[]{:S(2)}) collective-permute-start(f32[2,2,3,64,256]{4,3,2,1,0:T(8,128)S(1)} %get-tuple-element.57), channel_id=1, source_target_pairs={{0,1},{1,0},{2,3},{3,2},{4,5},{5,4},{6,7},{7,6},{8,9},{9,8},{10,11... | collective-permute-start | bytes 2359304 | tf_op jit(solution)/shard_map/ppermute | solution.py:174
  56.1 3.5 %copy-start = (s32[1,10,2]{1,2,0:T(2,128)S(1)}, s32[1,10,2]{1,2,0:T(2,128)}, u32[]{:S(2)}) copy-start(s32[1,10,2]{1,2,0:T(2,128)} %param.4) | copy-start | bytes 244
  56.2 12.0 %collective-permute-start.8 = (f32[2,3,64,256]{3,2,1,0:T(8,128)S(1)}, f32[2,3,64,256]{3,2,1,0:T(8,128)S(1)}, u32[]{:S(2)}, u32[]{:S(2)}) collective-permute-start(f32[2,3,64,256]{3,2,1,0:T(8,128)S(1)} %get-tuple-element.54), channel_id=1, source_target_pairs={{0,2},{2,0},{1,3},{3,1},{4,6},{6,4},{5,7},{7,5},{8,10},{10,8},{9,1... | collective-permute-start | bytes 1179656 | tf_op jit(solution)/shard_map/ppermute | solution.py:174
  58.0 18.6 %collective-permute-start.13 = (f32[2,3,64,256]{3,2,1,0:T(8,128)S(1)}, f32[2,3,64,256]{3,2,1,0:T(8,128)S(1)}, u32[]{:S(2)}, u32[]{:S(2)}) collective-permute-start(f32[2,3,64,256]{3,2,1,0:T(8,128)S(1)} %get-tuple-element.72), channel_id=1, source_target_pairs={{0,2},{2,0},{1,3},{3,1},{4,6},{6,4},{5,7},{7,5},{8,10},{10,8},{9,1... | collective-permute-start | bytes 1179656 | tf_op jit(solution)/shard_map/ppermute | solution.py:174
  59.7 27.5 %collective-permute-start.16 = (f32[2,3,64,256]{3,2,1,0:T(8,128)S(1)}, f32[2,3,64,256]{3,2,1,0:T(8,128)S(1)}, u32[]{:S(2)}, u32[]{:S(2)}) collective-permute-start(f32[2,3,64,256]{3,2,1,0:T(8,128)S(1)} %get-tuple-element.81), channel_id=1, source_target_pairs={{0,2},{2,0},{1,3},{3,1},{4,6},{6,4},{5,7},{7,5},{8,10},{10,8},{9,1... | collective-permute-start | bytes 1179656 | tf_op jit(solution)/shard_map/ppermute | solution.py:174
  68.2 6.1 %collective-permute-start.11 = (f32[3,64,256]{2,1,0:T(8,128)S(1)}, f32[3,64,256]{2,1,0:T(8,128)S(1)}, u32[]{:S(2)}, u32[]{:S(2)}) collective-permute-start(f32[3,64,256]{2,1,0:T(8,128)S(1)} %get-tuple-element.69), channel_id=1, source_target_pairs={{0,8},{8,0},{16,24},{24,16},{1,9},{9,1},{17,25},{25,17},{2,10},{10... | collective-permute-start | bytes 589832 | tf_op jit(solution)/shard_map/ppermute | solution.py:174
  74.3 10.4 %collective-permute-start.12 = (f32[3,64,256]{2,1,0:T(8,128)S(1)}, f32[3,64,256]{2,1,0:T(8,128)S(1)}, u32[]{:S(2)}, u32[]{:S(2)}) collective-permute-start(f32[3,64,256]{2,1,0:T(8,128)S(1)} %sum_z.3.refs_0_), channel_id=1, source_target_pairs={{0,16},{8,24},{16,0},{24,8},{1,17},{9,25},{17,1},{25,9},{2,18},{10... | collective-permute-start | bytes 589832 | tf_op jit(solution)/shard_map/ppermute | solution.py:174
  76.6 10.1 %collective-permute-start.14 = (f32[3,64,256]{2,1,0:T(8,128)S(1)}, f32[3,64,256]{2,1,0:T(8,128)S(1)}, u32[]{:S(2)}, u32[]{:S(2)}) collective-permute-start(f32[3,64,256]{2,1,0:T(8,128)S(1)} %get-tuple-element.78), channel_id=1, source_target_pairs={{0,8},{8,0},{16,24},{24,16},{1,9},{9,1},{17,25},{25,17},{2,10},{10... | collective-permute-start | bytes 589832 | tf_op jit(solution)/shard_map/ppermute | solution.py:174
  86.7 11.1 %collective-permute-start.15 = (f32[3,64,256]{2,1,0:T(8,128)S(1)}, f32[3,64,256]{2,1,0:T(8,128)S(1)}, u32[]{:S(2)}, u32[]{:S(2)}) collective-permute-start(f32[3,64,256]{2,1,0:T(8,128)S(1)} %sum_z.4.left), channel_id=1, source_target_pairs={{0,16},{8,24},{16,0},{24,8},{1,17},{9,25},{17,1},{25,9},{2,18},{10... | collective-permute-start | bytes 589832 | tf_op jit(solution)/shard_map/ppermute | solution.py:174
  87.2 10.9 %collective-permute-start.17 = (f32[3,64,256]{2,1,0:T(8,128)S(1)}, f32[3,64,256]{2,1,0:T(8,128)S(1)}, u32[]{:S(2)}, u32[]{:S(2)}) collective-permute-start(f32[3,64,256]{2,1,0:T(8,128)S(1)} %get-tuple-element.87), channel_id=1, source_target_pairs={{0,8},{8,0},{16,24},{24,16},{1,9},{9,1},{17,25},{25,17},{2,10},{10... | collective-permute-start | bytes 589832 | tf_op jit(solution)/shard_map/ppermute | solution.py:174
  98.1 15.3 %collective-permute-start.18 = (f32[3,64,256]{2,1,0:T(8,128)S(1)}, f32[3,64,256]{2,1,0:T(8,128)S(1)}, u32[]{:S(2)}, u32[]{:S(2)}) collective-permute-start(f32[3,64,256]{2,1,0:T(8,128)S(1)} %sum_z.5.refs_0_), channel_id=1, source_target_pairs={{0,16},{8,24},{16,0},{24,8},{1,17},{9,25},{17,1},{25,9},{2,18},{10... | collective-permute-start | bytes 589832 | tf_op jit(solution)/shard_map/ppermute | solution.py:174
  113.6 17.0 %collective-permute-start.21 = (s32[104,256]{1,0:T(8,128)S(1)}, s32[104,256]{1,0:T(8,128)S(1)}, u32[]{:S(2)}, u32[]{:S(2)}) collective-permute-start(s32[104,256]{1,0:T(8,128)S(1)} %finish.5), channel_id=1, source_target_pairs={{0,12},{4,8},{8,4},{12,0},{16,28},{20,24},{24,20},{28,16},{1,13},{... | collective-permute-start | bytes 319496 | tf_op jit(solution)/shard_map/ppermute | solution.py:295
  116.1 14.5 %collective-permute-start.20 = (s32[104,256]{1,0:T(8,128)S(1)}, s32[104,256]{1,0:T(8,128)S(1)}, u32[]{:S(2)}, u32[]{:S(2)}) collective-permute-start(s32[104,256]{1,0:T(8,128)S(1)} %finish.5), channel_id=1, source_target_pairs={{0,4},{4,0},{1,5},{5,1},{2,6},{6,2},{3,7},{7,3},{8,12},{12,8},{9,1... | collective-permute-start | bytes 319496 | tf_op jit(solution)/shard_map/ppermute | solution.py:174
  116.6 14.0 %collective-permute-start.19 = (s32[104,256]{1,0:T(8,128)S(1)}, s32[104,256]{1,0:T(8,128)S(1)}, u32[]{:S(2)}, u32[]{:S(2)}) collective-permute-start(s32[104,256]{1,0:T(8,128)S(1)} %finish.5), channel_id=1, source_target_pairs={{0,8},{8,0},{16,24},{24,16},{1,9},{9,1},{17,25},{25,17},{2,10},{10... | collective-permute-start | bytes 319496 | tf_op jit(solution)/shard_map/ppermute | solution.py:174

commit v11 on v8

--- a/solution.py
+++ b/solution.py
@@ -12,9 +12,10 @@
 VMEM_LIMIT = 24 * 2**20
 GROUPS = 3
 BATCHES = ((0, 1), (2,))
+LOW_FIRST = (0,)
 ORDER = (
-    ("x", 0), ("low", 0), ("x", 1), ("high", 0), ("low", 1),
-    ("x", 2), ("low", 2), ("finish", BATCHES[0]), ("finish", BATCHES[1]),
+    ("core", 0), ("core", 1), ("x", 1), ("low", 0), ("low", 1), ("core", 2), ("x", 0),
+    ("x", 2), ("high", 1), ("low", 2), ("finish", BATCHES[0]), ("finish", BATCHES[1]),
 )
 CODE_TOP = 32767.0
 SCALE_ROWS = 16
@@ -30,7 +31,7 @@
     return [len(piece) for piece in np.array_split(np.arange(quarter), GROUPS)]
 
 
-def multiply_tiles(scalars, first_pair, blocks, keep_ref, send_ref):
+def multiply_tiles(scalars, first_pair, blocks, keep_ref, send_ref, low_first):
     x, core = scalars[2], scalars[3]
     group_size = keep_ref.shape[2]
     rows_dev = keep_ref.shape[3]
@@ -49,16 +50,17 @@
             for step in range(part_count // 2):
                 even, odd = parts[2 * step], parts[2 * step + 1]
                 target = x ^ step
-                keep_ref[target, low, slot] = jnp.where(core == 0, even, odd)
-                send_ref[target, low, slot] = jnp.where(core == 0, odd, even)
+                place = (low, target) if low_first else (target, low)
+                keep_ref[place[0], place[1], slot] = jnp.where(core == 0, even, odd)
+                send_ref[place[0], place[1], slot] = jnp.where(core == 0, odd, even)
         return carry
 
     lax.fori_loop(0, group_size, one_slot, 0)
 
 
-def multiply_groups(scalars, first_pair, blocks, outs):
-    for keep_ref, send_ref in zip(outs[::2], outs[1::2]):
-        multiply_tiles(scalars, first_pair, blocks, keep_ref, send_ref)
+def multiply_groups(scalars, first_pair, blocks, groups, outs):
+    for index, keep_ref, send_ref in zip(groups, outs[::2], outs[1::2]):
+        multiply_tiles(scalars, first_pair, blocks, keep_ref, send_ref, index in LOW_FIRST)
         first_pair += 4 * keep_ref.shape[2]
 
 
@@ -72,11 +74,11 @@
         for index in range(piece.shape[0]):
             start = (component + index) * cells
             blocks[block, :, start : start + cells] = piece[index]
-    multiply_groups(scalars, first_pair, blocks, refs[len(layout) + 1 :])
+    multiply_groups(scalars, first_pair, blocks, range(1), refs[len(layout) + 1 :])
 
 
 def second_kernel(first_pair, scalars, blocks, *outs):
-    multiply_groups(scalars, first_pair, blocks, outs)
+    multiply_groups(scalars, first_pair, blocks, range(1, GROUPS), outs)
 
 
 def split_sum_kernel(left, right, *outs):
@@ -199,8 +201,9 @@
     layout += [(step, 1, component) for step, component in pieces]
     chunks = list(pieces.values()) + [swap(piece, "y", 1) for piece in pieces.values()]
 
-    def sums_shape(size):
-        return jax.ShapeDtypeStruct((x_count, 2, size, rows_dev, block_size), jnp.float32)
+    def sums_shape(index):
+        lead = (2, x_count) if index in LOW_FIRST else (x_count, 2)
+        return jax.ShapeDtypeStruct((*lead, sizes[index], rows_dev, block_size), jnp.float32)
 
     def call(kernel, size, out_shape, operands, name):
         vmem = pl.BlockSpec(memory_space=pltpu.VMEM)
@@ -212,13 +215,13 @@
             compiler_params=pltpu.CompilerParams(vmem_limit_bytes=VMEM_LIMIT),
             cost_estimate=pl.CostEstimate(
                 flops=4 * size * block_size * block_size * components * cells,
-                bytes_accessed=4 * 2**20,
+                bytes_accessed=0,
                 transcendentals=0,
             ),
             name=name,
         )(scalars, *operands)
 
-    shapes = [sums_shape(size) for size in sizes for _ in range(2)]
+    shapes = [sums_shape(index) for index in range(GROUPS) for _ in range(2)]
     blocks_shape = jax.ShapeDtypeStruct(
         (block_count, block_size, components * cells), jnp.bfloat16
     )
@@ -259,30 +262,50 @@
     def float_shape(*shape):
         return jax.ShapeDtypeStruct((*shape, rows_dev, block_size), jnp.float32)
 
+    def split_sum(shape, left, right, name):
+        shapes = [float_shape(*shape[1:])] * shape[0]
+        mine, *away = step_call(split_sum_kernel, shapes, left, right, name=name)
+        return mine, away
+
+    def plain_sum(left, right, name):
+        shape = jax.ShapeDtypeStruct(left.shape, left.dtype)
+        return step_call(sum_kernel, [shape], left, right, name=name)[0]
+
+    def over_x(away):
+        return [swap(value, "x", step + 1) for step, value in enumerate(away)]
+
+    def over_high(mine):
+        bits = 2
+        while 2 * bits < z_count:
+            mine = plain_sum(mine, swap(mine, "z", bits), "sum_z")
+            bits *= 2
+        return mine, swap(mine, "z", bits)
+
     def sum_core(index):
-        keep, send = sums[2 * index], swap(sums[2 * index + 1], "core", 1)
-        shapes = [float_shape(2, sizes[index])] * x_count
-        mine, *away = step_call(split_sum_kernel, shapes, keep, send, name="sum_core")
-        return mine, [swap(value, "x", step + 1) for step, value in enumerate(away)]
+        keep, send = sums[2 * index : 2 * index + 2]
+        send = swap(send, "core", 1)
+        if index in LOW_FIRST:
+            mine, away = split_sum((2, x_count, sizes[index]), keep, send, "sum_core")
+            return mine, swap(away[0], "z", 1)
+        mine, away = split_sum((x_count, 2, sizes[index]), keep, send, "sum_core")
+        if index > 1:
+            arrived = state[0][1]
+            away = lax.optimization_barrier((*away, *arrived))[: len(away)]
+        return mine, over_x(away)
 
     def sum_x(index, mine, arrived):
         for value in arrived[:-1]:
-            (mine,) = step_call(
-                sum_kernel, [float_shape(2, sizes[index])], mine, value, name="sum_x"
-            )
-        shapes = [float_shape(sizes[index])] * 2
-        mine, away = step_call(split_sum_kernel, shapes, mine, arrived[-1], name="sum_x")
-        return mine, swap(away, "z", 1)
+            mine = plain_sum(mine, value, "sum_x")
+        if index in LOW_FIRST:
+            return over_high(plain_sum(mine, arrived[-1], "sum_x"))
+        mine, away = split_sum((2, sizes[index]), mine, arrived[-1], "sum_x")
+        return mine, swap(away[0], "z", 1)
 
     def sum_low(index, mine, arrived):
-        (mine,) = step_call(sum_kernel, [float_shape(sizes[index])], mine, arrived, name="sum_z")
-        bits = 2
-        while 2 * bits < z_count:
-            (mine,) = step_call(
-                sum_kernel, [float_shape(sizes[index])], mine, swap(mine, "z", bits), name="sum_z"
-            )
-            bits *= 2
-        return mine, swap(mine, "z", bits)
+        if index in LOW_FIRST:
+            mine, away = split_sum((x_count, sizes[index]), mine, arrived, "sum_z")
+            return mine, over_x(away)
+        return over_high(plain_sum(mine, arrived, "sum_z"))
 
     def to_owners(value):
         both = [(i, i ^ (y_count + 1)) for i in range(block_count)]
@@ -290,16 +313,16 @@
         return [value, swap(value, "z", 1), swap(value, "y", 1), over_both]
 
     parts = []
-    state = [sum_core(index) for index in range(GROUPS)]
+    state = {}
     for stage, which in ORDER:
-        if stage == "x":
+        if stage == "core":
+            state[which] = sum_core(which)
+        elif stage == "x":
             state[which] = sum_x(which, *state[which])
         elif stage == "low":
             state[which] = sum_low(which, *state[which])
         elif stage == "high":
-            state[which] = step_call(
-                sum_kernel, [float_shape(sizes[which])], *state[which], name="sum_high"
-            )
+            state[which] = [plain_sum(*state[which], "sum_high")]
         else:
             counts = [sizes[index] for index in which]
             shape = (SCALE_ROWS + sum(counts) * rows_dev, block_size)

time: 120 us -> 120 us (level)
  starting transfers between devices: 30.3 us -> 27 us
  waiting for transfers between devices: 78.8 us -> 81.6 us
    ppermute x23, starting transfers between devices: 27.9 us -> 26 us  [swap(): return lax.ppermute(value, axis, [(i, i ^ bits) for i in range(size)])]
    ppermute x2, starting transfers between devices: 2.45 us -> 0.97 us  [to_owners(): over_both = lax.ppermute(value, ('z', 'y'), both)]
    ppermute x2, waiting for transfers between devices: 3.96 us -> 5.38 us  [to_owners(): over_both = lax.ppermute(value, ('z', 'y'), both)]
    ppermute x23, waiting for transfers between devices: 74.8 us -> 76.2 us  [swap(): return lax.ppermute(value, axis, [(i, i ^ bits) for i in range(size)])]
  transfers between devices with their start and end apart: 25 -> 25, of which waited for: 16 -> 19; matrix products, arithmetic and copies ran while one was open for 1% -> 1% of each run, Pallas kernels for 3% -> 3%
where the time goes in v11:
time: 120 us
  waiting for transfers between devices  81.6 us (68%)
  starting transfers between devices  27 us (22%)
  Pallas kernels  8.52 us (7%)
  local copies, waits for them, and re-layouts  2.33 us (2%)
    ppermute x23, waiting for transfers between devices, swap(): return lax.ppermute(value, axis, [(i, i ^ bits) for i in range(size)])  76.2 us
    ppermute x23, starting transfers between devices, swap(): return lax.ppermute(value, axis, [(i, i ^ bits) for i in range(size)])  26 us
    ppermute x2, waiting for transfers between devices, to_owners(): over_both = lax.ppermute(value, ('z', 'y'), both)  5.38 us
    pallas_call x2, Pallas kernels, call(): pl.pallas_call(kernel, out_shape=out_shape, in_specs=[pl.BlockSpec(memory...  5.06 us
    pallas_call x1, Pallas kernels, per_device(): pl.pallas_call(functools.partial(place_kernel, scale_factor / (CODE_TOP *...  2.44 us
  transfers between devices with their start and end apart: 25, of which 19 were waited for; matrix products, arithmetic and copies ran while one was open for 1% of the time, Pallas kernels for 3%

profile of v11, /device:TPU:0, one launch (start us, length us, event | category | flops | bytes accessed | tf_op | source)
XLA Modules:
  0.0 119.6 jit_solution(8188138345509869280)
XLA Ops:
  0.0 1.5 %constant_dynamic-slice_fusion = (bf16[3,256,256]{2,1,0:T(8,128)(2,1)S(1)}, bf16[3,256,256]{2,1,0:T(8,128)(2,1)S(1)}, bf16[3,256,256]{2,1,0:T(8,128)(2,1)S(1)}, bf16[3,256,256]{2,1,0:T(8,128)(2,1)S(1)}) fusion(bf16[3,256,1024]{2,1,0:T(8,128)(2,1)} %param.3, s32[]{:T(128)S(6)} %select_n.97, s32[]{:T(128)S(6)} %select_n.95, s32[]{:T(128)S(6)} %select_n.94, ...), kind=kLoop, calls=%fused_computation.12 | loop fusion | bytes 3145744 | tf_op jit(solution)/shard_map/dynamic_slice | solution.py:195
  1.5 5.1 %collective-permute-start.2 = (bf16[3,256,256]{2,1,0:T(8,128)(2,1)S(1)}, bf16[3,256,256]{2,1,0:T(8,128)(2,1)S(1)}, u32[]{:S(2)}, u32[]{:S(2)}) collective-permute-start(bf16[3,256,256]{2,1,0:T(8,128)(2,1)S(1)} %get-tuple-element.100), channel_id=1, source_target_pairs={{0,24},{8,16},{16,8},{24,0},{1,25},{9,17},{17,9},{25,1},{2,26},{10... | collective-permute-start | bytes 1179656 | tf_op jit(solution)/shard_map/ppermute | solution.py:172
  6.6 0.0 collective-permute-start
  6.6 0.6 collective-permute-start.1
  7.2 1.7 %collective-permute-start.3 = (bf16[3,256,256]{2,1,0:T(8,128)(2,1)S(1)}, bf16[3,256,256]{2,1,0:T(8,128)(2,1)S(1)}, u32[]{:S(2)}, u32[]{:S(2)}) collective-permute-start(bf16[3,256,256]{2,1,0:T(8,128)(2,1)S(1)} %get-tuple-element.102.refs_0_), channel_id=1, source_target_pairs={{0,4},{4,0},{1,5},{5,1},{2,6},{6,2},{3,7},{7,3},{8,12},{12,8},{9,1... | collective-permute-start | bytes 1179656 | tf_op jit(solution)/shard_map/ppermute | solution.py:172
  8.9 7.7 %collective-permute-done.2.refs_3_ = bf16[3,256,256]{2,1,0:T(8,128)(2,1)S(1)} collective-permute-done((bf16[3,256,256]{2,1,0:T(8,128)(2,1)S(1)}, bf16[3,256,256]{2,1,0:T(8,128)(2,1)S(1)}, u32[]{:S(2)}, u32[]{:S(2)}) %collective-permute-start.2) | collective-permute-done | bytes 393248 | tf_op jit(solution)/shard_map/ppermute | solution.py:172
  16.6 1.7 %collective-permute-start.6 = (bf16[3,256,256]{2,1,0:T(8,128)(2,1)S(1)}, bf16[3,256,256]{2,1,0:T(8,128)(2,1)S(1)}, u32[]{:S(2)}, u32[]{:S(2)}) collective-permute-start(bf16[3,256,256]{2,1,0:T(8,128)(2,1)S(1)} %collective-permute-done.2.refs_3_), channel_id=1, source_target_pairs={{0,4},{4,0},{1,5},{5,1},{2,6},{6,2},{3,7},{7,3},{8,12},{12,8},{9,1... | collective-permute-start | bytes 1179656 | tf_op jit(solution)/shard_map/ppermute | solution.py:172
  18.3 6.9 %collective-permute-done.refs_1_ = bf16[3,256,256]{2,1,0:T(8,128)(2,1)S(1)} collective-permute-done((bf16[3,256,256]{2,1,0:T(8,128)(2,1)S(1)}, bf16[3,256,256]{2,1,0:T(8,128)(2,1)S(1)}, u32[]{:S(2)}, u32[]{:S(2)}) %collective-permute-start) | collective-permute-done | bytes 393248 | tf_op jit(solution)/shard_map/ppermute | solution.py:172
  25.3 1.4 %collective-permute-start.4 = (bf16[3,256,256]{2,1,0:T(8,128)(2,1)S(1)}, bf16[3,256,256]{2,1,0:T(8,128)(2,1)S(1)}, u32[]{:S(2)}, u32[]{:S(2)}) collective-permute-start(bf16[3,256,256]{2,1,0:T(8,128)(2,1)S(1)} %collective-permute-done.refs_1_), channel_id=1, source_target_pairs={{0,4},{4,0},{1,5},{5,1},{2,6},{6,2},{3,7},{7,3},{8,12},{12,8},{9,1... | collective-permute-start | bytes 1179656 | tf_op jit(solution)/shard_map/ppermute | solution.py:172
  26.7 13.5 %collective-permute-done.1.refs_2_ = bf16[3,256,256]{2,1,0:T(8,128)(2,1)S(1)} collective-permute-done((bf16[3,256,256]{2,1,0:T(8,128)(2,1)S(1)}, bf16[3,256,256]{2,1,0:T(8,128)(2,1)S(1)}, u32[]{:S(2)}, u32[]{:S(2)}) %collective-permute-start.1) | collective-permute-done | bytes 393248 | tf_op jit(solution)/shard_map/ppermute | solution.py:172
  40.1 1.5 %collective-permute-start.5 = (bf16[3,256,256]{2,1,0:T(8,128)(2,1)S(1)}, bf16[3,256,256]{2,1,0:T(8,128)(2,1)S(1)}, u32[]{:S(2)}, u32[]{:S(2)}) collective-permute-start(bf16[3,256,256]{2,1,0:T(8,128)(2,1)S(1)} %collective-permute-done.1.refs_2_), channel_id=1, source_target_pairs={{0,4},{4,0},{1,5},{5,1},{2,6},{6,2},{3,7},{7,3},{8,12},{12,8},{9,1... | collective-permute-start | bytes 1179656 | tf_op jit(solution)/shard_map/ppermute | solution.py:172
  41.7 0.7 fusion.2
  42.3 0.1 concatenate.7.scalars
  42.4 0.0 collective-permute-done.3.refs_4_
  42.4 0.0 collective-permute-done.6.refs_7_
  42.4 0.0 collective-permute-done.4.refs_5_
  42.4 7.9 %collective-permute-done.5.refs_6_ = bf16[3,256,256]{2,1,0:T(8,128)(2,1)S(1)} collective-permute-done((bf16[3,256,256]{2,1,0:T(8,128)(2,1)S(1)}, bf16[3,256,256]{2,1,0:T(8,128)(2,1)S(1)}, u32[]{:S(2)}, u32[]{:S(2)}) %collective-permute-start.5) | collective-permute-done | bytes 393248 | tf_op jit(solution)/shard_map/ppermute | solution.py:172
  50.3 2.0 %tiles_first.1 = (bf16[8,256,768]{2,1,0:T(8,128)(2,1)S(1)}, f32[2,2,3,64,256]{4,3,2,1,0:T(8,128)S(1)}, f32[2,2,3,64,256]{4,3,2,1,0:T(8,128)S(1)}) custom-call(s32[40]{0:T(128)S(1)} %concatenate.7.scalars, bf16[3,256,256]{2,1,0:T(8,128)(2,1)S(1)} %get-tuple-element.102.refs_0_, bf16[3,256,256]{2,1,0:T(8,128)(2,1)S(1)} %collective-permute-done.refs_1_, ...), custom_call_target="tpu_custom_call" | custom-call | flops 603979776 | tf_op jit(solution)/shard_map/tiles_first/pallas_call | solution.py:210
  52.3 0.1 collective-permute-start.7
  52.4 3.1 %tiles_second.1 = (f32[2,2,3,64,256]{4,3,2,1,0:T(8,128)S(1)}, f32[2,2,3,64,256]{4,3,2,1,0:T(8,128)S(1)}, f32[2,2,3,64,256]{4,3,2,1,0:T(8,128)S(1)}, f32[2,2,3,64,256]{4,3,2,1,0:T(8,128)S(1)}) custom-call(s32[40]{0:T(128)S(1)} %concatenate.7.scalars, bf16[8,256,768]{2,1,0:T(8,128)(2,1)S(1)} %get-tuple-element.56.blocks), custom_call_target="tpu_custom_call" | custom-call | flops 1207959552 | tf_op jit(solution)/shard_map/tiles_second/pallas_call | solution.py:210
  55.5 0.6 collective-permute-start.9
  56.0 0.1 collective-permute-start.12
  56.1 0.0 collective-permute-done.7.right
  56.1 0.1 sum_core.3
  56.2 1.7 %collective-permute-done.9.right = f32[2,2,3,64,256]{4,3,2,1,0:T(8,128)S(1)} collective-permute-done((f32[2,2,3,64,256]{4,3,2,1,0:T(8,128)S(1)}, f32[2,2,3,64,256]{4,3,2,1,0:T(8,128)S(1)}, u32[]{:S(2)}, u32[]{:S(2)}) %collective-permute-start.9) | collective-permute-done | bytes 786464 | tf_op jit(solution)/shard_map/ppermute | solution.py:172
  57.9 0.1 sum_core.4
  58.0 1.6 %collective-permute-start.10 = (f32[2,3,64,256]{3,2,1,0:T(8,128)S(1)}, f32[2,3,64,256]{3,2,1,0:T(8,128)S(1)}, u32[]{:S(2)}, u32[]{:S(2)}) collective-permute-start(f32[2,3,64,256]{3,2,1,0:T(8,128)S(1)} %get-tuple-element.62), channel_id=1, source_target_pairs={{0,2},{2,0},{1,3},{3,1},{4,6},{6,4},{5,7},{7,5},{8,10},{10,8},{9,1... | collective-permute-start | bytes 1179656 | tf_op jit(solution)/shard_map/ppermute | solution.py:172
  59.6 0.6 collective-permute-start.8
  60.2 9.3 %collective-permute-done.10.right = f32[2,3,64,256]{3,2,1,0:T(8,128)S(1)} collective-permute-done((f32[2,3,64,256]{3,2,1,0:T(8,128)S(1)}, f32[2,3,64,256]{3,2,1,0:T(8,128)S(1)}, u32[]{:S(2)}, u32[]{:S(2)}) %collective-permute-start.10) | collective-permute-done | bytes 393248 | tf_op jit(solution)/shard_map/ppermute | solution.py:172
  69.5 0.6 collective-permute-start.13
  70.2 0.5 collective-permute-done.8.right
  70.7 1.0 collective-permute-start.11
  71.8 4.2 %collective-permute-done.13.right = f32[3,64,256]{2,1,0:T(8,128)S(1)} collective-permute-done((f32[3,64,256]{2,1,0:T(8,128)S(1)}, f32[3,64,256]{2,1,0:T(8,128)S(1)}, u32[]{:S(2)}, u32[]{:S(2)}) %collective-permute-start.13) | collective-permute-done | bytes 196640 | tf_op jit(solution)/shard_map/ppermute | solution.py:172
  76.0 0.0 copy-start
  76.0 0.0 collective-permute-done.12.right
  76.0 0.1 sum_core.5
  76.1 0.8 collective-permute-done.11.right
  76.8 1.0 collective-permute-start.16
  77.8 2.3 %collective-permute-start.15 = (f32[3,64,256]{2,1,0:T(8,128)S(1)}, f32[3,64,256]{2,1,0:T(8,128)S(1)}, u32[]{:S(2)}, u32[]{:S(2)}) collective-permute-start(f32[3,64,256]{2,1,0:T(8,128)S(1)} %sum_z.4.left), channel_id=1, source_target_pairs={{0,16},{8,24},{16,0},{24,8},{1,17},{9,25},{17,1},{25,9},{2,18},{10... | collective-permute-start | bytes 589832 | tf_op jit(solution)/shard_map/ppermute | solution.py:172
  80.2 0.7 collective-permute-start.14
  80.9 5.3 %collective-permute-done.16.right = f32[2,3,64,256]{3,2,1,0:T(8,128)S(1)} collective-permute-done((f32[2,3,64,256]{3,2,1,0:T(8,128)S(1)}, f32[2,3,64,256]{3,2,1,0:T(8,128)S(1)}, u32[]{:S(2)}, u32[]{:S(2)}) %collective-permute-start.16) | collective-permute-done | bytes 393248 | tf_op jit(solution)/shard_map/ppermute | solution.py:172
  86.2 1.1 collective-permute-start.17
  87.3 0.0 copy-done
  87.3 5.9 %collective-permute-done.15.right = f32[3,64,256]{2,1,0:T(8,128)S(1)} collective-permute-done((f32[3,64,256]{2,1,0:T(8,128)S(1)}, f32[3,64,256]{2,1,0:T(8,128)S(1)}, u32[]{:S(2)}, u32[]{:S(2)}) %collective-permute-start.15) | collective-permute-done | bytes 196640 | tf_op jit(solution)/shard_map/ppermute | solution.py:172
  93.2 3.6 %collective-permute-done.17.right = f32[3,64,256]{2,1,0:T(8,128)S(1)} collective-permute-done((f32[3,64,256]{2,1,0:T(8,128)S(1)}, f32[3,64,256]{2,1,0:T(8,128)S(1)}, u32[]{:S(2)}, u32[]{:S(2)}) %collective-permute-start.17) | collective-permute-done | bytes 196640 | tf_op jit(solution)/shard_map/ppermute | solution.py:172
  96.9 0.1 collective-permute-start.21
  97.0 2.5 %collective-permute-done.14.refs_1_ = f32[3,64,256]{2,1,0:T(8,128)S(1)} collective-permute-done((f32[3,64,256]{2,1,0:T(8,128)S(1)}, f32[3,64,256]{2,1,0:T(8,128)S(1)}, u32[]{:S(2)}, u32[]{:S(2)}) %collective-permute-start.14) | collective-permute-done | bytes 196640 | tf_op jit(solution)/shard_map/ppermute | solution.py:172
  99.5 0.3 finish.2.refs_0_
  99.8 0.5 collective-permute-start.20
  100.3 1.2 collective-permute-start.19
  101.5 1.9 %collective-permute-start.18 = (s16[400,256]{1,0:T(8,128)(2,1)S(1)}, s16[400,256]{1,0:T(8,128)(2,1)S(1)}, u32[]{:S(2)}, u32[]{:S(2)}) collective-permute-start(s16[400,256]{1,0:T(8,128)(2,1)S(1)} %finish.2.refs_0_), channel_id=1, source_target_pairs={{0,8},{8,0},{16,24},{24,16},{1,9},{9,1},{17,25},{25,17},{2,10},{10... | collective-permute-start | bytes 614408 | tf_op jit(solution)/shard_map/ppermute | solution.py:172
  103.4 1.5 %collective-permute-done.21.refs_1_ = f32[3,64,256]{2,1,0:T(8,128)S(1)} collective-permute-done((f32[3,64,256]{2,1,0:T(8,128)S(1)}, f32[3,64,256]{2,1,0:T(8,128)S(1)}, u32[]{:S(2)}, u32[]{:S(2)}) %collective-permute-start.21) | collective-permute-done | bytes 196640 | tf_op jit(solution)/shard_map/ppermute | solution.py:172
  104.9 0.2 finish.3.refs_4_
  105.2 0.5 collective-permute-start.24
  105.6 1.2 collective-permute-start.23
  106.8 3.2 %collective-permute-done.20.refs_3_ = s16[400,256]{1,0:T(8,128)(2,1)S(1)} collective-permute-done((s16[400,256]{1,0:T(8,128)(2,1)S(1)}, s16[400,256]{1,0:T(8,128)(2,1)S(1)}, u32[]{:S(2)}, u32[]{:S(2)}) %collective-permute-start.20) | collective-permute-done | bytes 204832 | tf_op jit(solution)/shard_map/ppermute | solution.py:312
  110.0 0.0 collective-permute-start.22
  110.0 0.1 concatenate.6.scalars
  110.1 0.8 collective-permute-done.19.refs_2_
  110.9 2.9 %collective-permute-done.18.refs_1_ = s16[400,256]{1,0:T(8,128)(2,1)S(1)} collective-permute-done((s16[400,256]{1,0:T(8,128)(2,1)S(1)}, s16[400,256]{1,0:T(8,128)(2,1)S(1)}, u32[]{:S(2)}, u32[]{:S(2)}) %collective-permute-start.18) | collective-permute-done | bytes 204832 | tf_op jit(solution)/shard_map/ppermute | solution.py:172
  113.8 2.2 %collective-permute-done.24.refs_7_ = s16[208,256]{1,0:T(8,128)(2,1)S(1)} collective-permute-done((s16[208,256]{1,0:T(8,128)(2,1)S(1)}, s16[208,256]{1,0:T(8,128)(2,1)S(1)}, u32[]{:S(2)}, u32[]{:S(2)}) %collective-permute-start.24) | collective-permute-done | bytes 106528 | tf_op jit(solution)/shard_map/ppermute | solution.py:312
  116.0 0.0 collective-permute-done.23.refs_6_
  116.0 1.1 collective-permute-done.22.refs_5_
  117.1 2.4 %place_tiles.1 = f32[10,64,256]{2,1,0:T(8,128)} custom-call(s32[50]{0:T(128)S(1)} %concatenate.6.scalars, s16[400,256]{1,0:T(8,128)(2,1)S(1)} %finish.2.refs_0_, s16[400,256]{1,0:T(8,128)(2,1)S(1)} %collective-permute-done.18.refs_1_, s16[400,256]{1,0:T(8,128)(2,1)S(1)} %collective-permute-done.19.refs_2_, ...), custom_call_target="tpu_custom_call" | custom-call | flops 163840 | tf_op jit(solution)/shard_map/place_tiles/pallas_call | solution.py:359
  (10 shorter events, 0.3 us)
Async XLA Ops:
  1.5 15.1 %collective-permute-start.2 = (bf16[3,256,256]{2,1,0:T(8,128)(2,1)S(1)}, bf16[3,256,256]{2,1,0:T(8,128)(2,1)S(1)}, u32[]{:S(2)}, u32[]{:S(2)}) collective-permute-start(bf16[3,256,256]{2,1,0:T(8,128)(2,1)S(1)} %get-tuple-element.100), channel_id=1, source_target_pairs={{0,24},{8,16},{16,8},{24,0},{1,25},{9,17},{17,9},{25,1},{2,26},{10... | collective-permute-start | bytes 1179656 | tf_op jit(solution)/shard_map/ppermute | solution.py:172
  6.6 18.7 %collective-permute-start = (bf16[3,256,256]{2,1,0:T(8,128)(2,1)S(1)}, bf16[3,256,256]{2,1,0:T(8,128)(2,1)S(1)}, u32[]{:S(2)}, u32[]{:S(2)}) collective-permute-start(bf16[3,256,256]{2,1,0:T(8,128)(2,1)S(1)} %get-tuple-element.101), channel_id=1, source_target_pairs={{0,8},{8,0},{16,24},{24,16},{1,9},{9,1},{17,25},{25,17},{2,10},{10... | collective-permute-start | bytes 1179656 | tf_op jit(solution)/shard_map/ppermute | solution.py:172
  6.6 33.5 %collective-permute-start.1 = (bf16[3,256,256]{2,1,0:T(8,128)(2,1)S(1)}, bf16[3,256,256]{2,1,0:T(8,128)(2,1)S(1)}, u32[]{:S(2)}, u32[]{:S(2)}) collective-permute-start(bf16[3,256,256]{2,1,0:T(8,128)(2,1)S(1)} %get-tuple-element.103), channel_id=1, source_target_pairs={{0,16},{8,24},{16,0},{24,8},{1,17},{9,25},{17,1},{25,9},{2,18},{10... | collective-permute-start | bytes 1179656 | tf_op jit(solution)/shard_map/ppermute | solution.py:172
  7.2 35.2 %collective-permute-start.3 = (bf16[3,256,256]{2,1,0:T(8,128)(2,1)S(1)}, bf16[3,256,256]{2,1,0:T(8,128)(2,1)S(1)}, u32[]{:S(2)}, u32[]{:S(2)}) collective-permute-start(bf16[3,256,256]{2,1,0:T(8,128)(2,1)S(1)} %get-tuple-element.102.refs_0_), channel_id=1, source_target_pairs={{0,4},{4,0},{1,5},{5,1},{2,6},{6,2},{3,7},{7,3},{8,12},{12,8},{9,1... | collective-permute-start | bytes 1179656 | tf_op jit(solution)/shard_map/ppermute | solution.py:172
  16.6 25.8 %collective-permute-start.6 = (bf16[3,256,256]{2,1,0:T(8,128)(2,1)S(1)}, bf16[3,256,256]{2,1,0:T(8,128)(2,1)S(1)}, u32[]{:S(2)}, u32[]{:S(2)}) collective-permute-start(bf16[3,256,256]{2,1,0:T(8,128)(2,1)S(1)} %collective-permute-done.2.refs_3_), channel_id=1, source_target_pairs={{0,4},{4,0},{1,5},{5,1},{2,6},{6,2},{3,7},{7,3},{8,12},{12,8},{9,1... | collective-permute-start | bytes 1179656 | tf_op jit(solution)/shard_map/ppermute | solution.py:172
  25.3 17.2 %collective-permute-start.4 = (bf16[3,256,256]{2,1,0:T(8,128)(2,1)S(1)}, bf16[3,256,256]{2,1,0:T(8,128)(2,1)S(1)}, u32[]{:S(2)}, u32[]{:S(2)}) collective-permute-start(bf16[3,256,256]{2,1,0:T(8,128)(2,1)S(1)} %collective-permute-done.refs_1_), channel_id=1, source_target_pairs={{0,4},{4,0},{1,5},{5,1},{2,6},{6,2},{3,7},{7,3},{8,12},{12,8},{9,1... | collective-permute-start | bytes 1179656 | tf_op jit(solution)/shard_map/ppermute | solution.py:172
  40.1 10.2 %collective-permute-start.5 = (bf16[3,256,256]{2,1,0:T(8,128)(2,1)S(1)}, bf16[3,256,256]{2,1,0:T(8,128)(2,1)S(1)}, u32[]{:S(2)}, u32[]{:S(2)}) collective-permute-start(bf16[3,256,256]{2,1,0:T(8,128)(2,1)S(1)} %collective-permute-done.1.refs_2_), channel_id=1, source_target_pairs={{0,4},{4,0},{1,5},{5,1},{2,6},{6,2},{3,7},{7,3},{8,12},{12,8},{9,1... | collective-permute-start | bytes 1179656 | tf_op jit(solution)/shard_map/ppermute | solution.py:172
  52.3 3.8 %collective-permute-start.7 = (f32[2,2,3,64,256]{4,3,2,1,0:T(8,128)S(1)}, f32[2,2,3,64,256]{4,3,2,1,0:T(8,128)S(1)}, u32[]{:S(2)}, u32[]{:S(2)}) collective-permute-start(f32[2,2,3,64,256]{4,3,2,1,0:T(8,128)S(1)} %get-tuple-element.51), channel_id=1, source_target_pairs={{0,1},{1,0},{2,3},{3,2},{4,5},{5,4},{6,7},{7,6},{8,9},{9,8},{10,11... | collective-permute-start | bytes 2359304 | tf_op jit(solution)/shard_map/ppermute | solution.py:172
  55.5 2.5 %collective-permute-start.9 = (f32[2,2,3,64,256]{4,3,2,1,0:T(8,128)S(1)}, f32[2,2,3,64,256]{4,3,2,1,0:T(8,128)S(1)}, u32[]{:S(2)}, u32[]{:S(2)}) collective-permute-start(f32[2,2,3,64,256]{4,3,2,1,0:T(8,128)S(1)} %get-tuple-element.58), channel_id=1, source_target_pairs={{0,1},{1,0},{2,3},{3,2},{4,5},{5,4},{6,7},{7,6},{8,9},{9,8},{10,11... | collective-permute-start | bytes 2359304 | tf_op jit(solution)/shard_map/ppermute | solution.py:172
  56.0 20.0 %collective-permute-start.12 = (f32[2,2,3,64,256]{4,3,2,1,0:T(8,128)S(1)}, f32[2,2,3,64,256]{4,3,2,1,0:T(8,128)S(1)}, u32[]{:S(2)}, u32[]{:S(2)}) collective-permute-start(f32[2,2,3,64,256]{4,3,2,1,0:T(8,128)S(1)} %get-tuple-element.71), channel_id=1, source_target_pairs={{0,1},{1,0},{2,3},{3,2},{4,5},{5,4},{6,7},{7,6},{8,9},{9,8},{10,11... | collective-permute-start | bytes 2359304 | tf_op jit(solution)/shard_map/ppermute | solution.py:172
  58.0 11.5 %collective-permute-start.10 = (f32[2,3,64,256]{3,2,1,0:T(8,128)S(1)}, f32[2,3,64,256]{3,2,1,0:T(8,128)S(1)}, u32[]{:S(2)}, u32[]{:S(2)}) collective-permute-start(f32[2,3,64,256]{3,2,1,0:T(8,128)S(1)} %get-tuple-element.62), channel_id=1, source_target_pairs={{0,2},{2,0},{1,3},{3,1},{4,6},{6,4},{5,7},{7,5},{8,10},{10,8},{9,1... | collective-permute-start | bytes 1179656 | tf_op jit(solution)/shard_map/ppermute | solution.py:172
  59.6 11.1 %collective-permute-start.8 = (f32[2,3,64,256]{3,2,1,0:T(8,128)S(1)}, f32[2,3,64,256]{3,2,1,0:T(8,128)S(1)}, u32[]{:S(2)}, u32[]{:S(2)}) collective-permute-start(f32[2,3,64,256]{3,2,1,0:T(8,128)S(1)} %get-tuple-element.55), channel_id=1, source_target_pairs={{0,8},{8,0},{16,24},{24,16},{1,9},{9,1},{17,25},{25,17},{2,10},{10... | collective-permute-start | bytes 1179656 | tf_op jit(solution)/shard_map/ppermute | solution.py:172
  69.5 6.4 %collective-permute-start.13 = (f32[3,64,256]{2,1,0:T(8,128)S(1)}, f32[3,64,256]{2,1,0:T(8,128)S(1)}, u32[]{:S(2)}, u32[]{:S(2)}) collective-permute-start(f32[3,64,256]{2,1,0:T(8,128)S(1)} %get-tuple-element.72), channel_id=1, source_target_pairs={{0,8},{8,0},{16,24},{24,16},{1,9},{9,1},{17,25},{25,17},{2,10},{10... | collective-permute-start | bytes 589832 | tf_op jit(solution)/shard_map/ppermute | solution.py:172
  70.7 6.1 %collective-permute-start.11 = (f32[3,64,256]{2,1,0:T(8,128)S(1)}, f32[3,64,256]{2,1,0:T(8,128)S(1)}, u32[]{:S(2)}, u32[]{:S(2)}) collective-permute-start(f32[3,64,256]{2,1,0:T(8,128)S(1)} %get-tuple-element.69), channel_id=1, source_target_pairs={{0,2},{2,0},{1,3},{3,1},{4,6},{6,4},{5,7},{7,5},{8,10},{10,8},{9,1... | collective-permute-start | bytes 589832 | tf_op jit(solution)/shard_map/ppermute | solution.py:172
  76.0 11.3 %copy-start = (s32[1,10,2]{1,2,0:T(2,128)S(1)}, s32[1,10,2]{1,2,0:T(2,128)}, u32[]{:S(2)}) copy-start(s32[1,10,2]{1,2,0:T(2,128)} %param.4) | copy-start | bytes 244
  76.8 9.3 %collective-permute-start.16 = (f32[2,3,64,256]{3,2,1,0:T(8,128)S(1)}, f32[2,3,64,256]{3,2,1,0:T(8,128)S(1)}, u32[]{:S(2)}, u32[]{:S(2)}) collective-permute-start(f32[2,3,64,256]{3,2,1,0:T(8,128)S(1)} %get-tuple-element.81), channel_id=1, source_target_pairs={{0,2},{2,0},{1,3},{3,1},{4,6},{6,4},{5,7},{7,5},{8,10},{10,8},{9,1... | collective-permute-start | bytes 1179656 | tf_op jit(solution)/shard_map/ppermute | solution.py:172
  77.8 15.4 %collective-permute-start.15 = (f32[3,64,256]{2,1,0:T(8,128)S(1)}, f32[3,64,256]{2,1,0:T(8,128)S(1)}, u32[]{:S(2)}, u32[]{:S(2)}) collective-permute-start(f32[3,64,256]{2,1,0:T(8,128)S(1)} %sum_z.4.left), channel_id=1, source_target_pairs={{0,16},{8,24},{16,0},{24,8},{1,17},{9,25},{17,1},{25,9},{2,18},{10... | collective-permute-start | bytes 589832 | tf_op jit(solution)/shard_map/ppermute | solution.py:172
  80.2 19.3 %collective-permute-start.14 = (f32[3,64,256]{2,1,0:T(8,128)S(1)}, f32[3,64,256]{2,1,0:T(8,128)S(1)}, u32[]{:S(2)}, u32[]{:S(2)}) collective-permute-start(f32[3,64,256]{2,1,0:T(8,128)S(1)} %sum_x.4.refs_0_), channel_id=1, source_target_pairs={{0,16},{8,24},{16,0},{24,8},{1,17},{9,25},{17,1},{25,9},{2,18},{10... | collective-permute-start | bytes 589832 | tf_op jit(solution)/shard_map/ppermute | solution.py:172
  86.2 10.6 %collective-permute-start.17 = (f32[3,64,256]{2,1,0:T(8,128)S(1)}, f32[3,64,256]{2,1,0:T(8,128)S(1)}, u32[]{:S(2)}, u32[]{:S(2)}) collective-permute-start(f32[3,64,256]{2,1,0:T(8,128)S(1)} %get-tuple-element.87), channel_id=1, source_target_pairs={{0,8},{8,0},{16,24},{24,16},{1,9},{9,1},{17,25},{25,17},{2,10},{10... | collective-permute-start | bytes 589832 | tf_op jit(solution)/shard_map/ppermute | solution.py:172
  96.9 8.0 %collective-permute-start.21 = (f32[3,64,256]{2,1,0:T(8,128)S(1)}, f32[3,64,256]{2,1,0:T(8,128)S(1)}, u32[]{:S(2)}, u32[]{:S(2)}) collective-permute-start(f32[3,64,256]{2,1,0:T(8,128)S(1)} %sum_z.5.refs_0_), channel_id=1, source_target_pairs={{0,16},{8,24},{16,0},{24,8},{1,17},{9,25},{17,1},{25,9},{2,18},{10... | collective-permute-start | bytes 589832 | tf_op jit(solution)/shard_map/ppermute | solution.py:172
  99.8 10.2 %collective-permute-start.20 = (s16[400,256]{1,0:T(8,128)(2,1)S(1)}, s16[400,256]{1,0:T(8,128)(2,1)S(1)}, u32[]{:S(2)}, u32[]{:S(2)}) collective-permute-start(s16[400,256]{1,0:T(8,128)(2,1)S(1)} %finish.2.refs_0_), channel_id=1, source_target_pairs={{0,12},{4,8},{8,4},{12,0},{16,28},{20,24},{24,20},{28,16},{1,13},{... | collective-permute-start | bytes 614408 | tf_op jit(solution)/shard_map/ppermute | solution.py:312
  100.3 10.6 %collective-permute-start.19 = (s16[400,256]{1,0:T(8,128)(2,1)S(1)}, s16[400,256]{1,0:T(8,128)(2,1)S(1)}, u32[]{:S(2)}, u32[]{:S(2)}) collective-permute-start(s16[400,256]{1,0:T(8,128)(2,1)S(1)} %finish.2.refs_0_), channel_id=1, source_target_pairs={{0,4},{4,0},{1,5},{5,1},{2,6},{6,2},{3,7},{7,3},{8,12},{12,8},{9,1... | collective-permute-start | bytes 614408 | tf_op jit(solution)/shard_map/ppermute | solution.py:172
  101.5 12.3 %collective-permute-start.18 = (s16[400,256]{1,0:T(8,128)(2,1)S(1)}, s16[400,256]{1,0:T(8,128)(2,1)S(1)}, u32[]{:S(2)}, u32[]{:S(2)}) collective-permute-start(s16[400,256]{1,0:T(8,128)(2,1)S(1)} %finish.2.refs_0_), channel_id=1, source_target_pairs={{0,8},{8,0},{16,24},{24,16},{1,9},{9,1},{17,25},{25,17},{2,10},{10... | collective-permute-start | bytes 614408 | tf_op jit(solution)/shard_map/ppermute | solution.py:172
  105.2 10.8 %collective-permute-start.24 = (s16[208,256]{1,0:T(8,128)(2,1)S(1)}, s16[208,256]{1,0:T(8,128)(2,1)S(1)}, u32[]{:S(2)}, u32[]{:S(2)}) collective-permute-start(s16[208,256]{1,0:T(8,128)(2,1)S(1)} %finish.3.refs_4_), channel_id=1, source_target_pairs={{0,12},{4,8},{8,4},{12,0},{16,28},{20,24},{24,20},{28,16},{1,13},{... | collective-permute-start | bytes 319496 | tf_op jit(solution)/shard_map/ppermute | solution.py:312
  105.6 10.4 %collective-permute-start.23 = (s16[208,256]{1,0:T(8,128)(2,1)S(1)}, s16[208,256]{1,0:T(8,128)(2,1)S(1)}, u32[]{:S(2)}, u32[]{:S(2)}) collective-permute-start(s16[208,256]{1,0:T(8,128)(2,1)S(1)} %finish.3.refs_4_), channel_id=1, source_target_pairs={{0,4},{4,0},{1,5},{5,1},{2,6},{6,2},{3,7},{7,3},{8,12},{12,8},{9,1... | collective-permute-start | bytes 319496 | tf_op jit(solution)/shard_map/ppermute | solution.py:172
  110.0 7.1 %collective-permute-start.22 = (s16[208,256]{1,0:T(8,128)(2,1)S(1)}, s16[208,256]{1,0:T(8,128)(2,1)S(1)}, u32[]{:S(2)}, u32[]{:S(2)}) collective-permute-start(s16[208,256]{1,0:T(8,128)(2,1)S(1)} %finish.3.refs_4_), channel_id=1, source_target_pairs={{0,8},{8,0},{16,24},{24,16},{1,9},{9,1},{17,25},{25,17},{2,10},{10... | collective-permute-start | bytes 319496 | tf_op jit(solution)/shard_map/ppermute | solution.py:172

commit v12 on v11

--- a/solution.py
+++ b/solution.py
@@ -12,10 +12,12 @@
 VMEM_LIMIT = 24 * 2**20
 GROUPS = 3
 BATCHES = ((0, 1), (2,))
+CALLS = ((0, 1), (2,))
 LOW_FIRST = (0,)
 ORDER = (
-    ("core", 0), ("core", 1), ("x", 1), ("low", 0), ("low", 1), ("core", 2), ("x", 0),
+    ("core", 0), ("x", 1), ("low", 0), ("low", 1), ("core", 1), ("x", 0),
     ("x", 2), ("high", 1), ("low", 2), ("finish", BATCHES[0]), ("finish", BATCHES[1]),
+    ("stack", None),
 )
 CODE_TOP = 32767.0
 SCALE_ROWS = 16
@@ -31,15 +33,14 @@
     return [len(piece) for piece in np.array_split(np.arange(quarter), GROUPS)]
 
 
-def multiply_tiles(scalars, first_pair, blocks, keep_ref, send_ref, low_first):
+def multiply_tiles(scalars, first_pair, blocks, keep_ref, send_ref, offset, size, low_first):
     x, core = scalars[2], scalars[3]
-    group_size = keep_ref.shape[2]
-    rows_dev = keep_ref.shape[3]
+    rows_dev = keep_ref.shape[2]
     part_count = blocks.shape[1] // rows_dev
 
     def one_slot(slot, carry):
         for low in range(2):
-            where = first_pair + 2 * (low * group_size + slot)
+            where = first_pair + 2 * (low * size + slot)
             tile = lax.dot_general(
                 blocks[scalars[where]],
                 blocks[scalars[where + 1]],
@@ -50,21 +51,25 @@
             for step in range(part_count // 2):
                 even, odd = parts[2 * step], parts[2 * step + 1]
                 target = x ^ step
-                place = (low, target) if low_first else (target, low)
-                keep_ref[place[0], place[1], slot] = jnp.where(core == 0, even, odd)
-                send_ref[place[0], place[1], slot] = jnp.where(core == 0, odd, even)
+                place = low * (part_count // 2) + target if low_first else 2 * target + low
+                keep_ref[place, offset + slot] = jnp.where(core == 0, even, odd)
+                send_ref[place, offset + slot] = jnp.where(core == 0, odd, even)
         return carry
 
-    lax.fori_loop(0, group_size, one_slot, 0)
-
-
-def multiply_groups(scalars, first_pair, blocks, groups, outs):
-    for index, keep_ref, send_ref in zip(groups, outs[::2], outs[1::2]):
-        multiply_tiles(scalars, first_pair, blocks, keep_ref, send_ref, index in LOW_FIRST)
-        first_pair += 4 * keep_ref.shape[2]
-
-
-def first_kernel(layout, first_pair, scalars, *refs):
+    lax.fori_loop(0, size, one_slot, 0)
+
+
+def multiply_groups(scalars, first_pair, sizes, blocks, groups, outs):
+    offset = 0
+    for index in groups:
+        multiply_tiles(
+            scalars, first_pair, blocks, *outs, offset, sizes[index], index in LOW_FIRST
+        )
+        first_pair += 4 * sizes[index]
+        offset += sizes[index]
+
+
+def first_kernel(layout, first_pair, sizes, scalars, *refs):
     pieces = refs[: len(layout)]
     blocks = refs[len(layout)]
     z, y = scalars[0], scalars[1]
@@ -74,11 +79,19 @@
         for index in range(piece.shape[0]):
             start = (component + index) * cells
             blocks[block, :, start : start + cells] = piece[index]
-    multiply_groups(scalars, first_pair, blocks, range(1), refs[len(layout) + 1 :])
-
-
-def second_kernel(first_pair, scalars, blocks, *outs):
-    multiply_groups(scalars, first_pair, blocks, range(1, GROUPS), outs)
+    multiply_groups(scalars, first_pair, sizes, blocks, CALLS[0], refs[len(layout) + 1 :])
+
+
+def second_kernel(first_pair, sizes, scalars, blocks, *outs):
+    multiply_groups(scalars, first_pair, sizes, blocks, CALLS[1], outs)
+
+
+def core_sum_kernel(cuts, keep, send, *outs):
+    outs = list(outs)
+    for offset, size, block in cuts:
+        for start in range(0, keep.shape[0], block):
+            place = (slice(start, start + block), slice(offset, offset + size))
+            outs.pop(0)[...] = keep[place] + send[place]
 
 
 def split_sum_kernel(left, right, *outs):
@@ -124,24 +137,36 @@
     code[:SCALE_ROWS, :] = header.astype(jnp.int32).astype(jnp.int16)
 
 
-def place_kernel(factor, scalars, *refs):
-    out, codes, headers = refs[-3:]
+def stack_kernel(*refs):
+    out = refs[-1]
+    for index, part in enumerate(refs[:-1]):
+        out[index] = part[...]
+
+
+def place_kernel(factor, batch_count, scalars, *refs):
+    out, headers = refs[-2 - batch_count : -batch_count]
+    stacks = list(refs[-batch_count:])
     slots, rows, columns = out.shape
-    at = 0
-    for index, part in enumerate(refs[:-3]):
-        count = part.shape[0] - SCALE_ROWS
-        start = index * SCALE_ROWS
-        headers[start : start + SCALE_ROWS, :] = (
-            part[:SCALE_ROWS, :].astype(jnp.int32).astype(jnp.float32)
-        )
-        codes[at : at + count, :] = part[SCALE_ROWS:, :]
-        at += count
+    refs = list(refs[: -2 - batch_count])
+    for index in range(batch_count):
+        if len(refs[0].shape) == 3:
+            stacks[index] = refs.pop(0)
+            parts = [stacks[index].at[part] for part in range(4)]
+        else:
+            parts, refs = refs[:4], refs[4:]
+            for part, ref in enumerate(parts):
+                stacks[index][part] = ref[...]
+        for part, ref in enumerate(parts):
+            start = (4 * index + part) * SCALE_ROWS
+            headers[start : start + SCALE_ROWS, :] = (
+                ref[:SCALE_ROWS, :].astype(jnp.int32).astype(jnp.float32)
+            )
     row_of = lax.broadcasted_iota(jnp.int32, (rows, columns), 0)
     lane_of = lax.broadcasted_iota(jnp.int32, (rows, columns), 1)
 
     def one_slot(slot, carry):
-        tile, lane, exponent_row, steps_row, filled = (
-            scalars[kind * slots + slot] for kind in range(5)
+        batch, part, row, lane, exponent_row, steps_row, filled = (
+            scalars[kind * slots + slot] for kind in range(7)
         )
         exponent = headers[pl.ds(exponent_row, 1), :]
         steps = headers[pl.ds(steps_row, 1), :]
@@ -150,8 +175,13 @@
         column = jnp.sum(
             jnp.where(lane_of == row_of + lane, scale, 0.0), axis=1, keepdims=True
         )
-        code = codes[pl.ds(pl.multiple_of(tile * rows, rows), rows), :]
-        out[slot] = code.astype(jnp.int32).astype(jnp.float32) * column
+        for index, stack in enumerate(stacks):
+
+            @pl.when(batch == index)
+            def _():
+                code = stack[part, pl.ds(pl.multiple_of(row, SCALE_ROWS), rows), :]
+                out[slot] = code.astype(jnp.int32).astype(jnp.float32) * column
+
         return carry
 
     lax.fori_loop(0, slots, one_slot, 0)
@@ -191,19 +221,22 @@
     pairs = lax.dynamic_index_in_dim(jnp.asarray(ordered), y * 2 + low_bit, 0, keepdims=False)
     scalars = jnp.concatenate([jnp.stack([z, y, x, core]).astype(jnp.int32), pairs])
 
-    def part(step):
-        return lax.dynamic_slice_in_dim(snapshots, (z ^ step) * cells, cells, 2)
-
-    pieces = {(0, 0): part(0)}
+    def part(step, values):
+        return lax.dynamic_slice_in_dim(values, (z ^ step) * cells, cells, 2)
+
+    cut = {step: part(step, snapshots) for step in range(1, z_count, 2)}
+    again = lax.optimization_barrier((snapshots, *cut.values()))[0]
+    cut.update({step: part(step, again) for step in range(0, z_count, 2)})
+    pieces = {(0, 0): cut[0]}
     for step in range(1, z_count):
-        pieces[step, 0] = swap(part(step), "z", step)
+        pieces[step, 0] = swap(cut[step], "z", step)
     layout = [(step, 0, component) for step, component in pieces]
     layout += [(step, 1, component) for step, component in pieces]
     chunks = list(pieces.values()) + [swap(piece, "y", 1) for piece in pieces.values()]
 
-    def sums_shape(index):
-        lead = (2, x_count) if index in LOW_FIRST else (x_count, 2)
-        return jax.ShapeDtypeStruct((*lead, sizes[index], rows_dev, block_size), jnp.float32)
+    def sums_shape(groups):
+        count = sum(sizes[index] for index in groups)
+        return jax.ShapeDtypeStruct((2 * x_count, count, rows_dev, block_size), jnp.float32)
 
     def call(kernel, size, out_shape, operands, name):
         vmem = pl.BlockSpec(memory_space=pltpu.VMEM)
@@ -221,21 +254,21 @@
             name=name,
         )(scalars, *operands)
 
-    shapes = [sums_shape(index) for index in range(GROUPS) for _ in range(2)]
     blocks_shape = jax.ShapeDtypeStruct(
         (block_count, block_size, components * cells), jnp.bfloat16
     )
+    counts = [sum(sizes[index] for index in groups) for groups in CALLS]
     blocks, *sums = call(
-        functools.partial(first_kernel, layout, 4),
-        sizes[0],
-        [blocks_shape] + shapes[:2],
+        functools.partial(first_kernel, layout, 4, sizes),
+        counts[0],
+        [blocks_shape] + [sums_shape(CALLS[0])] * 2,
         chunks,
         "tiles_first",
     )
     sums += call(
-        functools.partial(second_kernel, 4 + 4 * sizes[0]),
-        sum(sizes[1:]),
-        shapes[2:],
+        functools.partial(second_kernel, 4 + 4 * counts[0], sizes),
+        counts[1],
+        [sums_shape(CALLS[1])] * 2,
         [blocks],
         "tiles_second",
     )
@@ -281,17 +314,29 @@
             bits *= 2
         return mine, swap(mine, "z", bits)
 
-    def sum_core(index):
-        keep, send = sums[2 * index : 2 * index + 2]
+    def sum_core(which):
+        keep, send = sums[2 * which : 2 * which + 2]
         send = swap(send, "core", 1)
-        if index in LOW_FIRST:
-            mine, away = split_sum((2, x_count, sizes[index]), keep, send, "sum_core")
-            return mine, swap(away[0], "z", 1)
-        mine, away = split_sum((x_count, 2, sizes[index]), keep, send, "sum_core")
-        if index > 1:
-            arrived = state[0][1]
-            away = lax.optimization_barrier((*away, *arrived))[: len(away)]
-        return mine, over_x(away)
+        cuts, shapes, offset = [], [], 0
+        for index in CALLS[which]:
+            block = x_count if index in LOW_FIRST else 2
+            cuts.append((offset, sizes[index], block))
+            shapes += [float_shape(block, sizes[index])] * (2 * x_count // block)
+            offset += sizes[index]
+        outs = list(
+            step_call(
+                functools.partial(core_sum_kernel, cuts), shapes, keep, send, name="sum_core"
+            )
+        )
+        for index, (_, _, block) in zip(CALLS[which], cuts):
+            count = 2 * x_count // block
+            (mine, *away), outs = outs[:count], outs[count:]
+            if index in LOW_FIRST:
+                state[index] = mine, swap(away[0], "z", 1)
+                continue
+            if which > 0:
+                away = lax.optimization_barrier((*away, *state[0][1]))[: len(away)]
+            state[index] = mine, over_x(away)
 
     def sum_x(index, mine, arrived):
         for value in arrived[:-1]:
@@ -316,13 +361,16 @@
     state = {}
     for stage, which in ORDER:
         if stage == "core":
-            state[which] = sum_core(which)
+            sum_core(which)
         elif stage == "x":
             state[which] = sum_x(which, *state[which])
         elif stage == "low":
             state[which] = sum_low(which, *state[which])
         elif stage == "high":
             state[which] = [plain_sum(*state[which], "sum_high")]
+        elif stage == "stack":
+            shape = jax.ShapeDtypeStruct((4, *parts[0].shape), parts[0].dtype)
+            parts[:4] = step_call(stack_kernel, [shape], *parts[:4], name="stack")
         else:
             counts = [sizes[index] for index in which]
             shape = (SCALE_ROWS + sum(counts) * rows_dev, block_size)
@@ -341,29 +389,36 @@
     pair = first * block_count - (first * (first - 1)) // 2 + second - first
     of_list, slot = pair // quarter, pair % quarter
     off = ((of_list // 2) ^ y) * 2 + ((of_list % 2) ^ low_bit)
-    tile, lane, exponent_row, steps_row = (jnp.zeros_like(slot) for _ in range(4))
+    in_batch, row, lane, exponent_row, steps_row = (jnp.zeros_like(slot) for _ in range(5))
     for index, batch in enumerate(BATCHES):
         start, end = int(starts[batch[0]]), int(starts[batch[-1] + 1])
         inside = (slot >= start) & (slot < end)
         header_rows = -(-(end - start) * rows_dev // block_size)
         at = (slot - start) * rows_dev
         top = (4 * index + off) * SCALE_ROWS + at // block_size
-        tile = jnp.where(inside, 4 * start + off * (end - start) + slot - start, tile)
+        in_batch = jnp.where(inside, index, in_batch)
+        row = jnp.where(inside, SCALE_ROWS + at, row)
         lane = jnp.where(inside, at % block_size, lane)
         exponent_row = jnp.where(inside, top, exponent_row)
         steps_row = jnp.where(inside, top + header_rows, steps_row)
-    places = jnp.concatenate(
-        [tile, lane, exponent_row, steps_row, (row_block >= 0).astype(jnp.int32)]
-    )
+    filled = (row_block >= 0).astype(jnp.int32)
+    places = jnp.concatenate([in_batch, off, row, lane, exponent_row, steps_row, filled])
     vmem = pl.BlockSpec(memory_space=pltpu.VMEM)
     result = pl.pallas_call(
-        functools.partial(place_kernel, scale_factor / (CODE_TOP * SCALE_STEPS)),
+        functools.partial(
+            place_kernel, scale_factor / (CODE_TOP * SCALE_STEPS), len(BATCHES)
+        ),
         out_shape=float_shape(table.shape[0]),
         in_specs=[pl.BlockSpec(memory_space=pltpu.SMEM)] + [vmem] * len(parts),
         out_specs=vmem,
         scratch_shapes=[
-            pltpu.VMEM((4 * quarter * rows_dev, block_size), jnp.int16),
-            pltpu.VMEM((len(parts) * SCALE_ROWS, block_size), jnp.float32),
+            pltpu.VMEM((4 * len(BATCHES) * SCALE_ROWS, block_size), jnp.float32)
+        ] + [
+            pltpu.VMEM(
+                (4, SCALE_ROWS + sum(sizes[index] for index in batch) * rows_dev, block_size),
+                jnp.int16,
+            )
+            for batch in BATCHES
         ],
         compiler_params=pltpu.CompilerParams(vmem_limit_bytes=VMEM_LIMIT),
         cost_estimate=pl.CostEstimate(

time: 120 us -> 118 us (0.983)
  waiting for transfers between devices: 81.6 us -> 80.1 us
    ppermute x23 -> x22, waiting for transfers between devices: 76.2 us -> 74.3 us  [swap(): return lax.ppermute(value, axis, [(i, i ^ bits) for i in range(size)])]
    ppermute x23 -> x22, starting transfers between devices: 26 us -> 26 us  [swap(): return lax.ppermute(value, axis, [(i, i ^ bits) for i in range(size)])]
  transfers between devices with their start and end apart: 25 -> 24, of which waited for: 19 -> 19; matrix products, arithmetic and copies ran while one was open for 1% -> 1% of each run, Pallas kernels for 3% -> 2%
where the time goes in v12:
time: 118 us
  waiting for transfers between devices  80.1 us (68%)
  starting transfers between devices  27 us (23%)
  Pallas kernels  8.55 us (7%)
  local copies, waits for them, and re-layouts  2.25 us (2%)
    ppermute x22, waiting for transfers between devices, swap(): return lax.ppermute(value, axis, [(i, i ^ bits) for i in range(size)])  74.3 us
    ppermute x22, starting transfers between devices, swap(): return lax.ppermute(value, axis, [(i, i ^ bits) for i in range(size)])  26 us
    ppermute x2, waiting for transfers between devices, to_owners(): over_both = lax.ppermute(value, ('z', 'y'), both)  5.82 us
    pallas_call x2, Pallas kernels, call(): pl.pallas_call(kernel, out_shape=out_shape, in_specs=[pl.BlockSpec(memory...  5.06 us
    pallas_call x1, Pallas kernels, per_device(): pl.pallas_call(functools.partial(place_kernel, scale_factor / (CODE_TOP *...  2.39 us
  transfers between devices with their start and end apart: 24, of which 19 were waited for; matrix products, arithmetic and copies ran while one was open for 1% of the time, Pallas kernels for 2%

profile of v12, /device:TPU:0, one launch (start us, length us, event | category | flops | bytes accessed | tf_op | source)
XLA Modules:
  0.0 118.1 jit_solution(15076260657635431152)
XLA Ops:
  0.0 1.3 %constant_dynamic-slice_fusion.2 = (bf16[3,256,256]{2,1,0:T(8,128)(2,1)S(1)}, bf16[3,256,256]{2,1,0:T(8,128)(2,1)S(1)}) fusion(bf16[3,256,1024]{2,1,0:T(8,128)(2,1)} %param.3, s32[]{:T(128)S(6)} %select_n.107, s32[]{:T(128)S(6)} %select_n.106), kind=kLoop, calls=%fused_computation.14 | loop fusion | bytes 1572872 | tf_op jit(solution)/shard_map/dynamic_slice | solution.py:225
  1.3 5.1 %collective-permute-start.2 = (bf16[3,256,256]{2,1,0:T(8,128)(2,1)S(1)}, bf16[3,256,256]{2,1,0:T(8,128)(2,1)S(1)}, u32[]{:S(2)}, u32[]{:S(2)}) collective-permute-start(bf16[3,256,256]{2,1,0:T(8,128)(2,1)S(1)} %get-tuple-element.104), channel_id=1, source_target_pairs={{0,24},{8,16},{16,8},{24,0},{1,25},{9,17},{17,9},{25,1},{2,26},{10... | collective-permute-start | bytes 1179656 | tf_op jit(solution)/shard_map/ppermute | solution.py:202
  6.4 0.0 collective-permute-start
  6.4 0.0 copy-done
  6.4 0.1 constant_dynamic-slice_fusion
  6.5 0.7 collective-permute-start.1
  7.2 1.7 %collective-permute-start.3 = (bf16[3,256,256]{2,1,0:T(8,128)(2,1)S(1)}, bf16[3,256,256]{2,1,0:T(8,128)(2,1)S(1)}, u32[]{:S(2)}, u32[]{:S(2)}) collective-permute-start(bf16[3,256,256]{2,1,0:T(8,128)(2,1)S(1)} %get-tuple-element.103.refs_0_), channel_id=1, source_target_pairs={{0,4},{4,0},{1,5},{5,1},{2,6},{6,2},{3,7},{7,3},{8,12},{12,8},{9,1... | collective-permute-start | bytes 1179656 | tf_op jit(solution)/shard_map/ppermute | solution.py:202
  8.9 7.6 %collective-permute-done.2.refs_3_ = bf16[3,256,256]{2,1,0:T(8,128)(2,1)S(1)} collective-permute-done((bf16[3,256,256]{2,1,0:T(8,128)(2,1)S(1)}, bf16[3,256,256]{2,1,0:T(8,128)(2,1)S(1)}, u32[]{:S(2)}, u32[]{:S(2)}) %collective-permute-start.2) | collective-permute-done | bytes 393248 | tf_op jit(solution)/shard_map/ppermute | solution.py:202
  16.4 1.7 %collective-permute-start.6 = (bf16[3,256,256]{2,1,0:T(8,128)(2,1)S(1)}, bf16[3,256,256]{2,1,0:T(8,128)(2,1)S(1)}, u32[]{:S(2)}, u32[]{:S(2)}) collective-permute-start(bf16[3,256,256]{2,1,0:T(8,128)(2,1)S(1)} %collective-permute-done.2.refs_3_), channel_id=1, source_target_pairs={{0,4},{4,0},{1,5},{5,1},{2,6},{6,2},{3,7},{7,3},{8,12},{12,8},{9,1... | collective-permute-start | bytes 1179656 | tf_op jit(solution)/shard_map/ppermute | solution.py:202
  18.2 6.9 %collective-permute-done.refs_1_ = bf16[3,256,256]{2,1,0:T(8,128)(2,1)S(1)} collective-permute-done((bf16[3,256,256]{2,1,0:T(8,128)(2,1)S(1)}, bf16[3,256,256]{2,1,0:T(8,128)(2,1)S(1)}, u32[]{:S(2)}, u32[]{:S(2)}) %collective-permute-start) | collective-permute-done | bytes 393248 | tf_op jit(solution)/shard_map/ppermute | solution.py:202
  25.1 1.4 %collective-permute-start.4 = (bf16[3,256,256]{2,1,0:T(8,128)(2,1)S(1)}, bf16[3,256,256]{2,1,0:T(8,128)(2,1)S(1)}, u32[]{:S(2)}, u32[]{:S(2)}) collective-permute-start(bf16[3,256,256]{2,1,0:T(8,128)(2,1)S(1)} %collective-permute-done.refs_1_), channel_id=1, source_target_pairs={{0,4},{4,0},{1,5},{5,1},{2,6},{6,2},{3,7},{7,3},{8,12},{12,8},{9,1... | collective-permute-start | bytes 1179656 | tf_op jit(solution)/shard_map/ppermute | solution.py:202
  26.5 13.5 %collective-permute-done.1.refs_2_ = bf16[3,256,256]{2,1,0:T(8,128)(2,1)S(1)} collective-permute-done((bf16[3,256,256]{2,1,0:T(8,128)(2,1)S(1)}, bf16[3,256,256]{2,1,0:T(8,128)(2,1)S(1)}, u32[]{:S(2)}, u32[]{:S(2)}) %collective-permute-start.1) | collective-permute-done | bytes 393248 | tf_op jit(solution)/shard_map/ppermute | solution.py:202
  40.0 1.5 %collective-permute-start.5 = (bf16[3,256,256]{2,1,0:T(8,128)(2,1)S(1)}, bf16[3,256,256]{2,1,0:T(8,128)(2,1)S(1)}, u32[]{:S(2)}, u32[]{:S(2)}) collective-permute-start(bf16[3,256,256]{2,1,0:T(8,128)(2,1)S(1)} %collective-permute-done.1.refs_2_), channel_id=1, source_target_pairs={{0,4},{4,0},{1,5},{5,1},{2,6},{6,2},{3,7},{7,3},{8,12},{12,8},{9,1... | collective-permute-start | bytes 1179656 | tf_op jit(solution)/shard_map/ppermute | solution.py:202
  41.5 0.7 fusion.2
  42.2 0.1 concatenate.7.scalars
  42.2 0.0 collective-permute-done.3.refs_4_
  42.3 0.0 collective-permute-done.6.refs_7_
  42.3 0.0 collective-permute-done.4.refs_5_
  42.3 7.9 %collective-permute-done.5.refs_6_ = bf16[3,256,256]{2,1,0:T(8,128)(2,1)S(1)} collective-permute-done((bf16[3,256,256]{2,1,0:T(8,128)(2,1)S(1)}, bf16[3,256,256]{2,1,0:T(8,128)(2,1)S(1)}, u32[]{:S(2)}, u32[]{:S(2)}) %collective-permute-start.5) | collective-permute-done | bytes 393248 | tf_op jit(solution)/shard_map/ppermute | solution.py:202
  50.1 3.3 %tiles_first.1 = (bf16[8,256,768]{2,1,0:T(8,128)(2,1)S(1)}, f32[4,6,64,256]{3,2,1,0:T(8,128)S(1)}, f32[4,6,64,256]{3,2,1,0:T(8,128)S(1)}) custom-call(s32[40]{0:T(128)S(1)} %concatenate.7.scalars, bf16[3,256,256]{2,1,0:T(8,128)(2,1)S(1)} %get-tuple-element.103.refs_0_, bf16[3,256,256]{2,1,0:T(8,128)(2,1)S(1)} %collective-permute-done.refs_1_, ...), custom_call_target="tpu_custom_call" | custom-call | flops 1207959552 | tf_op jit(solution)/shard_map/tiles_first/pallas_call | solution.py:243
  53.4 0.1 collective-permute-start.7
  53.5 1.8 %tiles_second.1 = (f32[4,3,64,256]{3,2,1,0:T(8,128)S(1)}, f32[4,3,64,256]{3,2,1,0:T(8,128)S(1)}) custom-call(s32[40]{0:T(128)S(1)} %concatenate.7.scalars, bf16[8,256,768]{2,1,0:T(8,128)(2,1)S(1)} %get-tuple-element.67.blocks), custom_call_target="tpu_custom_call" | custom-call | flops 603979776 | tf_op jit(solution)/shard_map/tiles_second/pallas_call | solution.py:243
  55.3 0.6 collective-permute-start.11
  55.8 1.0 collective-permute-done.7.send
  56.9 0.2 sum_core.2
  57.0 1.6 %collective-permute-start.9 = (f32[2,3,64,256]{3,2,1,0:T(8,128)S(1)}, f32[2,3,64,256]{3,2,1,0:T(8,128)S(1)}, u32[]{:S(2)}, u32[]{:S(2)}) collective-permute-start(f32[2,3,64,256]{3,2,1,0:T(8,128)S(1)} %get-tuple-element.59), channel_id=1, source_target_pairs={{0,2},{2,0},{1,3},{3,1},{4,6},{6,4},{5,7},{7,5},{8,10},{10,8},{9,1... | collective-permute-start | bytes 1179656 | tf_op jit(solution)/shard_map/ppermute | solution.py:202
  58.6 0.6 collective-permute-start.8
  59.2 9.1 %collective-permute-done.9.right = f32[2,3,64,256]{3,2,1,0:T(8,128)S(1)} collective-permute-done((f32[2,3,64,256]{3,2,1,0:T(8,128)S(1)}, f32[2,3,64,256]{3,2,1,0:T(8,128)S(1)}, u32[]{:S(2)}, u32[]{:S(2)}) %collective-permute-start.9) | collective-permute-done | bytes 393248 | tf_op jit(solution)/shard_map/ppermute | solution.py:202
  68.3 0.6 collective-permute-start.12
  68.9 0.5 collective-permute-done.8.right
  69.5 1.0 collective-permute-start.10
  70.5 3.9 %collective-permute-done.12.right = f32[3,64,256]{2,1,0:T(8,128)S(1)} collective-permute-done((f32[3,64,256]{2,1,0:T(8,128)S(1)}, f32[3,64,256]{2,1,0:T(8,128)S(1)}, u32[]{:S(2)}, u32[]{:S(2)}) %collective-permute-start.12) | collective-permute-done | bytes 196640 | tf_op jit(solution)/shard_map/ppermute | solution.py:202
  74.5 0.0 copy-start.1
  74.5 0.0 collective-permute-done.11.send
  74.5 0.1 sum_core.3
  74.6 0.7 collective-permute-done.10.right
  75.4 1.0 collective-permute-start.15
  76.4 2.3 %collective-permute-start.14 = (f32[3,64,256]{2,1,0:T(8,128)S(1)}, f32[3,64,256]{2,1,0:T(8,128)S(1)}, u32[]{:S(2)}, u32[]{:S(2)}) collective-permute-start(f32[3,64,256]{2,1,0:T(8,128)S(1)} %sum_z.4.left), channel_id=1, source_target_pairs={{0,16},{8,24},{16,0},{24,8},{1,17},{9,25},{17,1},{25,9},{2,18},{10... | collective-permute-start | bytes 589832 | tf_op jit(solution)/shard_map/ppermute | solution.py:202
  78.7 0.7 collective-permute-start.13
  79.4 5.1 %collective-permute-done.15.right = f32[2,3,64,256]{3,2,1,0:T(8,128)S(1)} collective-permute-done((f32[2,3,64,256]{3,2,1,0:T(8,128)S(1)}, f32[2,3,64,256]{3,2,1,0:T(8,128)S(1)}, u32[]{:S(2)}, u32[]{:S(2)}) %collective-permute-start.15) | collective-permute-done | bytes 393248 | tf_op jit(solution)/shard_map/ppermute | solution.py:202
  84.5 1.1 collective-permute-start.16
  85.6 0.0 copy-done.1
  85.6 5.9 %collective-permute-done.14.right = f32[3,64,256]{2,1,0:T(8,128)S(1)} collective-permute-done((f32[3,64,256]{2,1,0:T(8,128)S(1)}, f32[3,64,256]{2,1,0:T(8,128)S(1)}, u32[]{:S(2)}, u32[]{:S(2)}) %collective-permute-start.14) | collective-permute-done | bytes 196640 | tf_op jit(solution)/shard_map/ppermute | solution.py:202
  91.5 3.4 %collective-permute-done.16.right = f32[3,64,256]{2,1,0:T(8,128)S(1)} collective-permute-done((f32[3,64,256]{2,1,0:T(8,128)S(1)}, f32[3,64,256]{2,1,0:T(8,128)S(1)}, u32[]{:S(2)}, u32[]{:S(2)}) %collective-permute-start.16) | collective-permute-done | bytes 196640 | tf_op jit(solution)/shard_map/ppermute | solution.py:202
  94.9 0.1 collective-permute-start.20
  95.0 2.7 %collective-permute-done.13.refs_1_ = f32[3,64,256]{2,1,0:T(8,128)S(1)} collective-permute-done((f32[3,64,256]{2,1,0:T(8,128)S(1)}, f32[3,64,256]{2,1,0:T(8,128)S(1)}, u32[]{:S(2)}, u32[]{:S(2)}) %collective-permute-start.13) | collective-permute-done | bytes 196640 | tf_op jit(solution)/shard_map/ppermute | solution.py:202
  97.8 0.3 finish.2.refs_0_
  98.1 0.5 collective-permute-start.19
  98.6 1.2 collective-permute-start.18
  99.8 1.9 %collective-permute-start.17 = (s16[400,256]{1,0:T(8,128)(2,1)S(1)}, s16[400,256]{1,0:T(8,128)(2,1)S(1)}, u32[]{:S(2)}, u32[]{:S(2)}) collective-permute-start(s16[400,256]{1,0:T(8,128)(2,1)S(1)} %finish.2.refs_0_), channel_id=1, source_target_pairs={{0,8},{8,0},{16,24},{24,16},{1,9},{9,1},{17,25},{25,17},{2,10},{10... | collective-permute-start | bytes 614408 | tf_op jit(solution)/shard_map/ppermute | solution.py:202
  101.7 1.5 %collective-permute-done.20.refs_1_ = f32[3,64,256]{2,1,0:T(8,128)S(1)} collective-permute-done((f32[3,64,256]{2,1,0:T(8,128)S(1)}, f32[3,64,256]{2,1,0:T(8,128)S(1)}, u32[]{:S(2)}, u32[]{:S(2)}) %collective-permute-start.20) | collective-permute-done | bytes 196640 | tf_op jit(solution)/shard_map/ppermute | solution.py:202
  103.2 0.2 finish.3.refs_1_
  103.5 0.4 collective-permute-start.23
  103.9 1.2 %collective-permute-start.22 = (s16[208,256]{1,0:T(8,128)(2,1)S(1)}, s16[208,256]{1,0:T(8,128)(2,1)S(1)}, u32[]{:S(2)}, u32[]{:S(2)}) collective-permute-start(s16[208,256]{1,0:T(8,128)(2,1)S(1)} %finish.3.refs_1_), channel_id=1, source_target_pairs={{0,4},{4,0},{1,5},{5,1},{2,6},{6,2},{3,7},{7,3},{8,12},{12,8},{9,1... | collective-permute-start | bytes 319496 | tf_op jit(solution)/shard_map/ppermute | solution.py:202
  105.1 3.4 %collective-permute-done.19.refs_3_ = s16[400,256]{1,0:T(8,128)(2,1)S(1)} collective-permute-done((s16[400,256]{1,0:T(8,128)(2,1)S(1)}, s16[400,256]{1,0:T(8,128)(2,1)S(1)}, u32[]{:S(2)}, u32[]{:S(2)}) %collective-permute-start.19) | collective-permute-done | bytes 204832 | tf_op jit(solution)/shard_map/ppermute | solution.py:357
  108.6 0.0 collective-permute-start.21
  108.6 0.1 concatenate.6.scalars
  108.6 0.4 collective-permute-done.18.refs_2_
  109.1 3.0 %collective-permute-done.17.refs_1_ = s16[400,256]{1,0:T(8,128)(2,1)S(1)} collective-permute-done((s16[400,256]{1,0:T(8,128)(2,1)S(1)}, s16[400,256]{1,0:T(8,128)(2,1)S(1)}, u32[]{:S(2)}, u32[]{:S(2)}) %collective-permute-start.17) | collective-permute-done | bytes 204832 | tf_op jit(solution)/shard_map/ppermute | solution.py:202
  112.1 0.1 stack.17.refs_0_
  112.2 2.4 %collective-permute-done.23.refs_4_ = s16[208,256]{1,0:T(8,128)(2,1)S(1)} collective-permute-done((s16[208,256]{1,0:T(8,128)(2,1)S(1)}, s16[208,256]{1,0:T(8,128)(2,1)S(1)}, u32[]{:S(2)}, u32[]{:S(2)}) %collective-permute-start.23) | collective-permute-done | bytes 106528 | tf_op jit(solution)/shard_map/ppermute | solution.py:357
  114.6 0.0 collective-permute-done.22.refs_3_
  114.6 1.1 collective-permute-done.21.refs_2_
  115.7 2.4 %place_tiles.1 = f32[10,64,256]{2,1,0:T(8,128)} custom-call(s32[70]{0:T(128)S(1)} %concatenate.6.scalars, s16[4,400,256]{2,1,0:T(8,128)(2,1)S(1)} %stack.17.refs_0_, s16[208,256]{1,0:T(8,128)(2,1)S(1)} %finish.3.refs_1_, s16[208,256]{1,0:T(8,128)(2,1)S(1)} %collective-permute-done.21.refs_2_, s16[208,256]{1,0:T(8,128)(2,1)S(1)} %collective-permute-done.22.refs_3_, ...), custom_call_target="tpu_custom_call" | custom-call | flops 163840 | tf_op jit(solution)/shard_map/place_tiles/pallas_call | solution.py:407
  (11 shorter events, 0.3 us)
Async XLA Ops:
  0.0 6.4 %copy-start = (bf16[3,256,1024]{2,1,0:T(8,128)(2,1)S(1)}, bf16[3,256,1024]{2,1,0:T(8,128)(2,1)}, u32[]{:S(2)}) copy-start(bf16[3,256,1024]{2,1,0:T(8,128)(2,1)} %param.3) | copy-start | bytes 4718596
  1.3 15.1 %collective-permute-start.2 = (bf16[3,256,256]{2,1,0:T(8,128)(2,1)S(1)}, bf16[3,256,256]{2,1,0:T(8,128)(2,1)S(1)}, u32[]{:S(2)}, u32[]{:S(2)}) collective-permute-start(bf16[3,256,256]{2,1,0:T(8,128)(2,1)S(1)} %get-tuple-element.104), channel_id=1, source_target_pairs={{0,24},{8,16},{16,8},{24,0},{1,25},{9,17},{17,9},{25,1},{2,26},{10... | collective-permute-start | bytes 1179656 | tf_op jit(solution)/shard_map/ppermute | solution.py:202
  6.4 18.7 %collective-permute-start = (bf16[3,256,256]{2,1,0:T(8,128)(2,1)S(1)}, bf16[3,256,256]{2,1,0:T(8,128)(2,1)S(1)}, u32[]{:S(2)}, u32[]{:S(2)}) collective-permute-start(bf16[3,256,256]{2,1,0:T(8,128)(2,1)S(1)} %get-tuple-element.105), channel_id=1, source_target_pairs={{0,8},{8,0},{16,24},{24,16},{1,9},{9,1},{17,25},{25,17},{2,10},{10... | collective-permute-start | bytes 1179656 | tf_op jit(solution)/shard_map/ppermute | solution.py:202
  6.5 33.4 %collective-permute-start.1 = (bf16[3,256,256]{2,1,0:T(8,128)(2,1)S(1)}, bf16[3,256,256]{2,1,0:T(8,128)(2,1)S(1)}, u32[]{:S(2)}, u32[]{:S(2)}) collective-permute-start(bf16[3,256,256]{2,1,0:T(8,128)(2,1)S(1)} %get-tuple-element.102), channel_id=1, source_target_pairs={{0,16},{8,24},{16,0},{24,8},{1,17},{9,25},{17,1},{25,9},{2,18},{10... | collective-permute-start | bytes 1179656 | tf_op jit(solution)/shard_map/ppermute | solution.py:202
  7.2 35.0 %collective-permute-start.3 = (bf16[3,256,256]{2,1,0:T(8,128)(2,1)S(1)}, bf16[3,256,256]{2,1,0:T(8,128)(2,1)S(1)}, u32[]{:S(2)}, u32[]{:S(2)}) collective-permute-start(bf16[3,256,256]{2,1,0:T(8,128)(2,1)S(1)} %get-tuple-element.103.refs_0_), channel_id=1, source_target_pairs={{0,4},{4,0},{1,5},{5,1},{2,6},{6,2},{3,7},{7,3},{8,12},{12,8},{9,1... | collective-permute-start | bytes 1179656 | tf_op jit(solution)/shard_map/ppermute | solution.py:202
  16.4 25.8 %collective-permute-start.6 = (bf16[3,256,256]{2,1,0:T(8,128)(2,1)S(1)}, bf16[3,256,256]{2,1,0:T(8,128)(2,1)S(1)}, u32[]{:S(2)}, u32[]{:S(2)}) collective-permute-start(bf16[3,256,256]{2,1,0:T(8,128)(2,1)S(1)} %collective-permute-done.2.refs_3_), channel_id=1, source_target_pairs={{0,4},{4,0},{1,5},{5,1},{2,6},{6,2},{3,7},{7,3},{8,12},{12,8},{9,1... | collective-permute-start | bytes 1179656 | tf_op jit(solution)/shard_map/ppermute | solution.py:202
  25.1 17.2 %collective-permute-start.4 = (bf16[3,256,256]{2,1,0:T(8,128)(2,1)S(1)}, bf16[3,256,256]{2,1,0:T(8,128)(2,1)S(1)}, u32[]{:S(2)}, u32[]{:S(2)}) collective-permute-start(bf16[3,256,256]{2,1,0:T(8,128)(2,1)S(1)} %collective-permute-done.refs_1_), channel_id=1, source_target_pairs={{0,4},{4,0},{1,5},{5,1},{2,6},{6,2},{3,7},{7,3},{8,12},{12,8},{9,1... | collective-permute-start | bytes 1179656 | tf_op jit(solution)/shard_map/ppermute | solution.py:202
  40.0 10.2 %collective-permute-start.5 = (bf16[3,256,256]{2,1,0:T(8,128)(2,1)S(1)}, bf16[3,256,256]{2,1,0:T(8,128)(2,1)S(1)}, u32[]{:S(2)}, u32[]{:S(2)}) collective-permute-start(bf16[3,256,256]{2,1,0:T(8,128)(2,1)S(1)} %collective-permute-done.1.refs_2_), channel_id=1, source_target_pairs={{0,4},{4,0},{1,5},{5,1},{2,6},{6,2},{3,7},{7,3},{8,12},{12,8},{9,1... | collective-permute-start | bytes 1179656 | tf_op jit(solution)/shard_map/ppermute | solution.py:202
  53.4 3.5 %collective-permute-start.7 = (f32[4,6,64,256]{3,2,1,0:T(8,128)S(1)}, f32[4,6,64,256]{3,2,1,0:T(8,128)S(1)}, u32[]{:S(2)}, u32[]{:S(2)}) collective-permute-start(f32[4,6,64,256]{3,2,1,0:T(8,128)S(1)} %get-tuple-element.53), channel_id=1, source_target_pairs={{0,1},{1,0},{2,3},{3,2},{4,5},{5,4},{6,7},{7,6},{8,9},{9,8},{10,11... | collective-permute-start | bytes 4718600 | tf_op jit(solution)/shard_map/ppermute | solution.py:202
  55.3 19.2 %collective-permute-start.11 = (f32[4,3,64,256]{3,2,1,0:T(8,128)S(1)}, f32[4,3,64,256]{3,2,1,0:T(8,128)S(1)}, u32[]{:S(2)}, u32[]{:S(2)}) collective-permute-start(f32[4,3,64,256]{3,2,1,0:T(8,128)S(1)} %get-tuple-element.69), channel_id=1, source_target_pairs={{0,1},{1,0},{2,3},{3,2},{4,5},{5,4},{6,7},{7,6},{8,9},{9,8},{10,11... | collective-permute-start | bytes 2359304 | tf_op jit(solution)/shard_map/ppermute | solution.py:202
  57.0 11.2 %collective-permute-start.9 = (f32[2,3,64,256]{3,2,1,0:T(8,128)S(1)}, f32[2,3,64,256]{3,2,1,0:T(8,128)S(1)}, u32[]{:S(2)}, u32[]{:S(2)}) collective-permute-start(f32[2,3,64,256]{3,2,1,0:T(8,128)S(1)} %get-tuple-element.59), channel_id=1, source_target_pairs={{0,2},{2,0},{1,3},{3,1},{4,6},{6,4},{5,7},{7,5},{8,10},{10,8},{9,1... | collective-permute-start | bytes 1179656 | tf_op jit(solution)/shard_map/ppermute | solution.py:202
  58.6 10.9 %collective-permute-start.8 = (f32[2,3,64,256]{3,2,1,0:T(8,128)S(1)}, f32[2,3,64,256]{3,2,1,0:T(8,128)S(1)}, u32[]{:S(2)}, u32[]{:S(2)}) collective-permute-start(f32[2,3,64,256]{3,2,1,0:T(8,128)S(1)} %get-tuple-element.57), channel_id=1, source_target_pairs={{0,8},{8,0},{16,24},{24,16},{1,9},{9,1},{17,25},{25,17},{2,10},{10... | collective-permute-start | bytes 1179656 | tf_op jit(solution)/shard_map/ppermute | solution.py:202
  68.3 6.2 %collective-permute-start.12 = (f32[3,64,256]{2,1,0:T(8,128)S(1)}, f32[3,64,256]{2,1,0:T(8,128)S(1)}, u32[]{:S(2)}, u32[]{:S(2)}) collective-permute-start(f32[3,64,256]{2,1,0:T(8,128)S(1)} %get-tuple-element.70), channel_id=1, source_target_pairs={{0,8},{8,0},{16,24},{24,16},{1,9},{9,1},{17,25},{25,17},{2,10},{10... | collective-permute-start | bytes 589832 | tf_op jit(solution)/shard_map/ppermute | solution.py:202
  69.5 5.9 %collective-permute-start.10 = (f32[3,64,256]{2,1,0:T(8,128)S(1)}, f32[3,64,256]{2,1,0:T(8,128)S(1)}, u32[]{:S(2)}, u32[]{:S(2)}) collective-permute-start(f32[3,64,256]{2,1,0:T(8,128)S(1)} %get-tuple-element.66), channel_id=1, source_target_pairs={{0,2},{2,0},{1,3},{3,1},{4,6},{6,4},{5,7},{7,5},{8,10},{10,8},{9,1... | collective-permute-start | bytes 589832 | tf_op jit(solution)/shard_map/ppermute | solution.py:202
  74.5 11.1 %copy-start.1 = (s32[1,10,2]{1,2,0:T(2,128)S(1)}, s32[1,10,2]{1,2,0:T(2,128)}, u32[]{:S(2)}) copy-start(s32[1,10,2]{1,2,0:T(2,128)} %param.4) | copy-start | bytes 244
  75.4 9.1 %collective-permute-start.15 = (f32[2,3,64,256]{3,2,1,0:T(8,128)S(1)}, f32[2,3,64,256]{3,2,1,0:T(8,128)S(1)}, u32[]{:S(2)}, u32[]{:S(2)}) collective-permute-start(f32[2,3,64,256]{3,2,1,0:T(8,128)S(1)} %get-tuple-element.79), channel_id=1, source_target_pairs={{0,2},{2,0},{1,3},{3,1},{4,6},{6,4},{5,7},{7,5},{8,10},{10,8},{9,1... | collective-permute-start | bytes 1179656 | tf_op jit(solution)/shard_map/ppermute | solution.py:202
  76.4 15.1 %collective-permute-start.14 = (f32[3,64,256]{2,1,0:T(8,128)S(1)}, f32[3,64,256]{2,1,0:T(8,128)S(1)}, u32[]{:S(2)}, u32[]{:S(2)}) collective-permute-start(f32[3,64,256]{2,1,0:T(8,128)S(1)} %sum_z.4.left), channel_id=1, source_target_pairs={{0,16},{8,24},{16,0},{24,8},{1,17},{9,25},{17,1},{25,9},{2,18},{10... | collective-permute-start | bytes 589832 | tf_op jit(solution)/shard_map/ppermute | solution.py:202
  78.7 19.1 %collective-permute-start.13 = (f32[3,64,256]{2,1,0:T(8,128)S(1)}, f32[3,64,256]{2,1,0:T(8,128)S(1)}, u32[]{:S(2)}, u32[]{:S(2)}) collective-permute-start(f32[3,64,256]{2,1,0:T(8,128)S(1)} %sum_x.4.refs_0_), channel_id=1, source_target_pairs={{0,16},{8,24},{16,0},{24,8},{1,17},{9,25},{17,1},{25,9},{2,18},{10... | collective-permute-start | bytes 589832 | tf_op jit(solution)/shard_map/ppermute | solution.py:202
  84.5 10.4 %collective-permute-start.16 = (f32[3,64,256]{2,1,0:T(8,128)S(1)}, f32[3,64,256]{2,1,0:T(8,128)S(1)}, u32[]{:S(2)}, u32[]{:S(2)}) collective-permute-start(f32[3,64,256]{2,1,0:T(8,128)S(1)} %get-tuple-element.85), channel_id=1, source_target_pairs={{0,8},{8,0},{16,24},{24,16},{1,9},{9,1},{17,25},{25,17},{2,10},{10... | collective-permute-start | bytes 589832 | tf_op jit(solution)/shard_map/ppermute | solution.py:202
  94.9 8.3 %collective-permute-start.20 = (f32[3,64,256]{2,1,0:T(8,128)S(1)}, f32[3,64,256]{2,1,0:T(8,128)S(1)}, u32[]{:S(2)}, u32[]{:S(2)}) collective-permute-start(f32[3,64,256]{2,1,0:T(8,128)S(1)} %sum_z.5.refs_0_), channel_id=1, source_target_pairs={{0,16},{8,24},{16,0},{24,8},{1,17},{9,25},{17,1},{25,9},{2,18},{10... | collective-permute-start | bytes 589832 | tf_op jit(solution)/shard_map/ppermute | solution.py:202
  98.1 10.5 %collective-permute-start.19 = (s16[400,256]{1,0:T(8,128)(2,1)S(1)}, s16[400,256]{1,0:T(8,128)(2,1)S(1)}, u32[]{:S(2)}, u32[]{:S(2)}) collective-permute-start(s16[400,256]{1,0:T(8,128)(2,1)S(1)} %finish.2.refs_0_), channel_id=1, source_target_pairs={{0,12},{4,8},{8,4},{12,0},{16,28},{20,24},{24,20},{28,16},{1,13},{... | collective-permute-start | bytes 614408 | tf_op jit(solution)/shard_map/ppermute | solution.py:357
  98.6 10.5 %collective-permute-start.18 = (s16[400,256]{1,0:T(8,128)(2,1)S(1)}, s16[400,256]{1,0:T(8,128)(2,1)S(1)}, u32[]{:S(2)}, u32[]{:S(2)}) collective-permute-start(s16[400,256]{1,0:T(8,128)(2,1)S(1)} %finish.2.refs_0_), channel_id=1, source_target_pairs={{0,4},{4,0},{1,5},{5,1},{2,6},{6,2},{3,7},{7,3},{8,12},{12,8},{9,1... | collective-permute-start | bytes 614408 | tf_op jit(solution)/shard_map/ppermute | solution.py:202
  99.8 12.3 %collective-permute-start.17 = (s16[400,256]{1,0:T(8,128)(2,1)S(1)}, s16[400,256]{1,0:T(8,128)(2,1)S(1)}, u32[]{:S(2)}, u32[]{:S(2)}) collective-permute-start(s16[400,256]{1,0:T(8,128)(2,1)S(1)} %finish.2.refs_0_), channel_id=1, source_target_pairs={{0,8},{8,0},{16,24},{24,16},{1,9},{9,1},{17,25},{25,17},{2,10},{10... | collective-permute-start | bytes 614408 | tf_op jit(solution)/shard_map/ppermute | solution.py:202
  103.5 11.1 %collective-permute-start.23 = (s16[208,256]{1,0:T(8,128)(2,1)S(1)}, s16[208,256]{1,0:T(8,128)(2,1)S(1)}, u32[]{:S(2)}, u32[]{:S(2)}) collective-permute-start(s16[208,256]{1,0:T(8,128)(2,1)S(1)} %finish.3.refs_1_), channel_id=1, source_target_pairs={{0,12},{4,8},{8,4},{12,0},{16,28},{20,24},{24,20},{28,16},{1,13},{... | collective-permute-start | bytes 319496 | tf_op jit(solution)/shard_map/ppermute | solution.py:357
  103.9 10.7 %collective-permute-start.22 = (s16[208,256]{1,0:T(8,128)(2,1)S(1)}, s16[208,256]{1,0:T(8,128)(2,1)S(1)}, u32[]{:S(2)}, u32[]{:S(2)}) collective-permute-start(s16[208,256]{1,0:T(8,128)(2,1)S(1)} %finish.3.refs_1_), channel_id=1, source_target_pairs={{0,4},{4,0},{1,5},{5,1},{2,6},{6,2},{3,7},{7,3},{8,12},{12,8},{9,1... | collective-permute-start | bytes 319496 | tf_op jit(solution)/shard_map/ppermute | solution.py:202
  108.6 7.1 %collective-permute-start.21 = (s16[208,256]{1,0:T(8,128)(2,1)S(1)}, s16[208,256]{1,0:T(8,128)(2,1)S(1)}, u32[]{:S(2)}, u32[]{:S(2)}) collective-permute-start(s16[208,256]{1,0:T(8,128)(2,1)S(1)} %finish.3.refs_1_), channel_id=1, source_target_pairs={{0,8},{8,0},{16,24},{24,16},{1,9},{9,1},{17,25},{25,17},{2,10},{10... | collective-permute-start | bytes 319496 | tf_op jit(solution)/shard_map/ppermute | solution.py:202

commit v13 on v12

--- a/solution.py
+++ b/solution.py
@@ -9,6 +9,7 @@
 from jax.experimental.pallas import tpu as pltpu
 from jax.sharding import Mesh, PartitionSpec as P
 
+UNROLL = 4
 VMEM_LIMIT = 24 * 2**20
 GROUPS = 3
 BATCHES = ((0, 1), (2,))
@@ -17,7 +18,7 @@
 ORDER = (
     ("core", 0), ("x", 1), ("low", 0), ("low", 1), ("core", 1), ("x", 0),
     ("x", 2), ("high", 1), ("low", 2), ("finish", BATCHES[0]), ("finish", BATCHES[1]),
-    ("stack", None),
+    ("place", 0), ("place", 1),
 )
 CODE_TOP = 32767.0
 SCALE_ROWS = 16
@@ -56,7 +57,7 @@
                 send_ref[place, offset + slot] = jnp.where(core == 0, odd, even)
         return carry
 
-    lax.fori_loop(0, size, one_slot, 0)
+    lax.fori_loop(0, size, one_slot, 0, unroll=size <= UNROLL)
 
 
 def multiply_groups(scalars, first_pair, sizes, blocks, groups, outs):
@@ -137,50 +138,35 @@
     code[:SCALE_ROWS, :] = header.astype(jnp.int32).astype(jnp.int16)
 
 
-def stack_kernel(*refs):
-    out = refs[-1]
-    for index, part in enumerate(refs[:-1]):
-        out[index] = part[...]
-
-
-def place_kernel(factor, batch_count, scalars, *refs):
-    out, headers = refs[-2 - batch_count : -batch_count]
-    stacks = list(refs[-batch_count:])
+def place_kernel(factor, batch, scalars, *refs):
+    parts, before = refs[:4], refs[4:-3]
+    out, headers, stack = refs[-3:]
     slots, rows, columns = out.shape
-    refs = list(refs[: -2 - batch_count])
-    for index in range(batch_count):
-        if len(refs[0].shape) == 3:
-            stacks[index] = refs.pop(0)
-            parts = [stacks[index].at[part] for part in range(4)]
-        else:
-            parts, refs = refs[:4], refs[4:]
-            for part, ref in enumerate(parts):
-                stacks[index][part] = ref[...]
-        for part, ref in enumerate(parts):
-            start = (4 * index + part) * SCALE_ROWS
-            headers[start : start + SCALE_ROWS, :] = (
-                ref[:SCALE_ROWS, :].astype(jnp.int32).astype(jnp.float32)
-            )
+    for index, part in enumerate(parts):
+        start = index * SCALE_ROWS
+        headers[start : start + SCALE_ROWS, :] = (
+            part[:SCALE_ROWS, :].astype(jnp.int32).astype(jnp.float32)
+        )
+        stack[index] = part[...]
+    out[...] = before[0][...] if before else jnp.zeros_like(out)
     row_of = lax.broadcasted_iota(jnp.int32, (rows, columns), 0)
     lane_of = lax.broadcasted_iota(jnp.int32, (rows, columns), 1)
 
     def one_slot(slot, carry):
-        batch, part, row, lane, exponent_row, steps_row, filled = (
-            scalars[kind * slots + slot] for kind in range(7)
+        batch_of, part, row, lane, exponent_row, steps_row = (
+            scalars[kind * slots + slot] for kind in range(6)
         )
-        exponent = headers[pl.ds(exponent_row, 1), :]
-        steps = headers[pl.ds(steps_row, 1), :]
-        scale = steps * jnp.exp(exponent * math.log(2.0)) * factor
-        scale = jnp.where(filled > 0, scale, 0.0)
-        column = jnp.sum(
-            jnp.where(lane_of == row_of + lane, scale, 0.0), axis=1, keepdims=True
-        )
-        for index, stack in enumerate(stacks):
-
-            @pl.when(batch == index)
-            def _():
-                code = stack[part, pl.ds(pl.multiple_of(row, SCALE_ROWS), rows), :]
-                out[slot] = code.astype(jnp.int32).astype(jnp.float32) * column
+
+        @pl.when(batch_of == batch)
+        def _():
+            exponent = headers[pl.ds(exponent_row, 1), :]
+            steps = headers[pl.ds(steps_row, 1), :]
+            scale = steps * jnp.exp(exponent * math.log(2.0)) * factor
+            column = jnp.sum(
+                jnp.where(lane_of == row_of + lane, scale, 0.0), axis=1, keepdims=True
+            )
+            code = stack[part, pl.ds(pl.multiple_of(row, SCALE_ROWS), rows), :]
+            out[slot] = code.astype(jnp.int32).astype(jnp.float32) * column
 
         return carry
 
@@ -357,30 +343,6 @@
         over_both = lax.ppermute(value, ("z", "y"), both)
         return [value, swap(value, "z", 1), swap(value, "y", 1), over_both]
 
-    parts = []
-    state = {}
-    for stage, which in ORDER:
-        if stage == "core":
-            sum_core(which)
-        elif stage == "x":
-            state[which] = sum_x(which, *state[which])
-        elif stage == "low":
-            state[which] = sum_low(which, *state[which])
-        elif stage == "high":
-            state[which] = [plain_sum(*state[which], "sum_high")]
-        elif stage == "stack":
-            shape = jax.ShapeDtypeStruct((4, *parts[0].shape), parts[0].dtype)
-            parts[:4] = step_call(stack_kernel, [shape], *parts[:4], name="stack")
-        else:
-            counts = [sizes[index] for index in which]
-            shape = (SCALE_ROWS + sum(counts) * rows_dev, block_size)
-            kernel = functools.partial(code_kernel, counts, [len(state[i]) for i in which])
-            operands = [value for index in which for value in state[index]]
-            (code,) = step_call(
-                kernel, [jax.ShapeDtypeStruct(shape, jnp.int16)], *operands, name="finish"
-            )
-            parts += to_owners(code)
-
     table = tile_table[0]
     row_block = table[:, 0]
     col_block = table[:, 1]
@@ -395,38 +357,63 @@
         inside = (slot >= start) & (slot < end)
         header_rows = -(-(end - start) * rows_dev // block_size)
         at = (slot - start) * rows_dev
-        top = (4 * index + off) * SCALE_ROWS + at // block_size
+        top = off * SCALE_ROWS + at // block_size
         in_batch = jnp.where(inside, index, in_batch)
         row = jnp.where(inside, SCALE_ROWS + at, row)
         lane = jnp.where(inside, at % block_size, lane)
         exponent_row = jnp.where(inside, top, exponent_row)
         steps_row = jnp.where(inside, top + header_rows, steps_row)
-    filled = (row_block >= 0).astype(jnp.int32)
-    places = jnp.concatenate([in_batch, off, row, lane, exponent_row, steps_row, filled])
-    vmem = pl.BlockSpec(memory_space=pltpu.VMEM)
-    result = pl.pallas_call(
-        functools.partial(
-            place_kernel, scale_factor / (CODE_TOP * SCALE_STEPS), len(BATCHES)
-        ),
-        out_shape=float_shape(table.shape[0]),
-        in_specs=[pl.BlockSpec(memory_space=pltpu.SMEM)] + [vmem] * len(parts),
-        out_specs=vmem,
-        scratch_shapes=[
-            pltpu.VMEM((4 * len(BATCHES) * SCALE_ROWS, block_size), jnp.float32)
-        ] + [
-            pltpu.VMEM(
-                (4, SCALE_ROWS + sum(sizes[index] for index in batch) * rows_dev, block_size),
-                jnp.int16,
+    in_batch = jnp.where(row_block >= 0, in_batch, -1)
+    places = jnp.concatenate([in_batch, off, row, lane, exponent_row, steps_row])
+
+    parts, result = [], []
+    state = {}
+    for stage, which in ORDER:
+        if stage == "core":
+            sum_core(which)
+        elif stage == "x":
+            state[which] = sum_x(which, *state[which])
+        elif stage == "low":
+            state[which] = sum_low(which, *state[which])
+        elif stage == "high":
+            state[which] = [plain_sum(*state[which], "sum_high")]
+        elif stage == "place":
+            four = parts[4 * which : 4 * which + 4]
+            operands = lax.optimization_barrier((places, *four, *result, *last))[:-1]
+            vmem = pl.BlockSpec(memory_space=pltpu.VMEM)
+            result = [
+                pl.pallas_call(
+                    functools.partial(
+                        place_kernel, scale_factor / (CODE_TOP * SCALE_STEPS), which
+                    ),
+                    out_shape=float_shape(table.shape[0]),
+                    in_specs=[pl.BlockSpec(memory_space=pltpu.SMEM)]
+                    + [vmem] * (len(operands) - 1),
+                    out_specs=vmem,
+                    scratch_shapes=[
+                        pltpu.VMEM((4 * SCALE_ROWS, block_size), jnp.float32),
+                        pltpu.VMEM((4, *four[0].shape), jnp.int16),
+                    ],
+                    compiler_params=pltpu.CompilerParams(vmem_limit_bytes=VMEM_LIMIT),
+                    cost_estimate=pl.CostEstimate(
+                        flops=table.shape[0] * rows_dev * block_size,
+                        bytes_accessed=0,
+                        transcendentals=0,
+                    ),
+                    name="place_tiles",
+                )(*operands)
+            ]
+        else:
+            counts = [sizes[index] for index in which]
+            shape = (SCALE_ROWS + sum(counts) * rows_dev, block_size)
+            kernel = functools.partial(code_kernel, counts, [len(state[i]) for i in which])
+            operands = [value for index in which for value in state[index]]
+            (code,) = step_call(
+                kernel, [jax.ShapeDtypeStruct(shape, jnp.int16)], *operands, name="finish"
             )
-            for batch in BATCHES
-        ],
-        compiler_params=pltpu.CompilerParams(vmem_limit_bytes=VMEM_LIMIT),
-        cost_estimate=pl.CostEstimate(
-            flops=table.shape[0] * rows_dev * block_size, bytes_accessed=0, transcendentals=0
-        ),
-        name="place_tiles",
-    )(places, *parts)
-    return result[None]
+            parts += to_owners(code)
+
+    return result[0][None]
 
 
 def solution(mesh):

time: 118 us -> 117 us (level)
  waiting for transfers between devices: 80.1 us -> 77.8 us
  starting transfers between devices: 27 us -> 28.7 us
    ppermute x2, waiting for transfers between devices: 5.82 us -> 2.18 us  [to_owners(): over_both = lax.ppermute(value, ('z', 'y'), both)]
    ppermute x2, starting transfers between devices: 0.94 us -> 2.66 us  [to_owners(): over_both = lax.ppermute(value, ('z', 'y'), both)]
    pallas_call x2, Pallas kernels: 5.06 us -> 3.68 us  [call(): pl.pallas_call(kernel, out_shape=out_shape, in_specs=[pl.BlockSpec(memory...]
    ppermute x22, waiting for transfers between devices: 74.3 us -> 75.7 us  [swap(): return lax.ppermute(value, axis, [(i, i ^ bits) for i in range(size)])]
    pallas_call x1 -> x2, Pallas kernels: 2.39 us -> 2.75 us  [per_device(): pl.pallas_call(functools.partial(place_kernel, scale_factor / (CODE_TOP *...]
  transfers between devices with their start and end apart: 24 -> 24, of which waited for: 19 -> 17; matrix products, arithmetic and copies ran while one was open for 1% -> 1% of each run, Pallas kernels for 2% -> 3%
where the time goes in v13:
time: 117 us; the launch traced here: 116 us
  waiting for transfers between devices  77.8 us (66%)
  starting transfers between devices  28.7 us (25%)
  Pallas kernels  7.47 us (6%)
  local copies, waits for them, and re-layouts  2.25 us (2%)
    ppermute x22, waiting for transfers between devices, swap(): return lax.ppermute(value, axis, [(i, i ^ bits) for i in range(size)])  75.7 us
    ppermute x22, starting transfers between devices, swap(): return lax.ppermute(value, axis, [(i, i ^ bits) for i in range(size)])  26 us
    pallas_call x2, Pallas kernels, call(): pl.pallas_call(kernel, out_shape=out_shape, in_specs=[pl.BlockSpec(memory...  3.68 us
    pallas_call x2, Pallas kernels, per_device(): pl.pallas_call(functools.partial(place_kernel, scale_factor / (CODE_TOP *...  2.75 us
    ppermute x2, starting transfers between devices, to_owners(): over_both = lax.ppermute(value, ('z', 'y'), both)  2.66 us
  transfers between devices with their start and end apart: 24, of which 17 were waited for; matrix products, arithmetic and copies ran while one was open for 1% of the time, Pallas kernels for 3%

profile of v13, /device:TPU:0, one launch (start us, length us, event | category | flops | bytes accessed | tf_op | source)
XLA Modules:
  0.0 116.4 jit_solution(7092843146910204374)
XLA Ops:
  0.0 1.3 %constant_dynamic-slice_fusion.2 = (bf16[3,256,256]{2,1,0:T(8,128)(2,1)S(1)}, bf16[3,256,256]{2,1,0:T(8,128)(2,1)S(1)}) fusion(bf16[3,256,1024]{2,1,0:T(8,128)(2,1)} %param.3, s32[]{:T(128)S(6)} %select_n.112, s32[]{:T(128)S(6)} %select_n.111), kind=kLoop, calls=%fused_computation.14 | loop fusion | bytes 1572872 | tf_op jit(solution)/shard_map/dynamic_slice | solution.py:211
  1.3 5.1 %collective-permute-start.2 = (bf16[3,256,256]{2,1,0:T(8,128)(2,1)S(1)}, bf16[3,256,256]{2,1,0:T(8,128)(2,1)S(1)}, u32[]{:S(2)}, u32[]{:S(2)}) collective-permute-start(bf16[3,256,256]{2,1,0:T(8,128)(2,1)S(1)} %get-tuple-element.118), channel_id=1, source_target_pairs={{0,24},{8,16},{16,8},{24,0},{1,25},{9,17},{17,9},{25,1},{2,26},{10... | collective-permute-start | bytes 1179656 | tf_op jit(solution)/shard_map/ppermute | solution.py:188
  6.4 0.0 collective-permute-start
  6.4 0.0 copy-done
  6.4 0.1 constant_dynamic-slice_fusion
  6.5 0.7 collective-permute-start.1
  7.2 1.7 %collective-permute-start.3 = (bf16[3,256,256]{2,1,0:T(8,128)(2,1)S(1)}, bf16[3,256,256]{2,1,0:T(8,128)(2,1)S(1)}, u32[]{:S(2)}, u32[]{:S(2)}) collective-permute-start(bf16[3,256,256]{2,1,0:T(8,128)(2,1)S(1)} %get-tuple-element.117.refs_0_), channel_id=1, source_target_pairs={{0,4},{4,0},{1,5},{5,1},{2,6},{6,2},{3,7},{7,3},{8,12},{12,8},{9,1... | collective-permute-start | bytes 1179656 | tf_op jit(solution)/shard_map/ppermute | solution.py:188
  8.9 7.6 %collective-permute-done.2.refs_3_ = bf16[3,256,256]{2,1,0:T(8,128)(2,1)S(1)} collective-permute-done((bf16[3,256,256]{2,1,0:T(8,128)(2,1)S(1)}, bf16[3,256,256]{2,1,0:T(8,128)(2,1)S(1)}, u32[]{:S(2)}, u32[]{:S(2)}) %collective-permute-start.2) | collective-permute-done | bytes 393248 | tf_op jit(solution)/shard_map/ppermute | solution.py:188
  16.4 1.7 %collective-permute-start.6 = (bf16[3,256,256]{2,1,0:T(8,128)(2,1)S(1)}, bf16[3,256,256]{2,1,0:T(8,128)(2,1)S(1)}, u32[]{:S(2)}, u32[]{:S(2)}) collective-permute-start(bf16[3,256,256]{2,1,0:T(8,128)(2,1)S(1)} %collective-permute-done.2.refs_3_), channel_id=1, source_target_pairs={{0,4},{4,0},{1,5},{5,1},{2,6},{6,2},{3,7},{7,3},{8,12},{12,8},{9,1... | collective-permute-start | bytes 1179656 | tf_op jit(solution)/shard_map/ppermute | solution.py:188
  18.2 6.9 %collective-permute-done.refs_1_ = bf16[3,256,256]{2,1,0:T(8,128)(2,1)S(1)} collective-permute-done((bf16[3,256,256]{2,1,0:T(8,128)(2,1)S(1)}, bf16[3,256,256]{2,1,0:T(8,128)(2,1)S(1)}, u32[]{:S(2)}, u32[]{:S(2)}) %collective-permute-start) | collective-permute-done | bytes 393248 | tf_op jit(solution)/shard_map/ppermute | solution.py:188
  25.1 1.4 %collective-permute-start.4 = (bf16[3,256,256]{2,1,0:T(8,128)(2,1)S(1)}, bf16[3,256,256]{2,1,0:T(8,128)(2,1)S(1)}, u32[]{:S(2)}, u32[]{:S(2)}) collective-permute-start(bf16[3,256,256]{2,1,0:T(8,128)(2,1)S(1)} %collective-permute-done.refs_1_), channel_id=1, source_target_pairs={{0,4},{4,0},{1,5},{5,1},{2,6},{6,2},{3,7},{7,3},{8,12},{12,8},{9,1... | collective-permute-start | bytes 1179656 | tf_op jit(solution)/shard_map/ppermute | solution.py:188
  26.5 13.5 %collective-permute-done.1.refs_2_ = bf16[3,256,256]{2,1,0:T(8,128)(2,1)S(1)} collective-permute-done((bf16[3,256,256]{2,1,0:T(8,128)(2,1)S(1)}, bf16[3,256,256]{2,1,0:T(8,128)(2,1)S(1)}, u32[]{:S(2)}, u32[]{:S(2)}) %collective-permute-start.1) | collective-permute-done | bytes 393248 | tf_op jit(solution)/shard_map/ppermute | solution.py:188
  40.0 1.5 %collective-permute-start.5 = (bf16[3,256,256]{2,1,0:T(8,128)(2,1)S(1)}, bf16[3,256,256]{2,1,0:T(8,128)(2,1)S(1)}, u32[]{:S(2)}, u32[]{:S(2)}) collective-permute-start(bf16[3,256,256]{2,1,0:T(8,128)(2,1)S(1)} %collective-permute-done.1.refs_2_), channel_id=1, source_target_pairs={{0,4},{4,0},{1,5},{5,1},{2,6},{6,2},{3,7},{7,3},{8,12},{12,8},{9,1... | collective-permute-start | bytes 1179656 | tf_op jit(solution)/shard_map/ppermute | solution.py:188
  41.5 0.7 fusion.2
  42.2 0.1 concatenate.7.scalars
  42.2 0.0 collective-permute-done.3.refs_4_
  42.3 0.0 collective-permute-done.6.refs_7_
  42.3 0.0 collective-permute-done.4.refs_5_
  42.3 7.9 %collective-permute-done.5.refs_6_ = bf16[3,256,256]{2,1,0:T(8,128)(2,1)S(1)} collective-permute-done((bf16[3,256,256]{2,1,0:T(8,128)(2,1)S(1)}, bf16[3,256,256]{2,1,0:T(8,128)(2,1)S(1)}, u32[]{:S(2)}, u32[]{:S(2)}) %collective-permute-start.5) | collective-permute-done | bytes 393248 | tf_op jit(solution)/shard_map/ppermute | solution.py:188
  50.1 2.3 %tiles_first.1 = (bf16[8,256,768]{2,1,0:T(8,128)(2,1)S(1)}, f32[4,6,64,256]{3,2,1,0:T(8,128)S(1)}, f32[4,6,64,256]{3,2,1,0:T(8,128)S(1)}) custom-call(s32[40]{0:T(128)S(1)} %concatenate.7.scalars, bf16[3,256,256]{2,1,0:T(8,128)(2,1)S(1)} %get-tuple-element.117.refs_0_, bf16[3,256,256]{2,1,0:T(8,128)(2,1)S(1)} %collective-permute-done.refs_1_, ...), custom_call_target="tpu_custom_call" | custom-call | flops 1207959552 | tf_op jit(solution)/shard_map/tiles_first/pallas_call | solution.py:229
  52.4 0.1 collective-permute-start.8
  52.5 1.4 %tiles_second.1 = (f32[4,3,64,256]{3,2,1,0:T(8,128)S(1)}, f32[4,3,64,256]{3,2,1,0:T(8,128)S(1)}) custom-call(s32[40]{0:T(128)S(1)} %concatenate.7.scalars, bf16[8,256,768]{2,1,0:T(8,128)(2,1)S(1)} %get-tuple-element.59.blocks), custom_call_target="tpu_custom_call" | custom-call | flops 603979776 | tf_op jit(solution)/shard_map/tiles_second/pallas_call | solution.py:229
  53.9 0.6 collective-permute-start.7
  54.5 1.4 %collective-permute-done.8.send = f32[4,6,64,256]{3,2,1,0:T(8,128)S(1)} collective-permute-done((f32[4,6,64,256]{3,2,1,0:T(8,128)S(1)}, f32[4,6,64,256]{3,2,1,0:T(8,128)S(1)}, u32[]{:S(2)}, u32[]{:S(2)}) %collective-permute-start.8) | collective-permute-done | bytes 1572896 | tf_op jit(solution)/shard_map/ppermute | solution.py:188
  55.9 0.2 sum_core.2
  56.0 1.6 %collective-permute-start.9 = (f32[2,3,64,256]{3,2,1,0:T(8,128)S(1)}, f32[2,3,64,256]{3,2,1,0:T(8,128)S(1)}, u32[]{:S(2)}, u32[]{:S(2)}) collective-permute-start(f32[2,3,64,256]{3,2,1,0:T(8,128)S(1)} %get-tuple-element.67), channel_id=1, source_target_pairs={{0,2},{2,0},{1,3},{3,1},{4,6},{6,4},{5,7},{7,5},{8,10},{10,8},{9,1... | collective-permute-start | bytes 1179656 | tf_op jit(solution)/shard_map/ppermute | solution.py:188
  57.6 0.6 collective-permute-start.11
  58.2 9.1 %collective-permute-done.9.right = f32[2,3,64,256]{3,2,1,0:T(8,128)S(1)} collective-permute-done((f32[2,3,64,256]{3,2,1,0:T(8,128)S(1)}, f32[2,3,64,256]{3,2,1,0:T(8,128)S(1)}, u32[]{:S(2)}, u32[]{:S(2)}) %collective-permute-start.9) | collective-permute-done | bytes 393248 | tf_op jit(solution)/shard_map/ppermute | solution.py:188
  67.3 0.6 collective-permute-start.10
  67.9 0.5 collective-permute-done.11.right
  68.5 1.0 collective-permute-start.12
  69.5 3.9 %collective-permute-done.10.right = f32[3,64,256]{2,1,0:T(8,128)S(1)} collective-permute-done((f32[3,64,256]{2,1,0:T(8,128)S(1)}, f32[3,64,256]{2,1,0:T(8,128)S(1)}, u32[]{:S(2)}, u32[]{:S(2)}) %collective-permute-start.10) | collective-permute-done | bytes 196640 | tf_op jit(solution)/shard_map/ppermute | solution.py:188
  73.5 0.0 collective-permute-done.7.send
  73.5 0.1 sum_core.3
  73.6 0.7 collective-permute-done.12.right
  74.4 1.0 collective-permute-start.13
  75.4 2.3 %collective-permute-start.15 = (f32[3,64,256]{2,1,0:T(8,128)S(1)}, f32[3,64,256]{2,1,0:T(8,128)S(1)}, u32[]{:S(2)}, u32[]{:S(2)}) collective-permute-start(f32[3,64,256]{2,1,0:T(8,128)S(1)} %sum_z.4.left), channel_id=1, source_target_pairs={{0,16},{8,24},{16,0},{24,8},{1,17},{9,25},{17,1},{25,9},{2,18},{10... | collective-permute-start | bytes 589832 | tf_op jit(solution)/shard_map/ppermute | solution.py:188
  77.7 0.0 copy-start.1
  77.7 5.8 %collective-permute-done.13.right = f32[2,3,64,256]{3,2,1,0:T(8,128)S(1)} collective-permute-done((f32[2,3,64,256]{3,2,1,0:T(8,128)S(1)}, f32[2,3,64,256]{3,2,1,0:T(8,128)S(1)}, u32[]{:S(2)}, u32[]{:S(2)}) %collective-permute-start.13) | collective-permute-done | bytes 393248 | tf_op jit(solution)/shard_map/ppermute | solution.py:188
  83.5 1.1 collective-permute-start.14
  84.6 1.8 %collective-permute-start.17 = (f32[3,64,256]{2,1,0:T(8,128)S(1)}, f32[3,64,256]{2,1,0:T(8,128)S(1)}, u32[]{:S(2)}, u32[]{:S(2)}) collective-permute-start(f32[3,64,256]{2,1,0:T(8,128)S(1)} %sum_x.4.refs_0_), channel_id=1, source_target_pairs={{0,16},{8,24},{16,0},{24,8},{1,17},{9,25},{17,1},{25,9},{2,18},{10... | collective-permute-start | bytes 589832 | tf_op jit(solution)/shard_map/ppermute | solution.py:188
  86.4 0.0 collective-permute-done.15.right
  86.5 6.7 %collective-permute-done.14.right = f32[3,64,256]{2,1,0:T(8,128)S(1)} collective-permute-done((f32[3,64,256]{2,1,0:T(8,128)S(1)}, f32[3,64,256]{2,1,0:T(8,128)S(1)}, u32[]{:S(2)}, u32[]{:S(2)}) %collective-permute-start.14) | collective-permute-done | bytes 196640 | tf_op jit(solution)/shard_map/ppermute | solution.py:188
  93.1 0.1 collective-permute-start.16
  93.2 0.5 collective-permute-done.17.refs_1_
  93.8 0.3 finish.2.refs_0_
  94.1 2.6 %collective-permute-start.23 = (s16[400,256]{1,0:T(8,128)(2,1)S(1)}, s16[400,256]{1,0:T(8,128)(2,1)S(1)}, u32[]{:S(2)}, u32[]{:S(2)}) collective-permute-start(s16[400,256]{1,0:T(8,128)(2,1)S(1)} %finish.2.refs_0_), channel_id=1, source_target_pairs={{0,12},{4,8},{8,4},{12,0},{16,28},{20,24},{24,20},{28,16},{1,13},{... | collective-permute-start | bytes 614408 | tf_op jit(solution)/shard_map/ppermute | solution.py:343
  96.7 0.0 copy-done.1
  96.7 0.6 collective-permute-start.22
  97.3 0.5 collective-permute-start.21
  97.8 6.2 %collective-permute-done.16.refs_1_ = f32[3,64,256]{2,1,0:T(8,128)S(1)} collective-permute-done((f32[3,64,256]{2,1,0:T(8,128)S(1)}, f32[3,64,256]{2,1,0:T(8,128)S(1)}, u32[]{:S(2)}, u32[]{:S(2)}) %collective-permute-start.16) | collective-permute-done | bytes 196640 | tf_op jit(solution)/shard_map/ppermute | solution.py:188
  104.0 0.2 finish.3.refs_0_
  104.2 0.1 collective-permute-start.20
  104.3 1.6 %collective-permute-start.19 = (s16[208,256]{1,0:T(8,128)(2,1)S(1)}, s16[208,256]{1,0:T(8,128)(2,1)S(1)}, u32[]{:S(2)}, u32[]{:S(2)}) collective-permute-start(s16[208,256]{1,0:T(8,128)(2,1)S(1)} %finish.3.refs_0_), channel_id=1, source_target_pairs={{0,4},{4,0},{1,5},{5,1},{2,6},{6,2},{3,7},{7,3},{8,12},{12,8},{9,1... | collective-permute-start | bytes 319496 | tf_op jit(solution)/shard_map/ppermute | solution.py:188
  105.9 1.3 %collective-permute-done.23.refs_3_ = s16[400,256]{1,0:T(8,128)(2,1)S(1)} collective-permute-done((s16[400,256]{1,0:T(8,128)(2,1)S(1)}, s16[400,256]{1,0:T(8,128)(2,1)S(1)}, u32[]{:S(2)}, u32[]{:S(2)}) %collective-permute-start.23) | collective-permute-done | bytes 204832 | tf_op jit(solution)/shard_map/ppermute | solution.py:343
  107.2 0.6 collective-permute-start.18
  107.8 0.1 concatenate.6.scalars
  107.9 0.0 collective-permute-done.22.refs_2_
  107.9 3.8 %collective-permute-done.21.refs_1_ = s16[400,256]{1,0:T(8,128)(2,1)S(1)} collective-permute-done((s16[400,256]{1,0:T(8,128)(2,1)S(1)}, s16[400,256]{1,0:T(8,128)(2,1)S(1)}, u32[]{:S(2)}, u32[]{:S(2)}) %collective-permute-start.21) | collective-permute-done | bytes 204832 | tf_op jit(solution)/shard_map/ppermute | solution.py:188
  111.6 0.8 place_tiles.2.refs_4_
  112.4 0.9 collective-permute-done.20.refs_3_
  113.3 0.0 collective-permute-done.19.refs_2_
  113.3 1.2 %collective-permute-done.18.refs_1_ = s16[208,256]{1,0:T(8,128)(2,1)S(1)} collective-permute-done((s16[208,256]{1,0:T(8,128)(2,1)S(1)}, s16[208,256]{1,0:T(8,128)(2,1)S(1)}, u32[]{:S(2)}, u32[]{:S(2)}) %collective-permute-start.18) | collective-permute-done | bytes 106528 | tf_op jit(solution)/shard_map/ppermute | solution.py:188
  114.5 1.9 %place_tiles.3 = f32[10,64,256]{2,1,0:T(8,128)} custom-call(s32[60]{0:T(128)S(1)} %concatenate.6.scalars, s16[208,256]{1,0:T(8,128)(2,1)S(1)} %finish.3.refs_0_, s16[208,256]{1,0:T(8,128)(2,1)S(1)} %collective-permute-done.18.refs_1_, s16[208,256]{1,0:T(8,128)(2,1)S(1)} %collective-permute-done.19.refs_2_, ...), custom_call_target="tpu_custom_call" | custom-call | flops 163840 | tf_op jit(solution)/shard_map/place_tiles/pallas_call | solution.py:385
  (10 shorter events, 0.3 us)
Async XLA Ops:
  0.0 6.4 %copy-start = (bf16[3,256,1024]{2,1,0:T(8,128)(2,1)S(1)}, bf16[3,256,1024]{2,1,0:T(8,128)(2,1)}, u32[]{:S(2)}) copy-start(bf16[3,256,1024]{2,1,0:T(8,128)(2,1)} %param.3) | copy-start | bytes 4718596
  1.3 15.1 %collective-permute-start.2 = (bf16[3,256,256]{2,1,0:T(8,128)(2,1)S(1)}, bf16[3,256,256]{2,1,0:T(8,128)(2,1)S(1)}, u32[]{:S(2)}, u32[]{:S(2)}) collective-permute-start(bf16[3,256,256]{2,1,0:T(8,128)(2,1)S(1)} %get-tuple-element.118), channel_id=1, source_target_pairs={{0,24},{8,16},{16,8},{24,0},{1,25},{9,17},{17,9},{25,1},{2,26},{10... | collective-permute-start | bytes 1179656 | tf_op jit(solution)/shard_map/ppermute | solution.py:188
  6.4 18.7 %collective-permute-start = (bf16[3,256,256]{2,1,0:T(8,128)(2,1)S(1)}, bf16[3,256,256]{2,1,0:T(8,128)(2,1)S(1)}, u32[]{:S(2)}, u32[]{:S(2)}) collective-permute-start(bf16[3,256,256]{2,1,0:T(8,128)(2,1)S(1)} %get-tuple-element.119), channel_id=1, source_target_pairs={{0,8},{8,0},{16,24},{24,16},{1,9},{9,1},{17,25},{25,17},{2,10},{10... | collective-permute-start | bytes 1179656 | tf_op jit(solution)/shard_map/ppermute | solution.py:188
  6.5 33.4 %collective-permute-start.1 = (bf16[3,256,256]{2,1,0:T(8,128)(2,1)S(1)}, bf16[3,256,256]{2,1,0:T(8,128)(2,1)S(1)}, u32[]{:S(2)}, u32[]{:S(2)}) collective-permute-start(bf16[3,256,256]{2,1,0:T(8,128)(2,1)S(1)} %get-tuple-element.116), channel_id=1, source_target_pairs={{0,16},{8,24},{16,0},{24,8},{1,17},{9,25},{17,1},{25,9},{2,18},{10... | collective-permute-start | bytes 1179656 | tf_op jit(solution)/shard_map/ppermute | solution.py:188
  7.2 35.0 %collective-permute-start.3 = (bf16[3,256,256]{2,1,0:T(8,128)(2,1)S(1)}, bf16[3,256,256]{2,1,0:T(8,128)(2,1)S(1)}, u32[]{:S(2)}, u32[]{:S(2)}) collective-permute-start(bf16[3,256,256]{2,1,0:T(8,128)(2,1)S(1)} %get-tuple-element.117.refs_0_), channel_id=1, source_target_pairs={{0,4},{4,0},{1,5},{5,1},{2,6},{6,2},{3,7},{7,3},{8,12},{12,8},{9,1... | collective-permute-start | bytes 1179656 | tf_op jit(solution)/shard_map/ppermute | solution.py:188
  16.4 25.8 %collective-permute-start.6 = (bf16[3,256,256]{2,1,0:T(8,128)(2,1)S(1)}, bf16[3,256,256]{2,1,0:T(8,128)(2,1)S(1)}, u32[]{:S(2)}, u32[]{:S(2)}) collective-permute-start(bf16[3,256,256]{2,1,0:T(8,128)(2,1)S(1)} %collective-permute-done.2.refs_3_), channel_id=1, source_target_pairs={{0,4},{4,0},{1,5},{5,1},{2,6},{6,2},{3,7},{7,3},{8,12},{12,8},{9,1... | collective-permute-start | bytes 1179656 | tf_op jit(solution)/shard_map/ppermute | solution.py:188
  25.1 17.2 %collective-permute-start.4 = (bf16[3,256,256]{2,1,0:T(8,128)(2,1)S(1)}, bf16[3,256,256]{2,1,0:T(8,128)(2,1)S(1)}, u32[]{:S(2)}, u32[]{:S(2)}) collective-permute-start(bf16[3,256,256]{2,1,0:T(8,128)(2,1)S(1)} %collective-permute-done.refs_1_), channel_id=1, source_target_pairs={{0,4},{4,0},{1,5},{5,1},{2,6},{6,2},{3,7},{7,3},{8,12},{12,8},{9,1... | collective-permute-start | bytes 1179656 | tf_op jit(solution)/shard_map/ppermute | solution.py:188
  40.0 10.2 %collective-permute-start.5 = (bf16[3,256,256]{2,1,0:T(8,128)(2,1)S(1)}, bf16[3,256,256]{2,1,0:T(8,128)(2,1)S(1)}, u32[]{:S(2)}, u32[]{:S(2)}) collective-permute-start(bf16[3,256,256]{2,1,0:T(8,128)(2,1)S(1)} %collective-permute-done.1.refs_2_), channel_id=1, source_target_pairs={{0,4},{4,0},{1,5},{5,1},{2,6},{6,2},{3,7},{7,3},{8,12},{12,8},{9,1... | collective-permute-start | bytes 1179656 | tf_op jit(solution)/shard_map/ppermute | solution.py:188
  52.4 3.5 %collective-permute-start.8 = (f32[4,6,64,256]{3,2,1,0:T(8,128)S(1)}, f32[4,6,64,256]{3,2,1,0:T(8,128)S(1)}, u32[]{:S(2)}, u32[]{:S(2)}) collective-permute-start(f32[4,6,64,256]{3,2,1,0:T(8,128)S(1)} %get-tuple-element.63), channel_id=1, source_target_pairs={{0,1},{1,0},{2,3},{3,2},{4,5},{5,4},{6,7},{7,6},{8,9},{9,8},{10,11... | collective-permute-start | bytes 4718600 | tf_op jit(solution)/shard_map/ppermute | solution.py:188
  53.9 19.6 %collective-permute-start.7 = (f32[4,3,64,256]{3,2,1,0:T(8,128)S(1)}, f32[4,3,64,256]{3,2,1,0:T(8,128)S(1)}, u32[]{:S(2)}, u32[]{:S(2)}) collective-permute-start(f32[4,3,64,256]{3,2,1,0:T(8,128)S(1)} %get-tuple-element.61), channel_id=1, source_target_pairs={{0,1},{1,0},{2,3},{3,2},{4,5},{5,4},{6,7},{7,6},{8,9},{9,8},{10,11... | collective-permute-start | bytes 2359304 | tf_op jit(solution)/shard_map/ppermute | solution.py:188
  56.0 11.2 %collective-permute-start.9 = (f32[2,3,64,256]{3,2,1,0:T(8,128)S(1)}, f32[2,3,64,256]{3,2,1,0:T(8,128)S(1)}, u32[]{:S(2)}, u32[]{:S(2)}) collective-permute-start(f32[2,3,64,256]{3,2,1,0:T(8,128)S(1)} %get-tuple-element.67), channel_id=1, source_target_pairs={{0,2},{2,0},{1,3},{3,1},{4,6},{6,4},{5,7},{7,5},{8,10},{10,8},{9,1... | collective-permute-start | bytes 1179656 | tf_op jit(solution)/shard_map/ppermute | solution.py:188
  57.6 10.9 %collective-permute-start.11 = (f32[2,3,64,256]{3,2,1,0:T(8,128)S(1)}, f32[2,3,64,256]{3,2,1,0:T(8,128)S(1)}, u32[]{:S(2)}, u32[]{:S(2)}) collective-permute-start(f32[2,3,64,256]{3,2,1,0:T(8,128)S(1)} %get-tuple-element.73), channel_id=1, source_target_pairs={{0,8},{8,0},{16,24},{24,16},{1,9},{9,1},{17,25},{25,17},{2,10},{10... | collective-permute-start | bytes 1179656 | tf_op jit(solution)/shard_map/ppermute | solution.py:188
  67.3 6.2 %collective-permute-start.10 = (f32[3,64,256]{2,1,0:T(8,128)S(1)}, f32[3,64,256]{2,1,0:T(8,128)S(1)}, u32[]{:S(2)}, u32[]{:S(2)}) collective-permute-start(f32[3,64,256]{2,1,0:T(8,128)S(1)} %get-tuple-element.72), channel_id=1, source_target_pairs={{0,8},{8,0},{16,24},{24,16},{1,9},{9,1},{17,25},{25,17},{2,10},{10... | collective-permute-start | bytes 589832 | tf_op jit(solution)/shard_map/ppermute | solution.py:188
  68.5 5.9 %collective-permute-start.12 = (f32[3,64,256]{2,1,0:T(8,128)S(1)}, f32[3,64,256]{2,1,0:T(8,128)S(1)}, u32[]{:S(2)}, u32[]{:S(2)}) collective-permute-start(f32[3,64,256]{2,1,0:T(8,128)S(1)} %get-tuple-element.83), channel_id=1, source_target_pairs={{0,2},{2,0},{1,3},{3,1},{4,6},{6,4},{5,7},{7,5},{8,10},{10,8},{9,1... | collective-permute-start | bytes 589832 | tf_op jit(solution)/shard_map/ppermute | solution.py:188
  74.4 9.1 %collective-permute-start.13 = (f32[2,3,64,256]{3,2,1,0:T(8,128)S(1)}, f32[2,3,64,256]{3,2,1,0:T(8,128)S(1)}, u32[]{:S(2)}, u32[]{:S(2)}) collective-permute-start(f32[2,3,64,256]{3,2,1,0:T(8,128)S(1)} %get-tuple-element.84), channel_id=1, source_target_pairs={{0,2},{2,0},{1,3},{3,1},{4,6},{6,4},{5,7},{7,5},{8,10},{10,8},{9,1... | collective-permute-start | bytes 1179656 | tf_op jit(solution)/shard_map/ppermute | solution.py:188
  75.4 11.0 %collective-permute-start.15 = (f32[3,64,256]{2,1,0:T(8,128)S(1)}, f32[3,64,256]{2,1,0:T(8,128)S(1)}, u32[]{:S(2)}, u32[]{:S(2)}) collective-permute-start(f32[3,64,256]{2,1,0:T(8,128)S(1)} %sum_z.4.left), channel_id=1, source_target_pairs={{0,16},{8,24},{16,0},{24,8},{1,17},{9,25},{17,1},{25,9},{2,18},{10... | collective-permute-start | bytes 589832 | tf_op jit(solution)/shard_map/ppermute | solution.py:188
  77.7 19.0 %copy-start.1 = (s32[1,10,2]{1,2,0:T(2,128)S(1)}, s32[1,10,2]{1,2,0:T(2,128)}, u32[]{:S(2)}) copy-start(s32[1,10,2]{1,2,0:T(2,128)} %param.4) | copy-start | bytes 244
  83.5 9.6 %collective-permute-start.14 = (f32[3,64,256]{2,1,0:T(8,128)S(1)}, f32[3,64,256]{2,1,0:T(8,128)S(1)}, u32[]{:S(2)}, u32[]{:S(2)}) collective-permute-start(f32[3,64,256]{2,1,0:T(8,128)S(1)} %get-tuple-element.90), channel_id=1, source_target_pairs={{0,8},{8,0},{16,24},{24,16},{1,9},{9,1},{17,25},{25,17},{2,10},{10... | collective-permute-start | bytes 589832 | tf_op jit(solution)/shard_map/ppermute | solution.py:188
  84.6 9.2 %collective-permute-start.17 = (f32[3,64,256]{2,1,0:T(8,128)S(1)}, f32[3,64,256]{2,1,0:T(8,128)S(1)}, u32[]{:S(2)}, u32[]{:S(2)}) collective-permute-start(f32[3,64,256]{2,1,0:T(8,128)S(1)} %sum_x.4.refs_0_), channel_id=1, source_target_pairs={{0,16},{8,24},{16,0},{24,8},{1,17},{9,25},{17,1},{25,9},{2,18},{10... | collective-permute-start | bytes 589832 | tf_op jit(solution)/shard_map/ppermute | solution.py:188
  93.1 10.8 %collective-permute-start.16 = (f32[3,64,256]{2,1,0:T(8,128)S(1)}, f32[3,64,256]{2,1,0:T(8,128)S(1)}, u32[]{:S(2)}, u32[]{:S(2)}) collective-permute-start(f32[3,64,256]{2,1,0:T(8,128)S(1)} %sum_z.5.refs_0_), channel_id=1, source_target_pairs={{0,16},{8,24},{16,0},{24,8},{1,17},{9,25},{17,1},{25,9},{2,18},{10... | collective-permute-start | bytes 589832 | tf_op jit(solution)/shard_map/ppermute | solution.py:188
  94.1 13.1 %collective-permute-start.23 = (s16[400,256]{1,0:T(8,128)(2,1)S(1)}, s16[400,256]{1,0:T(8,128)(2,1)S(1)}, u32[]{:S(2)}, u32[]{:S(2)}) collective-permute-start(s16[400,256]{1,0:T(8,128)(2,1)S(1)} %finish.2.refs_0_), channel_id=1, source_target_pairs={{0,12},{4,8},{8,4},{12,0},{16,28},{20,24},{24,20},{28,16},{1,13},{... | collective-permute-start | bytes 614408 | tf_op jit(solution)/shard_map/ppermute | solution.py:343
  96.7 11.1 %collective-permute-start.22 = (s16[400,256]{1,0:T(8,128)(2,1)S(1)}, s16[400,256]{1,0:T(8,128)(2,1)S(1)}, u32[]{:S(2)}, u32[]{:S(2)}) collective-permute-start(s16[400,256]{1,0:T(8,128)(2,1)S(1)} %finish.2.refs_0_), channel_id=1, source_target_pairs={{0,4},{4,0},{1,5},{5,1},{2,6},{6,2},{3,7},{7,3},{8,12},{12,8},{9,1... | collective-permute-start | bytes 614408 | tf_op jit(solution)/shard_map/ppermute | solution.py:188
  97.3 14.3 %collective-permute-start.21 = (s16[400,256]{1,0:T(8,128)(2,1)S(1)}, s16[400,256]{1,0:T(8,128)(2,1)S(1)}, u32[]{:S(2)}, u32[]{:S(2)}) collective-permute-start(s16[400,256]{1,0:T(8,128)(2,1)S(1)} %finish.2.refs_0_), channel_id=1, source_target_pairs={{0,8},{8,0},{16,24},{24,16},{1,9},{9,1},{17,25},{25,17},{2,10},{10... | collective-permute-start | bytes 614408 | tf_op jit(solution)/shard_map/ppermute | solution.py:188
  104.2 9.1 %collective-permute-start.20 = (s16[208,256]{1,0:T(8,128)(2,1)S(1)}, s16[208,256]{1,0:T(8,128)(2,1)S(1)}, u32[]{:S(2)}, u32[]{:S(2)}) collective-permute-start(s16[208,256]{1,0:T(8,128)(2,1)S(1)} %finish.3.refs_0_), channel_id=1, source_target_pairs={{0,12},{4,8},{8,4},{12,0},{16,28},{20,24},{24,20},{28,16},{1,13},{... | collective-permute-start | bytes 319496 | tf_op jit(solution)/shard_map/ppermute | solution.py:343
  104.3 9.0 %collective-permute-start.19 = (s16[208,256]{1,0:T(8,128)(2,1)S(1)}, s16[208,256]{1,0:T(8,128)(2,1)S(1)}, u32[]{:S(2)}, u32[]{:S(2)}) collective-permute-start(s16[208,256]{1,0:T(8,128)(2,1)S(1)} %finish.3.refs_0_), channel_id=1, source_target_pairs={{0,4},{4,0},{1,5},{5,1},{2,6},{6,2},{3,7},{7,3},{8,12},{12,8},{9,1... | collective-permute-start | bytes 319496 | tf_op jit(solution)/shard_map/ppermute | solution.py:188
  107.2 7.3 %collective-permute-start.18 = (s16[208,256]{1,0:T(8,128)(2,1)S(1)}, s16[208,256]{1,0:T(8,128)(2,1)S(1)}, u32[]{:S(2)}, u32[]{:S(2)}) collective-permute-start(s16[208,256]{1,0:T(8,128)(2,1)S(1)} %finish.3.refs_0_), channel_id=1, source_target_pairs={{0,8},{8,0},{16,24},{24,16},{1,9},{9,1},{17,25},{25,17},{2,10},{10... | collective-permute-start | bytes 319496 | tf_op jit(solution)/shard_map/ppermute | solution.py:188

commit v14 on v13

--- a/solution.py
+++ b/solution.py
@@ -85,6 +85,10 @@
 
 def second_kernel(first_pair, sizes, scalars, blocks, *outs):
     multiply_groups(scalars, first_pair, sizes, blocks, CALLS[1], outs)
+
+
+def copy_kernel(value, out):
+    out[...] = value[...]
 
 
 def core_sum_kernel(cuts, keep, send, *outs):
@@ -213,12 +217,37 @@
     cut = {step: part(step, snapshots) for step in range(1, z_count, 2)}
     again = lax.optimization_barrier((snapshots, *cut.values()))[0]
     cut.update({step: part(step, again) for step in range(0, z_count, 2)})
-    pieces = {(0, 0): cut[0]}
-    for step in range(1, z_count):
-        pieces[step, 0] = swap(cut[step], "z", step)
+    head = (2 * components) // 3
+    sent = [(1, 0, cut[1][:head]), (z_count - 1, 0, cut[z_count - 1]), (1, head, cut[1][head:])]
+    sent += [(step, 0, cut[step]) for step in range(2, z_count - 1)]
+    near = 3
+    pieces, over_y, earlier = {(0, 0): cut[0]}, {}, []
+
+    def arrived(value):
+        value, *_ = lax.optimization_barrier((value, *earlier))
+        earlier[:] = [
+            pl.pallas_call(
+                copy_kernel,
+                out_shape=jax.ShapeDtypeStruct(value.shape, value.dtype),
+                in_specs=[pl.BlockSpec(memory_space=pltpu.VMEM)],
+                out_specs=pl.BlockSpec(memory_space=pltpu.VMEM),
+                compiler_params=pltpu.CompilerParams(vmem_limit_bytes=VMEM_LIMIT),
+                cost_estimate=pl.CostEstimate(flops=0, bytes_accessed=0, transcendentals=0),
+                name="arrived",
+            )(value)
+        ]
+        return earlier[0]
+
+    over_y[0, 0] = swap(cut[0], "y", 1)
+    early = {1: [(0, 0)], near: [(1, 0), (1, head)]}
+    for index, (step, at, value) in enumerate(sent):
+        for key in early.get(index, []):
+            over_y[key] = arrived(over_y[key])
+        pieces[step, at] = arrived(swap(value, "z", step))
+        over_y[step, at] = swap(pieces[step, at], "y", 1)
     layout = [(step, 0, component) for step, component in pieces]
     layout += [(step, 1, component) for step, component in pieces]
-    chunks = list(pieces.values()) + [swap(piece, "y", 1) for piece in pieces.values()]
+    chunks = list(pieces.values()) + [over_y[key] for key in pieces]
 
     def sums_shape(groups):
         count = sum(sizes[index] for index in groups)

time: 117 us -> 119 us (1.017)
  waiting for transfers between devices: 77.8 us -> 74.1 us
  starting transfers between devices: 28.7 us -> 32 us
  local copies, waits for them, and re-layouts: 2.25 us -> 4.93 us
    ppermute x22 -> x24, waiting for transfers between devices: 75.7 us -> 72.4 us  [swap(): return lax.ppermute(value, axis, [(i, i ^ bits) for i in range(size)])]
    ppermute x22 -> x24, starting transfers between devices: 26 us -> 29 us  [swap(): return lax.ppermute(value, axis, [(i, i ^ bits) for i in range(size)])]
    slice x0 -> x2, local copies, waits for them, and re-layouts: none -> 1.88 us  [the longest x1 0.97 us: per_device(): cut[1][:head]]
  transfers between devices with their start and end apart: 24 -> 26, of which waited for: 17 -> 19; matrix products, arithmetic and copies ran while one was open for 1% -> 3% of each run, Pallas kernels for 3% -> 3%
where the time goes in v14:
time: 119 us
  waiting for transfers between devices  74.1 us (62%)
  starting transfers between devices  32 us (27%)
  Pallas kernels  7.49 us (6%)
  local copies, waits for them, and re-layouts  4.93 us (4%)
    ppermute x24, waiting for transfers between devices, swap(): return lax.ppermute(value, axis, [(i, i ^ bits) for i in range(size)])  72.4 us
    ppermute x24, starting transfers between devices, swap(): return lax.ppermute(value, axis, [(i, i ^ bits) for i in range(size)])  29 us
    pallas_call x2, Pallas kernels, call(): pl.pallas_call(kernel, out_shape=out_shape, in_specs=[pl.BlockSpec(memory...  3.67 us
    ppermute x2, starting transfers between devices, to_owners(): over_both = lax.ppermute(value, ('z', 'y'), both)  3.02 us
    pallas_call x2, Pallas kernels, per_device(): pl.pallas_call(functools.partial(place_kernel, scale_factor / (CODE_TOP *...  2.64 us
  transfers between devices with their start and end apart: 26, of which 19 were waited for; matrix products, arithmetic and copies ran while one was open for 3% of the time, Pallas kernels for 3%

profile of v14, /device:TPU:0, one launch (start us, length us, event | category | flops | bytes accessed | tf_op | source)
XLA Modules:
  0.0 118.8 jit_solution(8822741374376849083)
XLA Ops:
  0.0 1.0 constant_dynamic-slice_fusion.4
  1.0 5.1 %collective-permute-start.1 = (bf16[3,256,256]{2,1,0:T(8,128)(2,1)S(1)}, bf16[3,256,256]{2,1,0:T(8,128)(2,1)S(1)}, u32[]{:S(2)}, u32[]{:S(2)}) collective-permute-start(bf16[3,256,256]{2,1,0:T(8,128)(2,1)S(1)} %constant_dynamic-slice_fusion.4), channel_id=1, source_target_pairs={{0,24},{8,16},{16,8},{24,0},{1,25},{9,17},{17,9},{25,1},{2,26},{10... | collective-permute-start | bytes 1179656 | tf_op jit(solution)/shard_map/ppermute | solution.py:192
  6.1 1.2 constant_dynamic-slice_fusion.2
  7.3 1.6 %collective-permute-start.2 = (bf16[3,256,256]{2,1,0:T(8,128)(2,1)S(1)}, bf16[3,256,256]{2,1,0:T(8,128)(2,1)S(1)}, u32[]{:S(2)}, u32[]{:S(2)}) collective-permute-start(bf16[3,256,256]{2,1,0:T(8,128)(2,1)S(1)} %get-tuple-element.129.refs_0_), channel_id=1, source_target_pairs={{0,4},{4,0},{1,5},{5,1},{2,6},{6,2},{3,7},{7,3},{8,12},{12,8},{9,1... | collective-permute-start | bytes 1179656 | tf_op jit(solution)/shard_map/ppermute | solution.py:192
  8.9 1.0 constant_dynamic-slice_fusion.1
  9.9 0.1 collective-permute-start
  9.9 0.8 collective-permute-start.4
  10.7 0.9 constant_dynamic-slice_fusion
  11.6 1.3 %collective-permute-start.3 = (bf16[1,256,256]{2,1,0:T(8,128)(2,1)S(1)}, bf16[1,256,256]{2,1,0:T(8,128)(2,1)S(1)}, u32[]{:S(2)}, u32[]{:S(2)}) collective-permute-start(bf16[1,256,256]{2,1,0:T(8,128)(2,1)S(1)} %constant_dynamic-slice_fusion), channel_id=1, source_target_pairs={{0,8},{8,0},{16,24},{24,16},{1,9},{9,1},{17,25},{25,17},{2,10},{10... | collective-permute-start | bytes 393224 | tf_op jit(solution)/shard_map/ppermute | solution.py:192
  12.9 8.4 %collective-permute-done.value = bf16[2,256,256]{2,1,0:T(8,128)(2,1)S(1)} collective-permute-done((bf16[2,256,256]{2,1,0:T(8,128)(2,1)S(1)}, bf16[2,256,256]{2,1,0:T(8,128)(2,1)S(1)}, u32[]{:S(2)}, u32[]{:S(2)}) %collective-permute-start) | collective-permute-done | bytes 262176 | tf_op jit(solution)/shard_map/ppermute | solution.py:192
  21.3 1.6 %collective-permute-start.6 = (bf16[2,256,256]{2,1,0:T(8,128)(2,1)S(1)}, bf16[2,256,256]{2,1,0:T(8,128)(2,1)S(1)}, u32[]{:S(2)}, u32[]{:S(2)}) collective-permute-start(bf16[2,256,256]{2,1,0:T(8,128)(2,1)S(1)} %arrived.7.refs_1_), channel_id=1, source_target_pairs={{0,4},{4,0},{1,5},{5,1},{2,6},{6,2},{3,7},{7,3},{8,12},{12,8},{9,1... | collective-permute-start | bytes 786440 | tf_op jit(solution)/shard_map/ppermute | solution.py:192
  22.9 0.0 collective-permute-done.2.value
  23.0 0.0 collective-permute-done.1.value
  23.0 8.5 %collective-permute-done.3.value = bf16[1,256,256]{2,1,0:T(8,128)(2,1)S(1)} collective-permute-done((bf16[1,256,256]{2,1,0:T(8,128)(2,1)S(1)}, bf16[1,256,256]{2,1,0:T(8,128)(2,1)S(1)}, u32[]{:S(2)}, u32[]{:S(2)}) %collective-permute-start.3) | collective-permute-done | bytes 131104 | tf_op jit(solution)/shard_map/ppermute | solution.py:192
  31.5 1.6 %collective-permute-start.5 = (bf16[1,256,256]{2,1,0:T(8,128)(2,1)S(1)}, bf16[1,256,256]{2,1,0:T(8,128)(2,1)S(1)}, u32[]{:S(2)}, u32[]{:S(2)}) collective-permute-start(bf16[1,256,256]{2,1,0:T(8,128)(2,1)S(1)} %arrived.10.refs_3_), channel_id=1, source_target_pairs={{0,4},{4,0},{1,5},{5,1},{2,6},{6,2},{3,7},{7,3},{8,12},{12,8},{9,1... | collective-permute-start | bytes 393224 | tf_op jit(solution)/shard_map/ppermute | solution.py:192
  33.1 0.5 collective-permute-start.7
  33.6 0.0 collective-permute-done.6.value
  33.6 4.4 %collective-permute-done.5.value = bf16[1,256,256]{2,1,0:T(8,128)(2,1)S(1)} collective-permute-done((bf16[1,256,256]{2,1,0:T(8,128)(2,1)S(1)}, bf16[1,256,256]{2,1,0:T(8,128)(2,1)S(1)}, u32[]{:S(2)}, u32[]{:S(2)}) %collective-permute-start.5) | collective-permute-done | bytes 131104 | tf_op jit(solution)/shard_map/ppermute | solution.py:192
  38.0 1.7 %collective-permute-done.4.value = bf16[3,256,256]{2,1,0:T(8,128)(2,1)S(1)} collective-permute-done((bf16[3,256,256]{2,1,0:T(8,128)(2,1)S(1)}, bf16[3,256,256]{2,1,0:T(8,128)(2,1)S(1)}, u32[]{:S(2)}, u32[]{:S(2)}) %collective-permute-start.4) | collective-permute-done | bytes 393248 | tf_op jit(solution)/shard_map/ppermute | solution.py:192
  39.7 1.6 %collective-permute-start.8 = (bf16[3,256,256]{2,1,0:T(8,128)(2,1)S(1)}, bf16[3,256,256]{2,1,0:T(8,128)(2,1)S(1)}, u32[]{:S(2)}, u32[]{:S(2)}) collective-permute-start(bf16[3,256,256]{2,1,0:T(8,128)(2,1)S(1)} %arrived.13.refs_4_), channel_id=1, source_target_pairs={{0,4},{4,0},{1,5},{5,1},{2,6},{6,2},{3,7},{7,3},{8,12},{12,8},{9,1... | collective-permute-start | bytes 1179656 | tf_op jit(solution)/shard_map/ppermute | solution.py:192
  41.3 0.7 fusion.2
  42.0 0.1 concatenate.7.scalars
  42.1 4.4 %collective-permute-done.7.refs_7_ = bf16[3,256,256]{2,1,0:T(8,128)(2,1)S(1)} collective-permute-done((bf16[3,256,256]{2,1,0:T(8,128)(2,1)S(1)}, bf16[3,256,256]{2,1,0:T(8,128)(2,1)S(1)}, u32[]{:S(2)}, u32[]{:S(2)}) %collective-permute-start.7) | collective-permute-done | bytes 393248 | tf_op jit(solution)/shard_map/ppermute | solution.py:192
  46.4 6.4 %collective-permute-done.8.refs_9_ = bf16[3,256,256]{2,1,0:T(8,128)(2,1)S(1)} collective-permute-done((bf16[3,256,256]{2,1,0:T(8,128)(2,1)S(1)}, bf16[3,256,256]{2,1,0:T(8,128)(2,1)S(1)}, u32[]{:S(2)}, u32[]{:S(2)}) %collective-permute-start.8) | collective-permute-done | bytes 393248 | tf_op jit(solution)/shard_map/ppermute | solution.py:192
  52.8 2.3 %tiles_first.1 = (bf16[8,256,768]{2,1,0:T(8,128)(2,1)S(1)}, f32[4,6,64,256]{3,2,1,0:T(8,128)S(1)}, f32[4,6,64,256]{3,2,1,0:T(8,128)S(1)}) custom-call(s32[40]{0:T(128)S(1)} %concatenate.7.scalars, bf16[3,256,256]{2,1,0:T(8,128)(2,1)S(1)} %get-tuple-element.129.refs_0_, bf16[2,256,256]{2,1,0:T(8,128)(2,1)S(1)} %arrived.7.refs_1_, ...), custom_call_target="tpu_custom_call" | custom-call | flops 1207959552 | tf_op jit(solution)/shard_map/tiles_first/pallas_call | solution.py:258
  55.1 0.1 collective-permute-start.10
  55.2 1.4 %tiles_second.1 = (f32[4,3,64,256]{3,2,1,0:T(8,128)S(1)}, f32[4,3,64,256]{3,2,1,0:T(8,128)S(1)}) custom-call(s32[40]{0:T(128)S(1)} %concatenate.7.scalars, bf16[8,256,768]{2,1,0:T(8,128)(2,1)S(1)} %get-tuple-element.71.blocks), custom_call_target="tpu_custom_call" | custom-call | flops 603979776 | tf_op jit(solution)/shard_map/tiles_second/pallas_call | solution.py:258
  56.6 0.6 collective-permute-start.9
  57.2 1.4 %collective-permute-done.10.send = f32[4,6,64,256]{3,2,1,0:T(8,128)S(1)} collective-permute-done((f32[4,6,64,256]{3,2,1,0:T(8,128)S(1)}, f32[4,6,64,256]{3,2,1,0:T(8,128)S(1)}, u32[]{:S(2)}, u32[]{:S(2)}) %collective-permute-start.10) | collective-permute-done | bytes 1572896 | tf_op jit(solution)/shard_map/ppermute | solution.py:192
  58.6 0.2 sum_core.2
  58.8 1.6 %collective-permute-start.11 = (f32[2,3,64,256]{3,2,1,0:T(8,128)S(1)}, f32[2,3,64,256]{3,2,1,0:T(8,128)S(1)}, u32[]{:S(2)}, u32[]{:S(2)}) collective-permute-start(f32[2,3,64,256]{3,2,1,0:T(8,128)S(1)} %get-tuple-element.79), channel_id=1, source_target_pairs={{0,2},{2,0},{1,3},{3,1},{4,6},{6,4},{5,7},{7,5},{8,10},{10,8},{9,1... | collective-permute-start | bytes 1179656 | tf_op jit(solution)/shard_map/ppermute | solution.py:192
  60.3 2.5 %collective-permute-start.13 = (f32[2,3,64,256]{3,2,1,0:T(8,128)S(1)}, f32[2,3,64,256]{3,2,1,0:T(8,128)S(1)}, u32[]{:S(2)}, u32[]{:S(2)}) collective-permute-start(f32[2,3,64,256]{3,2,1,0:T(8,128)S(1)} %get-tuple-element.85), channel_id=1, source_target_pairs={{0,8},{8,0},{16,24},{24,16},{1,9},{9,1},{17,25},{25,17},{2,10},{10... | collective-permute-start | bytes 1179656 | tf_op jit(solution)/shard_map/ppermute | solution.py:192
  62.8 7.2 %collective-permute-done.11.right = f32[2,3,64,256]{3,2,1,0:T(8,128)S(1)} collective-permute-done((f32[2,3,64,256]{3,2,1,0:T(8,128)S(1)}, f32[2,3,64,256]{3,2,1,0:T(8,128)S(1)}, u32[]{:S(2)}, u32[]{:S(2)}) %collective-permute-start.11) | collective-permute-done | bytes 393248 | tf_op jit(solution)/shard_map/ppermute | solution.py:192
  70.0 2.6 %collective-permute-start.12 = (f32[3,64,256]{2,1,0:T(8,128)S(1)}, f32[3,64,256]{2,1,0:T(8,128)S(1)}, u32[]{:S(2)}, u32[]{:S(2)}) collective-permute-start(f32[3,64,256]{2,1,0:T(8,128)S(1)} %get-tuple-element.84), channel_id=1, source_target_pairs={{0,8},{8,0},{16,24},{24,16},{1,9},{9,1},{17,25},{25,17},{2,10},{10... | collective-permute-start | bytes 589832 | tf_op jit(solution)/shard_map/ppermute | solution.py:192
  72.6 1.6 %collective-permute-start.14 = (f32[3,64,256]{2,1,0:T(8,128)S(1)}, f32[3,64,256]{2,1,0:T(8,128)S(1)}, u32[]{:S(2)}, u32[]{:S(2)}) collective-permute-start(f32[3,64,256]{2,1,0:T(8,128)S(1)} %get-tuple-element.95), channel_id=1, source_target_pairs={{0,2},{2,0},{1,3},{3,1},{4,6},{6,4},{5,7},{7,5},{8,10},{10,8},{9,1... | collective-permute-start | bytes 589832 | tf_op jit(solution)/shard_map/ppermute | solution.py:192
  74.2 2.8 %collective-permute-done.12.right = f32[3,64,256]{2,1,0:T(8,128)S(1)} collective-permute-done((f32[3,64,256]{2,1,0:T(8,128)S(1)}, f32[3,64,256]{2,1,0:T(8,128)S(1)}, u32[]{:S(2)}, u32[]{:S(2)}) %collective-permute-start.12) | collective-permute-done | bytes 196640 | tf_op jit(solution)/shard_map/ppermute | solution.py:192
  77.0 0.0 collective-permute-done.9.send
  77.0 0.1 sum_core.3
  77.1 1.4 %collective-permute-done.14.right = f32[3,64,256]{2,1,0:T(8,128)S(1)} collective-permute-done((f32[3,64,256]{2,1,0:T(8,128)S(1)}, f32[3,64,256]{2,1,0:T(8,128)S(1)}, u32[]{:S(2)}, u32[]{:S(2)}) %collective-permute-start.14) | collective-permute-done | bytes 196640 | tf_op jit(solution)/shard_map/ppermute | solution.py:192
  78.5 1.5 %collective-permute-start.15 = (f32[2,3,64,256]{3,2,1,0:T(8,128)S(1)}, f32[2,3,64,256]{3,2,1,0:T(8,128)S(1)}, u32[]{:S(2)}, u32[]{:S(2)}) collective-permute-start(f32[2,3,64,256]{3,2,1,0:T(8,128)S(1)} %get-tuple-element.96), channel_id=1, source_target_pairs={{0,2},{2,0},{1,3},{3,1},{4,6},{6,4},{5,7},{7,5},{8,10},{10,8},{9,1... | collective-permute-start | bytes 1179656 | tf_op jit(solution)/shard_map/ppermute | solution.py:192
  80.0 0.0 collective-permute-start.17
  80.0 7.6 %collective-permute-done.15.right = f32[2,3,64,256]{3,2,1,0:T(8,128)S(1)} collective-permute-done((f32[2,3,64,256]{3,2,1,0:T(8,128)S(1)}, f32[2,3,64,256]{3,2,1,0:T(8,128)S(1)}, u32[]{:S(2)}, u32[]{:S(2)}) %collective-permute-start.15) | collective-permute-done | bytes 393248 | tf_op jit(solution)/shard_map/ppermute | solution.py:192
  87.7 1.1 collective-permute-start.16
  88.8 0.1 collective-permute-start.19
  88.9 3.2 %collective-permute-done.17.right = f32[3,64,256]{2,1,0:T(8,128)S(1)} collective-permute-done((f32[3,64,256]{2,1,0:T(8,128)S(1)}, f32[3,64,256]{2,1,0:T(8,128)S(1)}, u32[]{:S(2)}, u32[]{:S(2)}) %collective-permute-start.17) | collective-permute-done | bytes 196640 | tf_op jit(solution)/shard_map/ppermute | solution.py:192
  92.1 4.0 %collective-permute-done.16.right = f32[3,64,256]{2,1,0:T(8,128)S(1)} collective-permute-done((f32[3,64,256]{2,1,0:T(8,128)S(1)}, f32[3,64,256]{2,1,0:T(8,128)S(1)}, u32[]{:S(2)}, u32[]{:S(2)}) %collective-permute-start.16) | collective-permute-done | bytes 196640 | tf_op jit(solution)/shard_map/ppermute | solution.py:192
  96.1 0.7 collective-permute-start.18
  96.8 1.5 %collective-permute-done.19.refs_1_ = f32[3,64,256]{2,1,0:T(8,128)S(1)} collective-permute-done((f32[3,64,256]{2,1,0:T(8,128)S(1)}, f32[3,64,256]{2,1,0:T(8,128)S(1)}, u32[]{:S(2)}, u32[]{:S(2)}) %collective-permute-start.19) | collective-permute-done | bytes 196640 | tf_op jit(solution)/shard_map/ppermute | solution.py:192
  98.2 0.3 finish.2.refs_0_
  98.6 2.0 %collective-permute-start.25 = (s16[400,256]{1,0:T(8,128)(2,1)S(1)}, s16[400,256]{1,0:T(8,128)(2,1)S(1)}, u32[]{:S(2)}, u32[]{:S(2)}) collective-permute-start(s16[400,256]{1,0:T(8,128)(2,1)S(1)} %finish.2.refs_0_), channel_id=1, source_target_pairs={{0,12},{4,8},{8,4},{12,0},{16,28},{20,24},{24,20},{28,16},{1,13},{... | collective-permute-start | bytes 614408 | tf_op jit(solution)/shard_map/ppermute | solution.py:372
  100.7 0.6 collective-permute-start.24
  101.2 1.0 collective-permute-start.23
  102.2 4.6 %collective-permute-done.18.refs_1_ = f32[3,64,256]{2,1,0:T(8,128)S(1)} collective-permute-done((f32[3,64,256]{2,1,0:T(8,128)S(1)}, f32[3,64,256]{2,1,0:T(8,128)S(1)}, u32[]{:S(2)}, u32[]{:S(2)}) %collective-permute-start.18) | collective-permute-done | bytes 196640 | tf_op jit(solution)/shard_map/ppermute | solution.py:192
  106.8 0.2 finish.3.refs_0_
  107.1 1.0 collective-permute-start.22
  108.1 0.7 collective-permute-start.21
  108.7 1.4 %collective-permute-done.25.refs_3_ = s16[400,256]{1,0:T(8,128)(2,1)S(1)} collective-permute-done((s16[400,256]{1,0:T(8,128)(2,1)S(1)}, s16[400,256]{1,0:T(8,128)(2,1)S(1)}, u32[]{:S(2)}, u32[]{:S(2)}) %collective-permute-start.25) | collective-permute-done | bytes 204832 | tf_op jit(solution)/shard_map/ppermute | solution.py:372
  110.1 0.5 collective-permute-start.20
  110.6 0.1 concatenate.6.scalars
  110.7 4.2 %collective-permute-done.23.refs_1_ = s16[400,256]{1,0:T(8,128)(2,1)S(1)} collective-permute-done((s16[400,256]{1,0:T(8,128)(2,1)S(1)}, s16[400,256]{1,0:T(8,128)(2,1)S(1)}, u32[]{:S(2)}, u32[]{:S(2)}) %collective-permute-start.23) | collective-permute-done | bytes 204832 | tf_op jit(solution)/shard_map/ppermute | solution.py:192
  114.9 1.1 place_tiles.2.refs_4_
  115.9 0.3 collective-permute-done.22.refs_3_
  116.3 0.9 collective-permute-done.20.refs_1_
  117.2 1.6 %place_tiles.3 = f32[10,64,256]{2,1,0:T(8,128)} custom-call(s32[60]{0:T(128)S(1)} %concatenate.6.scalars, s16[208,256]{1,0:T(8,128)(2,1)S(1)} %finish.3.refs_0_, s16[208,256]{1,0:T(8,128)(2,1)S(1)} %collective-permute-done.20.refs_1_, s16[208,256]{1,0:T(8,128)(2,1)S(1)} %collective-permute-done.21.refs_2_, ...), custom_call_target="tpu_custom_call" | custom-call | flops 163840 | tf_op jit(solution)/shard_map/place_tiles/pallas_call | solution.py:414
  (21 shorter events, 0.4 us)
Async XLA Ops:
  1.0 21.9 %collective-permute-start.1 = (bf16[3,256,256]{2,1,0:T(8,128)(2,1)S(1)}, bf16[3,256,256]{2,1,0:T(8,128)(2,1)S(1)}, u32[]{:S(2)}, u32[]{:S(2)}) collective-permute-start(bf16[3,256,256]{2,1,0:T(8,128)(2,1)S(1)} %constant_dynamic-slice_fusion.4), channel_id=1, source_target_pairs={{0,24},{8,16},{16,8},{24,0},{1,25},{9,17},{17,9},{25,1},{2,26},{10... | collective-permute-start | bytes 1179656 | tf_op jit(solution)/shard_map/ppermute | solution.py:192
  7.3 15.6 %collective-permute-start.2 = (bf16[3,256,256]{2,1,0:T(8,128)(2,1)S(1)}, bf16[3,256,256]{2,1,0:T(8,128)(2,1)S(1)}, u32[]{:S(2)}, u32[]{:S(2)}) collective-permute-start(bf16[3,256,256]{2,1,0:T(8,128)(2,1)S(1)} %get-tuple-element.129.refs_0_), channel_id=1, source_target_pairs={{0,4},{4,0},{1,5},{5,1},{2,6},{6,2},{3,7},{7,3},{8,12},{12,8},{9,1... | collective-permute-start | bytes 1179656 | tf_op jit(solution)/shard_map/ppermute | solution.py:192
  9.9 11.5 %collective-permute-start = (bf16[2,256,256]{2,1,0:T(8,128)(2,1)S(1)}, bf16[2,256,256]{2,1,0:T(8,128)(2,1)S(1)}, u32[]{:S(2)}, u32[]{:S(2)}) collective-permute-start(bf16[2,256,256]{2,1,0:T(8,128)(2,1)S(1)} %constant_dynamic-slice_fusion.1), channel_id=1, source_target_pairs={{0,8},{8,0},{16,24},{24,16},{1,9},{9,1},{17,25},{25,17},{2,10},{10... | collective-permute-start | bytes 786440 | tf_op jit(solution)/shard_map/ppermute | solution.py:192
  9.9 29.7 %collective-permute-start.4 = (bf16[3,256,256]{2,1,0:T(8,128)(2,1)S(1)}, bf16[3,256,256]{2,1,0:T(8,128)(2,1)S(1)}, u32[]{:S(2)}, u32[]{:S(2)}) collective-permute-start(bf16[3,256,256]{2,1,0:T(8,128)(2,1)S(1)} %get-tuple-element.128), channel_id=1, source_target_pairs={{0,16},{8,24},{16,0},{24,8},{1,17},{9,25},{17,1},{25,9},{2,18},{10... | collective-permute-start | bytes 1179656 | tf_op jit(solution)/shard_map/ppermute | solution.py:192
  11.6 19.9 %collective-permute-start.3 = (bf16[1,256,256]{2,1,0:T(8,128)(2,1)S(1)}, bf16[1,256,256]{2,1,0:T(8,128)(2,1)S(1)}, u32[]{:S(2)}, u32[]{:S(2)}) collective-permute-start(bf16[1,256,256]{2,1,0:T(8,128)(2,1)S(1)} %constant_dynamic-slice_fusion), channel_id=1, source_target_pairs={{0,8},{8,0},{16,24},{24,16},{1,9},{9,1},{17,25},{25,17},{2,10},{10... | collective-permute-start | bytes 393224 | tf_op jit(solution)/shard_map/ppermute | solution.py:192
  21.3 12.3 %collective-permute-start.6 = (bf16[2,256,256]{2,1,0:T(8,128)(2,1)S(1)}, bf16[2,256,256]{2,1,0:T(8,128)(2,1)S(1)}, u32[]{:S(2)}, u32[]{:S(2)}) collective-permute-start(bf16[2,256,256]{2,1,0:T(8,128)(2,1)S(1)} %arrived.7.refs_1_), channel_id=1, source_target_pairs={{0,4},{4,0},{1,5},{5,1},{2,6},{6,2},{3,7},{7,3},{8,12},{12,8},{9,1... | collective-permute-start | bytes 786440 | tf_op jit(solution)/shard_map/ppermute | solution.py:192
  31.5 6.5 %collective-permute-start.5 = (bf16[1,256,256]{2,1,0:T(8,128)(2,1)S(1)}, bf16[1,256,256]{2,1,0:T(8,128)(2,1)S(1)}, u32[]{:S(2)}, u32[]{:S(2)}) collective-permute-start(bf16[1,256,256]{2,1,0:T(8,128)(2,1)S(1)} %arrived.10.refs_3_), channel_id=1, source_target_pairs={{0,4},{4,0},{1,5},{5,1},{2,6},{6,2},{3,7},{7,3},{8,12},{12,8},{9,1... | collective-permute-start | bytes 393224 | tf_op jit(solution)/shard_map/ppermute | solution.py:192
  33.1 13.3 %collective-permute-start.7 = (bf16[3,256,256]{2,1,0:T(8,128)(2,1)S(1)}, bf16[3,256,256]{2,1,0:T(8,128)(2,1)S(1)}, u32[]{:S(2)}, u32[]{:S(2)}) collective-permute-start(bf16[3,256,256]{2,1,0:T(8,128)(2,1)S(1)} %arrived.9.refs_2_), channel_id=1, source_target_pairs={{0,4},{4,0},{1,5},{5,1},{2,6},{6,2},{3,7},{7,3},{8,12},{12,8},{9,1... | collective-permute-start | bytes 1179656 | tf_op jit(solution)/shard_map/ppermute | solution.py:192
  39.7 13.1 %collective-permute-start.8 = (bf16[3,256,256]{2,1,0:T(8,128)(2,1)S(1)}, bf16[3,256,256]{2,1,0:T(8,128)(2,1)S(1)}, u32[]{:S(2)}, u32[]{:S(2)}) collective-permute-start(bf16[3,256,256]{2,1,0:T(8,128)(2,1)S(1)} %arrived.13.refs_4_), channel_id=1, source_target_pairs={{0,4},{4,0},{1,5},{5,1},{2,6},{6,2},{3,7},{7,3},{8,12},{12,8},{9,1... | collective-permute-start | bytes 1179656 | tf_op jit(solution)/shard_map/ppermute | solution.py:192
  55.1 3.5 %collective-permute-start.10 = (f32[4,6,64,256]{3,2,1,0:T(8,128)S(1)}, f32[4,6,64,256]{3,2,1,0:T(8,128)S(1)}, u32[]{:S(2)}, u32[]{:S(2)}) collective-permute-start(f32[4,6,64,256]{3,2,1,0:T(8,128)S(1)} %get-tuple-element.75), channel_id=1, source_target_pairs={{0,1},{1,0},{2,3},{3,2},{4,5},{5,4},{6,7},{7,6},{8,9},{9,8},{10,11... | collective-permute-start | bytes 4718600 | tf_op jit(solution)/shard_map/ppermute | solution.py:192
  56.6 20.4 %collective-permute-start.9 = (f32[4,3,64,256]{3,2,1,0:T(8,128)S(1)}, f32[4,3,64,256]{3,2,1,0:T(8,128)S(1)}, u32[]{:S(2)}, u32[]{:S(2)}) collective-permute-start(f32[4,3,64,256]{3,2,1,0:T(8,128)S(1)} %get-tuple-element.73), channel_id=1, source_target_pairs={{0,1},{1,0},{2,3},{3,2},{4,5},{5,4},{6,7},{7,6},{8,9},{9,8},{10,11... | collective-permute-start | bytes 2359304 | tf_op jit(solution)/shard_map/ppermute | solution.py:192
  58.8 11.2 %collective-permute-start.11 = (f32[2,3,64,256]{3,2,1,0:T(8,128)S(1)}, f32[2,3,64,256]{3,2,1,0:T(8,128)S(1)}, u32[]{:S(2)}, u32[]{:S(2)}) collective-permute-start(f32[2,3,64,256]{3,2,1,0:T(8,128)S(1)} %get-tuple-element.79), channel_id=1, source_target_pairs={{0,2},{2,0},{1,3},{3,1},{4,6},{6,4},{5,7},{7,5},{8,10},{10,8},{9,1... | collective-permute-start | bytes 1179656 | tf_op jit(solution)/shard_map/ppermute | solution.py:192
  60.3 12.3 %collective-permute-start.13 = (f32[2,3,64,256]{3,2,1,0:T(8,128)S(1)}, f32[2,3,64,256]{3,2,1,0:T(8,128)S(1)}, u32[]{:S(2)}, u32[]{:S(2)}) collective-permute-start(f32[2,3,64,256]{3,2,1,0:T(8,128)S(1)} %get-tuple-element.85), channel_id=1, source_target_pairs={{0,8},{8,0},{16,24},{24,16},{1,9},{9,1},{17,25},{25,17},{2,10},{10... | collective-permute-start | bytes 1179656 | tf_op jit(solution)/shard_map/ppermute | solution.py:192
  70.0 6.9 %collective-permute-start.12 = (f32[3,64,256]{2,1,0:T(8,128)S(1)}, f32[3,64,256]{2,1,0:T(8,128)S(1)}, u32[]{:S(2)}, u32[]{:S(2)}) collective-permute-start(f32[3,64,256]{2,1,0:T(8,128)S(1)} %get-tuple-element.84), channel_id=1, source_target_pairs={{0,8},{8,0},{16,24},{24,16},{1,9},{9,1},{17,25},{25,17},{2,10},{10... | collective-permute-start | bytes 589832 | tf_op jit(solution)/shard_map/ppermute | solution.py:192
  72.6 5.9 %collective-permute-start.14 = (f32[3,64,256]{2,1,0:T(8,128)S(1)}, f32[3,64,256]{2,1,0:T(8,128)S(1)}, u32[]{:S(2)}, u32[]{:S(2)}) collective-permute-start(f32[3,64,256]{2,1,0:T(8,128)S(1)} %get-tuple-element.95), channel_id=1, source_target_pairs={{0,2},{2,0},{1,3},{3,1},{4,6},{6,4},{5,7},{7,5},{8,10},{10,8},{9,1... | collective-permute-start | bytes 589832 | tf_op jit(solution)/shard_map/ppermute | solution.py:192
  78.5 9.1 %collective-permute-start.15 = (f32[2,3,64,256]{3,2,1,0:T(8,128)S(1)}, f32[2,3,64,256]{3,2,1,0:T(8,128)S(1)}, u32[]{:S(2)}, u32[]{:S(2)}) collective-permute-start(f32[2,3,64,256]{3,2,1,0:T(8,128)S(1)} %get-tuple-element.96), channel_id=1, source_target_pairs={{0,2},{2,0},{1,3},{3,1},{4,6},{6,4},{5,7},{7,5},{8,10},{10,8},{9,1... | collective-permute-start | bytes 1179656 | tf_op jit(solution)/shard_map/ppermute | solution.py:192
  80.0 12.0 %collective-permute-start.17 = (f32[3,64,256]{2,1,0:T(8,128)S(1)}, f32[3,64,256]{2,1,0:T(8,128)S(1)}, u32[]{:S(2)}, u32[]{:S(2)}) collective-permute-start(f32[3,64,256]{2,1,0:T(8,128)S(1)} %sum_z.4.left), channel_id=1, source_target_pairs={{0,16},{8,24},{16,0},{24,8},{1,17},{9,25},{17,1},{25,9},{2,18},{10... | collective-permute-start | bytes 589832 | tf_op jit(solution)/shard_map/ppermute | solution.py:192
  80.0 20.6 %copy-start = (s32[1,10,2]{1,2,0:T(2,128)S(1)}, s32[1,10,2]{1,2,0:T(2,128)}, u32[]{:S(2)}) copy-start(s32[1,10,2]{1,2,0:T(2,128)} %param.4) | copy-start | bytes 244
  87.7 8.3 %collective-permute-start.16 = (f32[3,64,256]{2,1,0:T(8,128)S(1)}, f32[3,64,256]{2,1,0:T(8,128)S(1)}, u32[]{:S(2)}, u32[]{:S(2)}) collective-permute-start(f32[3,64,256]{2,1,0:T(8,128)S(1)} %get-tuple-element.102), channel_id=1, source_target_pairs={{0,8},{8,0},{16,24},{24,16},{1,9},{9,1},{17,25},{25,17},{2,10},{10... | collective-permute-start | bytes 589832 | tf_op jit(solution)/shard_map/ppermute | solution.py:192
  88.8 9.5 %collective-permute-start.19 = (f32[3,64,256]{2,1,0:T(8,128)S(1)}, f32[3,64,256]{2,1,0:T(8,128)S(1)}, u32[]{:S(2)}, u32[]{:S(2)}) collective-permute-start(f32[3,64,256]{2,1,0:T(8,128)S(1)} %sum_x.4.refs_0_), channel_id=1, source_target_pairs={{0,16},{8,24},{16,0},{24,8},{1,17},{9,25},{17,1},{25,9},{2,18},{10... | collective-permute-start | bytes 589832 | tf_op jit(solution)/shard_map/ppermute | solution.py:192
  96.1 10.8 %collective-permute-start.18 = (f32[3,64,256]{2,1,0:T(8,128)S(1)}, f32[3,64,256]{2,1,0:T(8,128)S(1)}, u32[]{:S(2)}, u32[]{:S(2)}) collective-permute-start(f32[3,64,256]{2,1,0:T(8,128)S(1)} %sum_z.5.refs_0_), channel_id=1, source_target_pairs={{0,16},{8,24},{16,0},{24,8},{1,17},{9,25},{17,1},{25,9},{2,18},{10... | collective-permute-start | bytes 589832 | tf_op jit(solution)/shard_map/ppermute | solution.py:192
  98.6 11.5 %collective-permute-start.25 = (s16[400,256]{1,0:T(8,128)(2,1)S(1)}, s16[400,256]{1,0:T(8,128)(2,1)S(1)}, u32[]{:S(2)}, u32[]{:S(2)}) collective-permute-start(s16[400,256]{1,0:T(8,128)(2,1)S(1)} %finish.2.refs_0_), channel_id=1, source_target_pairs={{0,12},{4,8},{8,4},{12,0},{16,28},{20,24},{24,20},{28,16},{1,13},{... | collective-permute-start | bytes 614408 | tf_op jit(solution)/shard_map/ppermute | solution.py:372
  100.7 10.1 %collective-permute-start.24 = (s16[400,256]{1,0:T(8,128)(2,1)S(1)}, s16[400,256]{1,0:T(8,128)(2,1)S(1)}, u32[]{:S(2)}, u32[]{:S(2)}) collective-permute-start(s16[400,256]{1,0:T(8,128)(2,1)S(1)} %finish.2.refs_0_), channel_id=1, source_target_pairs={{0,4},{4,0},{1,5},{5,1},{2,6},{6,2},{3,7},{7,3},{8,12},{12,8},{9,1... | collective-permute-start | bytes 614408 | tf_op jit(solution)/shard_map/ppermute | solution.py:192
  101.2 13.7 %collective-permute-start.23 = (s16[400,256]{1,0:T(8,128)(2,1)S(1)}, s16[400,256]{1,0:T(8,128)(2,1)S(1)}, u32[]{:S(2)}, u32[]{:S(2)}) collective-permute-start(s16[400,256]{1,0:T(8,128)(2,1)S(1)} %finish.2.refs_0_), channel_id=1, source_target_pairs={{0,8},{8,0},{16,24},{24,16},{1,9},{9,1},{17,25},{25,17},{2,10},{10... | collective-permute-start | bytes 614408 | tf_op jit(solution)/shard_map/ppermute | solution.py:192
  107.1 9.2 %collective-permute-start.22 = (s16[208,256]{1,0:T(8,128)(2,1)S(1)}, s16[208,256]{1,0:T(8,128)(2,1)S(1)}, u32[]{:S(2)}, u32[]{:S(2)}) collective-permute-start(s16[208,256]{1,0:T(8,128)(2,1)S(1)} %finish.3.refs_0_), channel_id=1, source_target_pairs={{0,12},{4,8},{8,4},{12,0},{16,28},{20,24},{24,20},{28,16},{1,13},{... | collective-permute-start | bytes 319496 | tf_op jit(solution)/shard_map/ppermute | solution.py:372
  108.1 8.2 %collective-permute-start.21 = (s16[208,256]{1,0:T(8,128)(2,1)S(1)}, s16[208,256]{1,0:T(8,128)(2,1)S(1)}, u32[]{:S(2)}, u32[]{:S(2)}) collective-permute-start(s16[208,256]{1,0:T(8,128)(2,1)S(1)} %finish.3.refs_0_), channel_id=1, source_target_pairs={{0,4},{4,0},{1,5},{5,1},{2,6},{6,2},{3,7},{7,3},{8,12},{12,8},{9,1... | collective-permute-start | bytes 319496 | tf_op jit(solution)/shard_map/ppermute | solution.py:192
  110.1 7.1 %collective-permute-start.20 = (s16[208,256]{1,0:T(8,128)(2,1)S(1)}, s16[208,256]{1,0:T(8,128)(2,1)S(1)}, u32[]{:S(2)}, u32[]{:S(2)}) collective-permute-start(s16[208,256]{1,0:T(8,128)(2,1)S(1)} %finish.3.refs_0_), channel_id=1, source_target_pairs={{0,8},{8,0},{16,24},{24,16},{1,9},{9,1},{17,25},{25,17},{2,10},{10... | collective-permute-start | bytes 319496 | tf_op jit(solution)/shard_map/ppermute | solution.py:192

commit v15 on v13

--- a/solution.py
+++ b/solution.py
@@ -16,8 +16,8 @@
 CALLS = ((0, 1), (2,))
 LOW_FIRST = (0,)
 ORDER = (
-    ("core", 0), ("x", 1), ("low", 0), ("low", 1), ("core", 1), ("x", 0),
-    ("x", 2), ("high", 1), ("low", 2), ("finish", BATCHES[0]), ("finish", BATCHES[1]),
+    ("core", 0), ("core", 1), ("x", 1), ("low", 0), ("low", 1), ("x", 2),
+    ("high", 1), ("low", 2), ("finish", BATCHES[0]), ("finish", BATCHES[1]),
     ("place", 0), ("place", 1),
 )
 CODE_TOP = 32767.0
@@ -93,6 +93,30 @@
         for start in range(0, keep.shape[0], block):
             place = (slice(start, start + block), slice(offset, offset + size))
             outs.pop(0)[...] = keep[place] + send[place]
+
+
+def low_first_kernel(left, right, *refs):
+    count = len(refs) // 2
+    others, mine, merged = refs[:count], refs[count], refs[count + 1 :]
+    size = mine.shape[0]
+    mine[...] = left[0] + right[0]
+    for step, (other, out) in enumerate(zip(others, merged)):
+        out[:size] = left[step + 1] + right[step + 1]
+        for index in range(other.shape[0]):
+            start = size + index * other.shape[1]
+            out[start : start + other.shape[1]] = other[index]
+
+
+def merged_x_kernel(first, second, *refs):
+    arrived, (out, mine, away) = refs[:-3], refs[-3:]
+    size, other = first.shape[0], second.shape[1]
+
+    def total(value, start):
+        return sum((ref[start : start + value.shape[0]] for ref in arrived), value)
+
+    out[...] = total(first[...], 0)
+    mine[...] = total(second[0], size)
+    away[...] = total(second[1], size + other)
 
 
 def split_sum_kernel(left, right, *outs):
@@ -320,22 +344,31 @@
             if index in LOW_FIRST:
                 state[index] = mine, swap(away[0], "z", 1)
                 continue
-            if which > 0:
-                away = lax.optimization_barrier((*away, *state[0][1]))[: len(away)]
-            state[index] = mine, over_x(away)
+            state[index] = mine, away if which > 0 else over_x(away)
 
     def sum_x(index, mine, arrived):
+        if index == 2:
+            shapes = [float_shape(sizes[0])] + [float_shape(sizes[2])] * 2
+            first, mine, away = step_call(
+                merged_x_kernel, shapes, state[0][0], mine, *arrived, name="sum_x"
+            )
+            state[0] = over_high(first)
+            return mine, swap(away, "z", 1)
         for value in arrived[:-1]:
             mine = plain_sum(mine, value, "sum_x")
-        if index in LOW_FIRST:
-            return over_high(plain_sum(mine, arrived[-1], "sum_x"))
         mine, away = split_sum((2, sizes[index]), mine, arrived[-1], "sum_x")
         return mine, swap(away[0], "z", 1)
 
     def sum_low(index, mine, arrived):
         if index in LOW_FIRST:
-            mine, away = split_sum((x_count, sizes[index]), mine, arrived, "sum_z")
-            return mine, over_x(away)
+            others = state[2][1]
+            merged = float_shape(sizes[0] + 2 * sizes[2])
+            shapes = [float_shape(sizes[0])] + [merged] * (x_count - 1)
+            mine, *away = step_call(
+                low_first_kernel, shapes, mine, arrived, *others, name="sum_z"
+            )
+            state[2] = state[2][0], over_x(away)
+            return (mine,)
         return over_high(plain_sum(mine, arrived, "sum_z"))
 
     def to_owners(value):

time: 117 us -> 116 us (level)
  starting transfers between devices: 28.7 us -> 26.9 us
  waiting for transfers between devices: 77.8 us -> 79.3 us
    ppermute x22 -> x21, starting transfers between devices: 26 us -> 23.9 us  [swap(): return lax.ppermute(value, axis, [(i, i ^ bits) for i in range(size)])]
    ppermute x22 -> x21, waiting for transfers between devices: 75.7 us -> 77.5 us  [swap(): return lax.ppermute(value, axis, [(i, i ^ bits) for i in range(size)])]
  transfers between devices with their start and end apart: 24 -> 23, of which waited for: 17 -> 16; matrix products, arithmetic and copies ran while one was open for 1% -> 1% of each run, Pallas kernels for 3% -> 3%
where the time goes in v15:
time: 116 us
  waiting for transfers between devices  79.3 us (68%)
  starting transfers between devices  26.9 us (23%)
  Pallas kernels  7.55 us (7%)
  local copies, waits for them, and re-layouts  2.25 us (2%)
    ppermute x21, waiting for transfers between devices, swap(): return lax.ppermute(value, axis, [(i, i ^ bits) for i in range(size)])  77.5 us
    ppermute x21, starting transfers between devices, swap(): return lax.ppermute(value, axis, [(i, i ^ bits) for i in range(size)])  23.9 us
    pallas_call x2, Pallas kernels, call(): pl.pallas_call(kernel, out_shape=out_shape, in_specs=[pl.BlockSpec(memory...  3.68 us
    ppermute x2, starting transfers between devices, to_owners(): over_both = lax.ppermute(value, ('z', 'y'), both)  2.93 us
    pallas_call x2, Pallas kernels, per_device(): pl.pallas_call(functools.partial(place_kernel, scale_factor / (CODE_TOP *...  2.84 us
  transfers between devices with their start and end apart: 23, of which 16 were waited for; matrix products, arithmetic and copies ran while one was open for 1% of the time, Pallas kernels for 3%

profile of v15, /device:TPU:0, one launch (start us, length us, event | category | flops | bytes accessed | tf_op | source)
XLA Modules:
  0.0 116.1 jit_solution(3798096912001369440)
XLA Ops:
  0.0 1.3 %constant_dynamic-slice_fusion.2 = (bf16[3,256,256]{2,1,0:T(8,128)(2,1)S(1)}, bf16[3,256,256]{2,1,0:T(8,128)(2,1)S(1)}) fusion(bf16[3,256,1024]{2,1,0:T(8,128)(2,1)} %param.3, s32[]{:T(128)S(6)} %select_n.112, s32[]{:T(128)S(6)} %select_n.111), kind=kLoop, calls=%fused_computation.14 | loop fusion | bytes 1572872 | tf_op jit(solution)/shard_map/dynamic_slice | solution.py:235
  1.3 5.1 %collective-permute-start.2 = (bf16[3,256,256]{2,1,0:T(8,128)(2,1)S(1)}, bf16[3,256,256]{2,1,0:T(8,128)(2,1)S(1)}, u32[]{:S(2)}, u32[]{:S(2)}) collective-permute-start(bf16[3,256,256]{2,1,0:T(8,128)(2,1)S(1)} %get-tuple-element.118), channel_id=1, source_target_pairs={{0,24},{8,16},{16,8},{24,0},{1,25},{9,17},{17,9},{25,1},{2,26},{10... | collective-permute-start | bytes 1179656 | tf_op jit(solution)/shard_map/ppermute | solution.py:212
  6.4 0.0 collective-permute-start
  6.4 0.0 copy-done
  6.4 0.1 constant_dynamic-slice_fusion
  6.5 0.7 collective-permute-start.1
  7.2 1.7 %collective-permute-start.3 = (bf16[3,256,256]{2,1,0:T(8,128)(2,1)S(1)}, bf16[3,256,256]{2,1,0:T(8,128)(2,1)S(1)}, u32[]{:S(2)}, u32[]{:S(2)}) collective-permute-start(bf16[3,256,256]{2,1,0:T(8,128)(2,1)S(1)} %get-tuple-element.117.refs_0_), channel_id=1, source_target_pairs={{0,4},{4,0},{1,5},{5,1},{2,6},{6,2},{3,7},{7,3},{8,12},{12,8},{9,1... | collective-permute-start | bytes 1179656 | tf_op jit(solution)/shard_map/ppermute | solution.py:212
  8.9 7.6 %collective-permute-done.2.refs_3_ = bf16[3,256,256]{2,1,0:T(8,128)(2,1)S(1)} collective-permute-done((bf16[3,256,256]{2,1,0:T(8,128)(2,1)S(1)}, bf16[3,256,256]{2,1,0:T(8,128)(2,1)S(1)}, u32[]{:S(2)}, u32[]{:S(2)}) %collective-permute-start.2) | collective-permute-done | bytes 393248 | tf_op jit(solution)/shard_map/ppermute | solution.py:212
  16.4 1.7 %collective-permute-start.6 = (bf16[3,256,256]{2,1,0:T(8,128)(2,1)S(1)}, bf16[3,256,256]{2,1,0:T(8,128)(2,1)S(1)}, u32[]{:S(2)}, u32[]{:S(2)}) collective-permute-start(bf16[3,256,256]{2,1,0:T(8,128)(2,1)S(1)} %collective-permute-done.2.refs_3_), channel_id=1, source_target_pairs={{0,4},{4,0},{1,5},{5,1},{2,6},{6,2},{3,7},{7,3},{8,12},{12,8},{9,1... | collective-permute-start | bytes 1179656 | tf_op jit(solution)/shard_map/ppermute | solution.py:212
  18.2 6.9 %collective-permute-done.refs_1_ = bf16[3,256,256]{2,1,0:T(8,128)(2,1)S(1)} collective-permute-done((bf16[3,256,256]{2,1,0:T(8,128)(2,1)S(1)}, bf16[3,256,256]{2,1,0:T(8,128)(2,1)S(1)}, u32[]{:S(2)}, u32[]{:S(2)}) %collective-permute-start) | collective-permute-done | bytes 393248 | tf_op jit(solution)/shard_map/ppermute | solution.py:212
  25.1 1.4 %collective-permute-start.4 = (bf16[3,256,256]{2,1,0:T(8,128)(2,1)S(1)}, bf16[3,256,256]{2,1,0:T(8,128)(2,1)S(1)}, u32[]{:S(2)}, u32[]{:S(2)}) collective-permute-start(bf16[3,256,256]{2,1,0:T(8,128)(2,1)S(1)} %collective-permute-done.refs_1_), channel_id=1, source_target_pairs={{0,4},{4,0},{1,5},{5,1},{2,6},{6,2},{3,7},{7,3},{8,12},{12,8},{9,1... | collective-permute-start | bytes 1179656 | tf_op jit(solution)/shard_map/ppermute | solution.py:212
  26.5 13.5 %collective-permute-done.1.refs_2_ = bf16[3,256,256]{2,1,0:T(8,128)(2,1)S(1)} collective-permute-done((bf16[3,256,256]{2,1,0:T(8,128)(2,1)S(1)}, bf16[3,256,256]{2,1,0:T(8,128)(2,1)S(1)}, u32[]{:S(2)}, u32[]{:S(2)}) %collective-permute-start.1) | collective-permute-done | bytes 393248 | tf_op jit(solution)/shard_map/ppermute | solution.py:212
  40.0 1.5 %collective-permute-start.5 = (bf16[3,256,256]{2,1,0:T(8,128)(2,1)S(1)}, bf16[3,256,256]{2,1,0:T(8,128)(2,1)S(1)}, u32[]{:S(2)}, u32[]{:S(2)}) collective-permute-start(bf16[3,256,256]{2,1,0:T(8,128)(2,1)S(1)} %collective-permute-done.1.refs_2_), channel_id=1, source_target_pairs={{0,4},{4,0},{1,5},{5,1},{2,6},{6,2},{3,7},{7,3},{8,12},{12,8},{9,1... | collective-permute-start | bytes 1179656 | tf_op jit(solution)/shard_map/ppermute | solution.py:212
  41.5 0.7 fusion.2
  42.2 0.1 concatenate.7.scalars
  42.2 0.0 collective-permute-done.3.refs_4_
  42.3 0.0 collective-permute-done.6.refs_7_
  42.3 0.0 collective-permute-done.4.refs_5_
  42.3 7.9 %collective-permute-done.5.refs_6_ = bf16[3,256,256]{2,1,0:T(8,128)(2,1)S(1)} collective-permute-done((bf16[3,256,256]{2,1,0:T(8,128)(2,1)S(1)}, bf16[3,256,256]{2,1,0:T(8,128)(2,1)S(1)}, u32[]{:S(2)}, u32[]{:S(2)}) %collective-permute-start.5) | collective-permute-done | bytes 393248 | tf_op jit(solution)/shard_map/ppermute | solution.py:212
  50.1 2.3 %tiles_first.1 = (bf16[8,256,768]{2,1,0:T(8,128)(2,1)S(1)}, f32[4,6,64,256]{3,2,1,0:T(8,128)S(1)}, f32[4,6,64,256]{3,2,1,0:T(8,128)S(1)}) custom-call(s32[40]{0:T(128)S(1)} %concatenate.7.scalars, bf16[3,256,256]{2,1,0:T(8,128)(2,1)S(1)} %get-tuple-element.117.refs_0_, bf16[3,256,256]{2,1,0:T(8,128)(2,1)S(1)} %collective-permute-done.refs_1_, ...), custom_call_target="tpu_custom_call" | custom-call | flops 1207959552 | tf_op jit(solution)/shard_map/tiles_first/pallas_call | solution.py:253
  52.4 0.1 collective-permute-start.7
  52.5 1.4 %tiles_second.1 = (f32[4,3,64,256]{3,2,1,0:T(8,128)S(1)}, f32[4,3,64,256]{3,2,1,0:T(8,128)S(1)}) custom-call(s32[40]{0:T(128)S(1)} %concatenate.7.scalars, bf16[8,256,768]{2,1,0:T(8,128)(2,1)S(1)} %get-tuple-element.65.blocks), custom_call_target="tpu_custom_call" | custom-call | flops 603979776 | tf_op jit(solution)/shard_map/tiles_second/pallas_call | solution.py:253
  53.9 0.6 collective-permute-start.9
  54.5 1.4 %collective-permute-done.7.send = f32[4,6,64,256]{3,2,1,0:T(8,128)S(1)} collective-permute-done((f32[4,6,64,256]{3,2,1,0:T(8,128)S(1)}, f32[4,6,64,256]{3,2,1,0:T(8,128)S(1)}, u32[]{:S(2)}, u32[]{:S(2)}) %collective-permute-start.7) | collective-permute-done | bytes 1572896 | tf_op jit(solution)/shard_map/ppermute | solution.py:212
  55.9 0.2 sum_core.2
  56.0 1.6 %collective-permute-start.10 = (f32[2,3,64,256]{3,2,1,0:T(8,128)S(1)}, f32[2,3,64,256]{3,2,1,0:T(8,128)S(1)}, u32[]{:S(2)}, u32[]{:S(2)}) collective-permute-start(f32[2,3,64,256]{3,2,1,0:T(8,128)S(1)} %get-tuple-element.72), channel_id=1, source_target_pairs={{0,2},{2,0},{1,3},{3,1},{4,6},{6,4},{5,7},{7,5},{8,10},{10,8},{9,1... | collective-permute-start | bytes 1179656 | tf_op jit(solution)/shard_map/ppermute | solution.py:212
  57.6 0.6 collective-permute-start.8
  58.2 0.0 collective-permute-done.9.send
  58.2 0.1 sum_core.3
  58.3 9.0 %collective-permute-done.10.right = f32[2,3,64,256]{3,2,1,0:T(8,128)S(1)} collective-permute-done((f32[2,3,64,256]{3,2,1,0:T(8,128)S(1)}, f32[2,3,64,256]{3,2,1,0:T(8,128)S(1)}, u32[]{:S(2)}, u32[]{:S(2)}) %collective-permute-start.10) | collective-permute-done | bytes 393248 | tf_op jit(solution)/shard_map/ppermute | solution.py:212
  67.3 1.2 %collective-permute-done.8.right = f32[2,3,64,256]{3,2,1,0:T(8,128)S(1)} collective-permute-done((f32[2,3,64,256]{3,2,1,0:T(8,128)S(1)}, f32[2,3,64,256]{3,2,1,0:T(8,128)S(1)}, u32[]{:S(2)}, u32[]{:S(2)}) %collective-permute-start.8) | collective-permute-done | bytes 393248 | tf_op jit(solution)/shard_map/ppermute | solution.py:212
  68.5 0.1 sum_z.3
  68.5 0.6 collective-permute-start.11
  69.2 0.6 collective-permute-start.12
  69.7 5.1 %collective-permute-done.12.right = f32[3,64,256]{2,1,0:T(8,128)S(1)} collective-permute-done((f32[3,64,256]{2,1,0:T(8,128)S(1)}, f32[3,64,256]{2,1,0:T(8,128)S(1)}, u32[]{:S(2)}, u32[]{:S(2)}) %collective-permute-start.12) | collective-permute-done | bytes 196640 | tf_op jit(solution)/shard_map/ppermute | solution.py:212
  74.8 0.0 copy-start.1
  74.9 1.5 %collective-permute-start.14 = (f32[3,64,256]{2,1,0:T(8,128)S(1)}, f32[3,64,256]{2,1,0:T(8,128)S(1)}, u32[]{:S(2)}, u32[]{:S(2)}) collective-permute-start(f32[3,64,256]{2,1,0:T(8,128)S(1)} %sum_z.4.left), channel_id=1, source_target_pairs={{0,16},{8,24},{16,0},{24,8},{1,17},{9,25},{17,1},{25,9},{2,18},{10... | collective-permute-start | bytes 589832 | tf_op jit(solution)/shard_map/ppermute | solution.py:212
  76.3 6.5 %collective-permute-done.11.refs_0_ = f32[9,64,256]{2,1,0:T(8,128)S(1)} collective-permute-done((f32[9,64,256]{2,1,0:T(8,128)S(1)}, f32[9,64,256]{2,1,0:T(8,128)S(1)}, u32[]{:S(2)}, u32[]{:S(2)}) %collective-permute-start.11) | collective-permute-done | bytes 589856 | tf_op jit(solution)/shard_map/ppermute | solution.py:212
  82.8 0.1 sum_x.3
  82.9 0.6 collective-permute-start.13
  83.5 2.3 %collective-permute-start.16 = (f32[3,64,256]{2,1,0:T(8,128)S(1)}, f32[3,64,256]{2,1,0:T(8,128)S(1)}, u32[]{:S(2)}, u32[]{:S(2)}) collective-permute-start(f32[3,64,256]{2,1,0:T(8,128)S(1)} %get-tuple-element.95.refs_0_), channel_id=1, source_target_pairs={{0,16},{8,24},{16,0},{24,8},{1,17},{9,25},{17,1},{25,9},{2,18},{10... | collective-permute-start | bytes 589832 | tf_op jit(solution)/shard_map/ppermute | solution.py:212
  85.8 0.0 collective-permute-done.14.right
  85.8 7.1 %collective-permute-done.13.right = f32[3,64,256]{2,1,0:T(8,128)S(1)} collective-permute-done((f32[3,64,256]{2,1,0:T(8,128)S(1)}, f32[3,64,256]{2,1,0:T(8,128)S(1)}, u32[]{:S(2)}, u32[]{:S(2)}) %collective-permute-start.13) | collective-permute-done | bytes 196640 | tf_op jit(solution)/shard_map/ppermute | solution.py:212
  93.0 0.1 collective-permute-start.15
  93.0 0.3 collective-permute-done.16.refs_1_
  93.3 0.3 finish.2.refs_0_
  93.6 2.9 %collective-permute-start.22 = (s16[400,256]{1,0:T(8,128)(2,1)S(1)}, s16[400,256]{1,0:T(8,128)(2,1)S(1)}, u32[]{:S(2)}, u32[]{:S(2)}) collective-permute-start(s16[400,256]{1,0:T(8,128)(2,1)S(1)} %finish.2.refs_0_), channel_id=1, source_target_pairs={{0,12},{4,8},{8,4},{12,0},{16,28},{20,24},{24,20},{28,16},{1,13},{... | collective-permute-start | bytes 614408 | tf_op jit(solution)/shard_map/ppermute | solution.py:376
  96.5 0.0 copy-done.1
  96.5 0.6 collective-permute-start.21
  97.1 0.2 collective-permute-start.20
  97.3 6.7 %collective-permute-done.15.refs_1_ = f32[3,64,256]{2,1,0:T(8,128)S(1)} collective-permute-done((f32[3,64,256]{2,1,0:T(8,128)S(1)}, f32[3,64,256]{2,1,0:T(8,128)S(1)}, u32[]{:S(2)}, u32[]{:S(2)}) %collective-permute-start.15) | collective-permute-done | bytes 196640 | tf_op jit(solution)/shard_map/ppermute | solution.py:212
  104.0 0.2 finish.3.refs_0_
  104.3 0.1 collective-permute-start.19
  104.3 1.6 %collective-permute-start.18 = (s16[208,256]{1,0:T(8,128)(2,1)S(1)}, s16[208,256]{1,0:T(8,128)(2,1)S(1)}, u32[]{:S(2)}, u32[]{:S(2)}) collective-permute-start(s16[208,256]{1,0:T(8,128)(2,1)S(1)} %finish.3.refs_0_), channel_id=1, source_target_pairs={{0,4},{4,0},{1,5},{5,1},{2,6},{6,2},{3,7},{7,3},{8,12},{12,8},{9,1... | collective-permute-start | bytes 319496 | tf_op jit(solution)/shard_map/ppermute | solution.py:212
  105.9 0.8 collective-permute-done.22.refs_3_
  106.7 1.1 collective-permute-start.17
  107.8 0.1 concatenate.6.scalars
  107.9 0.0 collective-permute-done.21.refs_2_
  107.9 3.2 %collective-permute-done.20.refs_1_ = s16[400,256]{1,0:T(8,128)(2,1)S(1)} collective-permute-done((s16[400,256]{1,0:T(8,128)(2,1)S(1)}, s16[400,256]{1,0:T(8,128)(2,1)S(1)}, u32[]{:S(2)}, u32[]{:S(2)}) %collective-permute-start.20) | collective-permute-done | bytes 204832 | tf_op jit(solution)/shard_map/ppermute | solution.py:212
  111.1 1.2 %place_tiles.2.refs_4_ = f32[10,64,256]{2,1,0:T(8,128)S(1)} custom-call(s32[60]{0:T(128)S(1)} %concatenate.6.scalars, s16[400,256]{1,0:T(8,128)(2,1)S(1)} %finish.2.refs_0_, s16[400,256]{1,0:T(8,128)(2,1)S(1)} %collective-permute-done.20.refs_1_, s16[400,256]{1,0:T(8,128)(2,1)S(1)} %collective-permute-done.21.refs_2_, ...), custom_call_target="tpu_custom_call" | custom-call | flops 163840 | tf_op jit(solution)/shard_map/place_tiles/pallas_call | solution.py:418
  112.4 1.0 collective-permute-done.19.refs_3_
  113.4 0.0 collective-permute-done.18.refs_2_
  113.4 1.2 collective-permute-done.17.refs_1_
  114.5 1.6 %place_tiles.3 = f32[10,64,256]{2,1,0:T(8,128)} custom-call(s32[60]{0:T(128)S(1)} %concatenate.6.scalars, s16[208,256]{1,0:T(8,128)(2,1)S(1)} %finish.3.refs_0_, s16[208,256]{1,0:T(8,128)(2,1)S(1)} %collective-permute-done.17.refs_1_, s16[208,256]{1,0:T(8,128)(2,1)S(1)} %collective-permute-done.18.refs_2_, ...), custom_call_target="tpu_custom_call" | custom-call | flops 163840 | tf_op jit(solution)/shard_map/place_tiles/pallas_call | solution.py:418
  (7 shorter events, 0.2 us)
Async XLA Ops:
  0.0 6.4 %copy-start = (bf16[3,256,1024]{2,1,0:T(8,128)(2,1)S(1)}, bf16[3,256,1024]{2,1,0:T(8,128)(2,1)}, u32[]{:S(2)}) copy-start(bf16[3,256,1024]{2,1,0:T(8,128)(2,1)} %param.3) | copy-start | bytes 4718596
  1.3 15.1 %collective-permute-start.2 = (bf16[3,256,256]{2,1,0:T(8,128)(2,1)S(1)}, bf16[3,256,256]{2,1,0:T(8,128)(2,1)S(1)}, u32[]{:S(2)}, u32[]{:S(2)}) collective-permute-start(bf16[3,256,256]{2,1,0:T(8,128)(2,1)S(1)} %get-tuple-element.118), channel_id=1, source_target_pairs={{0,24},{8,16},{16,8},{24,0},{1,25},{9,17},{17,9},{25,1},{2,26},{10... | collective-permute-start | bytes 1179656 | tf_op jit(solution)/shard_map/ppermute | solution.py:212
  6.4 18.7 %collective-permute-start = (bf16[3,256,256]{2,1,0:T(8,128)(2,1)S(1)}, bf16[3,256,256]{2,1,0:T(8,128)(2,1)S(1)}, u32[]{:S(2)}, u32[]{:S(2)}) collective-permute-start(bf16[3,256,256]{2,1,0:T(8,128)(2,1)S(1)} %get-tuple-element.119), channel_id=1, source_target_pairs={{0,8},{8,0},{16,24},{24,16},{1,9},{9,1},{17,25},{25,17},{2,10},{10... | collective-permute-start | bytes 1179656 | tf_op jit(solution)/shard_map/ppermute | solution.py:212
  6.5 33.4 %collective-permute-start.1 = (bf16[3,256,256]{2,1,0:T(8,128)(2,1)S(1)}, bf16[3,256,256]{2,1,0:T(8,128)(2,1)S(1)}, u32[]{:S(2)}, u32[]{:S(2)}) collective-permute-start(bf16[3,256,256]{2,1,0:T(8,128)(2,1)S(1)} %get-tuple-element.116), channel_id=1, source_target_pairs={{0,16},{8,24},{16,0},{24,8},{1,17},{9,25},{17,1},{25,9},{2,18},{10... | collective-permute-start | bytes 1179656 | tf_op jit(solution)/shard_map/ppermute | solution.py:212
  7.2 35.0 %collective-permute-start.3 = (bf16[3,256,256]{2,1,0:T(8,128)(2,1)S(1)}, bf16[3,256,256]{2,1,0:T(8,128)(2,1)S(1)}, u32[]{:S(2)}, u32[]{:S(2)}) collective-permute-start(bf16[3,256,256]{2,1,0:T(8,128)(2,1)S(1)} %get-tuple-element.117.refs_0_), channel_id=1, source_target_pairs={{0,4},{4,0},{1,5},{5,1},{2,6},{6,2},{3,7},{7,3},{8,12},{12,8},{9,1... | collective-permute-start | bytes 1179656 | tf_op jit(solution)/shard_map/ppermute | solution.py:212
  16.4 25.8 %collective-permute-start.6 = (bf16[3,256,256]{2,1,0:T(8,128)(2,1)S(1)}, bf16[3,256,256]{2,1,0:T(8,128)(2,1)S(1)}, u32[]{:S(2)}, u32[]{:S(2)}) collective-permute-start(bf16[3,256,256]{2,1,0:T(8,128)(2,1)S(1)} %collective-permute-done.2.refs_3_), channel_id=1, source_target_pairs={{0,4},{4,0},{1,5},{5,1},{2,6},{6,2},{3,7},{7,3},{8,12},{12,8},{9,1... | collective-permute-start | bytes 1179656 | tf_op jit(solution)/shard_map/ppermute | solution.py:212
  25.1 17.2 %collective-permute-start.4 = (bf16[3,256,256]{2,1,0:T(8,128)(2,1)S(1)}, bf16[3,256,256]{2,1,0:T(8,128)(2,1)S(1)}, u32[]{:S(2)}, u32[]{:S(2)}) collective-permute-start(bf16[3,256,256]{2,1,0:T(8,128)(2,1)S(1)} %collective-permute-done.refs_1_), channel_id=1, source_target_pairs={{0,4},{4,0},{1,5},{5,1},{2,6},{6,2},{3,7},{7,3},{8,12},{12,8},{9,1... | collective-permute-start | bytes 1179656 | tf_op jit(solution)/shard_map/ppermute | solution.py:212
  40.0 10.2 %collective-permute-start.5 = (bf16[3,256,256]{2,1,0:T(8,128)(2,1)S(1)}, bf16[3,256,256]{2,1,0:T(8,128)(2,1)S(1)}, u32[]{:S(2)}, u32[]{:S(2)}) collective-permute-start(bf16[3,256,256]{2,1,0:T(8,128)(2,1)S(1)} %collective-permute-done.1.refs_2_), channel_id=1, source_target_pairs={{0,4},{4,0},{1,5},{5,1},{2,6},{6,2},{3,7},{7,3},{8,12},{12,8},{9,1... | collective-permute-start | bytes 1179656 | tf_op jit(solution)/shard_map/ppermute | solution.py:212
  52.4 3.5 %collective-permute-start.7 = (f32[4,6,64,256]{3,2,1,0:T(8,128)S(1)}, f32[4,6,64,256]{3,2,1,0:T(8,128)S(1)}, u32[]{:S(2)}, u32[]{:S(2)}) collective-permute-start(f32[4,6,64,256]{3,2,1,0:T(8,128)S(1)} %get-tuple-element.60), channel_id=1, source_target_pairs={{0,1},{1,0},{2,3},{3,2},{4,5},{5,4},{6,7},{7,6},{8,9},{9,8},{10,11... | collective-permute-start | bytes 4718600 | tf_op jit(solution)/shard_map/ppermute | solution.py:212
  53.9 4.3 %collective-permute-start.9 = (f32[4,3,64,256]{3,2,1,0:T(8,128)S(1)}, f32[4,3,64,256]{3,2,1,0:T(8,128)S(1)}, u32[]{:S(2)}, u32[]{:S(2)}) collective-permute-start(f32[4,3,64,256]{3,2,1,0:T(8,128)S(1)} %get-tuple-element.67), channel_id=1, source_target_pairs={{0,1},{1,0},{2,3},{3,2},{4,5},{5,4},{6,7},{7,6},{8,9},{9,8},{10,11... | collective-permute-start | bytes 2359304 | tf_op jit(solution)/shard_map/ppermute | solution.py:212
  56.0 11.2 %collective-permute-start.10 = (f32[2,3,64,256]{3,2,1,0:T(8,128)S(1)}, f32[2,3,64,256]{3,2,1,0:T(8,128)S(1)}, u32[]{:S(2)}, u32[]{:S(2)}) collective-permute-start(f32[2,3,64,256]{3,2,1,0:T(8,128)S(1)} %get-tuple-element.72), channel_id=1, source_target_pairs={{0,2},{2,0},{1,3},{3,1},{4,6},{6,4},{5,7},{7,5},{8,10},{10,8},{9,1... | collective-permute-start | bytes 1179656 | tf_op jit(solution)/shard_map/ppermute | solution.py:212
  57.6 10.9 %collective-permute-start.8 = (f32[2,3,64,256]{3,2,1,0:T(8,128)S(1)}, f32[2,3,64,256]{3,2,1,0:T(8,128)S(1)}, u32[]{:S(2)}, u32[]{:S(2)}) collective-permute-start(f32[2,3,64,256]{3,2,1,0:T(8,128)S(1)} %get-tuple-element.64), channel_id=1, source_target_pairs={{0,8},{8,0},{16,24},{24,16},{1,9},{9,1},{17,25},{25,17},{2,10},{10... | collective-permute-start | bytes 1179656 | tf_op jit(solution)/shard_map/ppermute | solution.py:212
  68.5 14.3 %collective-permute-start.11 = (f32[9,64,256]{2,1,0:T(8,128)S(1)}, f32[9,64,256]{2,1,0:T(8,128)S(1)}, u32[]{:S(2)}, u32[]{:S(2)}) collective-permute-start(f32[9,64,256]{2,1,0:T(8,128)S(1)} %get-tuple-element.81), channel_id=1, source_target_pairs={{0,2},{2,0},{1,3},{3,1},{4,6},{6,4},{5,7},{7,5},{8,10},{10,8},{9,1... | collective-permute-start | bytes 1769480 | tf_op jit(solution)/shard_map/ppermute | solution.py:212
  69.2 5.7 %collective-permute-start.12 = (f32[3,64,256]{2,1,0:T(8,128)S(1)}, f32[3,64,256]{2,1,0:T(8,128)S(1)}, u32[]{:S(2)}, u32[]{:S(2)}) collective-permute-start(f32[3,64,256]{2,1,0:T(8,128)S(1)} %get-tuple-element.82), channel_id=1, source_target_pairs={{0,8},{8,0},{16,24},{24,16},{1,9},{9,1},{17,25},{25,17},{2,10},{10... | collective-permute-start | bytes 589832 | tf_op jit(solution)/shard_map/ppermute | solution.py:212
  74.8 21.6 %copy-start.1 = (s32[1,10,2]{1,2,0:T(2,128)S(1)}, s32[1,10,2]{1,2,0:T(2,128)}, u32[]{:S(2)}) copy-start(s32[1,10,2]{1,2,0:T(2,128)} %param.4) | copy-start | bytes 244
  74.9 11.0 %collective-permute-start.14 = (f32[3,64,256]{2,1,0:T(8,128)S(1)}, f32[3,64,256]{2,1,0:T(8,128)S(1)}, u32[]{:S(2)}, u32[]{:S(2)}) collective-permute-start(f32[3,64,256]{2,1,0:T(8,128)S(1)} %sum_z.4.left), channel_id=1, source_target_pairs={{0,16},{8,24},{16,0},{24,8},{1,17},{9,25},{17,1},{25,9},{2,18},{10... | collective-permute-start | bytes 589832 | tf_op jit(solution)/shard_map/ppermute | solution.py:212
  82.9 10.0 %collective-permute-start.13 = (f32[3,64,256]{2,1,0:T(8,128)S(1)}, f32[3,64,256]{2,1,0:T(8,128)S(1)}, u32[]{:S(2)}, u32[]{:S(2)}) collective-permute-start(f32[3,64,256]{2,1,0:T(8,128)S(1)} %get-tuple-element.89), channel_id=1, source_target_pairs={{0,8},{8,0},{16,24},{24,16},{1,9},{9,1},{17,25},{25,17},{2,10},{10... | collective-permute-start | bytes 589832 | tf_op jit(solution)/shard_map/ppermute | solution.py:212
  83.5 9.8 %collective-permute-start.16 = (f32[3,64,256]{2,1,0:T(8,128)S(1)}, f32[3,64,256]{2,1,0:T(8,128)S(1)}, u32[]{:S(2)}, u32[]{:S(2)}) collective-permute-start(f32[3,64,256]{2,1,0:T(8,128)S(1)} %get-tuple-element.95.refs_0_), channel_id=1, source_target_pairs={{0,16},{8,24},{16,0},{24,8},{1,17},{9,25},{17,1},{25,9},{2,18},{10... | collective-permute-start | bytes 589832 | tf_op jit(solution)/shard_map/ppermute | solution.py:212
  93.0 11.1 %collective-permute-start.15 = (f32[3,64,256]{2,1,0:T(8,128)S(1)}, f32[3,64,256]{2,1,0:T(8,128)S(1)}, u32[]{:S(2)}, u32[]{:S(2)}) collective-permute-start(f32[3,64,256]{2,1,0:T(8,128)S(1)} %sum_z.5.refs_0_), channel_id=1, source_target_pairs={{0,16},{8,24},{16,0},{24,8},{1,17},{9,25},{17,1},{25,9},{2,18},{10... | collective-permute-start | bytes 589832 | tf_op jit(solution)/shard_map/ppermute | solution.py:212
  93.6 13.1 %collective-permute-start.22 = (s16[400,256]{1,0:T(8,128)(2,1)S(1)}, s16[400,256]{1,0:T(8,128)(2,1)S(1)}, u32[]{:S(2)}, u32[]{:S(2)}) collective-permute-start(s16[400,256]{1,0:T(8,128)(2,1)S(1)} %finish.2.refs_0_), channel_id=1, source_target_pairs={{0,12},{4,8},{8,4},{12,0},{16,28},{20,24},{24,20},{28,16},{1,13},{... | collective-permute-start | bytes 614408 | tf_op jit(solution)/shard_map/ppermute | solution.py:376
  96.5 11.4 %collective-permute-start.21 = (s16[400,256]{1,0:T(8,128)(2,1)S(1)}, s16[400,256]{1,0:T(8,128)(2,1)S(1)}, u32[]{:S(2)}, u32[]{:S(2)}) collective-permute-start(s16[400,256]{1,0:T(8,128)(2,1)S(1)} %finish.2.refs_0_), channel_id=1, source_target_pairs={{0,4},{4,0},{1,5},{5,1},{2,6},{6,2},{3,7},{7,3},{8,12},{12,8},{9,1... | collective-permute-start | bytes 614408 | tf_op jit(solution)/shard_map/ppermute | solution.py:212
  97.1 14.0 %collective-permute-start.20 = (s16[400,256]{1,0:T(8,128)(2,1)S(1)}, s16[400,256]{1,0:T(8,128)(2,1)S(1)}, u32[]{:S(2)}, u32[]{:S(2)}) collective-permute-start(s16[400,256]{1,0:T(8,128)(2,1)S(1)} %finish.2.refs_0_), channel_id=1, source_target_pairs={{0,8},{8,0},{16,24},{24,16},{1,9},{9,1},{17,25},{25,17},{2,10},{10... | collective-permute-start | bytes 614408 | tf_op jit(solution)/shard_map/ppermute | solution.py:212
  104.3 9.1 %collective-permute-start.19 = (s16[208,256]{1,0:T(8,128)(2,1)S(1)}, s16[208,256]{1,0:T(8,128)(2,1)S(1)}, u32[]{:S(2)}, u32[]{:S(2)}) collective-permute-start(s16[208,256]{1,0:T(8,128)(2,1)S(1)} %finish.3.refs_0_), channel_id=1, source_target_pairs={{0,12},{4,8},{8,4},{12,0},{16,28},{20,24},{24,20},{28,16},{1,13},{... | collective-permute-start | bytes 319496 | tf_op jit(solution)/shard_map/ppermute | solution.py:376
  104.3 9.0 %collective-permute-start.18 = (s16[208,256]{1,0:T(8,128)(2,1)S(1)}, s16[208,256]{1,0:T(8,128)(2,1)S(1)}, u32[]{:S(2)}, u32[]{:S(2)}) collective-permute-start(s16[208,256]{1,0:T(8,128)(2,1)S(1)} %finish.3.refs_0_), channel_id=1, source_target_pairs={{0,4},{4,0},{1,5},{5,1},{2,6},{6,2},{3,7},{7,3},{8,12},{12,8},{9,1... | collective-permute-start | bytes 319496 | tf_op jit(solution)/shard_map/ppermute | solution.py:212
  106.7 7.8 %collective-permute-start.17 = (s16[208,256]{1,0:T(8,128)(2,1)S(1)}, s16[208,256]{1,0:T(8,128)(2,1)S(1)}, u32[]{:S(2)}, u32[]{:S(2)}) collective-permute-start(s16[208,256]{1,0:T(8,128)(2,1)S(1)} %finish.3.refs_0_), channel_id=1, source_target_pairs={{0,8},{8,0},{16,24},{24,16},{1,9},{9,1},{17,25},{25,17},{2,10},{10... | collective-permute-start | bytes 319496 | tf_op jit(solution)/shard_map/ppermute | solution.py:212

commit v16 on v15

--- a/solution.py
+++ b/solution.py
@@ -31,7 +31,8 @@
 
 
 def group_sizes(quarter):
-    return [len(piece) for piece in np.array_split(np.arange(quarter), GROUPS)]
+    sizes = [len(piece) for piece in np.array_split(np.arange(quarter), GROUPS)]
+    return [sizes[0] + 1, *sizes[1:-1], sizes[-1] - 1]
 
 
 def multiply_tiles(scalars, first_pair, blocks, keep_ref, send_ref, offset, size, low_first):

time: 116 us -> 128 us (1.10)
  waiting for transfers between devices: 79.3 us -> 87.5 us
  starting transfers between devices: 26.9 us -> 29.6 us
    ppermute x21, waiting for transfers between devices: 77.5 us -> 87.5 us  [swap(): return lax.ppermute(value, axis, [(i, i ^ bits) for i in range(size)])]
    ppermute x2, waiting for transfers between devices: 1.8 us -> 0.01 us  [to_owners(): over_both = lax.ppermute(value, ('z', 'y'), both)]
    ppermute x2, starting transfers between devices: 2.93 us -> 4.36 us  [to_owners(): over_both = lax.ppermute(value, ('z', 'y'), both)]
    ppermute x21, starting transfers between devices: 23.9 us -> 25.3 us  [swap(): return lax.ppermute(value, axis, [(i, i ^ bits) for i in range(size)])]
  transfers between devices with their start and end apart: 23 -> 23, of which waited for: 16 -> 14; matrix products, arithmetic and copies ran while one was open for 1% -> 1% of each run, Pallas kernels for 3% -> 3%
where the time goes in v16:
time: 128 us
  waiting for transfers between devices  87.5 us (68%)
  starting transfers between devices  29.6 us (23%)
  Pallas kernels  7.9 us (6%)
  local copies, waits for them, and re-layouts  2.25 us (2%)
    ppermute x21, waiting for transfers between devices, swap(): return lax.ppermute(value, axis, [(i, i ^ bits) for i in range(size)])  87.5 us
    ppermute x21, starting transfers between devices, swap(): return lax.ppermute(value, axis, [(i, i ^ bits) for i in range(size)])  25.3 us
    ppermute x2, starting transfers between devices, to_owners(): over_both = lax.ppermute(value, ('z', 'y'), both)  4.36 us
    pallas_call x2, Pallas kernels, call(): pl.pallas_call(kernel, out_shape=out_shape, in_specs=[pl.BlockSpec(memory...  3.67 us
    pallas_call x2, Pallas kernels, per_device(): pl.pallas_call(functools.partial(place_kernel, scale_factor / (CODE_TOP *...  3.21 us
  transfers between devices with their start and end apart: 23, of which 14 were waited for; matrix products, arithmetic and copies ran while one was open for 1% of the time, Pallas kernels for 3%

profile of v16, /device:TPU:0, one launch (start us, length us, event | category | flops | bytes accessed | tf_op | source)
XLA Modules:
  0.0 127.5 jit_solution(12453861176261901291)
XLA Ops:
  0.0 1.3 %constant_dynamic-slice_fusion.2 = (bf16[3,256,256]{2,1,0:T(8,128)(2,1)S(1)}, bf16[3,256,256]{2,1,0:T(8,128)(2,1)S(1)}) fusion(bf16[3,256,1024]{2,1,0:T(8,128)(2,1)} %param.3, s32[]{:T(128)S(6)} %select_n.112, s32[]{:T(128)S(6)} %select_n.111), kind=kLoop, calls=%fused_computation.14 | loop fusion | bytes 1572872 | tf_op jit(solution)/shard_map/dynamic_slice | solution.py:236
  1.3 5.1 %collective-permute-start.2 = (bf16[3,256,256]{2,1,0:T(8,128)(2,1)S(1)}, bf16[3,256,256]{2,1,0:T(8,128)(2,1)S(1)}, u32[]{:S(2)}, u32[]{:S(2)}) collective-permute-start(bf16[3,256,256]{2,1,0:T(8,128)(2,1)S(1)} %get-tuple-element.118), channel_id=1, source_target_pairs={{0,24},{8,16},{16,8},{24,0},{1,25},{9,17},{17,9},{25,1},{2,26},{10... | collective-permute-start | bytes 1179656 | tf_op jit(solution)/shard_map/ppermute | solution.py:213
  6.4 0.0 collective-permute-start
  6.4 0.0 copy-done
  6.4 0.1 constant_dynamic-slice_fusion
  6.5 0.7 collective-permute-start.1
  7.2 1.7 %collective-permute-start.3 = (bf16[3,256,256]{2,1,0:T(8,128)(2,1)S(1)}, bf16[3,256,256]{2,1,0:T(8,128)(2,1)S(1)}, u32[]{:S(2)}, u32[]{:S(2)}) collective-permute-start(bf16[3,256,256]{2,1,0:T(8,128)(2,1)S(1)} %get-tuple-element.117.refs_0_), channel_id=1, source_target_pairs={{0,4},{4,0},{1,5},{5,1},{2,6},{6,2},{3,7},{7,3},{8,12},{12,8},{9,1... | collective-permute-start | bytes 1179656 | tf_op jit(solution)/shard_map/ppermute | solution.py:213
  8.9 7.6 %collective-permute-done.2.refs_3_ = bf16[3,256,256]{2,1,0:T(8,128)(2,1)S(1)} collective-permute-done((bf16[3,256,256]{2,1,0:T(8,128)(2,1)S(1)}, bf16[3,256,256]{2,1,0:T(8,128)(2,1)S(1)}, u32[]{:S(2)}, u32[]{:S(2)}) %collective-permute-start.2) | collective-permute-done | bytes 393248 | tf_op jit(solution)/shard_map/ppermute | solution.py:213
  16.4 1.7 %collective-permute-start.6 = (bf16[3,256,256]{2,1,0:T(8,128)(2,1)S(1)}, bf16[3,256,256]{2,1,0:T(8,128)(2,1)S(1)}, u32[]{:S(2)}, u32[]{:S(2)}) collective-permute-start(bf16[3,256,256]{2,1,0:T(8,128)(2,1)S(1)} %collective-permute-done.2.refs_3_), channel_id=1, source_target_pairs={{0,4},{4,0},{1,5},{5,1},{2,6},{6,2},{3,7},{7,3},{8,12},{12,8},{9,1... | collective-permute-start | bytes 1179656 | tf_op jit(solution)/shard_map/ppermute | solution.py:213
  18.2 6.9 %collective-permute-done.refs_1_ = bf16[3,256,256]{2,1,0:T(8,128)(2,1)S(1)} collective-permute-done((bf16[3,256,256]{2,1,0:T(8,128)(2,1)S(1)}, bf16[3,256,256]{2,1,0:T(8,128)(2,1)S(1)}, u32[]{:S(2)}, u32[]{:S(2)}) %collective-permute-start) | collective-permute-done | bytes 393248 | tf_op jit(solution)/shard_map/ppermute | solution.py:213
  25.1 1.4 %collective-permute-start.4 = (bf16[3,256,256]{2,1,0:T(8,128)(2,1)S(1)}, bf16[3,256,256]{2,1,0:T(8,128)(2,1)S(1)}, u32[]{:S(2)}, u32[]{:S(2)}) collective-permute-start(bf16[3,256,256]{2,1,0:T(8,128)(2,1)S(1)} %collective-permute-done.refs_1_), channel_id=1, source_target_pairs={{0,4},{4,0},{1,5},{5,1},{2,6},{6,2},{3,7},{7,3},{8,12},{12,8},{9,1... | collective-permute-start | bytes 1179656 | tf_op jit(solution)/shard_map/ppermute | solution.py:213
  26.5 13.5 %collective-permute-done.1.refs_2_ = bf16[3,256,256]{2,1,0:T(8,128)(2,1)S(1)} collective-permute-done((bf16[3,256,256]{2,1,0:T(8,128)(2,1)S(1)}, bf16[3,256,256]{2,1,0:T(8,128)(2,1)S(1)}, u32[]{:S(2)}, u32[]{:S(2)}) %collective-permute-start.1) | collective-permute-done | bytes 393248 | tf_op jit(solution)/shard_map/ppermute | solution.py:213
  40.0 1.5 %collective-permute-start.5 = (bf16[3,256,256]{2,1,0:T(8,128)(2,1)S(1)}, bf16[3,256,256]{2,1,0:T(8,128)(2,1)S(1)}, u32[]{:S(2)}, u32[]{:S(2)}) collective-permute-start(bf16[3,256,256]{2,1,0:T(8,128)(2,1)S(1)} %collective-permute-done.1.refs_2_), channel_id=1, source_target_pairs={{0,4},{4,0},{1,5},{5,1},{2,6},{6,2},{3,7},{7,3},{8,12},{12,8},{9,1... | collective-permute-start | bytes 1179656 | tf_op jit(solution)/shard_map/ppermute | solution.py:213
  41.5 0.7 fusion.2
  42.2 0.1 concatenate.7.scalars
  42.2 0.0 collective-permute-done.3.refs_4_
  42.3 0.0 collective-permute-done.6.refs_7_
  42.3 0.0 collective-permute-done.4.refs_5_
  42.3 7.9 %collective-permute-done.5.refs_6_ = bf16[3,256,256]{2,1,0:T(8,128)(2,1)S(1)} collective-permute-done((bf16[3,256,256]{2,1,0:T(8,128)(2,1)S(1)}, bf16[3,256,256]{2,1,0:T(8,128)(2,1)S(1)}, u32[]{:S(2)}, u32[]{:S(2)}) %collective-permute-start.5) | collective-permute-done | bytes 393248 | tf_op jit(solution)/shard_map/ppermute | solution.py:213
  50.1 2.5 %tiles_first.1 = (bf16[8,256,768]{2,1,0:T(8,128)(2,1)S(1)}, f32[4,7,64,256]{3,2,1,0:T(8,128)S(1)}, f32[4,7,64,256]{3,2,1,0:T(8,128)S(1)}) custom-call(s32[40]{0:T(128)S(1)} %concatenate.7.scalars, bf16[3,256,256]{2,1,0:T(8,128)(2,1)S(1)} %get-tuple-element.117.refs_0_, bf16[3,256,256]{2,1,0:T(8,128)(2,1)S(1)} %collective-permute-done.refs_1_, ...), custom_call_target="tpu_custom_call" | custom-call | flops 1409286144 | tf_op jit(solution)/shard_map/tiles_first/pallas_call | solution.py:254
  52.6 0.1 collective-permute-start.7
  52.7 1.2 tiles_second.1
  53.9 0.6 collective-permute-start.9
  54.5 2.0 %collective-permute-done.7.send = f32[4,7,64,256]{3,2,1,0:T(8,128)S(1)} collective-permute-done((f32[4,7,64,256]{3,2,1,0:T(8,128)S(1)}, f32[4,7,64,256]{3,2,1,0:T(8,128)S(1)}, u32[]{:S(2)}, u32[]{:S(2)}) %collective-permute-start.7) | collective-permute-done | bytes 1835040 | tf_op jit(solution)/shard_map/ppermute | solution.py:213
  56.5 0.2 sum_core.2
  56.7 0.6 collective-permute-start.8
  57.3 1.5 %collective-permute-start.10 = (f32[2,3,64,256]{3,2,1,0:T(8,128)S(1)}, f32[2,3,64,256]{3,2,1,0:T(8,128)S(1)}, u32[]{:S(2)}, u32[]{:S(2)}) collective-permute-start(f32[2,3,64,256]{3,2,1,0:T(8,128)S(1)} %get-tuple-element.72), channel_id=1, source_target_pairs={{0,2},{2,0},{1,3},{3,1},{4,6},{6,4},{5,7},{7,5},{8,10},{10,8},{9,1... | collective-permute-start | bytes 1179656 | tf_op jit(solution)/shard_map/ppermute | solution.py:213
  58.8 0.0 collective-permute-done.9.send
  58.8 0.1 sum_core.3
  58.8 9.3 %collective-permute-done.10.right = f32[2,3,64,256]{3,2,1,0:T(8,128)S(1)} collective-permute-done((f32[2,3,64,256]{3,2,1,0:T(8,128)S(1)}, f32[2,3,64,256]{3,2,1,0:T(8,128)S(1)}, u32[]{:S(2)}, u32[]{:S(2)}) %collective-permute-start.10) | collective-permute-done | bytes 393248 | tf_op jit(solution)/shard_map/ppermute | solution.py:213
  68.2 2.5 %collective-permute-done.8.right = f32[2,4,64,256]{3,2,1,0:T(8,128)S(1)} collective-permute-done((f32[2,4,64,256]{3,2,1,0:T(8,128)S(1)}, f32[2,4,64,256]{3,2,1,0:T(8,128)S(1)}, u32[]{:S(2)}, u32[]{:S(2)}) %collective-permute-start.8) | collective-permute-done | bytes 524320 | tf_op jit(solution)/shard_map/ppermute | solution.py:213
  70.7 0.1 sum_z.3
  70.8 0.0 copy-start.1
  70.8 1.6 %collective-permute-start.11 = (f32[8,64,256]{2,1,0:T(8,128)S(1)}, f32[8,64,256]{2,1,0:T(8,128)S(1)}, u32[]{:S(2)}, u32[]{:S(2)}) collective-permute-start(f32[8,64,256]{2,1,0:T(8,128)S(1)} %get-tuple-element.81), channel_id=1, source_target_pairs={{0,2},{2,0},{1,3},{3,1},{4,6},{6,4},{5,7},{7,5},{8,10},{10,8},{9,1... | collective-permute-start | bytes 1572872 | tf_op jit(solution)/shard_map/ppermute | solution.py:213
  72.3 0.6 collective-permute-start.12
  72.9 5.3 %collective-permute-done.12.right = f32[3,64,256]{2,1,0:T(8,128)S(1)} collective-permute-done((f32[3,64,256]{2,1,0:T(8,128)S(1)}, f32[3,64,256]{2,1,0:T(8,128)S(1)}, u32[]{:S(2)}, u32[]{:S(2)}) %collective-permute-start.12) | collective-permute-done | bytes 196640 | tf_op jit(solution)/shard_map/ppermute | solution.py:213
  78.2 5.8 %collective-permute-done.11.refs_0_ = f32[8,64,256]{2,1,0:T(8,128)S(1)} collective-permute-done((f32[8,64,256]{2,1,0:T(8,128)S(1)}, f32[8,64,256]{2,1,0:T(8,128)S(1)}, u32[]{:S(2)}, u32[]{:S(2)}) %collective-permute-start.11) | collective-permute-done | bytes 524320 | tf_op jit(solution)/shard_map/ppermute | solution.py:213
  84.0 0.1 sum_x.3
  84.0 1.5 %collective-permute-start.16 = (f32[4,64,256]{2,1,0:T(8,128)S(1)}, f32[4,64,256]{2,1,0:T(8,128)S(1)}, u32[]{:S(2)}, u32[]{:S(2)}) collective-permute-start(f32[4,64,256]{2,1,0:T(8,128)S(1)} %get-tuple-element.95.refs_0_), channel_id=1, source_target_pairs={{0,16},{8,24},{16,0},{24,8},{1,17},{9,25},{17,1},{25,9},{2,18},{10... | collective-permute-start | bytes 786440 | tf_op jit(solution)/shard_map/ppermute | solution.py:213
  85.5 1.5 %collective-permute-start.14 = (f32[3,64,256]{2,1,0:T(8,128)S(1)}, f32[3,64,256]{2,1,0:T(8,128)S(1)}, u32[]{:S(2)}, u32[]{:S(2)}) collective-permute-start(f32[3,64,256]{2,1,0:T(8,128)S(1)} %sum_z.4.left), channel_id=1, source_target_pairs={{0,16},{8,24},{16,0},{24,8},{1,17},{9,25},{17,1},{25,9},{2,18},{10... | collective-permute-start | bytes 589832 | tf_op jit(solution)/shard_map/ppermute | solution.py:213
  87.0 0.6 collective-permute-start.13
  87.6 18.0 %collective-permute-done.14.right = f32[3,64,256]{2,1,0:T(8,128)S(1)} collective-permute-done((f32[3,64,256]{2,1,0:T(8,128)S(1)}, f32[3,64,256]{2,1,0:T(8,128)S(1)}, u32[]{:S(2)}, u32[]{:S(2)}) %collective-permute-start.14) | collective-permute-done | bytes 196640 | tf_op jit(solution)/shard_map/ppermute | solution.py:213
  105.7 0.0 collective-permute-done.13.right
  105.7 0.0 collective-permute-done.16.refs_1_
  105.7 0.4 finish.2.refs_0_
  106.1 0.5 collective-permute-start.22
  106.6 3.4 %collective-permute-start.15 = (f32[2,64,256]{2,1,0:T(8,128)S(1)}, f32[2,64,256]{2,1,0:T(8,128)S(1)}, u32[]{:S(2)}, u32[]{:S(2)}) collective-permute-start(f32[2,64,256]{2,1,0:T(8,128)S(1)} %sum_z.5.refs_0_), channel_id=1, source_target_pairs={{0,16},{8,24},{16,0},{24,8},{1,17},{9,25},{17,1},{25,9},{2,18},{10... | collective-permute-start | bytes 393224 | tf_op jit(solution)/shard_map/ppermute | solution.py:213
  110.0 0.5 collective-permute-start.21
  110.5 0.1 collective-permute-start.20
  110.6 0.0 copy-done.1
  110.7 4.9 %collective-permute-done.15.refs_1_ = f32[2,64,256]{2,1,0:T(8,128)S(1)} collective-permute-done((f32[2,64,256]{2,1,0:T(8,128)S(1)}, f32[2,64,256]{2,1,0:T(8,128)S(1)}, u32[]{:S(2)}, u32[]{:S(2)}) %collective-permute-start.15) | collective-permute-done | bytes 131104 | tf_op jit(solution)/shard_map/ppermute | solution.py:213
  115.6 0.2 finish.3.refs_0_
  115.8 3.9 %collective-permute-start.19 = (s16[144,256]{1,0:T(8,128)(2,1)S(1)}, s16[144,256]{1,0:T(8,128)(2,1)S(1)}, u32[]{:S(2)}, u32[]{:S(2)}) collective-permute-start(s16[144,256]{1,0:T(8,128)(2,1)S(1)} %finish.3.refs_0_), channel_id=1, source_target_pairs={{0,12},{4,8},{8,4},{12,0},{16,28},{20,24},{24,20},{28,16},{1,13},{... | collective-permute-start | bytes 221192 | tf_op jit(solution)/shard_map/ppermute | solution.py:377
  119.6 0.5 collective-permute-start.18
  120.2 0.0 collective-permute-done.22.refs_3_
  120.2 0.1 collective-permute-start.17
  120.3 0.1 concatenate.6.scalars
  120.4 0.8 collective-permute-done.21.refs_2_
  121.2 2.5 %collective-permute-done.20.refs_1_ = s16[464,256]{1,0:T(8,128)(2,1)S(1)} collective-permute-done((s16[464,256]{1,0:T(8,128)(2,1)S(1)}, s16[464,256]{1,0:T(8,128)(2,1)S(1)}, u32[]{:S(2)}, u32[]{:S(2)}) %collective-permute-start.20) | collective-permute-done | bytes 237600 | tf_op jit(solution)/shard_map/ppermute | solution.py:213
  123.7 1.6 %place_tiles.2.refs_4_ = f32[10,64,256]{2,1,0:T(8,128)S(1)} custom-call(s32[60]{0:T(128)S(1)} %concatenate.6.scalars, s16[464,256]{1,0:T(8,128)(2,1)S(1)} %finish.2.refs_0_, s16[464,256]{1,0:T(8,128)(2,1)S(1)} %collective-permute-done.20.refs_1_, s16[464,256]{1,0:T(8,128)(2,1)S(1)} %collective-permute-done.21.refs_2_, ...), custom_call_target="tpu_custom_call" | custom-call | flops 163840 | tf_op jit(solution)/shard_map/place_tiles/pallas_call | solution.py:419
  125.3 0.0 collective-permute-done.19.refs_3_
  125.3 0.0 collective-permute-done.18.refs_2_
  125.3 0.6 collective-permute-done.17.refs_1_
  125.9 1.6 %place_tiles.3 = f32[10,64,256]{2,1,0:T(8,128)} custom-call(s32[60]{0:T(128)S(1)} %concatenate.6.scalars, s16[144,256]{1,0:T(8,128)(2,1)S(1)} %finish.3.refs_0_, s16[144,256]{1,0:T(8,128)(2,1)S(1)} %collective-permute-done.17.refs_1_, s16[144,256]{1,0:T(8,128)(2,1)S(1)} %collective-permute-done.18.refs_2_, ...), custom_call_target="tpu_custom_call" | custom-call | flops 163840 | tf_op jit(solution)/shard_map/place_tiles/pallas_call | solution.py:419
  (7 shorter events, 0.2 us)
Async XLA Ops:
  0.0 6.4 %copy-start = (bf16[3,256,1024]{2,1,0:T(8,128)(2,1)S(1)}, bf16[3,256,1024]{2,1,0:T(8,128)(2,1)}, u32[]{:S(2)}) copy-start(bf16[3,256,1024]{2,1,0:T(8,128)(2,1)} %param.3) | copy-start | bytes 4718596
  1.3 15.1 %collective-permute-start.2 = (bf16[3,256,256]{2,1,0:T(8,128)(2,1)S(1)}, bf16[3,256,256]{2,1,0:T(8,128)(2,1)S(1)}, u32[]{:S(2)}, u32[]{:S(2)}) collective-permute-start(bf16[3,256,256]{2,1,0:T(8,128)(2,1)S(1)} %get-tuple-element.118), channel_id=1, source_target_pairs={{0,24},{8,16},{16,8},{24,0},{1,25},{9,17},{17,9},{25,1},{2,26},{10... | collective-permute-start | bytes 1179656 | tf_op jit(solution)/shard_map/ppermute | solution.py:213
  6.4 18.7 %collective-permute-start = (bf16[3,256,256]{2,1,0:T(8,128)(2,1)S(1)}, bf16[3,256,256]{2,1,0:T(8,128)(2,1)S(1)}, u32[]{:S(2)}, u32[]{:S(2)}) collective-permute-start(bf16[3,256,256]{2,1,0:T(8,128)(2,1)S(1)} %get-tuple-element.119), channel_id=1, source_target_pairs={{0,8},{8,0},{16,24},{24,16},{1,9},{9,1},{17,25},{25,17},{2,10},{10... | collective-permute-start | bytes 1179656 | tf_op jit(solution)/shard_map/ppermute | solution.py:213
  6.5 33.4 %collective-permute-start.1 = (bf16[3,256,256]{2,1,0:T(8,128)(2,1)S(1)}, bf16[3,256,256]{2,1,0:T(8,128)(2,1)S(1)}, u32[]{:S(2)}, u32[]{:S(2)}) collective-permute-start(bf16[3,256,256]{2,1,0:T(8,128)(2,1)S(1)} %get-tuple-element.116), channel_id=1, source_target_pairs={{0,16},{8,24},{16,0},{24,8},{1,17},{9,25},{17,1},{25,9},{2,18},{10... | collective-permute-start | bytes 1179656 | tf_op jit(solution)/shard_map/ppermute | solution.py:213
  7.2 35.0 %collective-permute-start.3 = (bf16[3,256,256]{2,1,0:T(8,128)(2,1)S(1)}, bf16[3,256,256]{2,1,0:T(8,128)(2,1)S(1)}, u32[]{:S(2)}, u32[]{:S(2)}) collective-permute-start(bf16[3,256,256]{2,1,0:T(8,128)(2,1)S(1)} %get-tuple-element.117.refs_0_), channel_id=1, source_target_pairs={{0,4},{4,0},{1,5},{5,1},{2,6},{6,2},{3,7},{7,3},{8,12},{12,8},{9,1... | collective-permute-start | bytes 1179656 | tf_op jit(solution)/shard_map/ppermute | solution.py:213
  16.4 25.8 %collective-permute-start.6 = (bf16[3,256,256]{2,1,0:T(8,128)(2,1)S(1)}, bf16[3,256,256]{2,1,0:T(8,128)(2,1)S(1)}, u32[]{:S(2)}, u32[]{:S(2)}) collective-permute-start(bf16[3,256,256]{2,1,0:T(8,128)(2,1)S(1)} %collective-permute-done.2.refs_3_), channel_id=1, source_target_pairs={{0,4},{4,0},{1,5},{5,1},{2,6},{6,2},{3,7},{7,3},{8,12},{12,8},{9,1... | collective-permute-start | bytes 1179656 | tf_op jit(solution)/shard_map/ppermute | solution.py:213
  25.1 17.2 %collective-permute-start.4 = (bf16[3,256,256]{2,1,0:T(8,128)(2,1)S(1)}, bf16[3,256,256]{2,1,0:T(8,128)(2,1)S(1)}, u32[]{:S(2)}, u32[]{:S(2)}) collective-permute-start(bf16[3,256,256]{2,1,0:T(8,128)(2,1)S(1)} %collective-permute-done.refs_1_), channel_id=1, source_target_pairs={{0,4},{4,0},{1,5},{5,1},{2,6},{6,2},{3,7},{7,3},{8,12},{12,8},{9,1... | collective-permute-start | bytes 1179656 | tf_op jit(solution)/shard_map/ppermute | solution.py:213
  40.0 10.2 %collective-permute-start.5 = (bf16[3,256,256]{2,1,0:T(8,128)(2,1)S(1)}, bf16[3,256,256]{2,1,0:T(8,128)(2,1)S(1)}, u32[]{:S(2)}, u32[]{:S(2)}) collective-permute-start(bf16[3,256,256]{2,1,0:T(8,128)(2,1)S(1)} %collective-permute-done.1.refs_2_), channel_id=1, source_target_pairs={{0,4},{4,0},{1,5},{5,1},{2,6},{6,2},{3,7},{7,3},{8,12},{12,8},{9,1... | collective-permute-start | bytes 1179656 | tf_op jit(solution)/shard_map/ppermute | solution.py:213
  52.6 3.9 %collective-permute-start.7 = (f32[4,7,64,256]{3,2,1,0:T(8,128)S(1)}, f32[4,7,64,256]{3,2,1,0:T(8,128)S(1)}, u32[]{:S(2)}, u32[]{:S(2)}) collective-permute-start(f32[4,7,64,256]{3,2,1,0:T(8,128)S(1)} %get-tuple-element.60), channel_id=1, source_target_pairs={{0,1},{1,0},{2,3},{3,2},{4,5},{5,4},{6,7},{7,6},{8,9},{9,8},{10,11... | collective-permute-start | bytes 5505032 | tf_op jit(solution)/shard_map/ppermute | solution.py:213
  53.9 4.9 %collective-permute-start.9 = (f32[4,2,64,256]{3,2,1,0:T(8,128)S(1)}, f32[4,2,64,256]{3,2,1,0:T(8,128)S(1)}, u32[]{:S(2)}, u32[]{:S(2)}) collective-permute-start(f32[4,2,64,256]{3,2,1,0:T(8,128)S(1)} %get-tuple-element.67), channel_id=1, source_target_pairs={{0,1},{1,0},{2,3},{3,2},{4,5},{5,4},{6,7},{7,6},{8,9},{9,8},{10,11... | collective-permute-start | bytes 1572872 | tf_op jit(solution)/shard_map/ppermute | solution.py:213
  56.7 14.0 %collective-permute-start.8 = (f32[2,4,64,256]{3,2,1,0:T(8,128)S(1)}, f32[2,4,64,256]{3,2,1,0:T(8,128)S(1)}, u32[]{:S(2)}, u32[]{:S(2)}) collective-permute-start(f32[2,4,64,256]{3,2,1,0:T(8,128)S(1)} %get-tuple-element.64), channel_id=1, source_target_pairs={{0,8},{8,0},{16,24},{24,16},{1,9},{9,1},{17,25},{25,17},{2,10},{10... | collective-permute-start | bytes 1572872 | tf_op jit(solution)/shard_map/ppermute | solution.py:213
  57.3 10.9 %collective-permute-start.10 = (f32[2,3,64,256]{3,2,1,0:T(8,128)S(1)}, f32[2,3,64,256]{3,2,1,0:T(8,128)S(1)}, u32[]{:S(2)}, u32[]{:S(2)}) collective-permute-start(f32[2,3,64,256]{3,2,1,0:T(8,128)S(1)} %get-tuple-element.72), channel_id=1, source_target_pairs={{0,2},{2,0},{1,3},{3,1},{4,6},{6,4},{5,7},{7,5},{8,10},{10,8},{9,1... | collective-permute-start | bytes 1179656 | tf_op jit(solution)/shard_map/ppermute | solution.py:213
  70.8 39.8 %copy-start.1 = (s32[1,10,2]{1,2,0:T(2,128)S(1)}, s32[1,10,2]{1,2,0:T(2,128)}, u32[]{:S(2)}) copy-start(s32[1,10,2]{1,2,0:T(2,128)} %param.4) | copy-start | bytes 244
  70.8 13.2 %collective-permute-start.11 = (f32[8,64,256]{2,1,0:T(8,128)S(1)}, f32[8,64,256]{2,1,0:T(8,128)S(1)}, u32[]{:S(2)}, u32[]{:S(2)}) collective-permute-start(f32[8,64,256]{2,1,0:T(8,128)S(1)} %get-tuple-element.81), channel_id=1, source_target_pairs={{0,2},{2,0},{1,3},{3,1},{4,6},{6,4},{5,7},{7,5},{8,10},{10,8},{9,1... | collective-permute-start | bytes 1572872 | tf_op jit(solution)/shard_map/ppermute | solution.py:213
  72.3 5.8 %collective-permute-start.12 = (f32[3,64,256]{2,1,0:T(8,128)S(1)}, f32[3,64,256]{2,1,0:T(8,128)S(1)}, u32[]{:S(2)}, u32[]{:S(2)}) collective-permute-start(f32[3,64,256]{2,1,0:T(8,128)S(1)} %get-tuple-element.82), channel_id=1, source_target_pairs={{0,8},{8,0},{16,24},{24,16},{1,9},{9,1},{17,25},{25,17},{2,10},{10... | collective-permute-start | bytes 589832 | tf_op jit(solution)/shard_map/ppermute | solution.py:213
  84.0 21.7 %collective-permute-start.16 = (f32[4,64,256]{2,1,0:T(8,128)S(1)}, f32[4,64,256]{2,1,0:T(8,128)S(1)}, u32[]{:S(2)}, u32[]{:S(2)}) collective-permute-start(f32[4,64,256]{2,1,0:T(8,128)S(1)} %get-tuple-element.95.refs_0_), channel_id=1, source_target_pairs={{0,16},{8,24},{16,0},{24,8},{1,17},{9,25},{17,1},{25,9},{2,18},{10... | collective-permute-start | bytes 786440 | tf_op jit(solution)/shard_map/ppermute | solution.py:213
  85.5 20.2 %collective-permute-start.14 = (f32[3,64,256]{2,1,0:T(8,128)S(1)}, f32[3,64,256]{2,1,0:T(8,128)S(1)}, u32[]{:S(2)}, u32[]{:S(2)}) collective-permute-start(f32[3,64,256]{2,1,0:T(8,128)S(1)} %sum_z.4.left), channel_id=1, source_target_pairs={{0,16},{8,24},{16,0},{24,8},{1,17},{9,25},{17,1},{25,9},{2,18},{10... | collective-permute-start | bytes 589832 | tf_op jit(solution)/shard_map/ppermute | solution.py:213
  87.0 18.6 %collective-permute-start.13 = (f32[2,64,256]{2,1,0:T(8,128)S(1)}, f32[2,64,256]{2,1,0:T(8,128)S(1)}, u32[]{:S(2)}, u32[]{:S(2)}) collective-permute-start(f32[2,64,256]{2,1,0:T(8,128)S(1)} %get-tuple-element.89), channel_id=1, source_target_pairs={{0,8},{8,0},{16,24},{24,16},{1,9},{9,1},{17,25},{25,17},{2,10},{10... | collective-permute-start | bytes 393224 | tf_op jit(solution)/shard_map/ppermute | solution.py:213
  106.1 14.1 %collective-permute-start.22 = (s16[464,256]{1,0:T(8,128)(2,1)S(1)}, s16[464,256]{1,0:T(8,128)(2,1)S(1)}, u32[]{:S(2)}, u32[]{:S(2)}) collective-permute-start(s16[464,256]{1,0:T(8,128)(2,1)S(1)} %finish.2.refs_0_), channel_id=1, source_target_pairs={{0,12},{4,8},{8,4},{12,0},{16,28},{20,24},{24,20},{28,16},{1,13},{... | collective-permute-start | bytes 712712 | tf_op jit(solution)/shard_map/ppermute | solution.py:377
  106.6 9.0 %collective-permute-start.15 = (f32[2,64,256]{2,1,0:T(8,128)S(1)}, f32[2,64,256]{2,1,0:T(8,128)S(1)}, u32[]{:S(2)}, u32[]{:S(2)}) collective-permute-start(f32[2,64,256]{2,1,0:T(8,128)S(1)} %sum_z.5.refs_0_), channel_id=1, source_target_pairs={{0,16},{8,24},{16,0},{24,8},{1,17},{9,25},{17,1},{25,9},{2,18},{10... | collective-permute-start | bytes 393224 | tf_op jit(solution)/shard_map/ppermute | solution.py:213
  110.0 11.2 %collective-permute-start.21 = (s16[464,256]{1,0:T(8,128)(2,1)S(1)}, s16[464,256]{1,0:T(8,128)(2,1)S(1)}, u32[]{:S(2)}, u32[]{:S(2)}) collective-permute-start(s16[464,256]{1,0:T(8,128)(2,1)S(1)} %finish.2.refs_0_), channel_id=1, source_target_pairs={{0,4},{4,0},{1,5},{5,1},{2,6},{6,2},{3,7},{7,3},{8,12},{12,8},{9,1... | collective-permute-start | bytes 712712 | tf_op jit(solution)/shard_map/ppermute | solution.py:213
  110.5 13.2 %collective-permute-start.20 = (s16[464,256]{1,0:T(8,128)(2,1)S(1)}, s16[464,256]{1,0:T(8,128)(2,1)S(1)}, u32[]{:S(2)}, u32[]{:S(2)}) collective-permute-start(s16[464,256]{1,0:T(8,128)(2,1)S(1)} %finish.2.refs_0_), channel_id=1, source_target_pairs={{0,8},{8,0},{16,24},{24,16},{1,9},{9,1},{17,25},{25,17},{2,10},{10... | collective-permute-start | bytes 712712 | tf_op jit(solution)/shard_map/ppermute | solution.py:213
  115.8 9.5 %collective-permute-start.19 = (s16[144,256]{1,0:T(8,128)(2,1)S(1)}, s16[144,256]{1,0:T(8,128)(2,1)S(1)}, u32[]{:S(2)}, u32[]{:S(2)}) collective-permute-start(s16[144,256]{1,0:T(8,128)(2,1)S(1)} %finish.3.refs_0_), channel_id=1, source_target_pairs={{0,12},{4,8},{8,4},{12,0},{16,28},{20,24},{24,20},{28,16},{1,13},{... | collective-permute-start | bytes 221192 | tf_op jit(solution)/shard_map/ppermute | solution.py:377
  119.6 5.7 %collective-permute-start.18 = (s16[144,256]{1,0:T(8,128)(2,1)S(1)}, s16[144,256]{1,0:T(8,128)(2,1)S(1)}, u32[]{:S(2)}, u32[]{:S(2)}) collective-permute-start(s16[144,256]{1,0:T(8,128)(2,1)S(1)} %finish.3.refs_0_), channel_id=1, source_target_pairs={{0,4},{4,0},{1,5},{5,1},{2,6},{6,2},{3,7},{7,3},{8,12},{12,8},{9,1... | collective-permute-start | bytes 221192 | tf_op jit(solution)/shard_map/ppermute | solution.py:213
  120.2 5.8 %collective-permute-start.17 = (s16[144,256]{1,0:T(8,128)(2,1)S(1)}, s16[144,256]{1,0:T(8,128)(2,1)S(1)}, u32[]{:S(2)}, u32[]{:S(2)}) collective-permute-start(s16[144,256]{1,0:T(8,128)(2,1)S(1)} %finish.3.refs_0_), channel_id=1, source_target_pairs={{0,8},{8,0},{16,24},{24,16},{1,9},{9,1},{17,25},{25,17},{2,10},{10... | collective-permute-start | bytes 221192 | tf_op jit(solution)/shard_map/ppermute | solution.py:213

commit v17 on v13

--- a/solution.py
+++ b/solution.py
@@ -10,6 +10,7 @@
 from jax.sharding import Mesh, PartitionSpec as P
 
 UNROLL = 4
+UNROLL_SLOTS = 10
 VMEM_LIMIT = 24 * 2**20
 GROUPS = 3
 BATCHES = ((0, 1), (2,))
@@ -170,7 +171,7 @@
 
         return carry
 
-    lax.fori_loop(0, slots, one_slot, 0)
+    lax.fori_loop(0, slots, one_slot, 0, unroll=slots <= UNROLL_SLOTS)
 
 
 def per_device(z_count, y_count, x_count, core_count, snapshots, tile_table):

time: 117 us -> 116 us (level)
  no operation moved by 1% of the time
where the time goes in v17:
time: 116 us
  waiting for transfers between devices  77.8 us (67%)
  starting transfers between devices  28.7 us (25%)
  Pallas kernels  7.19 us (6%)
  local copies, waits for them, and re-layouts  2.25 us (2%)
    ppermute x22, waiting for transfers between devices, swap(): return lax.ppermute(value, axis, [(i, i ^ bits) for i in range(size)])  75.7 us
    ppermute x22, starting transfers between devices, swap(): return lax.ppermute(value, axis, [(i, i ^ bits) for i in range(size)])  26 us
    pallas_call x2, Pallas kernels, call(): pl.pallas_call(kernel, out_shape=out_shape, in_specs=[pl.BlockSpec(memory...  3.68 us
    ppermute x2, starting transfers between devices, to_owners(): over_both = lax.ppermute(value, ('z', 'y'), both)  2.66 us
    pallas_call x2, Pallas kernels, per_device(): pl.pallas_call(functools.partial(place_kernel, scale_factor / (CODE_TOP *...  2.47 us
  transfers between devices with their start and end apart: 24, of which 17 were waited for; matrix products, arithmetic and copies ran while one was open for 1% of the time, Pallas kernels for 3%

profile of v17, /device:TPU:0, one launch (start us, length us, event | category | flops | bytes accessed | tf_op | source)
XLA Modules:
  0.0 116.1 jit_solution(2312602619200457414)
XLA Ops:
  0.0 1.3 %constant_dynamic-slice_fusion.2 = (bf16[3,256,256]{2,1,0:T(8,128)(2,1)S(1)}, bf16[3,256,256]{2,1,0:T(8,128)(2,1)S(1)}) fusion(bf16[3,256,1024]{2,1,0:T(8,128)(2,1)} %param.3, s32[]{:T(128)S(6)} %select_n.112, s32[]{:T(128)S(6)} %select_n.111), kind=kLoop, calls=%fused_computation.14 | loop fusion | bytes 1572872 | tf_op jit(solution)/shard_map/dynamic_slice | solution.py:212
  1.3 5.1 %collective-permute-start.2 = (bf16[3,256,256]{2,1,0:T(8,128)(2,1)S(1)}, bf16[3,256,256]{2,1,0:T(8,128)(2,1)S(1)}, u32[]{:S(2)}, u32[]{:S(2)}) collective-permute-start(bf16[3,256,256]{2,1,0:T(8,128)(2,1)S(1)} %get-tuple-element.118), channel_id=1, source_target_pairs={{0,24},{8,16},{16,8},{24,0},{1,25},{9,17},{17,9},{25,1},{2,26},{10... | collective-permute-start | bytes 1179656 | tf_op jit(solution)/shard_map/ppermute | solution.py:189
  6.4 0.0 collective-permute-start
  6.4 0.0 copy-done
  6.4 0.1 constant_dynamic-slice_fusion
  6.5 0.7 collective-permute-start.1
  7.2 1.7 %collective-permute-start.3 = (bf16[3,256,256]{2,1,0:T(8,128)(2,1)S(1)}, bf16[3,256,256]{2,1,0:T(8,128)(2,1)S(1)}, u32[]{:S(2)}, u32[]{:S(2)}) collective-permute-start(bf16[3,256,256]{2,1,0:T(8,128)(2,1)S(1)} %get-tuple-element.117.refs_0_), channel_id=1, source_target_pairs={{0,4},{4,0},{1,5},{5,1},{2,6},{6,2},{3,7},{7,3},{8,12},{12,8},{9,1... | collective-permute-start | bytes 1179656 | tf_op jit(solution)/shard_map/ppermute | solution.py:189
  8.9 7.6 %collective-permute-done.2.refs_3_ = bf16[3,256,256]{2,1,0:T(8,128)(2,1)S(1)} collective-permute-done((bf16[3,256,256]{2,1,0:T(8,128)(2,1)S(1)}, bf16[3,256,256]{2,1,0:T(8,128)(2,1)S(1)}, u32[]{:S(2)}, u32[]{:S(2)}) %collective-permute-start.2) | collective-permute-done | bytes 393248 | tf_op jit(solution)/shard_map/ppermute | solution.py:189
  16.4 1.7 %collective-permute-start.6 = (bf16[3,256,256]{2,1,0:T(8,128)(2,1)S(1)}, bf16[3,256,256]{2,1,0:T(8,128)(2,1)S(1)}, u32[]{:S(2)}, u32[]{:S(2)}) collective-permute-start(bf16[3,256,256]{2,1,0:T(8,128)(2,1)S(1)} %collective-permute-done.2.refs_3_), channel_id=1, source_target_pairs={{0,4},{4,0},{1,5},{5,1},{2,6},{6,2},{3,7},{7,3},{8,12},{12,8},{9,1... | collective-permute-start | bytes 1179656 | tf_op jit(solution)/shard_map/ppermute | solution.py:189
  18.2 6.9 %collective-permute-done.refs_1_ = bf16[3,256,256]{2,1,0:T(8,128)(2,1)S(1)} collective-permute-done((bf16[3,256,256]{2,1,0:T(8,128)(2,1)S(1)}, bf16[3,256,256]{2,1,0:T(8,128)(2,1)S(1)}, u32[]{:S(2)}, u32[]{:S(2)}) %collective-permute-start) | collective-permute-done | bytes 393248 | tf_op jit(solution)/shard_map/ppermute | solution.py:189
  25.1 1.4 %collective-permute-start.4 = (bf16[3,256,256]{2,1,0:T(8,128)(2,1)S(1)}, bf16[3,256,256]{2,1,0:T(8,128)(2,1)S(1)}, u32[]{:S(2)}, u32[]{:S(2)}) collective-permute-start(bf16[3,256,256]{2,1,0:T(8,128)(2,1)S(1)} %collective-permute-done.refs_1_), channel_id=1, source_target_pairs={{0,4},{4,0},{1,5},{5,1},{2,6},{6,2},{3,7},{7,3},{8,12},{12,8},{9,1... | collective-permute-start | bytes 1179656 | tf_op jit(solution)/shard_map/ppermute | solution.py:189
  26.5 13.5 %collective-permute-done.1.refs_2_ = bf16[3,256,256]{2,1,0:T(8,128)(2,1)S(1)} collective-permute-done((bf16[3,256,256]{2,1,0:T(8,128)(2,1)S(1)}, bf16[3,256,256]{2,1,0:T(8,128)(2,1)S(1)}, u32[]{:S(2)}, u32[]{:S(2)}) %collective-permute-start.1) | collective-permute-done | bytes 393248 | tf_op jit(solution)/shard_map/ppermute | solution.py:189
  40.0 1.5 %collective-permute-start.5 = (bf16[3,256,256]{2,1,0:T(8,128)(2,1)S(1)}, bf16[3,256,256]{2,1,0:T(8,128)(2,1)S(1)}, u32[]{:S(2)}, u32[]{:S(2)}) collective-permute-start(bf16[3,256,256]{2,1,0:T(8,128)(2,1)S(1)} %collective-permute-done.1.refs_2_), channel_id=1, source_target_pairs={{0,4},{4,0},{1,5},{5,1},{2,6},{6,2},{3,7},{7,3},{8,12},{12,8},{9,1... | collective-permute-start | bytes 1179656 | tf_op jit(solution)/shard_map/ppermute | solution.py:189
  41.5 0.7 fusion.2
  42.2 0.1 concatenate.7.scalars
  42.2 0.0 collective-permute-done.3.refs_4_
  42.3 0.0 collective-permute-done.6.refs_7_
  42.3 0.0 collective-permute-done.4.refs_5_
  42.3 7.9 %collective-permute-done.5.refs_6_ = bf16[3,256,256]{2,1,0:T(8,128)(2,1)S(1)} collective-permute-done((bf16[3,256,256]{2,1,0:T(8,128)(2,1)S(1)}, bf16[3,256,256]{2,1,0:T(8,128)(2,1)S(1)}, u32[]{:S(2)}, u32[]{:S(2)}) %collective-permute-start.5) | collective-permute-done | bytes 393248 | tf_op jit(solution)/shard_map/ppermute | solution.py:189
  50.1 2.3 %tiles_first.1 = (bf16[8,256,768]{2,1,0:T(8,128)(2,1)S(1)}, f32[4,6,64,256]{3,2,1,0:T(8,128)S(1)}, f32[4,6,64,256]{3,2,1,0:T(8,128)S(1)}) custom-call(s32[40]{0:T(128)S(1)} %concatenate.7.scalars, bf16[3,256,256]{2,1,0:T(8,128)(2,1)S(1)} %get-tuple-element.117.refs_0_, bf16[3,256,256]{2,1,0:T(8,128)(2,1)S(1)} %collective-permute-done.refs_1_, ...), custom_call_target="tpu_custom_call" | custom-call | flops 1207959552 | tf_op jit(solution)/shard_map/tiles_first/pallas_call | solution.py:230
  52.4 0.1 collective-permute-start.8
  52.5 1.4 %tiles_second.1 = (f32[4,3,64,256]{3,2,1,0:T(8,128)S(1)}, f32[4,3,64,256]{3,2,1,0:T(8,128)S(1)}) custom-call(s32[40]{0:T(128)S(1)} %concatenate.7.scalars, bf16[8,256,768]{2,1,0:T(8,128)(2,1)S(1)} %get-tuple-element.59.blocks), custom_call_target="tpu_custom_call" | custom-call | flops 603979776 | tf_op jit(solution)/shard_map/tiles_second/pallas_call | solution.py:230
  53.9 0.6 collective-permute-start.7
  54.5 1.4 %collective-permute-done.8.send = f32[4,6,64,256]{3,2,1,0:T(8,128)S(1)} collective-permute-done((f32[4,6,64,256]{3,2,1,0:T(8,128)S(1)}, f32[4,6,64,256]{3,2,1,0:T(8,128)S(1)}, u32[]{:S(2)}, u32[]{:S(2)}) %collective-permute-start.8) | collective-permute-done | bytes 1572896 | tf_op jit(solution)/shard_map/ppermute | solution.py:189
  55.9 0.2 sum_core.2
  56.0 1.6 %collective-permute-start.9 = (f32[2,3,64,256]{3,2,1,0:T(8,128)S(1)}, f32[2,3,64,256]{3,2,1,0:T(8,128)S(1)}, u32[]{:S(2)}, u32[]{:S(2)}) collective-permute-start(f32[2,3,64,256]{3,2,1,0:T(8,128)S(1)} %get-tuple-element.67), channel_id=1, source_target_pairs={{0,2},{2,0},{1,3},{3,1},{4,6},{6,4},{5,7},{7,5},{8,10},{10,8},{9,1... | collective-permute-start | bytes 1179656 | tf_op jit(solution)/shard_map/ppermute | solution.py:189
  57.6 0.6 collective-permute-start.11
  58.2 9.1 %collective-permute-done.9.right = f32[2,3,64,256]{3,2,1,0:T(8,128)S(1)} collective-permute-done((f32[2,3,64,256]{3,2,1,0:T(8,128)S(1)}, f32[2,3,64,256]{3,2,1,0:T(8,128)S(1)}, u32[]{:S(2)}, u32[]{:S(2)}) %collective-permute-start.9) | collective-permute-done | bytes 393248 | tf_op jit(solution)/shard_map/ppermute | solution.py:189
  67.3 0.6 collective-permute-start.10
  67.9 0.5 collective-permute-done.11.right
  68.5 1.0 collective-permute-start.12
  69.5 3.9 %collective-permute-done.10.right = f32[3,64,256]{2,1,0:T(8,128)S(1)} collective-permute-done((f32[3,64,256]{2,1,0:T(8,128)S(1)}, f32[3,64,256]{2,1,0:T(8,128)S(1)}, u32[]{:S(2)}, u32[]{:S(2)}) %collective-permute-start.10) | collective-permute-done | bytes 196640 | tf_op jit(solution)/shard_map/ppermute | solution.py:189
  73.5 0.0 collective-permute-done.7.send
  73.5 0.1 sum_core.3
  73.6 0.7 collective-permute-done.12.right
  74.4 1.0 collective-permute-start.13
  75.4 2.3 %collective-permute-start.15 = (f32[3,64,256]{2,1,0:T(8,128)S(1)}, f32[3,64,256]{2,1,0:T(8,128)S(1)}, u32[]{:S(2)}, u32[]{:S(2)}) collective-permute-start(f32[3,64,256]{2,1,0:T(8,128)S(1)} %sum_z.4.left), channel_id=1, source_target_pairs={{0,16},{8,24},{16,0},{24,8},{1,17},{9,25},{17,1},{25,9},{2,18},{10... | collective-permute-start | bytes 589832 | tf_op jit(solution)/shard_map/ppermute | solution.py:189
  77.7 0.0 copy-start.1
  77.7 5.8 %collective-permute-done.13.right = f32[2,3,64,256]{3,2,1,0:T(8,128)S(1)} collective-permute-done((f32[2,3,64,256]{3,2,1,0:T(8,128)S(1)}, f32[2,3,64,256]{3,2,1,0:T(8,128)S(1)}, u32[]{:S(2)}, u32[]{:S(2)}) %collective-permute-start.13) | collective-permute-done | bytes 393248 | tf_op jit(solution)/shard_map/ppermute | solution.py:189
  83.5 1.1 collective-permute-start.14
  84.6 1.8 %collective-permute-start.17 = (f32[3,64,256]{2,1,0:T(8,128)S(1)}, f32[3,64,256]{2,1,0:T(8,128)S(1)}, u32[]{:S(2)}, u32[]{:S(2)}) collective-permute-start(f32[3,64,256]{2,1,0:T(8,128)S(1)} %sum_x.4.refs_0_), channel_id=1, source_target_pairs={{0,16},{8,24},{16,0},{24,8},{1,17},{9,25},{17,1},{25,9},{2,18},{10... | collective-permute-start | bytes 589832 | tf_op jit(solution)/shard_map/ppermute | solution.py:189
  86.4 0.0 collective-permute-done.15.right
  86.5 6.7 %collective-permute-done.14.right = f32[3,64,256]{2,1,0:T(8,128)S(1)} collective-permute-done((f32[3,64,256]{2,1,0:T(8,128)S(1)}, f32[3,64,256]{2,1,0:T(8,128)S(1)}, u32[]{:S(2)}, u32[]{:S(2)}) %collective-permute-start.14) | collective-permute-done | bytes 196640 | tf_op jit(solution)/shard_map/ppermute | solution.py:189
  93.1 0.1 collective-permute-start.16
  93.2 0.5 collective-permute-done.17.refs_1_
  93.8 0.3 finish.2.refs_0_
  94.1 2.6 %collective-permute-start.23 = (s16[400,256]{1,0:T(8,128)(2,1)S(1)}, s16[400,256]{1,0:T(8,128)(2,1)S(1)}, u32[]{:S(2)}, u32[]{:S(2)}) collective-permute-start(s16[400,256]{1,0:T(8,128)(2,1)S(1)} %finish.2.refs_0_), channel_id=1, source_target_pairs={{0,12},{4,8},{8,4},{12,0},{16,28},{20,24},{24,20},{28,16},{1,13},{... | collective-permute-start | bytes 614408 | tf_op jit(solution)/shard_map/ppermute | solution.py:344
  96.7 0.0 copy-done.1
  96.7 0.6 collective-permute-start.22
  97.3 0.5 collective-permute-start.21
  97.8 6.2 %collective-permute-done.16.refs_1_ = f32[3,64,256]{2,1,0:T(8,128)S(1)} collective-permute-done((f32[3,64,256]{2,1,0:T(8,128)S(1)}, f32[3,64,256]{2,1,0:T(8,128)S(1)}, u32[]{:S(2)}, u32[]{:S(2)}) %collective-permute-start.16) | collective-permute-done | bytes 196640 | tf_op jit(solution)/shard_map/ppermute | solution.py:189
  104.0 0.2 finish.3.refs_0_
  104.2 0.1 collective-permute-start.20
  104.3 1.6 %collective-permute-start.19 = (s16[208,256]{1,0:T(8,128)(2,1)S(1)}, s16[208,256]{1,0:T(8,128)(2,1)S(1)}, u32[]{:S(2)}, u32[]{:S(2)}) collective-permute-start(s16[208,256]{1,0:T(8,128)(2,1)S(1)} %finish.3.refs_0_), channel_id=1, source_target_pairs={{0,4},{4,0},{1,5},{5,1},{2,6},{6,2},{3,7},{7,3},{8,12},{12,8},{9,1... | collective-permute-start | bytes 319496 | tf_op jit(solution)/shard_map/ppermute | solution.py:189
  105.9 1.3 %collective-permute-done.23.refs_3_ = s16[400,256]{1,0:T(8,128)(2,1)S(1)} collective-permute-done((s16[400,256]{1,0:T(8,128)(2,1)S(1)}, s16[400,256]{1,0:T(8,128)(2,1)S(1)}, u32[]{:S(2)}, u32[]{:S(2)}) %collective-permute-start.23) | collective-permute-done | bytes 204832 | tf_op jit(solution)/shard_map/ppermute | solution.py:344
  107.2 0.6 collective-permute-start.18
  107.8 0.1 concatenate.6.scalars
  107.9 0.0 collective-permute-done.22.refs_2_
  107.9 3.8 %collective-permute-done.21.refs_1_ = s16[400,256]{1,0:T(8,128)(2,1)S(1)} collective-permute-done((s16[400,256]{1,0:T(8,128)(2,1)S(1)}, s16[400,256]{1,0:T(8,128)(2,1)S(1)}, u32[]{:S(2)}, u32[]{:S(2)}) %collective-permute-start.21) | collective-permute-done | bytes 204832 | tf_op jit(solution)/shard_map/ppermute | solution.py:189
  111.6 0.8 place_tiles.2.refs_4_
  112.5 0.9 collective-permute-done.20.refs_3_
  113.3 0.0 collective-permute-done.19.refs_2_
  113.3 1.2 %collective-permute-done.18.refs_1_ = s16[208,256]{1,0:T(8,128)(2,1)S(1)} collective-permute-done((s16[208,256]{1,0:T(8,128)(2,1)S(1)}, s16[208,256]{1,0:T(8,128)(2,1)S(1)}, u32[]{:S(2)}, u32[]{:S(2)}) %collective-permute-start.18) | collective-permute-done | bytes 106528 | tf_op jit(solution)/shard_map/ppermute | solution.py:189
  114.5 1.6 %place_tiles.3 = f32[10,64,256]{2,1,0:T(8,128)} custom-call(s32[60]{0:T(128)S(1)} %concatenate.6.scalars, s16[208,256]{1,0:T(8,128)(2,1)S(1)} %finish.3.refs_0_, s16[208,256]{1,0:T(8,128)(2,1)S(1)} %collective-permute-done.18.refs_1_, s16[208,256]{1,0:T(8,128)(2,1)S(1)} %collective-permute-done.19.refs_2_, ...), custom_call_target="tpu_custom_call" | custom-call | flops 163840 | tf_op jit(solution)/shard_map/place_tiles/pallas_call | solution.py:386
  (10 shorter events, 0.3 us)
Async XLA Ops:
  0.0 6.4 %copy-start = (bf16[3,256,1024]{2,1,0:T(8,128)(2,1)S(1)}, bf16[3,256,1024]{2,1,0:T(8,128)(2,1)}, u32[]{:S(2)}) copy-start(bf16[3,256,1024]{2,1,0:T(8,128)(2,1)} %param.3) | copy-start | bytes 4718596
  1.3 15.1 %collective-permute-start.2 = (bf16[3,256,256]{2,1,0:T(8,128)(2,1)S(1)}, bf16[3,256,256]{2,1,0:T(8,128)(2,1)S(1)}, u32[]{:S(2)}, u32[]{:S(2)}) collective-permute-start(bf16[3,256,256]{2,1,0:T(8,128)(2,1)S(1)} %get-tuple-element.118), channel_id=1, source_target_pairs={{0,24},{8,16},{16,8},{24,0},{1,25},{9,17},{17,9},{25,1},{2,26},{10... | collective-permute-start | bytes 1179656 | tf_op jit(solution)/shard_map/ppermute | solution.py:189
  6.4 18.7 %collective-permute-start = (bf16[3,256,256]{2,1,0:T(8,128)(2,1)S(1)}, bf16[3,256,256]{2,1,0:T(8,128)(2,1)S(1)}, u32[]{:S(2)}, u32[]{:S(2)}) collective-permute-start(bf16[3,256,256]{2,1,0:T(8,128)(2,1)S(1)} %get-tuple-element.119), channel_id=1, source_target_pairs={{0,8},{8,0},{16,24},{24,16},{1,9},{9,1},{17,25},{25,17},{2,10},{10... | collective-permute-start | bytes 1179656 | tf_op jit(solution)/shard_map/ppermute | solution.py:189
  6.5 33.4 %collective-permute-start.1 = (bf16[3,256,256]{2,1,0:T(8,128)(2,1)S(1)}, bf16[3,256,256]{2,1,0:T(8,128)(2,1)S(1)}, u32[]{:S(2)}, u32[]{:S(2)}) collective-permute-start(bf16[3,256,256]{2,1,0:T(8,128)(2,1)S(1)} %get-tuple-element.116), channel_id=1, source_target_pairs={{0,16},{8,24},{16,0},{24,8},{1,17},{9,25},{17,1},{25,9},{2,18},{10... | collective-permute-start | bytes 1179656 | tf_op jit(solution)/shard_map/ppermute | solution.py:189
  7.2 35.0 %collective-permute-start.3 = (bf16[3,256,256]{2,1,0:T(8,128)(2,1)S(1)}, bf16[3,256,256]{2,1,0:T(8,128)(2,1)S(1)}, u32[]{:S(2)}, u32[]{:S(2)}) collective-permute-start(bf16[3,256,256]{2,1,0:T(8,128)(2,1)S(1)} %get-tuple-element.117.refs_0_), channel_id=1, source_target_pairs={{0,4},{4,0},{1,5},{5,1},{2,6},{6,2},{3,7},{7,3},{8,12},{12,8},{9,1... | collective-permute-start | bytes 1179656 | tf_op jit(solution)/shard_map/ppermute | solution.py:189
  16.4 25.8 %collective-permute-start.6 = (bf16[3,256,256]{2,1,0:T(8,128)(2,1)S(1)}, bf16[3,256,256]{2,1,0:T(8,128)(2,1)S(1)}, u32[]{:S(2)}, u32[]{:S(2)}) collective-permute-start(bf16[3,256,256]{2,1,0:T(8,128)(2,1)S(1)} %collective-permute-done.2.refs_3_), channel_id=1, source_target_pairs={{0,4},{4,0},{1,5},{5,1},{2,6},{6,2},{3,7},{7,3},{8,12},{12,8},{9,1... | collective-permute-start | bytes 1179656 | tf_op jit(solution)/shard_map/ppermute | solution.py:189
  25.1 17.2 %collective-permute-start.4 = (bf16[3,256,256]{2,1,0:T(8,128)(2,1)S(1)}, bf16[3,256,256]{2,1,0:T(8,128)(2,1)S(1)}, u32[]{:S(2)}, u32[]{:S(2)}) collective-permute-start(bf16[3,256,256]{2,1,0:T(8,128)(2,1)S(1)} %collective-permute-done.refs_1_), channel_id=1, source_target_pairs={{0,4},{4,0},{1,5},{5,1},{2,6},{6,2},{3,7},{7,3},{8,12},{12,8},{9,1... | collective-permute-start | bytes 1179656 | tf_op jit(solution)/shard_map/ppermute | solution.py:189
  40.0 10.2 %collective-permute-start.5 = (bf16[3,256,256]{2,1,0:T(8,128)(2,1)S(1)}, bf16[3,256,256]{2,1,0:T(8,128)(2,1)S(1)}, u32[]{:S(2)}, u32[]{:S(2)}) collective-permute-start(bf16[3,256,256]{2,1,0:T(8,128)(2,1)S(1)} %collective-permute-done.1.refs_2_), channel_id=1, source_target_pairs={{0,4},{4,0},{1,5},{5,1},{2,6},{6,2},{3,7},{7,3},{8,12},{12,8},{9,1... | collective-permute-start | bytes 1179656 | tf_op jit(solution)/shard_map/ppermute | solution.py:189
  52.4 3.5 %collective-permute-start.8 = (f32[4,6,64,256]{3,2,1,0:T(8,128)S(1)}, f32[4,6,64,256]{3,2,1,0:T(8,128)S(1)}, u32[]{:S(2)}, u32[]{:S(2)}) collective-permute-start(f32[4,6,64,256]{3,2,1,0:T(8,128)S(1)} %get-tuple-element.63), channel_id=1, source_target_pairs={{0,1},{1,0},{2,3},{3,2},{4,5},{5,4},{6,7},{7,6},{8,9},{9,8},{10,11... | collective-permute-start | bytes 4718600 | tf_op jit(solution)/shard_map/ppermute | solution.py:189
  53.9 19.6 %collective-permute-start.7 = (f32[4,3,64,256]{3,2,1,0:T(8,128)S(1)}, f32[4,3,64,256]{3,2,1,0:T(8,128)S(1)}, u32[]{:S(2)}, u32[]{:S(2)}) collective-permute-start(f32[4,3,64,256]{3,2,1,0:T(8,128)S(1)} %get-tuple-element.61), channel_id=1, source_target_pairs={{0,1},{1,0},{2,3},{3,2},{4,5},{5,4},{6,7},{7,6},{8,9},{9,8},{10,11... | collective-permute-start | bytes 2359304 | tf_op jit(solution)/shard_map/ppermute | solution.py:189
  56.0 11.2 %collective-permute-start.9 = (f32[2,3,64,256]{3,2,1,0:T(8,128)S(1)}, f32[2,3,64,256]{3,2,1,0:T(8,128)S(1)}, u32[]{:S(2)}, u32[]{:S(2)}) collective-permute-start(f32[2,3,64,256]{3,2,1,0:T(8,128)S(1)} %get-tuple-element.67), channel_id=1, source_target_pairs={{0,2},{2,0},{1,3},{3,1},{4,6},{6,4},{5,7},{7,5},{8,10},{10,8},{9,1... | collective-permute-start | bytes 1179656 | tf_op jit(solution)/shard_map/ppermute | solution.py:189
  57.6 10.9 %collective-permute-start.11 = (f32[2,3,64,256]{3,2,1,0:T(8,128)S(1)}, f32[2,3,64,256]{3,2,1,0:T(8,128)S(1)}, u32[]{:S(2)}, u32[]{:S(2)}) collective-permute-start(f32[2,3,64,256]{3,2,1,0:T(8,128)S(1)} %get-tuple-element.73), channel_id=1, source_target_pairs={{0,8},{8,0},{16,24},{24,16},{1,9},{9,1},{17,25},{25,17},{2,10},{10... | collective-permute-start | bytes 1179656 | tf_op jit(solution)/shard_map/ppermute | solution.py:189
  67.3 6.2 %collective-permute-start.10 = (f32[3,64,256]{2,1,0:T(8,128)S(1)}, f32[3,64,256]{2,1,0:T(8,128)S(1)}, u32[]{:S(2)}, u32[]{:S(2)}) collective-permute-start(f32[3,64,256]{2,1,0:T(8,128)S(1)} %get-tuple-element.72), channel_id=1, source_target_pairs={{0,8},{8,0},{16,24},{24,16},{1,9},{9,1},{17,25},{25,17},{2,10},{10... | collective-permute-start | bytes 589832 | tf_op jit(solution)/shard_map/ppermute | solution.py:189
  68.5 5.9 %collective-permute-start.12 = (f32[3,64,256]{2,1,0:T(8,128)S(1)}, f32[3,64,256]{2,1,0:T(8,128)S(1)}, u32[]{:S(2)}, u32[]{:S(2)}) collective-permute-start(f32[3,64,256]{2,1,0:T(8,128)S(1)} %get-tuple-element.83), channel_id=1, source_target_pairs={{0,2},{2,0},{1,3},{3,1},{4,6},{6,4},{5,7},{7,5},{8,10},{10,8},{9,1... | collective-permute-start | bytes 589832 | tf_op jit(solution)/shard_map/ppermute | solution.py:189
  74.4 9.1 %collective-permute-start.13 = (f32[2,3,64,256]{3,2,1,0:T(8,128)S(1)}, f32[2,3,64,256]{3,2,1,0:T(8,128)S(1)}, u32[]{:S(2)}, u32[]{:S(2)}) collective-permute-start(f32[2,3,64,256]{3,2,1,0:T(8,128)S(1)} %get-tuple-element.84), channel_id=1, source_target_pairs={{0,2},{2,0},{1,3},{3,1},{4,6},{6,4},{5,7},{7,5},{8,10},{10,8},{9,1... | collective-permute-start | bytes 1179656 | tf_op jit(solution)/shard_map/ppermute | solution.py:189
  75.4 11.0 %collective-permute-start.15 = (f32[3,64,256]{2,1,0:T(8,128)S(1)}, f32[3,64,256]{2,1,0:T(8,128)S(1)}, u32[]{:S(2)}, u32[]{:S(2)}) collective-permute-start(f32[3,64,256]{2,1,0:T(8,128)S(1)} %sum_z.4.left), channel_id=1, source_target_pairs={{0,16},{8,24},{16,0},{24,8},{1,17},{9,25},{17,1},{25,9},{2,18},{10... | collective-permute-start | bytes 589832 | tf_op jit(solution)/shard_map/ppermute | solution.py:189
  77.7 19.0 %copy-start.1 = (s32[1,10,2]{1,2,0:T(2,128)S(1)}, s32[1,10,2]{1,2,0:T(2,128)}, u32[]{:S(2)}) copy-start(s32[1,10,2]{1,2,0:T(2,128)} %param.4) | copy-start | bytes 244
  83.5 9.6 %collective-permute-start.14 = (f32[3,64,256]{2,1,0:T(8,128)S(1)}, f32[3,64,256]{2,1,0:T(8,128)S(1)}, u32[]{:S(2)}, u32[]{:S(2)}) collective-permute-start(f32[3,64,256]{2,1,0:T(8,128)S(1)} %get-tuple-element.90), channel_id=1, source_target_pairs={{0,8},{8,0},{16,24},{24,16},{1,9},{9,1},{17,25},{25,17},{2,10},{10... | collective-permute-start | bytes 589832 | tf_op jit(solution)/shard_map/ppermute | solution.py:189
  84.6 9.2 %collective-permute-start.17 = (f32[3,64,256]{2,1,0:T(8,128)S(1)}, f32[3,64,256]{2,1,0:T(8,128)S(1)}, u32[]{:S(2)}, u32[]{:S(2)}) collective-permute-start(f32[3,64,256]{2,1,0:T(8,128)S(1)} %sum_x.4.refs_0_), channel_id=1, source_target_pairs={{0,16},{8,24},{16,0},{24,8},{1,17},{9,25},{17,1},{25,9},{2,18},{10... | collective-permute-start | bytes 589832 | tf_op jit(solution)/shard_map/ppermute | solution.py:189
  93.1 10.8 %collective-permute-start.16 = (f32[3,64,256]{2,1,0:T(8,128)S(1)}, f32[3,64,256]{2,1,0:T(8,128)S(1)}, u32[]{:S(2)}, u32[]{:S(2)}) collective-permute-start(f32[3,64,256]{2,1,0:T(8,128)S(1)} %sum_z.5.refs_0_), channel_id=1, source_target_pairs={{0,16},{8,24},{16,0},{24,8},{1,17},{9,25},{17,1},{25,9},{2,18},{10... | collective-permute-start | bytes 589832 | tf_op jit(solution)/shard_map/ppermute | solution.py:189
  94.1 13.1 %collective-permute-start.23 = (s16[400,256]{1,0:T(8,128)(2,1)S(1)}, s16[400,256]{1,0:T(8,128)(2,1)S(1)}, u32[]{:S(2)}, u32[]{:S(2)}) collective-permute-start(s16[400,256]{1,0:T(8,128)(2,1)S(1)} %finish.2.refs_0_), channel_id=1, source_target_pairs={{0,12},{4,8},{8,4},{12,0},{16,28},{20,24},{24,20},{28,16},{1,13},{... | collective-permute-start | bytes 614408 | tf_op jit(solution)/shard_map/ppermute | solution.py:344
  96.7 11.1 %collective-permute-start.22 = (s16[400,256]{1,0:T(8,128)(2,1)S(1)}, s16[400,256]{1,0:T(8,128)(2,1)S(1)}, u32[]{:S(2)}, u32[]{:S(2)}) collective-permute-start(s16[400,256]{1,0:T(8,128)(2,1)S(1)} %finish.2.refs_0_), channel_id=1, source_target_pairs={{0,4},{4,0},{1,5},{5,1},{2,6},{6,2},{3,7},{7,3},{8,12},{12,8},{9,1... | collective-permute-start | bytes 614408 | tf_op jit(solution)/shard_map/ppermute | solution.py:189
  97.3 14.3 %collective-permute-start.21 = (s16[400,256]{1,0:T(8,128)(2,1)S(1)}, s16[400,256]{1,0:T(8,128)(2,1)S(1)}, u32[]{:S(2)}, u32[]{:S(2)}) collective-permute-start(s16[400,256]{1,0:T(8,128)(2,1)S(1)} %finish.2.refs_0_), channel_id=1, source_target_pairs={{0,8},{8,0},{16,24},{24,16},{1,9},{9,1},{17,25},{25,17},{2,10},{10... | collective-permute-start | bytes 614408 | tf_op jit(solution)/shard_map/ppermute | solution.py:189
  104.2 9.1 %collective-permute-start.20 = (s16[208,256]{1,0:T(8,128)(2,1)S(1)}, s16[208,256]{1,0:T(8,128)(2,1)S(1)}, u32[]{:S(2)}, u32[]{:S(2)}) collective-permute-start(s16[208,256]{1,0:T(8,128)(2,1)S(1)} %finish.3.refs_0_), channel_id=1, source_target_pairs={{0,12},{4,8},{8,4},{12,0},{16,28},{20,24},{24,20},{28,16},{1,13},{... | collective-permute-start | bytes 319496 | tf_op jit(solution)/shard_map/ppermute | solution.py:344
  104.3 9.0 %collective-permute-start.19 = (s16[208,256]{1,0:T(8,128)(2,1)S(1)}, s16[208,256]{1,0:T(8,128)(2,1)S(1)}, u32[]{:S(2)}, u32[]{:S(2)}) collective-permute-start(s16[208,256]{1,0:T(8,128)(2,1)S(1)} %finish.3.refs_0_), channel_id=1, source_target_pairs={{0,4},{4,0},{1,5},{5,1},{2,6},{6,2},{3,7},{7,3},{8,12},{12,8},{9,1... | collective-permute-start | bytes 319496 | tf_op jit(solution)/shard_map/ppermute | solution.py:189
  107.2 7.3 %collective-permute-start.18 = (s16[208,256]{1,0:T(8,128)(2,1)S(1)}, s16[208,256]{1,0:T(8,128)(2,1)S(1)}, u32[]{:S(2)}, u32[]{:S(2)}) collective-permute-start(s16[208,256]{1,0:T(8,128)(2,1)S(1)} %finish.3.refs_0_), channel_id=1, source_target_pairs={{0,8},{8,0},{16,24},{24,16},{1,9},{9,1},{17,25},{25,17},{2,10},{10... | collective-permute-start | bytes 319496 | tf_op jit(solution)/shard_map/ppermute | solution.py:189
